TPU v7x, 32 devices: a whole 2x2x4 slice. The times are simulated.
32 devices in a mesh: dp: 4 (over y, x), row: 2 (over core), col: 4 (over z).
Axes of the slice: x: 2, y: 2, z: 4, core: 2. Of those that a mesh axis runs over, the one named last changes fastest.
Arguments:
- tokens: bfloat16 [16384, 1024], P(('dp', 'row'), 'col'), may hold values from -16 to 16
- encoder: bfloat16 [4096, 1024], P(('dp', 'row'), 'col'), may hold values from -6 to 6
- cotangent: bfloat16 [16384, 1024], P(('dp', 'row'), 'col'), may hold values from -6 to 6
- dec_lengths: int32 [4, 4], P('dp'), may hold values from 1 to 3070, as said below
- src_lengths: int32 [4, 4], P('dp'), may hold values from 113 to 351, as said below
- self_norm_gain: float32 [1024], P('col'), may hold values from 0.25 to 1.75
- self_norm_bias: float32 [1024], P('col'), may hold values from -1.8 to 1.8
- self_query: bfloat16 [1024, 1024], P('col', 'row'), may hold values from -0.1875 to 0.1875
- self_key: bfloat16 [1024, 1024], P('col', 'row'), may hold values from -0.1875 to 0.1875
- self_value: bfloat16 [1024, 1024], P('col', 'row'), may hold values from -0.1875 to 0.1875
- self_query_bias: float32 [1024], P(('row', 'col')), may hold values from -1.8 to 1.8
- self_value_bias: float32 [1024], P(('row', 'col')), may hold values from -1.8 to 1.8
- self_out: bfloat16 [1024, 1024], P('row', 'col'), may hold values from -3 to 3
- self_out_bias: float32 [1024], P('col'), may hold values from -1.8 to 1.8
- cross_norm_gain: float32 [1024], P('col'), may hold values from 0.25 to 1.75
- cross_norm_bias: float32 [1024], P('col'), may hold values from -1.8 to 1.8
- cross_query: bfloat16 [1024, 1024], P('col', 'row'), may hold values from -0.1875 to 0.1875
- cross_key: bfloat16 [1024, 1024], P('col', 'row'), may hold values from -0.1875 to 0.1875
- cross_value: bfloat16 [1024, 1024], P('col', 'row'), may hold values from -0.1875 to 0.1875
- cross_query_bias: float32 [1024], P(('row', 'col')), may hold values from -1.8 to 1.8
- cross_value_bias: float32 [1024], P(('row', 'col')), may hold values from -1.8 to 1.8
- cross_out: bfloat16 [1024, 1024], P('row', 'col'), may hold values from -3 to 3
- cross_out_bias: float32 [1024], P('col'), may hold values from -1.8 to 1.8
- hidden_norm_gain: float32 [1024], P('col'), may hold values from 0.25 to 1.75
- hidden_norm_bias: float32 [1024], P('col'), may hold values from -1.8 to 1.8
- hidden_in: bfloat16 [1024, 8192], P('col', 'row'), may hold values from -0.1875 to 0.1875
- hidden_in_bias: float32 [8192], P(('row', 'col')), may hold values from -1.8 to 1.8
- hidden_out: bfloat16 [8192, 1024], P('row', 'col'), may hold values from -0.0625 to 0.0625
- hidden_out_bias: float32 [1024], P('col'), may hold values from -1.8 to 1.8
Outputs:
- layer_out: bfloat16 [16384, 1024], P(('dp', 'row'), 'col')
- tokens_grad: float32 [16384, 1024], P(('dp', 'row'), 'col')
- encoder_grad: float32 [4096, 1024], P(('dp', 'row'), 'col')
- self_norm_gain_grad: float32 [1024], P('col')
- self_norm_bias_grad: float32 [1024], P('col')
- self_query_grad: float32 [1024, 1024], P('col', 'row')
- self_key_grad: float32 [1024, 1024], P('col', 'row')
- self_value_grad: float32 [1024, 1024], P('col', 'row')
- self_query_bias_grad: float32 [1024], P(('row', 'col'))
- self_value_bias_grad: float32 [1024], P(('row', 'col'))
- self_out_grad: float32 [1024, 1024], P('row', 'col')
- self_out_bias_grad: float32 [1024], P('col')
- cross_norm_gain_grad: float32 [1024], P('col')
- cross_norm_bias_grad: float32 [1024], P('col')
- cross_query_grad: float32 [1024, 1024], P('col', 'row')
- cross_key_grad: float32 [1024, 1024], P('col', 'row')
- cross_value_grad: float32 [1024, 1024], P('col', 'row')
- cross_query_bias_grad: float32 [1024], P(('row', 'col'))
- cross_value_bias_grad: float32 [1024], P(('row', 'col'))
- cross_out_grad: float32 [1024, 1024], P('row', 'col')
- cross_out_bias_grad: float32 [1024], P('col')
- hidden_norm_gain_grad: float32 [1024], P('col')
- hidden_norm_bias_grad: float32 [1024], P('col')
- hidden_in_grad: float32 [1024, 8192], P('col', 'row')
- hidden_in_bias_grad: float32 [8192], P(('row', 'col'))
- hidden_out_grad: float32 [8192, 1024], P('row', 'col')
- hidden_out_bias_grad: float32 [1024], P('col')
Inputs may be any that keep to these rules, and one draw needn't show every extreme that they name: `dec_lengths`: row s holds the lengths of the 4 documents of sequence s laid end to end from its first position; the remaining 4096 minus their sum positions, 1 to 512 of them, are padding. `src_lengths`: row s holds the lengths of the 4 source documents of sequence s laid end to end from its first encoder position; the remaining 1024 minus their sum positions, 1 to 128 of them, are padding. Decoder document k reads source document k, decoder padding reads source padding.
All inputs are finite; a program needn't handle non-finite values.
Results may differ from a plain program's by a relative error of at most 0.025.
Values may be sent and summed in bfloat16 or wider, within the bound.
A program may use at most 384 MiB of HBM per device.

v0:
```python
import jax
import jax.numpy as jnp
from jax import lax
from jax.sharding import PartitionSpec as P

D = 1024
HEAD_DIM = 64
SEQ_LEN = 4096
ENC = 1024
WIN = 1024


block_limit = 512
norm_epsilon = 1e-05
masked_fill = -1e30


def doc_numbers(lengths, positions):
    bounds = jnp.cumsum(lengths, axis=1, dtype=jnp.int32)
    places = jnp.arange(positions, dtype=jnp.int32)
    return jnp.sum(
        (places[None, :, None] >= bounds[:, None, :]).astype(jnp.int32), axis=2, dtype=jnp.int32
    )


def norm_forward(stream, norm_gain, norm_bias):
    totals = lax.psum((jnp.sum(stream, axis=1), jnp.sum(stream * stream, axis=1)), "col")
    center = totals[0] / D
    spread = totals[1] / D - center * center
    scaling = lax.rsqrt(spread + norm_epsilon)[:, None]
    normed = (stream - center[:, None]) * scaling
    return ((normed * norm_gain + norm_bias).astype(jnp.bfloat16), normed, scaling)


def norm_backward(incoming, normed, scaling, norm_gain):
    gain_grad = jnp.sum(incoming * normed, axis=0)
    bias_grad = jnp.sum(incoming, axis=0)
    upstream = incoming * norm_gain
    totals = lax.psum((jnp.sum(upstream, axis=1), jnp.sum(upstream * normed, axis=1)), "col")
    result = scaling * (upstream - totals[0][:, None] / D - normed * (totals[1][:, None] / D))
    return (result, gain_grad, bias_grad)


def gather_rows(stacked):
    return lax.all_gather(stacked, "row", axis=1, tiled=True)


def feature_sums(stacked):
    return lax.psum_scatter(stacked, "col", scatter_dimension=2, tiled=True)


def feature_cols(stacked):
    return lax.all_gather(stacked, "col", axis=2, tiled=True)


def stream_sums(stacked):
    return lax.psum_scatter(
        stacked.astype(jnp.bfloat16), "row", scatter_dimension=1, tiled=True
    ).astype(jnp.float32)


def grad_rows(stacked):
    return lax.all_gather(stacked, "row", axis=1, tiled=True)


def grad_heads(stacked):
    return lax.psum_scatter(
        stacked.astype(jnp.bfloat16), "col", scatter_dimension=2, tiled=True
    ).astype(jnp.float32)


def grad_cols(stacked):
    return lax.all_gather(stacked, "col", axis=2, tiled=True)


def grad_stream(stacked):
    return lax.psum_scatter(
        stacked.astype(jnp.bfloat16), "row", scatter_dimension=1, tiled=True
    ).astype(jnp.float32)


def block_inputs(number, queries, pairs, query_ids, key_ids, windowed):
    zero_index = jnp.zeros((), jnp.int32)
    length = query_ids.shape[1]
    query_rows = min(block_limit, length)
    blocks_per = length // query_rows
    heads_here = queries.shape[2]
    sequence = number // blocks_per
    begin_row = number % blocks_per * query_rows
    if windowed:
        key_rows = pairs.shape[2] - length + query_rows
        key_start = begin_row
    else:
        key_rows = pairs.shape[2]
        key_start = zero_index
    query_block = lax.dynamic_slice(
        queries,
        (sequence, begin_row, zero_index, zero_index),
        (1, query_rows, heads_here, HEAD_DIM),
    )[0]
    pair_block = lax.dynamic_slice(
        pairs,
        (zero_index, sequence, key_start, zero_index, zero_index),
        (2, 1, key_rows, heads_here, HEAD_DIM),
    )[:, 0]
    query_doc = lax.dynamic_slice(query_ids, (sequence, begin_row), (1, query_rows))[0]
    key_doc = lax.dynamic_slice(key_ids, (sequence, key_start), (1, key_rows))[0]
    allowed = query_doc[:, None] == key_doc[None, :]
    if windowed:
        distance = (
            jnp.arange(query_rows, dtype=jnp.int32)[:, None]
            + (pairs.shape[2] - length)
            - jnp.arange(key_rows, dtype=jnp.int32)[None, :]
        )
        allowed = allowed & (distance >= 0) & (distance < WIN)
    return (sequence, begin_row, key_start, query_block, pair_block[0], pair_block[1], allowed)


def attend_forward(query_block, key_block, value_block, allowed):
    scores = jnp.einsum(
        "qhd,khd->hqk", query_block, key_block, preferred_element_type=jnp.float32
    ) * HEAD_DIM ** (-0.5)
    masked = jnp.where(allowed[None], scores, masked_fill)
    highest = jnp.max(masked, axis=2, keepdims=True)
    log_total = jnp.log(jnp.sum(jnp.exp(masked - highest), axis=2, keepdims=True)) + highest
    shares = jnp.exp(masked - log_total).astype(jnp.bfloat16)
    mixed_out = jnp.einsum("hqk,khd->qhd", shares, value_block, preferred_element_type=jnp.float32)
    return (mixed_out, log_total)


def attend_backward(query_block, key_block, value_block, allowed, grad_block, log_total):
    scaling = HEAD_DIM ** (-0.5)
    scores = (
        jnp.einsum("qhd,khd->hqk", query_block, key_block, preferred_element_type=jnp.float32)
        * scaling
    )
    masked = jnp.where(allowed[None], scores, masked_fill)
    shares = jnp.exp(masked - log_total)
    value_grad = jnp.einsum(
        "hqk,qhd->khd", shares.astype(jnp.bfloat16), grad_block, preferred_element_type=jnp.float32
    )
    share_grad = jnp.einsum(
        "qhd,khd->hqk", grad_block, value_block, preferred_element_type=jnp.float32
    )
    inner_sum = jnp.sum(shares * share_grad, axis=2, keepdims=True)
    score_grad = (shares * (share_grad - inner_sum)).astype(jnp.bfloat16)
    query_grad = (
        jnp.einsum("hqk,khd->qhd", score_grad, key_block, preferred_element_type=jnp.float32)
        * scaling
    )
    key_grad = (
        jnp.einsum("hqk,qhd->khd", score_grad, query_block, preferred_element_type=jnp.float32)
        * scaling
    )
    return (query_grad, key_grad, value_grad)


def attention_forward(queries, pairs, query_ids, key_ids, windowed):
    block_count = query_ids.shape[0] * (query_ids.shape[1] // min(block_limit, query_ids.shape[1]))

    def one_block(number):
        picked = block_inputs(number, queries, pairs, query_ids, key_ids, windowed)
        return attend_forward(picked[3], picked[4], picked[5], picked[6])

    outputs, log_totals = lax.map(one_block, jnp.arange(block_count, dtype=jnp.int32))
    return (outputs.reshape(-1, outputs.shape[2] * outputs.shape[3]), log_totals)


def attention_backward(queries, pairs, query_ids, key_ids, windowed, grad_out, log_totals):
    query_rows = min(block_limit, query_ids.shape[1])
    block_count = query_ids.shape[0] * (query_ids.shape[1] // query_rows)

    def one_block(running, number):
        zero_index = jnp.zeros((), jnp.int32)
        picked = block_inputs(number, queries, pairs, query_ids, key_ids, windowed)
        grad_block = lax.dynamic_slice(
            grad_out,
            (picked[0], picked[1], zero_index, zero_index),
            (1, query_rows, grad_out.shape[2], grad_out.shape[3]),
        )[0]
        query_grad, key_grad, value_grad = attend_backward(
            picked[3], picked[4], picked[5], picked[6], grad_block, log_totals[number]
        )
        corner = (zero_index, picked[0], picked[2], zero_index, zero_index)
        current = lax.dynamic_slice(running, corner, (2, 1) + key_grad.shape)
        updated = lax.dynamic_update_slice(
            running, current + jnp.stack([key_grad, value_grad])[:, None], corner
        )
        return (updated, query_grad)

    pair_grads, query_grads = lax.scan(
        one_block, jnp.zeros(pairs.shape, jnp.float32), jnp.arange(block_count, dtype=jnp.int32)
    )
    return (query_grads.reshape(-1, query_grads.shape[2] * query_grads.shape[3]), pair_grads)


def local(
    tokens,
    encoder,
    cotangent,
    dec_lengths,
    src_lengths,
    self_norm_gain,
    self_norm_bias,
    self_query,
    self_key,
    self_value,
    self_query_bias,
    self_value_bias,
    self_out,
    self_out_bias,
    cross_norm_gain,
    cross_norm_bias,
    cross_query,
    cross_key,
    cross_value,
    cross_query_bias,
    cross_value_bias,
    cross_out,
    cross_out_bias,
    hidden_norm_gain,
    hidden_norm_bias,
    hidden_in,
    hidden_in_bias,
    hidden_out,
    hidden_out_bias,
):
    stream = tokens.astype(jnp.float32)
    query_rows = min(block_limit, SEQ_LEN)
    window_pad = -(-WIN // query_rows) * query_rows
    query_ids = doc_numbers(dec_lengths, SEQ_LEN)
    source_ids = doc_numbers(src_lengths, ENC)
    sequences = dec_lengths.shape[0]
    padded_ids = jnp.pad(query_ids, ((0, 0), (window_pad, 0)), constant_values=-1)
    heads_here = self_query_bias.shape[0] // HEAD_DIM
    self_low, self_normed, self_scaling = norm_forward(stream, self_norm_gain, self_norm_bias)
    self_rows = gather_rows(self_low[None])[0]
    self_weights = jnp.stack([self_query, self_key, self_value])
    self_sums = feature_sums(
        jnp.einsum("td,kdf->ktf", self_rows, self_weights, preferred_element_type=jnp.float32)
    )
    self_biases = jnp.stack([self_query_bias, jnp.zeros_like(self_query_bias), self_value_bias])
    self_heads = (self_sums + self_biases[:, None, :]).astype(jnp.bfloat16)
    self_queries = self_heads[0].reshape(sequences, SEQ_LEN, heads_here, HEAD_DIM)
    self_pairs = jnp.pad(
        self_heads[1:].reshape(2, sequences, SEQ_LEN, heads_here, HEAD_DIM),
        ((0, 0), (0, 0), (window_pad, 0), (0, 0), (0, 0)),
    )
    self_mixed, self_totals = attention_forward(
        self_queries, self_pairs, query_ids, padded_ids, True
    )
    self_cols = feature_cols(self_mixed.astype(jnp.bfloat16)[None])[0]
    self_branch = stream_sums(
        jnp.dot(self_cols, self_out, preferred_element_type=jnp.float32)[None]
    )[0]
    after_self = stream + (self_branch + self_out_bias)
    cross_low, cross_normed, cross_scaling = norm_forward(
        after_self, cross_norm_gain, cross_norm_bias
    )
    cross_rows = gather_rows(cross_low[None])[0]
    source_rows = gather_rows(encoder[None])[0]
    cross_weights = jnp.stack([cross_key, cross_value])
    cross_query_sums = feature_sums(
        jnp.dot(cross_rows, cross_query, preferred_element_type=jnp.float32)[None]
    )[0]
    cross_pair_sums = feature_sums(
        jnp.einsum("td,kdf->ktf", source_rows, cross_weights, preferred_element_type=jnp.float32)
    )
    cross_flat = (cross_query_sums + cross_query_bias).astype(jnp.bfloat16)
    cross_biases = jnp.stack([jnp.zeros_like(cross_value_bias), cross_value_bias])
    cross_pair_flat = (cross_pair_sums + cross_biases[:, None, :]).astype(jnp.bfloat16)
    cross_queries = cross_flat.reshape(sequences, SEQ_LEN, heads_here, HEAD_DIM)
    cross_pairs = cross_pair_flat.reshape(2, sequences, ENC, heads_here, HEAD_DIM)
    cross_mixed, cross_totals = attention_forward(
        cross_queries, cross_pairs, query_ids, source_ids, False
    )
    cross_cols = feature_cols(cross_mixed.astype(jnp.bfloat16)[None])[0]
    cross_branch = stream_sums(
        jnp.dot(cross_cols, cross_out, preferred_element_type=jnp.float32)[None]
    )[0]
    after_cross = after_self + (cross_branch + cross_out_bias)
    hidden_low, hidden_normed, hidden_scaling = norm_forward(
        after_cross, hidden_norm_gain, hidden_norm_bias
    )
    hidden_rows = gather_rows(hidden_low[None])[0]
    half_rows = hidden_rows.shape[0] // 2
    pieces = []
    for portion in range(2):
        rows_part = hidden_rows[portion * half_rows : (portion + 1) * half_rows]
        pieces.append(
            feature_sums(jnp.dot(rows_part, hidden_in, preferred_element_type=jnp.float32)[None])[0]
        )
    hidden_sums = jnp.concatenate(pieces, axis=0)
    hidden_pre = hidden_sums + hidden_in_bias
    activated = jax.nn.gelu(hidden_pre).astype(jnp.bfloat16)
    active_cols = feature_cols(activated[None])[0]
    hidden_branch = stream_sums(
        jnp.dot(active_cols, hidden_out, preferred_element_type=jnp.float32)[None]
    )[0]
    layer_out = (after_cross + (hidden_branch + hidden_out_bias)).astype(jnp.bfloat16)
    grad_final = cotangent.astype(jnp.float32)
    out_rows = grad_rows(grad_final.astype(jnp.bfloat16)[None])[0]
    hidden_out_bias_grad = jnp.sum(out_rows, axis=0, dtype=jnp.float32)
    hidden_out_grad = jnp.einsum(
        "tf,td->fd", active_cols, out_rows, preferred_element_type=jnp.float32
    )
    act_pieces = []
    for portion in range(2):
        rows_part = out_rows[portion * half_rows : (portion + 1) * half_rows]
        act_pieces.append(
            grad_heads(
                jnp.einsum("td,fd->tf", rows_part, hidden_out, preferred_element_type=jnp.float32)[
                    None
                ]
            )[0]
        )
    act_grad = jnp.concatenate(act_pieces, axis=0)
    pre_low = jax.vjp(jax.nn.gelu, hidden_pre)[1](act_grad)[0].astype(jnp.bfloat16)
    hidden_in_bias_grad = jnp.sum(pre_low, axis=0, dtype=jnp.float32)
    pre_cols = grad_cols(pre_low[None])[0]
    hidden_in_grad = jnp.einsum(
        "td,tf->df", hidden_rows, pre_cols, preferred_element_type=jnp.float32
    )
    rows_grad = jnp.einsum("tf,df->td", pre_cols, hidden_in, preferred_element_type=jnp.float32)
    hidden_back, hidden_norm_gain_grad, hidden_norm_bias_grad = norm_backward(
        grad_stream(rows_grad[None])[0], hidden_normed, hidden_scaling, hidden_norm_gain
    )
    grad_cross = grad_final + hidden_back
    cross_out_rows = grad_rows(grad_cross.astype(jnp.bfloat16)[None])[0]
    cross_out_bias_grad = jnp.sum(cross_out_rows, axis=0, dtype=jnp.float32)
    cross_out_grad = jnp.einsum(
        "tf,td->fd", cross_cols, cross_out_rows, preferred_element_type=jnp.float32
    )
    cross_mixed_grad = grad_heads(
        jnp.einsum("td,fd->tf", cross_out_rows, cross_out, preferred_element_type=jnp.float32)[None]
    )[0].astype(jnp.bfloat16)
    cross_query_part, cross_pair_part = attention_backward(
        cross_queries,
        cross_pairs,
        query_ids,
        source_ids,
        False,
        cross_mixed_grad.reshape(sequences, SEQ_LEN, heads_here, HEAD_DIM),
        cross_totals,
    )
    cross_query_low = cross_query_part.astype(jnp.bfloat16)
    cross_pair_low = cross_pair_part.reshape(2, sequences * ENC, heads_here * HEAD_DIM).astype(
        jnp.bfloat16
    )
    cross_query_bias_grad = jnp.sum(cross_query_low, axis=0, dtype=jnp.float32)
    cross_value_bias_grad = jnp.sum(cross_pair_low[1], axis=0, dtype=jnp.float32)
    cross_query_cols = grad_cols(cross_query_low[None])[0]
    cross_pair_cols = grad_cols(cross_pair_low)
    cross_query_grad = jnp.einsum(
        "td,tf->df", cross_rows, cross_query_cols, preferred_element_type=jnp.float32
    )
    cross_pair_grad = jnp.einsum(
        "td,ktf->kdf", source_rows, cross_pair_cols, preferred_element_type=jnp.float32
    )
    cross_rows_grad = jnp.einsum(
        "tf,df->td", cross_query_cols, cross_query, preferred_element_type=jnp.float32
    )
    source_rows_grad = jnp.einsum(
        "ktf,kdf->td", cross_pair_cols, cross_weights, preferred_element_type=jnp.float32
    )
    encoder_grad = grad_stream(source_rows_grad[None])[0]
    cross_back, cross_norm_gain_grad, cross_norm_bias_grad = norm_backward(
        grad_stream(cross_rows_grad[None])[0], cross_normed, cross_scaling, cross_norm_gain
    )
    grad_self = grad_cross + cross_back
    self_out_rows = grad_rows(grad_self.astype(jnp.bfloat16)[None])[0]
    self_out_bias_grad = jnp.sum(self_out_rows, axis=0, dtype=jnp.float32)
    self_out_grad = jnp.einsum(
        "tf,td->fd", self_cols, self_out_rows, preferred_element_type=jnp.float32
    )
    self_mixed_grad = grad_heads(
        jnp.einsum("td,fd->tf", self_out_rows, self_out, preferred_element_type=jnp.float32)[None]
    )[0].astype(jnp.bfloat16)
    self_query_part, self_pair_part = attention_backward(
        self_queries,
        self_pairs,
        query_ids,
        padded_ids,
        True,
        self_mixed_grad.reshape(sequences, SEQ_LEN, heads_here, HEAD_DIM),
        self_totals,
    )
    self_pair_core = self_pair_part[:, :, window_pad:].reshape(
        2, sequences * SEQ_LEN, heads_here * HEAD_DIM
    )
    self_grads_low = jnp.concatenate([self_query_part[None], self_pair_core], axis=0).astype(
        jnp.bfloat16
    )
    self_query_bias_grad = jnp.sum(self_grads_low[0], axis=0, dtype=jnp.float32)
    self_value_bias_grad = jnp.sum(self_grads_low[2], axis=0, dtype=jnp.float32)
    self_grad_cols = grad_cols(self_grads_low)
    self_weight_grads = jnp.einsum(
        "td,ktf->kdf", self_rows, self_grad_cols, preferred_element_type=jnp.float32
    )
    self_rows_grad = jnp.einsum(
        "ktf,kdf->td", self_grad_cols, self_weights, preferred_element_type=jnp.float32
    )
    self_back, self_norm_gain_grad, self_norm_bias_grad = norm_backward(
        grad_stream(self_rows_grad[None])[0], self_normed, self_scaling, self_norm_gain
    )
    tokens_grad = grad_self + self_back
    summed = (
        lax.psum(self_weight_grads.astype(jnp.bfloat16), "dp").astype(jnp.float32),
        lax.psum(self_query_bias_grad.astype(jnp.bfloat16), "dp").astype(jnp.float32),
        lax.psum(self_value_bias_grad.astype(jnp.bfloat16), "dp").astype(jnp.float32),
        lax.psum(self_out_grad.astype(jnp.bfloat16), "dp").astype(jnp.float32),
        lax.psum(self_out_bias_grad.astype(jnp.bfloat16), "dp").astype(jnp.float32),
        lax.psum(cross_query_grad.astype(jnp.bfloat16), "dp").astype(jnp.float32),
        lax.psum(cross_pair_grad.astype(jnp.bfloat16), "dp").astype(jnp.float32),
        lax.psum(cross_query_bias_grad.astype(jnp.bfloat16), "dp").astype(jnp.float32),
        lax.psum(cross_value_bias_grad.astype(jnp.bfloat16), "dp").astype(jnp.float32),
        lax.psum(cross_out_grad.astype(jnp.bfloat16), "dp").astype(jnp.float32),
        lax.psum(cross_out_bias_grad.astype(jnp.bfloat16), "dp").astype(jnp.float32),
        lax.psum(hidden_in_grad.astype(jnp.bfloat16), "dp").astype(jnp.float32),
        lax.psum(hidden_in_bias_grad.astype(jnp.bfloat16), "dp").astype(jnp.float32),
        lax.psum(hidden_out_grad.astype(jnp.bfloat16), "dp").astype(jnp.float32),
        lax.psum(hidden_out_bias_grad.astype(jnp.bfloat16), "dp").astype(jnp.float32),
    )
    norm_sums = lax.psum(
        (
            self_norm_gain_grad,
            self_norm_bias_grad,
            cross_norm_gain_grad,
            cross_norm_bias_grad,
            hidden_norm_gain_grad,
            hidden_norm_bias_grad,
        ),
        ("dp", "row"),
    )
    return (
        layer_out,
        tokens_grad,
        encoder_grad,
        norm_sums[0],
        norm_sums[1],
        summed[0][0],
        summed[0][1],
        summed[0][2],
        summed[1],
        summed[2],
        summed[3],
        summed[4],
        norm_sums[2],
        norm_sums[3],
        summed[5],
        summed[6][0],
        summed[6][1],
        summed[7],
        summed[8],
        summed[9],
        summed[10],
        norm_sums[4],
        norm_sums[5],
        summed[11],
        summed[12],
        summed[13],
        summed[14],
    )


def solution(mesh):
    return jax.shard_map(
        local,
        mesh=mesh,
        in_specs=(
            P(("dp", "row"), "col"),
            P(("dp", "row"), "col"),
            P(("dp", "row"), "col"),
            P("dp", None),
            P("dp", None),
            P("col"),
            P("col"),
            P("col", "row"),
            P("col", "row"),
            P("col", "row"),
            P(("row", "col")),
            P(("row", "col")),
            P("row", "col"),
            P("col"),
            P("col"),
            P("col"),
            P("col", "row"),
            P("col", "row"),
            P("col", "row"),
            P(("row", "col")),
            P(("row", "col")),
            P("row", "col"),
            P("col"),
            P("col"),
            P("col"),
            P("col", "row"),
            P(("row", "col")),
            P("row", "col"),
            P("col"),
        ),
        out_specs=(
            P(("dp", "row"), "col"),
            P(("dp", "row"), "col"),
            P(("dp", "row"), "col"),
            P("col"),
            P("col"),
            P("col", "row"),
            P("col", "row"),
            P("col", "row"),
            P(("row", "col")),
            P(("row", "col")),
            P("row", "col"),
            P("col"),
            P("col"),
            P("col"),
            P("col", "row"),
            P("col", "row"),
            P("col", "row"),
            P(("row", "col")),
            P(("row", "col")),
            P("row", "col"),
            P("col"),
            P("col"),
            P("col"),
            P("col", "row"),
            P(("row", "col")),
            P("row", "col"),
            P("col"),
        ),
        check_vma=False,
    )
```

profile of v0, /device:TPU:8, one launch (start us, length us, event | category | flops | bytes accessed | tf_op | source)
XLA Modules:
  0.0 5132.6 jit_solution(2972771996888409431)
XLA Ops:
  9.3 15.4 all-reduce.9
  28.4 12.2 all-gather.35.cloned.1.call-done
  40.6 11.7 convolution_bitcast_fusion.2
  53.5 414.1 %reduce-scatter.21.cloned.1.call-done = f32[3,4096,128]{1,2,0:T(8,128)} async-done(((f32[3,4096,512]{1,2,0:T(8,128)}), f32[3,4096,128]{1,2,0:T(8,128)}) %reduce-scatter.21.cloned.1.call-update) | async-done | bytes 6291472 | tf_op jit(solution)/shard_map/reduce_scatter | solution.py:49
  474.3 90.0 %while.57 = (s32[]{:T(128)}, bf16[8,512,2,64]{1,3,2,0:T(8,128)(2,1)S(1)}, f32[8,2,512,1]{2,1,3,0:T(2,128)S(1)}, s32[8]{0:T(128)S(1)}, bf16[2,1,5120,2,64]{2,4,3,...) while((s32[]{:T(128)}, ...), condition=%wide.region_10.11_spmd, body=%wide.region_7.10_spmd.sunk | while | flops 424672768 | bytes 23261576 | solution.py:165
  568.5 80.1 %all-gather.21.cloned.1.call-done = bf16[1,4096,512]{1,2,0:T(8,128)(2,1)} async-done(((bf16[1,4096,128]{1,2,0:T(8,128)(2,1)}), bf16[1,4096,512]{1,2,0:T(8,128)(2,1)}) %all-gather.21.cloned.1.call-update) | async-done | bytes 4194320 | tf_op jit(solution)/shard_map/all_gather | solution.py:53
  653.6 11.1 reduce-scatter.23.cloned.1.call-done
  666.6 15.2 all-reduce.8
  704.2 73.3 %reduce-scatter.27.cloned.1.call-done = f32[2,1024,128]{1,2,0:T(8,128)} async-done(((f32[2,1024,512]{1,2,0:T(8,128)}), f32[2,1024,128]{1,2,0:T(8,128)}) %reduce-scatter.27.cloned.1.call-update) | async-done | bytes 1048592 | tf_op jit(solution)/shard_map/reduce_scatter | solution.py:49
  779.7 145.1 %reduce-scatter.25.cloned.1.call-done = f32[1,4096,128]{2,1,0:T(8,128)} async-done(((f32[1,4096,512]{2,1,0:T(8,128)}), f32[1,4096,128]{2,1,0:T(8,128)}) %reduce-scatter.25.cloned.1.call-update) | async-done | bytes 2097168 | tf_op jit(solution)/shard_map/reduce_scatter | solution.py:49
  931.5 65.4 %while.58 = (s32[]{:T(128)}, bf16[8,512,2,64]{1,3,2,0:T(8,128)(2,1)}, f32[8,2,512,1]{2,1,3,0:T(2,128)S(1)}, s32[8]{0:T(128)S(1)}, s32[1,4096]{1,0:T(1,128)S(1)},...) while((s32[]{:T(128)}, ...), condition=%wide.region_23.24_spmd, body=%wide.region_20.23_spmd.sunk | while | flops 280493056 | bytes 17738080 | solution.py:165
  1002.2 79.2 %all-gather.23.cloned.1.call-done = bf16[1,4096,512]{1,2,0:T(8,128)(2,1)} async-done(((bf16[1,4096,128]{1,2,0:T(8,128)(2,1)}), bf16[1,4096,512]{1,2,0:T(8,128)(2,1)}) %all-gather.23.cloned.1.call-update) | async-done | bytes 4194320 | tf_op jit(solution)/shard_map/all_gather | solution.py:53
  1100.9 15.2 all-reduce.7
  1118.9 13.1 convert_bitcast_fusion
  1132.1 12.8 convert_bitcast_fusion.1
  1145.2 14.5 convolution_bitcast_fusion
  1159.8 14.5 convolution_bitcast_fusion.1
  1174.3 237.5 %reduce-scatter.39.cloned.1.call-done = bf16[1,2048,1024]{2,1,0:T(8,128)(2,1)} async-done(((bf16[1,2048,4096]{2,1,0:T(8,128)(2,1)}), bf16[1,2048,1024]{2,1,0:T(8,128)(2,1)}) %reduce-scatter.39.cloned.1.call-update) | async-done | bytes 4194320 | tf_op jit(solution)/shard_map/reduce_scatter | solution.py:67
  1421.9 273.5 %reduce-scatter.37.cloned.1.call-done = bf16[1,2048,1024]{2,1,0:T(8,128)(2,1)} async-done(((bf16[1,2048,4096]{2,1,0:T(8,128)(2,1)}), bf16[1,2048,1024]{2,1,0:T(8,128)(2,1)}) %reduce-scatter.37.cloned.1.call-update) | async-done | bytes 4194320 | tf_op jit(solution)/shard_map/reduce_scatter | solution.py:67
  1705.5 544.9 %reduce-scatter.33.cloned.1.call-done = f32[1,2048,1024]{2,1,0:T(8,128)} async-done(((f32[1,2048,4096]{2,1,0:T(8,128)}), f32[1,2048,1024]{2,1,0:T(8,128)}) %reduce-scatter.33.cloned.1.call-update) | async-done | bytes 8388624 | tf_op jit(solution)/shard_map/reduce_scatter | solution.py:49
  2250.4 555.1 %reduce-scatter.31.cloned.1.call-done = f32[1,2048,1024]{2,1,0:T(8,128)} async-done(((f32[1,2048,4096]{2,1,0:T(8,128)}), f32[1,2048,1024]{2,1,0:T(8,128)}) %reduce-scatter.31.cloned.1.call-update) | async-done | bytes 8388624 | tf_op jit(solution)/shard_map/reduce_scatter | solution.py:49
  2805.5 21.5 fusion.106
  2827.9 561.7 %all-gather.27.cloned.1.call-done = bf16[1,4096,4096]{2,1,0:T(8,128)(2,1)} async-done(((bf16[1,4096,1024]{2,1,0:T(8,128)(2,1)}), bf16[1,4096,4096]{2,1,0:T(8,128)(2,1)}) %all-gather.27.cloned.1.call-update) | async-done | bytes 33554448 | tf_op jit(solution)/shard_map/all_gather | solution.py:73
  3389.6 17.5 fusion.134
  3407.2 543.4 %all-gather.25.cloned.1.call-done = bf16[1,4096,4096]{2,1,0:T(8,128)(2,1)} async-done(((bf16[1,4096,1024]{2,1,0:T(8,128)(2,1)}), bf16[1,4096,4096]{2,1,0:T(8,128)(2,1)}) %all-gather.25.cloned.1.call-update) | async-done | bytes 33554448 | tf_op jit(solution)/shard_map/all_gather | solution.py:53
  3950.6 17.5 fusion.137
  3972.7 17.8 all-reduce.6
  3995.9 10.5 all-gather.43.cloned.1.call-done
  4011.3 18.9 copy.165
  4030.2 10.1 copy.177
  4040.6 77.6 %reduce-scatter.49.cloned.1.call-done = bf16[128,4096]{1,0:T(8,128)(2,1)} async-done(((bf16[512,4096]{1,0:T(8,128)(2,1)}), bf16[128,4096]{1,0:T(8,128)(2,1)}) %reduce-scatter.49.cloned.1.call-update) | async-done | bytes 1048592
  4123.7 128.2 %while.60 = (s32[]{:T(128)}, f32[2,1,1024,2,64]{2,4,3,0,1:T(8,128)S(1)}, bf16[8,512,2,64]{1,3,2,0:T(8,128)(2,1)S(1)}, s32[8]{0:T(128)S(1)}, bf16[1,4096,2,64]{1,...) while((s32[]{:T(128)}, ...), condition=%wide.region_42.43_spmd.clone, body=%wide.region_40.42_spmd.clone.sunk | while | flops 688323584 | bytes 39360896 | solution.py:191
  4254.0 78.7 %all-gather.29.cloned.1.call-done = bf16[1,4096,512]{1,2,0:T(8,128)(2,1)} async-done(((bf16[1,4096,128]{1,2,0:T(8,128)(2,1)}), bf16[1,4096,512]{1,2,0:T(8,128)(2,1)}) %all-gather.29.cloned.1.call-update) | async-done | bytes 4194320 | tf_op jit(solution)/shard_map/all_gather | solution.py:73
  4337.6 11.1 reduce-scatter.43.cloned.1.call-done
  4352.0 15.5 all-reduce.5
  4372.7 12.6 all-gather.45.cloned.1.call-done
  4390.2 18.9 copy.167
  4409.1 10.1 copy.176
  4420.5 76.6 %reduce-scatter.51.cloned.1.call-done = bf16[128,4096]{1,0:T(8,128)(2,1)} async-done(((bf16[512,4096]{1,0:T(8,128)(2,1)}), bf16[128,4096]{1,0:T(8,128)(2,1)}) %reduce-scatter.51.cloned.1.call-update) | async-done | bytes 1048592
  4505.6 179.2 %while.59 = (s32[]{:T(128)}, f32[2,1,5120,2,64]{2,4,3,0,1:T(8,128)}, bf16[8,512,2,64]{1,3,2,0:T(8,128)(2,1)}, s32[8]{0:T(128)S(1)}, bf16[1,4096,2,64]{1,3,2,0:T(...) while((s32[]{:T(128)}, ...), condition=%wide.region_51.52_spmd, body=%wide.region_49.51_spmd.sunk | while | flops 1026555392 | bytes 65454588 | solution.py:191
  4706.1 19.4 fusion.124
  4728.8 191.1 %all-gather.31.cloned.1.call-done = bf16[3,4096,512]{2,1,0:T(8,128)(2,1)} async-done(((bf16[3,4096,128]{2,1,0:T(8,128)(2,1)}), bf16[3,4096,512]{2,1,0:T(8,128)(2,1)}) %all-gather.31.cloned.1.call-update) | async-done | bytes 12582928 | tf_op jit(solution)/shard_map/all_gather | solution.py:73
  4929.3 17.3 fusion.127
  4965.8 16.7 fusion.114
  4992.4 11.0 all-reduce.10
  5011.9 13.0 all-reduce.3
  5025.0 18.4 all-reduce.4
  5047.9 58.9 %all-reduce.14.cloned.1.call-done = (bf16[3,256,512]{1,2,0:T(8,128)(2,1)}, bf16[512,256]{1,0:T(8,128)(2,1)}, bf16[256,512]{1,0:T(8,128)(2,1)}, bf16[2,256,512]{1...) async-done(((bf16[3,256,512]{1,2,0:T(8,128)(2,1)}, bf16[512,256]{1,0:T(8,128)(2,1)}, bf16[256,512]{1,0:T(8,128)(2,1)}, ...) | async-done | bytes 6291472 | tf_op jit(solution)/shard_map/psum | solution.py:408
  (724 shorter events, 626.7 us)
Async XLA Ops:
  7.2 1138.0 %copy-start = (bf16[256,4096]{1,0:T(8,128)(2,1)S(1)}, bf16[256,4096]{1,0:T(8,128)(2,1)}, u32[]{:S(2)}) copy-start(bf16[256,4096]{1,0:T(8,128)(2,1)} %param.62) | copy-start | bytes 6291460
  7.2 33.4 all-gather.35.cloned.1.call-start
  27.9 439.7 %reduce-scatter.21.cloned.1.call-start = ((), (), s32[]{:S(2)}) async-start(), calls=%async_computation.16 | async-start | bytes 31457280 | tf_op jit(solution)/shard_map/reduce_scatter | solution.py:49
  52.4 596.2 %all-gather.21.cloned.1.call-start = ((), (), s32[]{:S(2)}) async-start(), calls=%async_computation.17 | async-start | bytes 5242880 | tf_op jit(solution)/shard_map/all_gather | solution.py:53
  564.3 89.1 %copy-start.45 = (s32[1,5120]{1,0:T(1,128)}, s32[1,5120]{1,0:T(1,128)S(1)}, u32[]{:S(2)}) copy-start(s32[1,5120]{1,0:T(1,128)S(1)} %get-tuple-element.1452) | copy-start | bytes 61444
  564.3 89.1 %copy-start.59 = (f32[8,2,512,1]{2,1,3,0:T(2,128)}, f32[8,2,512,1]{2,1,3,0:T(2,128)S(1)}, u32[]{:S(2)}) copy-start(f32[8,2,512,1]{2,1,3,0:T(2,128)S(1)} %get-tuple-element.1265) | copy-start | bytes 98308
  568.3 96.4 %copy-start.2 = (bf16[2048,256]{1,0:T(8,128)(2,1)S(1)}, bf16[2048,256]{1,0:T(8,128)(2,1)}, u32[]{:S(2)}) copy-start(bf16[2048,256]{1,0:T(8,128)(2,1)} %param.37) | copy-start | bytes 3145732
  568.3 96.4 %copy-start.61 = (f32[256]{0:T(256)S(1)}, f32[256]{0:T(256)}, u32[]{:S(2)}) copy-start(f32[256]{0:T(256)} %param.50) | copy-start | bytes 3076
  568.3 96.4 %reduce-scatter.23.cloned.1.call-start = ((), (), s32[]{:S(2)}) async-start(), calls=%async_computation.18 | async-start | bytes 3145728 | tf_op jit(solution)/shard_map/reduce_scatter | solution.py:57
  653.5 43.6 all-gather.37.cloned.1.call-start
  684.5 93.1 %reduce-scatter.27.cloned.1.call-start = ((), (), s32[]{:S(2)}) async-start(), calls=%async_computation.20 | async-start | bytes 5242880 | tf_op jit(solution)/shard_map/reduce_scatter | solution.py:49
  694.4 230.3 %reduce-scatter.25.cloned.1.call-start = ((), (), s32[]{:S(2)}) async-start(), calls=%async_computation.19 | async-start | bytes 10485760 | tf_op jit(solution)/shard_map/reduce_scatter | solution.py:49
  703.3 378.1 %all-gather.23.cloned.1.call-start = ((), (), s32[]{:S(2)}) async-start(), calls=%async_computation.21 | async-start | bytes 5242880 | tf_op jit(solution)/shard_map/all_gather | solution.py:53
  997.0 89.3 %copy-start.42 = (s32[1,1024]{1,0:T(1,128)}, s32[1,1024]{1,0:T(1,128)S(1)}, u32[]{:S(2)}) copy-start(s32[1,1024]{1,0:T(1,128)S(1)} %get-tuple-element.1448) | copy-start | bytes 12292
  997.0 89.3 %copy-start.44 = (s32[1,4096]{1,0:T(1,128)}, s32[1,4096]{1,0:T(1,128)S(1)}, u32[]{:S(2)}) copy-start(s32[1,4096]{1,0:T(1,128)S(1)} %get-tuple-element.1450) | copy-start | bytes 49156
  997.0 89.3 %copy-start.60 = (f32[8,2,512,1]{2,1,3,0:T(2,128)}, f32[8,2,512,1]{2,1,3,0:T(2,128)S(1)}, u32[]{:S(2)}) copy-start(f32[8,2,512,1]{2,1,3,0:T(2,128)S(1)} %get-tuple-element.1217) | copy-start | bytes 98308
  1002.1 95.4 %reduce-scatter.29.cloned.1.call-start = ((), (), s32[]{:S(2)}) async-start(), calls=%async_computation.22 | async-start | bytes 3145728 | tf_op jit(solution)/shard_map/reduce_scatter | solution.py:57
  1086.3 32.6 all-gather.41.cloned.1.call-start
  1086.9 58.3 %all-gather.39.cloned.1.call-start = ((), (), s32[]{:S(2)}) async-start(), calls=%async_computation.39 | async-start | bytes 3145728 | tf_op jit(solution)/shard_map/all_gather | solution.py:45
  1118.9 292.9 %reduce-scatter.39.cloned.1.call-start = ((), (), s32[]{:S(2)}) async-start(), calls=%async_computation.28 | async-start | bytes 20971520 | tf_op jit(solution)/shard_map/reduce_scatter | solution.py:67
  1132.1 563.3 %reduce-scatter.37.cloned.1.call-start = ((), (), s32[]{:S(2)}) async-start(), calls=%async_computation.27 | async-start | bytes 20971520 | tf_op jit(solution)/shard_map/reduce_scatter | solution.py:67
  1145.0 1105.4 %reduce-scatter.33.cloned.1.call-start = ((), (), s32[]{:S(2)}) async-start(), calls=%async_computation.24 | async-start | bytes 41943040 | tf_op jit(solution)/shard_map/reduce_scatter | solution.py:49
  1159.7 1645.8 %reduce-scatter.31.cloned.1.call-start = ((), (), s32[]{:S(2)}) async-start(), calls=%async_computation.23 | async-start | bytes 41943040 | tf_op jit(solution)/shard_map/reduce_scatter | solution.py:49
  1174.3 2215.3 %all-gather.27.cloned.1.call-start = ((), (), s32[]{:S(2)}) async-start(), calls=%async_computation.29 | async-start | bytes 41943040 | tf_op jit(solution)/shard_map/all_gather | solution.py:73
  1421.9 1383.6 %copy-start.63 = (f32[1024]{0:T(1024)S(1)}, f32[1024]{0:T(1024)}, u32[]{:S(2)}) copy-start(f32[1024]{0:T(1024)} %param.63) | copy-start | bytes 12292
  2827.0 1123.6 %all-gather.25.cloned.1.call-start = ((), (), s32[]{:S(2)}) async-start(), calls=%async_computation.25 | async-start | bytes 41943040 | tf_op jit(solution)/shard_map/all_gather | solution.py:53
  2827.6 1140.6 %reduce-scatter.41.cloned.1.call-start = ((), (), s32[]{:S(2)}) async-start(), calls=%async_computation.30 | async-start | bytes 3145728 | tf_op jit(solution)/shard_map/reduce_scatter | solution.py:77
  3407.1 583.4 %reduce-scatter.35.cloned.1.call-start = ((), (), s32[]{:S(2)}) async-start(), calls=%async_computation.26 | async-start | bytes 3145728 | tf_op jit(solution)/shard_map/reduce_scatter | solution.py:57
  3968.2 38.2 all-gather.43.cloned.1.call-start
  3995.5 122.7 %reduce-scatter.49.cloned.1.call-start = ((), (), s32[]{:S(2)}) async-start(), calls=%async_computation.43 | async-start | bytes 5242880
  4040.3 292.4 %all-gather.29.cloned.1.call-start = ((), (), s32[]{:S(2)}) async-start(), calls=%async_computation.31 | async-start | bytes 5242880 | tf_op jit(solution)/shard_map/all_gather | solution.py:73
  4253.9 94.8 %copy-start.3 = (bf16[2048,256]{1,0:T(8,128)(2,1)S(1)}, bf16[2048,256]{1,0:T(8,128)(2,1)}, u32[]{:S(2)}) copy-start(bf16[2048,256]{1,0:T(8,128)(2,1)} %param.37) | copy-start | bytes 3145732
  4253.9 94.8 %copy-start.8 = (bf16[1,2048,256]{2,1,0:T(8,128)(2,1)S(1)}, bf16[1,2048,256]{2,1,0:T(8,128)(2,1)}, u32[]{:S(2)}) copy-start(bf16[1,2048,256]{2,1,0:T(8,128)(2,1)} %reduce-scatter.23.cloned.1.call-done) | copy-start | bytes 3145732
  4253.9 94.8 %copy-start.56 = (f32[2048]{0:T(1024)S(1)}, f32[2048]{0:T(1024)}, u32[]{:S(2)}) copy-start(f32[2048]{0:T(1024)} %copy-done.55) | copy-start | bytes 24580
  4253.9 94.8 %copy-start.58 = (f32[2048]{0:T(1024)S(1)}, f32[2048]{0:T(1024)}, u32[]{:S(2)}) copy-start(f32[2048]{0:T(1024)} %copy-done.57) | copy-start | bytes 24580
  4253.9 94.8 %copy-start.62 = (f32[256]{0:T(256)S(1)}, f32[256]{0:T(256)}, u32[]{:S(2)}) copy-start(f32[256]{0:T(256)} %param.50) | copy-start | bytes 3076
  4254.0 94.8 %copy-start.66 = (f32[256]{0:T(256)S(1)}, f32[256]{0:T(256)}, u32[]{:S(2)}) copy-start(f32[256]{0:T(256)} %param.51) | copy-start | bytes 3076
  4254.0 94.8 %reduce-scatter.43.cloned.1.call-start = ((), (), s32[]{:S(2)}) async-start(), calls=%async_computation.32 | async-start | bytes 3145728 | tf_op jit(solution)/shard_map/reduce_scatter | solution.py:77
  4337.5 47.8 all-gather.45.cloned.1.call-start
  4372.7 124.4 %reduce-scatter.51.cloned.1.call-start = ((), (), s32[]{:S(2)}) async-start(), calls=%async_computation.44 | async-start | bytes 5242880
  4419.3 306.2 %all-gather.33.cloned.1.call-start = ((), (), s32[]{:S(2)}) async-start(), calls=%async_computation.35 | async-start | bytes 2621440 | tf_op jit(solution)/shard_map/all_gather | solution.py:73
  4420.5 499.4 %all-gather.31.cloned.1.call-start = ((), (), s32[]{:S(2)}) async-start(), calls=%async_computation.33 | async-start | bytes 15728640 | tf_op jit(solution)/shard_map/all_gather | solution.py:73
  4704.5 281.7 %reduce-scatter.47.cloned.1.call-start = ((), (), s32[]{:S(2)}) async-start(), calls=%async_computation.36 | async-start | bytes 786432 | tf_op jit(solution)/shard_map/reduce_scatter | solution.py:77
  4725.4 194.5 %copy-start.31 = (bf16[256,512]{0,1:T(8,128)(2,1)S(1)}, bf16[256,512]{0,1:T(8,128)(2,1)}, u32[]{:S(2)}) copy-start(bf16[256,512]{0,1:T(8,128)(2,1)} %copy-done.30) | copy-start | bytes 786436
  4725.4 194.5 %copy-start.33 = (bf16[256,512]{0,1:T(8,128)(2,1)S(1)}, bf16[256,512]{0,1:T(8,128)(2,1)}, u32[]{:S(2)}) copy-start(bf16[256,512]{0,1:T(8,128)(2,1)} %copy-done.32) | copy-start | bytes 786436
  4725.4 194.5 %copy-start.35 = (bf16[256,512]{0,1:T(8,128)(2,1)S(1)}, bf16[256,512]{0,1:T(8,128)(2,1)}, u32[]{:S(2)}) copy-start(bf16[256,512]{0,1:T(8,128)(2,1)} %copy-done.34) | copy-start | bytes 786436
  4728.7 279.1 %reduce-scatter.45.cloned.1.call-start = ((), (), s32[]{:S(2)}) async-start(), calls=%async_computation.34 | async-start | bytes 3145728 | tf_op jit(solution)/shard_map/reduce_scatter | solution.py:77
  4929.3 177.5 %all-reduce.14.cloned.1.call-start = ((), (), s32[]{:S(2)}) async-start(), calls=%async_computation.45 | async-start | bytes 12582912 | tf_op jit(solution)/shard_map/psum | solution.py:408
  (87 other events, 1032.1 us)
Sparse Core Ops, SparseCore 0:
  28.0 12.5 all-gather.34
  52.5 414.9 reduce-scatter.20
  568.4 80.1 all-gather.20
  653.6 11.0 reduce-scatter.22
  684.6 12.4 all-gather.36
  699.9 77.6 reduce-scatter.26
  780.0 144.7 reduce-scatter.24
  1002.2 79.1 all-gather.22
  1086.4 11.0 reduce-scatter.28
  1098.9 11.7 all-gather.40
  1119.0 12.5 all-gather.38
  1133.7 278.0 reduce-scatter.38
  1414.3 281.0 reduce-scatter.36
  1697.6 552.7 reduce-scatter.32
  2252.7 552.7 reduce-scatter.30
  2827.2 562.3 all-gather.26
  3391.0 559.5 all-gather.24
  3953.3 11.0 reduce-scatter.40
  3968.3 11.6 reduce-scatter.34
  3995.6 10.7 all-gather.42
  4040.5 77.6 reduce-scatter.48
  4254.0 78.6 all-gather.28
  4337.7 11.0 reduce-scatter.42
  4372.8 12.5 all-gather.44
  4419.4 77.6 reduce-scatter.50
  4499.2 45.4 all-gather.32
  4704.6 215.2 all-gather.30
  4922.8 9.3 reduce-scatter.46
  4935.0 10.7 reduce-scatter.44
  4963.7 142.9 all-reduce.13
where the time goes:
time: 5150 us; the launch traced here: 5130 us
  waiting for transfers between devices  4060 us (79%)
  matrix products  438 us (9%)
  other arithmetic  234 us (5%)
  local copies, waits for them, and re-layouts  170 us (3%)
  blocking collectives  124 us (2%)
  loops' own time  85.4 us (2%)
    reduce_scatter x5, waiting for transfers between devices, feature_sums(): return lax.psum_scatter(stacked, 'col', scatter_dimension=2, tiled=True)  1730 us
    all_gather x4, waiting for transfers between devices, grad_cols(): return lax.all_gather(stacked, 'col', axis=2, tiled=True)  831 us
    all_gather x3, waiting for transfers between devices, feature_cols(): return lax.all_gather(stacked, 'col', axis=2, tiled=True)  703 us
    reduce_scatter x2, waiting for transfers between devices, grad_heads(): lax.psum_scatter(stacked.astype(jnp.bfloat16), 'col', scatter_dimension=2...  511 us
    unnamed x32, waiting for transfers between devices  156 us
  transfers between devices with their start and end apart: 30, of which 23 were waited for; matrix products, arithmetic and copies ran while one was open for 8% of the time, Pallas kernels for 0%

commit v1 on v0

v1 whole, which is shorter than its diff:
```python
import functools

import jax
import jax.numpy as jnp
from jax import lax
from jax.experimental import pallas as pl
from jax.experimental.pallas import tpu as pltpu
from jax.sharding import PartitionSpec as P

D = 1024
HEAD_DIM = 64
SEQ_LEN = 4096
ENC = 1024
WIN = 1024

norm_epsilon = 1e-05
masked_fill = -1e30
low = jnp.bfloat16
f32 = jnp.float32
PARTS = 4
PAIR = 2 * HEAD_DIM
QUERY_ROWS = 256
VMEM = 56 * 1024 * 1024


def doc_numbers(lengths, positions):
    bounds = jnp.cumsum(lengths, axis=1, dtype=jnp.int32)
    places = jnp.arange(positions, dtype=jnp.int32)
    return jnp.sum(
        (places[None, :, None] >= bounds[:, None, :]).astype(jnp.int32), axis=2, dtype=jnp.int32
    )


def mm(a, b):
    return lax.dot_general(a, b, (((1,), (0,)), ((), ())), preferred_element_type=f32)


def mm_nt(a, b):
    return lax.dot_general(a, b, (((1,), (1,)), ((), ())), preferred_element_type=f32)


def mm_tn(a, b):
    return lax.dot_general(a, b, (((0,), (0,)), ((), ())), preferred_element_type=f32)


def head_masks():
    lane = lax.broadcasted_iota(jnp.int32, (1, PAIR), 1)
    first = jnp.where(lane < HEAD_DIM, 1.0, 0.0)
    return first.astype(low), (1.0 - first).astype(low), lane < HEAD_DIM


def attend_kernel(q_ref, k_ref, v_ref, qid_ref, kid_ref, o_ref, lse_ref, bias, *, span, windowed):
    rows = q_ref.shape[0]
    pairs = q_ref.shape[1] // PAIR
    start = pl.program_id(0) * rows if windowed else 0
    if windowed:
        start = pl.multiple_of(start, rows)
    allowed = qid_ref[...] == kid_ref[0:1, pl.ds(start, span)]
    if windowed:
        at_row = lax.broadcasted_iota(jnp.int32, (rows, span), 0)
        at_key = lax.broadcasted_iota(jnp.int32, (rows, span), 1)
        allowed = allowed & (at_key > at_row) & (at_key <= at_row + WIN)
    bias[...] = jnp.where(allowed, 0.0, masked_fill)
    first, second, is_first = head_masks()

    def one_pair(p, carry):
        lanes = pl.ds(pl.multiple_of(p * PAIR, PAIR), PAIR)
        q2 = q_ref[:, lanes]
        k2 = k_ref[pl.ds(start, span), lanes]
        v2 = v_ref[pl.ds(start, span), lanes]
        outs, logs = [], []
        for mask in (first, second):
            s = mm_nt(q2 * mask, k2) + bias[...]
            top = jnp.max(s, axis=1, keepdims=True)
            e = jnp.exp(s - top)
            total = jnp.sum(e, axis=1, keepdims=True)
            outs.append(mm(e.astype(low), v2) / total)
            logs.append(top + jnp.log(total))
        o_ref[:, lanes] = jnp.where(is_first, outs[0], outs[1]).astype(low)
        stats = jnp.where(is_first, logs[0], logs[1])
        turned = jnp.transpose(stats)
        lse_ref[p, 0:1, :] = turned[0:1]
        lse_ref[p, 1:2, :] = turned[HEAD_DIM : HEAD_DIM + 1]
        return carry

    lax.fori_loop(0, pairs, one_pair, 0)


def attend(q, k, v, qid, kid, windowed):
    tokens, width = q.shape
    keys = k.shape[0]
    pairs = width // PAIR
    rows = QUERY_ROWS
    span = WIN + rows if windowed else keys
    return pl.pallas_call(
        functools.partial(attend_kernel, span=span, windowed=windowed),
        grid=(tokens // rows,),
        in_specs=[
            pl.BlockSpec((rows, width), lambda i: (i, 0)),
            pl.BlockSpec((keys, width), lambda i: (0, 0)),
            pl.BlockSpec((keys, width), lambda i: (0, 0)),
            pl.BlockSpec((rows, 1), lambda i: (i, 0)),
            pl.BlockSpec((1, keys), lambda i: (0, 0)),
        ],
        out_specs=[
            pl.BlockSpec((rows, width), lambda i: (i, 0)),
            pl.BlockSpec((pairs, 8, rows), lambda i: (0, 0, i)),
        ],
        out_shape=[
            jax.ShapeDtypeStruct((tokens, width), low),
            jax.ShapeDtypeStruct((pairs, 8, tokens), f32),
        ],
        scratch_shapes=[pltpu.VMEM((rows, span), f32)],
        compiler_params=pltpu.CompilerParams(vmem_limit_bytes=VMEM),
        cost_estimate=pl.CostEstimate(
            flops=16 * tokens * span * width, bytes_accessed=4 * keys * width, transcendentals=0
        ),
        name="attend",
    )(q, k, v, qid[:, None], kid[None, :])


def attend_back_kernel(
    q_ref, k_ref, v_ref, do_ref, o_ref, lse_ref, qid_ref, kid_ref, dq_ref, dk_ref, dv_ref,
    bias, dk_sum, dv_sum, *, span, windowed,
):
    rows = q_ref.shape[0]
    pairs = q_ref.shape[1] // PAIR
    step = pl.program_id(0)
    start = pl.multiple_of(step * rows, rows) if windowed else 0
    keys = pl.ds(start, span)

    @pl.when(step == 0)
    def _():
        dk_sum[...] = jnp.zeros_like(dk_sum)
        dv_sum[...] = jnp.zeros_like(dv_sum)

    allowed = kid_ref[keys, :] == qid_ref[...]
    if windowed:
        at_key = lax.broadcasted_iota(jnp.int32, (span, rows), 0)
        at_row = lax.broadcasted_iota(jnp.int32, (span, rows), 1)
        allowed = allowed & (at_key > at_row) & (at_key <= at_row + WIN)
    bias[...] = jnp.where(allowed, 0.0, masked_fill)
    first, second, is_first = head_masks()

    def one_pair(p, carry):
        lanes = pl.ds(pl.multiple_of(p * PAIR, PAIR), PAIR)
        q2 = q_ref[:, lanes]
        k2 = k_ref[keys, lanes]
        v2 = v_ref[keys, lanes]
        do2 = do_ref[:, lanes]
        turned = jnp.transpose(do2.astype(f32) * o_ref[:, lanes].astype(f32))
        dk, dv, dqs = 0.0, 0.0, []
        for h, mask in enumerate((first, second)):
            qm, dom = q2 * mask, do2 * mask
            inner = jnp.sum(turned[h * HEAD_DIM : (h + 1) * HEAD_DIM], axis=0, keepdims=True)
            s = mm_nt(k2, qm) + bias[...]
            share = jnp.exp(s - lse_ref[p, h : h + 1, :])
            ds = (share * (mm_nt(v2, dom) - inner)).astype(low)
            dv = dv + mm(share.astype(low), dom)
            dk = dk + mm(ds, qm)
            dqs.append(mm_tn(ds, k2))
        dk_sum[keys, lanes] += dk
        dv_sum[keys, lanes] += dv
        dq_ref[:, lanes] = (jnp.where(is_first, dqs[0], dqs[1]) * HEAD_DIM**-0.5).astype(low)
        return carry

    lax.fori_loop(0, pairs, one_pair, 0)

    @pl.when(step == pl.num_programs(0) - 1)
    def _():
        dk_ref[...] = dk_sum[...].astype(low)
        dv_ref[...] = dv_sum[...].astype(low)


def attend_back(q, k, v, do, o, lse, qid, kid, windowed):
    tokens, width = q.shape
    keys = k.shape[0]
    pairs = width // PAIR
    rows = QUERY_ROWS
    span = WIN + rows if windowed else keys
    by_row = pl.BlockSpec((rows, width), lambda i: (i, 0))
    whole = pl.BlockSpec((keys, width), lambda i: (0, 0))
    return pl.pallas_call(
        functools.partial(attend_back_kernel, span=span, windowed=windowed),
        grid=(tokens // rows,),
        in_specs=[
            by_row,
            whole,
            whole,
            by_row,
            by_row,
            pl.BlockSpec((pairs, 8, rows), lambda i: (0, 0, i)),
            pl.BlockSpec((1, rows), lambda i: (0, i)),
            pl.BlockSpec((keys, 1), lambda i: (0, 0)),
        ],
        out_specs=[by_row, whole, whole],
        out_shape=[
            jax.ShapeDtypeStruct((tokens, width), low),
            jax.ShapeDtypeStruct((keys, width), low),
            jax.ShapeDtypeStruct((keys, width), low),
        ],
        scratch_shapes=[
            pltpu.VMEM((span, rows), f32),
            pltpu.VMEM((keys, width), f32),
            pltpu.VMEM((keys, width), f32),
        ],
        compiler_params=pltpu.CompilerParams(vmem_limit_bytes=VMEM),
        cost_estimate=pl.CostEstimate(
            flops=40 * tokens * span * width, bytes_accessed=8 * keys * width, transcendentals=0
        ),
        name="attend_back",
    )(q, k, v, do, o, lse, qid[None, :], kid[:, None])


ROOT = 0.7978845608028654
CUBE = 0.044715


def hidden_kernel(f_ref, w1_ref, b1_ref, w2_ref, act_ref, slope_ref, out_ref, total):
    step = pl.program_id(0) * pl.num_programs(1) + pl.program_id(1)
    last = pl.num_programs(0) * pl.num_programs(1) - 1

    @pl.when(step == 0)
    def _():
        total[...] = jnp.zeros_like(total)

    def one_part(t, carry):
        rows = pl.ds(pl.multiple_of(t * 256, 256), 256)
        h = mm(f_ref[rows, :], w1_ref[0]) + b1_ref[0]
        square = h * h
        bend = jnp.tanh(h * (ROOT + (ROOT * CUBE) * square))
        half = 0.5 + 0.5 * bend
        act = (h * half).astype(low)
        act_ref[0, rows, :] = act
        slope = half + (0.5 * h) * (1.0 - bend * bend) * (ROOT + (3.0 * ROOT * CUBE) * square)
        slope_ref[0, rows, :] = slope.astype(low)
        total[rows, :] += mm_nt(act, w2_ref[0])
        return carry

    lax.fori_loop(0, f_ref.shape[0] // 256, one_part, 0)

    @pl.when(step == last)
    def _():
        out_ref[...] = total[...].astype(low)


def hidden_forward(f, w1, b1, w2):
    parts, width, inner = w1.shape
    tokens = f.shape[0]
    block = min(512, inner)
    grid = (parts, inner // block)
    weight = pl.BlockSpec((1, width, block), lambda j, n: (j, 0, n))
    active = pl.BlockSpec((1, tokens, block), lambda j, n: (j, 0, n))
    return pl.pallas_call(
        hidden_kernel,
        grid=grid,
        in_specs=[
            pl.BlockSpec((tokens, width), lambda j, n: (0, 0)),
            weight,
            pl.BlockSpec((1, 1, block), lambda j, n: (j, 0, n)),
            weight,
        ],
        out_specs=[active, active, pl.BlockSpec((tokens, width), lambda j, n: (0, 0))],
        out_shape=[
            jax.ShapeDtypeStruct((parts, tokens, inner), low),
            jax.ShapeDtypeStruct((parts, tokens, inner), low),
            jax.ShapeDtypeStruct((tokens, width), low),
        ],
        scratch_shapes=[pltpu.VMEM((tokens, width), f32)],
        compiler_params=pltpu.CompilerParams(vmem_limit_bytes=VMEM),
        cost_estimate=pl.CostEstimate(
            flops=4 * tokens * width * parts * inner,
            bytes_accessed=8 * width * parts * inner,
            transcendentals=0,
        ),
        name="hidden_forward",
    )(f, w1, b1, w2)


def hidden_back_kernel(
    dz_ref, dzt_ref, ft_ref, w1_ref, w2_ref, act_ref, slope_ref,
    g1_ref, g2_ref, gb_ref, df_ref, dh_low, total,
):
    step = pl.program_id(0) * pl.num_programs(1) + pl.program_id(1)
    last = pl.num_programs(0) * pl.num_programs(1) - 1

    @pl.when(step == 0)
    def _():
        total[...] = jnp.zeros_like(total)

    gb_ref[...] = jnp.zeros_like(gb_ref)

    def one_part(t, carry):
        rows = pl.ds(pl.multiple_of(t * 256, 256), 256)
        dh = (mm(dz_ref[rows, :], w2_ref[0]) * slope_ref[0, rows, :].astype(f32)).astype(low)
        dh_low[rows, :] = dh
        gb_ref[0] += jnp.sum(dh.astype(f32), axis=0, keepdims=True)
        total[rows, :] += mm_nt(dh, w1_ref[0])
        return carry

    lax.fori_loop(0, dz_ref.shape[0] // 256, one_part, 0)

    def one_grad(t, carry):
        rows = pl.ds(pl.multiple_of(t * 256, 256), 256)
        g2_ref[0, rows, :] = mm(dzt_ref[rows, :], act_ref[0]).astype(low)
        g1_ref[0, rows, :] = mm(ft_ref[rows, :], dh_low[...]).astype(low)
        return carry

    lax.fori_loop(0, ft_ref.shape[0] // 256, one_grad, 0)

    @pl.when(step == last)
    def _():
        df_ref[...] = total[...].astype(low)


def hidden_backward(dz, f, w1, w2, act, slope):
    parts, width, inner = w1.shape
    tokens = f.shape[0]
    block = min(512, inner)
    grid = (parts, inner // block)
    weight = pl.BlockSpec((1, width, block), lambda j, n: (j, 0, n))
    active = pl.BlockSpec((1, tokens, block), lambda j, n: (j, 0, n))
    whole = pl.BlockSpec((tokens, width), lambda j, n: (0, 0))
    turned = pl.BlockSpec((width, tokens), lambda j, n: (0, 0))
    return pl.pallas_call(
        hidden_back_kernel,
        grid=grid,
        in_specs=[whole, turned, turned, weight, weight, active, active],
        out_specs=[weight, weight, pl.BlockSpec((1, 1, block), lambda j, n: (j, 0, n)), whole],
        out_shape=[
            jax.ShapeDtypeStruct(w1.shape, low),
            jax.ShapeDtypeStruct(w1.shape, low),
            jax.ShapeDtypeStruct((parts, 1, inner), f32),
            jax.ShapeDtypeStruct((tokens, width), low),
        ],
        scratch_shapes=[pltpu.VMEM((tokens, block), low), pltpu.VMEM((tokens, width), f32)],
        compiler_params=pltpu.CompilerParams(vmem_limit_bytes=VMEM),
        cost_estimate=pl.CostEstimate(
            flops=8 * tokens * width * parts * inner,
            bytes_accessed=16 * width * parts * inner,
            transcendentals=0,
        ),
        name="hidden_backward",
    )(dz, dz.T, f.T, w1, w2, act, slope)


def norm_forward(stream, gain, bias):
    center = jnp.mean(stream, axis=1, keepdims=True)
    spread = jnp.mean(stream * stream, axis=1, keepdims=True) - center * center
    scaling = lax.rsqrt(spread + norm_epsilon)
    normed = (stream - center) * scaling
    return (normed * gain + bias).astype(low), normed, scaling


def norm_backward(incoming, normed, scaling, gain):
    gain_grad = jnp.sum(incoming * normed, axis=0)
    bias_grad = jnp.sum(incoming, axis=0)
    upstream = incoming * gain
    mean_up = jnp.mean(upstream, axis=1, keepdims=True)
    mean_both = jnp.mean(upstream * normed, axis=1, keepdims=True)
    return scaling * (upstream - mean_up - normed * mean_both), gain_grad, bias_grad


def build_local(mesh):
    n_dp, n_col = mesh.shape["dp"], mesh.shape["col"]

    def swap(x):
        return lax.ppermute(x, "row", [(0, 1), (1, 0)])

    def from_col(x, k):
        return lax.ppermute(x, "col", [(i, (i - k) % n_col) for i in range(n_col)])

    def to_col(x, k):
        return lax.ppermute(x, "col", [(i, (i + k) % n_col) for i in range(n_col)])

    def across(x, bit):
        return lax.ppermute(x, "dp", [(i, i ^ bit) for i in range(n_dp)])

    def plane_gather(x):
        half = x.shape[0] // 2
        by_x, by_y = across(x, 1), across(x, 2)
        far = jnp.concatenate([across(by_x[:half], 2), across(by_y[half:], 1)], axis=0)
        return [x, by_x, by_y, far]

    def plane_scatter(parts):
        half = parts[0].shape[0] // 2
        a, b = [p[:half] for p in parts], [p[half:] for p in parts]
        got = across(jnp.stack([a[1], a[3]]), 1)
        a0, a2 = a[0] + got[0], a[2] + got[1]
        got = across(jnp.stack([b[2], b[3]]), 2)
        b0, b1 = b[0] + got[0], b[1] + got[1]
        a0 = a0 + across(a2, 2)
        b0 = b0 + across(b1, 1)
        return jnp.concatenate([a0, b0], axis=0)

    def local(
        tokens, encoder, cotangent, dec_lengths, src_lengths,
        self_norm_gain, self_norm_bias, self_query, self_key, self_value,
        self_query_bias, self_value_bias, self_out, self_out_bias,
        cross_norm_gain, cross_norm_bias, cross_query, cross_key, cross_value,
        cross_query_bias, cross_value_bias, cross_out, cross_out_bias,
        hidden_norm_gain, hidden_norm_bias, hidden_in, hidden_in_bias,
        hidden_out, hidden_out_bias,
    ):
        row, col = lax.axis_index("row"), lax.axis_index("col")
        place = lax.axis_index("dp") % PARTS
        wide = tokens.shape[1]
        chunk = tokens.shape[0] // n_col
        span = 2 * chunk

        def by_row(own, other):
            return jnp.where(
                row == 0,
                jnp.concatenate([own, other], axis=0),
                jnp.concatenate([other, own], axis=0),
            )

        def row_gather(own):
            return by_row(own, swap(own))

        def row_scatter(partial):
            half = partial.shape[0] // 2
            away = lax.dynamic_slice_in_dim(partial, (1 - row) * half, half, 0)
            mine = lax.dynamic_slice_in_dim(partial, row * half, half, 0)
            return mine.astype(f32) + swap(away.astype(low)).astype(f32)

        def spread_rows(x):
            cut = x.reshape(2, 2, chunk, wide)
            own = lax.dynamic_index_in_dim(cut, row, 1, keepdims=False)
            other = swap(lax.dynamic_index_in_dim(cut, 1 - row, 1, keepdims=False))
            every = by_row(own, other)
            pieces = []
            for k in range(n_col):
                piece = lax.dynamic_index_in_dim(every, (col - k) % n_col, 0, keepdims=False)
                pieces.append(from_col(piece, k) if k else piece)
            return jnp.concatenate(pieces, axis=1)

        def collect_rows(x):
            every = jnp.zeros((n_col, chunk, wide), x.dtype)
            for k in range(n_col):
                piece = x[:, k * wide : (k + 1) * wide]
                piece = to_col(piece, k) if k else piece
                every = lax.dynamic_update_index_in_dim(every, piece, (col - k) % n_col, 0)
            own = lax.dynamic_slice_in_dim(every, 2 * row, 2, 0)
            other = swap(lax.dynamic_slice_in_dim(every, 2 * (1 - row), 2, 0))
            both = jnp.where(
                row == 0, jnp.stack([own, other], axis=1), jnp.stack([other, own], axis=1)
            )
            return both.reshape(n_col * chunk, wide)

        def in_order(parts):
            stacked = jnp.stack(parts)
            return [
                lax.dynamic_index_in_dim(stacked, i ^ place, 0, keepdims=False)
                for i in range(PARTS)
            ]

        def weights_of(arrays):
            def own(j):
                cuts = []
                for w in arrays:
                    size = w.shape[1] // PARTS
                    cuts.append(lax.dynamic_slice_in_dim(w, (place ^ j) * size, size, 1))
                return jnp.concatenate(cuts, axis=1)

            mine = own(0)
            rest = jnp.concatenate([from_col(mine, k) for k in range(1, n_col)], axis=0)
            return [
                jnp.concatenate([own(j), part], axis=0)
                for j, part in enumerate(plane_gather(rest))
            ]

        def grads_of(parts):
            mine = plane_scatter(parts)
            total = mine[:wide].astype(f32)
            for k in range(1, n_col):
                total = total + to_col(mine[k * wide : (k + 1) * wide], k).astype(f32)
            bit = PARTS
            while bit < n_dp:
                total = total + across(total.astype(low), bit).astype(f32)
                bit *= 2
            return in_order(plane_gather(total.astype(low)))

        feature_vectors = jnp.stack([
            self_norm_gain, self_norm_bias, self_out_bias, cross_norm_gain, cross_norm_bias,
            cross_out_bias, hidden_norm_gain, hidden_norm_bias, hidden_out_bias,
        ])
        column_vectors = jnp.concatenate(
            [self_query_bias, self_value_bias, cross_query_bias, cross_value_bias, hidden_in_bias]
        )
        gathered = lax.all_gather(feature_vectors, "col", axis=0)
        rolled = lax.dynamic_slice_in_dim(jnp.concatenate([gathered, gathered]), col, n_col, 0)
        vectors = jnp.moveaxis(rolled, 0, 1).reshape(feature_vectors.shape[0], n_col * wide)
        (gain1, shift1, out_bias1, gain2, shift2, out_bias2, gain3, shift3, out_bias3) = vectors
        columns = lax.all_gather(column_vectors, "col", axis=0)

        def column_vector(start, size):
            flat = columns[:, start : start + size].reshape(-1)
            parts = flat.reshape(PARTS, -1)
            return jnp.concatenate(
                [
                    lax.dynamic_index_in_dim(parts, place ^ j, 0, keepdims=False)
                    for j in range(PARTS)
                ]
            )

        size = self_query_bias.shape[0]
        q_bias1 = column_vector(0, size)
        v_bias1 = column_vector(size, size)
        q_bias2 = column_vector(2 * size, size)
        v_bias2 = column_vector(3 * size, size)
        hidden_bias = column_vector(4 * size, hidden_in_bias.shape[0])

        self_parts = weights_of([self_query, self_key, self_value, self_out.T])
        cross_parts = weights_of([cross_query, cross_key, cross_value, cross_out.T])
        w1 = jnp.stack(weights_of([hidden_in]))
        w2 = jnp.stack(weights_of([hidden_out.T]))
        step = self_query.shape[1] // PARTS

        def columns_of(parts, index):
            return jnp.concatenate(
                [p[:, index * step : (index + 1) * step] for p in parts], axis=1
            )

        wq1, wk1, wv1, wo1 = [columns_of(self_parts, i) for i in range(4)]
        wq2, wk2, wv2, wo2 = [columns_of(cross_parts, i) for i in range(4)]

        dec_ids = doc_numbers(dec_lengths, SEQ_LEN)[0]
        src_ids = doc_numbers(src_lengths, ENC)[0]
        padded = jnp.pad(dec_ids, (WIN, 0), constant_values=-1)
        key_ids = lax.dynamic_slice_in_dim(padded, col * span, WIN + span, 0)
        query_ids = key_ids[WIN:]

        scale = low(HEAD_DIM**-0.5)
        stream = spread_rows(tokens).astype(f32)
        a_own, normed1, scaling1 = norm_forward(stream, gain1, shift1)
        a = row_gather(a_own)
        before = lax.ppermute(a_own, "col", [(i, i + 1) for i in range(n_col - 1)])
        before = jnp.concatenate([before[:, wide:], before[:, :wide]], axis=1)
        a_ext = jnp.concatenate([row_gather(before), a], axis=0)
        q1 = (mm(a, wq1) + q_bias1).astype(low) * scale
        k1 = mm(a_ext, wk1).astype(low)
        v1 = (mm(a_ext, wv1) + v_bias1).astype(low)
        o1, lse1 = attend(q1, k1, v1, query_ids, key_ids, True)
        x1 = stream + (row_scatter(mm_nt(o1, wo1)) + out_bias1)

        c_own, normed2, scaling2 = norm_forward(x1, gain2, shift2)
        c = row_gather(c_own)
        enc = row_gather(
            jnp.concatenate(
                [encoder] + [from_col(encoder, k) for k in range(1, n_col)], axis=1
            )
        )
        q2 = (mm(c, wq2) + q_bias2).astype(low) * scale
        k2 = mm(enc, wk2).astype(low)
        v2 = (mm(enc, wv2) + v_bias2).astype(low)
        o2, lse2 = attend(q2, k2, v2, query_ids, src_ids, False)
        x2 = x1 + (row_scatter(mm_nt(o2, wo2)) + out_bias2)

        f_own, normed3, scaling3 = norm_forward(x2, gain3, shift3)
        f = row_gather(f_own)
        act, slope, branch = hidden_forward(f, w1, hidden_bias.reshape(PARTS, 1, -1), w2)
        layer_out = collect_rows((x2 + (row_scatter(branch) + out_bias3)).astype(low))

        dz_own = spread_rows(cotangent)
        dz = row_gather(dz_own)
        g1, g2, hidden_bias_grad, df = hidden_backward(dz, f, w1, w2, act, slope)
        g1_parts = grads_of([g1[j] for j in range(PARTS)])
        g2_parts = grads_of([g2[j] for j in range(PARTS)])
        back3, gain_grad3, shift_grad3 = norm_backward(row_scatter(df), normed3, scaling3, gain3)
        dx2 = dz_own.astype(f32) + back3

        dyc_own = dx2.astype(low)
        dyc = row_gather(dyc_own)
        doc = mm(dyc, wo2).astype(low)
        dq2, dk2, dv2 = attend_back(q2, k2, v2, doc, o2, lse2, query_ids, src_ids, False)
        grads = [
            mm_tn(c, dq2).astype(low),
            mm_tn(enc, dk2).astype(low),
            mm_tn(enc, dv2).astype(low),
            mm_tn(dyc, o2).astype(low),
        ]

        def by_part(arrays):
            return [
                jnp.concatenate([g[:, j * step : (j + 1) * step] for g in arrays], axis=1)
                for j in range(PARTS)
            ]

        cross_grads = grads_of(by_part(grads))
        enc_back = row_scatter(mm_nt(dk2, wk2) + mm_nt(dv2, wv2))
        encoder_grad = enc_back[:, :wide]
        for k in range(1, n_col):
            encoder_grad = encoder_grad + to_col(
                enc_back[:, k * wide : (k + 1) * wide].astype(low), k
            ).astype(f32)
        back2, gain_grad2, shift_grad2 = norm_backward(
            row_scatter(mm_nt(dq2, wq2)), normed2, scaling2, gain2
        )
        dx1 = dx2 + back2

        dy_own = dx1.astype(low)
        dy = row_gather(dy_own)
        do = mm(dy, wo1).astype(low)
        dq1, dk1, dv1 = attend_back(q1, k1, v1, do, o1, lse1, query_ids, key_ids, True)
        da_ext = mm_nt(dk1, wk1) + mm_nt(dv1, wv1)
        da_before = row_scatter(da_ext[:WIN]).astype(low)
        da_after = lax.ppermute(da_before, "col", [(i + 1, i) for i in range(n_col - 1)])
        da_after = jnp.concatenate([da_after[:, -wide:], da_after[:, :-wide]], axis=1)
        da = row_scatter(da_ext[WIN:] + mm_nt(dq1, wq1)) + da_after.astype(f32)
        grads = [
            mm_tn(a, dq1).astype(low),
            mm_tn(a_ext, dk1).astype(low),
            mm_tn(a_ext, dv1).astype(low),
            mm_tn(dy, o1).astype(low),
        ]
        self_grads = grads_of(by_part(grads))
        back1, gain_grad1, shift_grad1 = norm_backward(da, normed1, scaling1, gain1)
        tokens_grad = collect_rows((dx1 + back1).astype(low)).astype(f32)

        def total(x):
            return jnp.sum(x, axis=0, dtype=f32)

        feature_grads = jnp.stack([
            gain_grad1, shift_grad1, total(dy_own), gain_grad2, shift_grad2, total(dyc_own),
            gain_grad3, shift_grad3, total(dz_own),
        ])
        count = feature_grads.shape[0]
        chunks = jnp.moveaxis(feature_grads.reshape(count, n_col, wide), 1, 0)
        chunks = lax.dynamic_slice_in_dim(
            jnp.concatenate([chunks, chunks]), (n_col - col) % n_col, n_col, 0
        )
        chunks = lax.psum(chunks, ("dp", "row", "col"))
        feature_grads = lax.dynamic_index_in_dim(chunks, col, 0, keepdims=False)
        column_grads = []
        for vector in (total(dq1), total(dv1), total(dq2), total(dv2), hidden_bias_grad):
            parts = vector.reshape(PARTS, -1)
            column_grads.append(
                jnp.concatenate(in_order([parts[j] for j in range(PARTS)])).reshape(n_col, -1)
            )
        column_grads = lax.psum(jnp.concatenate(column_grads, axis=1), ("dp", "col"))
        column_grads = lax.dynamic_index_in_dim(column_grads, col, 0, keepdims=False)

        def whole(parts, index=None):
            if index is not None:
                parts = [p[:, index * step : (index + 1) * step] for p in parts]
            return jnp.concatenate(parts, axis=1).astype(f32)

        return (
            layer_out,
            tokens_grad,
            encoder_grad,
            feature_grads[0],
            feature_grads[1],
            whole(self_grads, 0),
            whole(self_grads, 1),
            whole(self_grads, 2),
            column_grads[:size],
            column_grads[size : 2 * size],
            whole(self_grads, 3).T,
            feature_grads[2],
            feature_grads[3],
            feature_grads[4],
            whole(cross_grads, 0),
            whole(cross_grads, 1),
            whole(cross_grads, 2),
            column_grads[2 * size : 3 * size],
            column_grads[3 * size : 4 * size],
            whole(cross_grads, 3).T,
            feature_grads[5],
            feature_grads[6],
            feature_grads[7],
            whole(g1_parts),
            column_grads[4 * size :],
            whole(g2_parts).T,
            feature_grads[8],
        )

    return local


def solution(mesh):
    rows = P(("dp", "row"), "col")
    features = P("col")
    columns = P(("row", "col"))
    into, out_of = P("col", "row"), P("row", "col")
    attention = (into, into, into, columns, columns, out_of, features)
    norm = (features, features)
    weights = (
        norm
        + attention
        + norm
        + attention
        + norm
        + (into, columns, out_of, features)
    )
    return jax.shard_map(
        build_local(mesh),
        mesh=mesh,
        in_specs=(rows, rows, rows, P("dp", None), P("dp", None)) + weights,
        out_specs=(rows, rows, rows) + weights,
        check_vma=False,
    )
```

time: 5150 us -> 1310 us (0.25)
  waiting for transfers between devices: 4060 us -> 404 us
  matrix products: 438 us -> 60.5 us
  Pallas kernels: 0 us -> 215 us
  starting transfers between devices: 2.82 us -> 131 us
  other arithmetic: 234 us -> 144 us
  loops' own time: 85.4 us -> 0 us
    reduce_scatter x14 -> x0, waiting for transfers between devices: 2280 us -> none  [the longest x5 1730 us: feature_sums(): return lax.psum_scatter(stacked, 'col', scatter_dimension=2, tiled=True)]
    all_gather x13 -> x0, waiting for transfers between devices: 1570 us -> none  [the longest x4 831 us: grad_cols(): return lax.all_gather(stacked, 'col', axis=2, tiled=True)]
    ppermute x0 -> x112, waiting for transfers between devices: none -> 404 us  [the longest x21 142 us: to_col(): return lax.ppermute(x, 'col', [(i, (i + k) % n_col) for i in range(n_col)])]
    dot_general x135 -> x24, matrix products: 438 us -> 60.5 us  [the longest x8 25.4 us: mm(): lax.dot_general(a, b, (((1,), (0,)), ((), ())), preferred_element_type=f32)]
    pallas_call x0 -> x6, Pallas kernels: none -> 215 us  [the longest x2 70.7 us: attend_back(): pl.pallas_call(functools.partial(attend_back_kernel, span=span, windowed=...]
    unnamed x32 -> x0, waiting for transfers between devices: 156 us -> none
    ppermute x0 -> x112, starting transfers between devices: none -> 131 us  [the longest x48 48.1 us: across(): return lax.ppermute(x, 'dp', [(i, i ^ bit) for i in range(n_dp)])]
    another operation x4 -> x0, loops' own time: 85.4 us -> none  [the longest x2 53.3 us: attention_backward(): lax.scan(one_block, jnp.zeros(pairs.shape, jnp.float32), jnp.arange(block...]
  transfers between devices with their start and end apart: 30 -> 112, of which waited for: 23 -> 38; matrix products, arithmetic and copies ran while one was open for 8% -> 25% of each run, Pallas kernels for 0% -> 8%
where the time goes in v1:
time: 1310 us; the launch traced here: 1290 us
  waiting for transfers between devices  404 us (31%)
  Pallas kernels  215 us (16%)
  local copies, waits for them, and re-layouts  170 us (13%)
  blocking collectives  163 us (12%)
  other arithmetic  144 us (11%)
  starting transfers between devices  131 us (10%)
  matrix products  60.5 us (5%)
    ppermute x21, waiting for transfers between devices, to_col(): return lax.ppermute(x, 'col', [(i, (i + k) % n_col) for i in range(n_col)])  142 us
    ppermute x48, waiting for transfers between devices, across(): return lax.ppermute(x, 'dp', [(i, i ^ bit) for i in range(n_dp)])  126 us
    ppermute x21, waiting for transfers between devices, from_col(): return lax.ppermute(x, 'col', [(i, (i - k) % n_col) for i in range(n_col)])  102 us
    pallas_call x2, Pallas kernels, attend_back(): pl.pallas_call(functools.partial(attend_back_kernel, span=span, windowed=...  70.7 us
    psum x1, blocking collectives, local(): lax.psum(jnp.concatenate(column_grads, axis=1), ('dp', 'col'))  68.3 us
    unnamed x530, local copies, waits for them, and re-layouts  67.6 us
    pallas_call x1, Pallas kernels, hidden_backward(): pl.pallas_call(hidden_back_kernel, grid=grid, in_specs=[whole, turned, tu...  56.1 us
    pallas_call x2, Pallas kernels, attend(): pl.pallas_call(functools.partial(attend_kernel, span=span, windowed=windo...  49.3 us
  transfers between devices with their start and end apart: 112, of which 38 were waited for; matrix products, arithmetic and copies ran while one was open for 25% of the time, Pallas kernels for 8%

profile of v1, /device:TPU:8, one launch (start us, length us, event | category | flops | bytes accessed | tf_op | source)
XLA Modules:
  0.0 1292.9 jit_solution(11207507064063549939)
XLA Ops:
  13.9 40.6 %all-gather.3 = f32[4,1,1536]{2,1,0:T(1,128)S(1)} all-gather(f32[1,1,1536]{2,1,0:T(1,128)S(1)} %reshape.404), channel_id=3, replica_groups=mesh['dp'=4,'row'=2,'col'=4] {'col'}, dimensions={0}, use_global_device_ids=true | all-gather | bytes 30720 | tf_op jit(solution)/shard_map/all_gather | solution.py:495
  58.8 12.6 all-gather.2
  128.0 13.6 %collective-permute-done.5 = bf16[256,512]{0,1:T(8,128)(2,1)S(1)} collective-permute-done((bf16[256,512]{0,1:T(8,128)(2,1)}, bf16[256,512]{0,1:T(8,128)(2,1)S(1)}, u32[]{:S(2)}, u32[]{:S(2)}) %collective-permute-start.5) | collective-permute-done | bytes 262176 | tf_op jit(solution)/shard_map/ppermute | solution.py:371
  141.6 10.7 collective-permute-start.36
  165.1 60.9 %collective-permute-done.29 = bf16[256,1024]{1,0:T(8,128)(2,1)S(1)} collective-permute-done((bf16[256,1024]{1,0:T(8,128)(2,1)S(1)}, bf16[256,1024]{1,0:T(8,128)(2,1)S(1)}, u32[]{:S(2)}, u32[]{:S(2)}) %collective-permute-start.29) | collective-permute-done | bytes 524320 | tf_op jit(solution)/shard_map/ppermute | solution.py:371
  232.3 10.2 collective-permute-start.3
  248.4 5.8 collective-permute-done.1
  259.1 6.8 collective-permute-done.3
  268.9 10.1 collective-permute-done.50
  285.2 5.3 collective-permute-start.12
  297.3 17.9 %collective-permute-done.12 = bf16[512,1024]{0,1:T(8,128)(2,1)S(1)} collective-permute-done((bf16[512,1024]{0,1:T(8,128)(2,1)S(1)}, bf16[512,1024]{0,1:T(8,128)(2,1)S(1)}, u32[]{:S(2)}, u32[]{:S(2)}) %collective-permute-start.12) | collective-permute-done | bytes 1048608 | tf_op jit(solution)/shard_map/ppermute | solution.py:538
  316.0 9.3 maximum_select_fusion.3
  336.1 6.8 maximum_select_fusion.1
  350.6 27.4 %attend.2 = (bf16[1024,512]{1,0:T(8,128)(2,1)}, f32[4,8,1024]{2,1,0:T(8,128)}) custom-call(bf16[1024,512]{1,0:T(8,128)(2,1)} %fusion.17.q_ref, bf16[2048,512]{1,0:T(8,128)(2,1)} %convolution_convert_fusion.k_ref, bf16[2048,512]{1,0:T(8,128)(2,1)} %add_convert_fusion.v_ref, s32[1024,1]{1,0:T(8,128)} %copy.346.qid_ref, s32[1,2048]{1,0:T(1,128)} %bitcast.466), custom_call_target="tpu_custom_call" | custom-call | flops 10737418240 | bytes 4194304 | tf_op jit(solution)/shard_map/attend/pallas_call | solution.py:95
  396.1 14.0 %maximum_select_fusion.5 = bf16[1024,1024]{0,1:T(8,128)(2,1)} fusion(bf16[512,1024]{0,1:T(8,128)(2,1)S(1)} %collective-permute-done.52, bf16[512,256]{0,1:T(8,128)(2,1)S(1)} %copy-done.89, bf16[512,256]{0,1:T(8,128)(2,1)S(1)} %copy-done.87, bf16[512,256]{0,1:T(8,128)(2,1)S(1)} %copy-done.85, bf16[512,256]{0,1:T(8,128)(2,1)S(1)} %get-tuple-element.321, ...), kind=kLoop, calls=%fused_computation.43 | loop fusion | flops 22020096 | bytes 4194305 | tf_op jit(solution)/shard_map/jit(_where)/select_n | solution.py:412
  410.1 3.9 copy.381.dz_ref
  428.4 7.0 collective-permute-done.41
  438.3 11.7 collective-permute-done.34
  451.6 4.6 fusion.18.q_ref
  456.3 21.9 %attend.3 = (bf16[1024,512]{1,0:T(8,128)(2,1)}, f32[4,8,1024]{2,1,0:T(8,128)}) custom-call(bf16[1024,512]{1,0:T(8,128)(2,1)} %fusion.18.q_ref, bf16[1024,512]{1,0:T(8,128)(2,1)} %convolution_convert_fusion.9.k_ref, bf16[1024,512]{1,0:T(8,128)(2,1)} %add_convert_fusion.4.v_ref, s32[1024,1]{1,0:T(8,128)} %copy.346.qid_ref, s32[1,1024]{1,0:T(1,128)} %bitcast.474), custom_call_target="tpu_custom_call" | custom-call | flops 8589934592 | bytes 2097152 | tf_op jit(solution)/shard_map/attend/pallas_call | solution.py:95
  489.7 3.9 pad_maximum_fusion.w1_ref
  495.5 3.9 copy.372.f_ref
  499.5 38.7 %hidden_forward.1 = (bf16[4,1024,1024]{2,1,0:T(8,128)(2,1)}, bf16[4,1024,1024]{2,1,0:T(8,128)(2,1)}, bf16[1024,1024]{1,0:T(8,128)(2,1)}) custom-call(bf16[1024,1024]{1,0:T(8,128)(2,1)} %copy.372.f_ref, bf16[4,1024,1024]{2,1,0:T(8,128)(2,1)} %pad_maximum_fusion.w1_ref, f32[4,1,1024]{2,1,0:T(1,128)} %pad_maximum_fusion.59.b1_ref, ...), custom_call_target="tpu_custom_call" | custom-call | flops 17179869184 | bytes 33554432 | tf_op jit(solution)/shard_map/hidden_forward/pallas_call | solution.py:254
  538.2 56.1 %hidden_backward.1 = (bf16[4,1024,1024]{2,1,0:T(8,128)(2,1)}, bf16[4,1024,1024]{2,1,0:T(8,128)(2,1)}, f32[4,1,1024]{2,1,0:T(1,128)}, bf16[1024,1024]{1,0:T(8,128)(2,1)}) custom-call(bf16[1024,1024]{1,0:T(8,128)(2,1)} %copy.381.dz_ref, bf16[1024,1024]{1,0:T(8,128)(2,1)} %bitcast.426, bf16[1024,1024]{1,0:T(8,128)(2,1)} %bitcast.427, ...), custom_call_target="tpu_custom_call" | custom-call | flops 34359738368 | bytes 67108864 | tf_op jit(solution)/shard_map/hidden_backward/pallas_call | solution.py:325
  594.2 3.9 copy.382
  614.9 3.9 copy.373
  631.0 4.3 collective-permute-start.45
  642.0 12.4 collective-permute-done.45
  676.0 32.1 %attend_back.2 = (bf16[1024,512]{1,0:T(8,128)(2,1)}, bf16[1024,512]{1,0:T(8,128)(2,1)}, bf16[1024,512]{1,0:T(8,128)(2,1)}) custom-call(bf16[1024,512]{1,0:T(8,128)(2,1)} %fusion.18.q_ref, bf16[1024,512]{1,0:T(8,128)(2,1)} %convolution_convert_fusion.9.k_ref, bf16[1024,512]{1,0:T(8,128)(2,1)} %add_convert_fusion.4.v_ref, ...), custom_call_target="tpu_custom_call" | custom-call | flops 21474836480 | bytes 4194304 | tf_op jit(solution)/shard_map/attend_back/pallas_call | solution.py:183
  749.6 9.4 collective-permute-done.79
  765.5 15.9 %collective-permute-done.105 = bf16[512,1024]{1,0:T(8,128)(2,1)} collective-permute-done((bf16[512,1024]{1,0:T(8,128)(2,1)}, bf16[512,1024]{1,0:T(8,128)(2,1)}, u32[]{:S(2)}, u32[]{:S(2)}) %collective-permute-start.105) | collective-permute-done | bytes 1048608 | tf_op jit(solution)/shard_map/ppermute | solution.py:377
  787.7 15.6 %collective-permute-done.94 = bf16[512,1024]{1,0:T(8,128)(2,1)S(1)} collective-permute-done((bf16[512,1024]{1,0:T(8,128)(2,1)}, bf16[512,1024]{1,0:T(8,128)(2,1)S(1)}, u32[]{:S(2)}, u32[]{:S(2)}) %collective-permute-start.94) | collective-permute-done | bytes 1048608 | tf_op jit(solution)/shard_map/ppermute | solution.py:377
  808.8 33.8 %collective-permute-done.67 = bf16[512,256]{1,0:T(8,128)(2,1)S(1)} collective-permute-done((bf16[512,256]{1,0:T(8,128)(2,1)S(1)}, bf16[512,256]{1,0:T(8,128)(2,1)S(1)}, u32[]{:S(2)}, u32[]{:S(2)}) %collective-permute-start.67) | collective-permute-done | bytes 262176 | tf_op jit(solution)/shard_map/ppermute | solution.py:374
  849.0 28.6 %collective-permute-done.95 = bf16[256,1024]{1,0:T(8,128)(2,1)S(1)} collective-permute-done((bf16[256,1024]{1,0:T(8,128)(2,1)S(1)}, bf16[256,1024]{1,0:T(8,128)(2,1)S(1)}, u32[]{:S(2)}, u32[]{:S(2)}) %collective-permute-start.95) | collective-permute-done | bytes 524320 | tf_op jit(solution)/shard_map/ppermute | solution.py:374
  878.1 12.0 collective-permute-done.96
  896.1 38.6 %attend_back.3 = (bf16[1024,512]{1,0:T(8,128)(2,1)}, bf16[2048,512]{1,0:T(8,128)(2,1)}, bf16[2048,512]{1,0:T(8,128)(2,1)}) custom-call(bf16[1024,512]{1,0:T(8,128)(2,1)} %fusion.17.q_ref, bf16[2048,512]{1,0:T(8,128)(2,1)} %convolution_convert_fusion.k_ref, bf16[2048,512]{1,0:T(8,128)(2,1)} %add_convert_fusion.v_ref, ...), custom_call_target="tpu_custom_call" | custom-call | flops 26843545600 | bytes 8388608 | tf_op jit(solution)/shard_map/attend_back/pallas_call | solution.py:183
  934.7 4.1 convolution_convert_fusion.10
  963.2 68.3 %psum.15 = f32[4,1536]{1,0:T(4,128)S(1)} all-reduce(f32[4,1536]{1,0:T(4,128)S(1)} %constant_dynamic-update-slice_fusion.22), channel_id=1, replica_groups=mesh['dp'=4,'row'=2,'col'=4] {'dp','col'}, use_global_device_ids=true, to_apply=%region_30.31 | all-reduce | flops 6144 | bytes 49152 | tf_op jit(solution)/shard_map/psum | solution.py:641
  1051.6 19.9 %collective-permute-done.100 = bf16[128,1024]{1,0:T(8,128)(2,1)S(1)} collective-permute-done((bf16[128,1024]{1,0:T(8,128)(2,1)S(1)}, bf16[128,1024]{1,0:T(8,128)(2,1)S(1)}, u32[]{:S(2)}, u32[]{:S(2)}) %collective-permute-start.100) | collective-permute-done | bytes 262176 | tf_op jit(solution)/shard_map/ppermute | solution.py:377
  1087.6 5.6 copy.403
  1093.2 5.9 collective-permute-done.84
  1099.2 5.9 collective-permute-done.85
  1121.3 31.2 %collective-permute-done.88 = bf16[128,512]{0,1:T(8,128)(2,1)S(1)} collective-permute-done((bf16[128,512]{0,1:T(8,128)(2,1)S(1)}, bf16[128,512]{0,1:T(8,128)(2,1)S(1)}, u32[]{:S(2)}, u32[]{:S(2)}) %collective-permute-start.88) | collective-permute-done | bytes 131104 | tf_op jit(solution)/shard_map/ppermute | solution.py:377
  1161.6 17.0 %collective-permute-done.59 = bf16[512,1024]{0,1:T(8,128)(2,1)} collective-permute-done((bf16[512,1024]{0,1:T(8,128)(2,1)}, bf16[512,1024]{0,1:T(8,128)(2,1)}, u32[]{:S(2)}, u32[]{:S(2)}) %collective-permute-start.59) | collective-permute-done | bytes 1048608 | tf_op jit(solution)/shard_map/ppermute | solution.py:608
  1191.1 15.7 %collective-permute-done.60 = bf16[512,256]{0,1:T(8,128)(2,1)S(1)} collective-permute-done((bf16[512,256]{0,1:T(8,128)(2,1)}, bf16[512,256]{0,1:T(8,128)(2,1)S(1)}, u32[]{:S(2)}, u32[]{:S(2)}) %collective-permute-start.60) | collective-permute-done | bytes 262176 | tf_op jit(solution)/shard_map/ppermute | solution.py:374
  1217.5 14.2 %collective-permute-done.73 = bf16[256,512]{0,1:T(8,128)(2,1)S(1)} collective-permute-done((bf16[256,512]{0,1:T(8,128)(2,1)S(1)}, bf16[256,512]{0,1:T(8,128)(2,1)S(1)}, u32[]{:S(2)}, u32[]{:S(2)}) %collective-permute-start.73) | collective-permute-done | bytes 262176 | tf_op jit(solution)/shard_map/ppermute | solution.py:374
  1231.7 5.3 collective-permute-done.74
  1238.7 41.2 %psum.14 = f32[4,9,256]{2,0,1:T(4,128)S(1)} all-reduce(f32[4,9,256]{2,0,1:T(4,128)S(1)} %fusion.52), channel_id=1, replica_groups=mesh['dp'=4,'row'=2,'col'=4] {'dp','row','col'}, use_global_device_ids=true, to_apply=%region_25.26 | all-reduce | flops 9216 | bytes 73728 | tf_op jit(solution)/shard_map/psum | solution.py:633
  (1024 shorter events, 439.2 us)
Async XLA Ops:
  6.6 113.8 %collective-permute-start.16 = (bf16[256,512]{0,1:T(8,128)(2,1)}, bf16[256,512]{0,1:T(8,128)(2,1)}, u32[]{:S(2)}, u32[]{:S(2)}) collective-permute-start(bf16[256,512]{0,1:T(8,128)(2,1)} %pad_maximum_fusion.42), channel_id=1, source_target_pairs={{0,3},{1,0},{2,1},{3,2},{4,7},{5,4},{6,5},{7,6},{8,11},{9,8},{10,9... | collective-permute-start | bytes 786440 | tf_op jit(solution)/shard_map/ppermute | solution.py:371
  6.6 117.6 %collective-permute-start.17 = (bf16[256,512]{0,1:T(8,128)(2,1)}, bf16[256,512]{0,1:T(8,128)(2,1)}, u32[]{:S(2)}, u32[]{:S(2)}) collective-permute-start(bf16[256,512]{0,1:T(8,128)(2,1)} %pad_maximum_fusion.42), channel_id=1, source_target_pairs={{0,2},{1,3},{2,0},{3,1},{4,6},{5,7},{6,4},{7,5},{8,10},{9,11},{10,... | collective-permute-start | bytes 786440 | tf_op jit(solution)/shard_map/ppermute | solution.py:371
  9.6 115.1 %collective-permute-start.18 = (bf16[256,512]{0,1:T(8,128)(2,1)}, bf16[256,512]{0,1:T(8,128)(2,1)}, u32[]{:S(2)}, u32[]{:S(2)}) collective-permute-start(bf16[256,512]{0,1:T(8,128)(2,1)} %pad_maximum_fusion.42), channel_id=1, source_target_pairs={{0,1},{1,2},{2,3},{3,0},{4,5},{5,6},{6,7},{7,4},{8,9},{9,10},{10,1... | collective-permute-start | bytes 786440 | tf_op jit(solution)/shard_map/ppermute | solution.py:371
  12.3 143.2 %collective-permute-start.23 = (bf16[512,256]{0,1:T(8,128)(2,1)S(1)}, bf16[512,256]{0,1:T(8,128)(2,1)}, u32[]{:S(2)}, u32[]{:S(2)}) collective-permute-start(bf16[512,256]{0,1:T(8,128)(2,1)S(1)} %copy.364), channel_id=1, source_target_pairs={{0,3},{1,0},{2,1},{3,2},{4,7},{5,4},{6,5},{7,6},{8,11},{9,8},{10,9... | collective-permute-start | bytes 786440 | tf_op jit(solution)/shard_map/ppermute | solution.py:371
  12.4 143.2 %collective-permute-start.24 = (bf16[512,256]{0,1:T(8,128)(2,1)S(1)}, bf16[512,256]{0,1:T(8,128)(2,1)}, u32[]{:S(2)}, u32[]{:S(2)}) collective-permute-start(bf16[512,256]{0,1:T(8,128)(2,1)S(1)} %copy.364), channel_id=1, source_target_pairs={{0,2},{1,3},{2,0},{3,1},{4,6},{5,7},{6,4},{7,5},{8,10},{9,11},{10,... | collective-permute-start | bytes 786440 | tf_op jit(solution)/shard_map/ppermute | solution.py:371
  155.5 73.2 %collective-permute-start.37 = (bf16[256,1024]{1,0:T(8,128)(2,1)S(1)}, bf16[256,1024]{1,0:T(8,128)(2,1)S(1)}, u32[]{:S(2)}, u32[]{:S(2)}) collective-permute-start(bf16[256,1024]{1,0:T(8,128)(2,1)S(1)} %bitcast.434), channel_id=1, source_target_pairs={{0,2},{1,3},{2,0},{3,1},{4,6},{5,7},{6,4},{7,5},{8,10},{9,11},{10,... | collective-permute-start | bytes 1572872 | tf_op jit(solution)/shard_map/ppermute | solution.py:371
  155.6 75.2 %collective-permute-start.38 = (bf16[256,1024]{1,0:T(8,128)(2,1)S(1)}, bf16[256,1024]{1,0:T(8,128)(2,1)S(1)}, u32[]{:S(2)}, u32[]{:S(2)}) collective-permute-start(bf16[256,1024]{1,0:T(8,128)(2,1)S(1)} %bitcast.435), channel_id=1, source_target_pairs={{0,1},{1,2},{2,3},{3,0},{4,5},{5,6},{6,7},{7,4},{8,9},{9,10},{10,1... | collective-permute-start | bytes 1572872 | tf_op jit(solution)/shard_map/ppermute | solution.py:371
  157.1 69.0 %collective-permute-start.29 = (bf16[256,1024]{1,0:T(8,128)(2,1)S(1)}, bf16[256,1024]{1,0:T(8,128)(2,1)S(1)}, u32[]{:S(2)}, u32[]{:S(2)}) collective-permute-start(bf16[256,1024]{1,0:T(8,128)(2,1)S(1)} %copy-done.56), channel_id=1, source_target_pairs={{0,3},{1,0},{2,1},{3,2},{4,7},{5,4},{6,5},{7,6},{8,11},{9,8},{10,9... | collective-permute-start | bytes 1572872 | tf_op jit(solution)/shard_map/ppermute | solution.py:371
  159.8 67.1 %collective-permute-start.48 = (bf16[2,512,256]{1,2,0:T(8,128)(2,1)S(1)}, bf16[2,512,256]{1,2,0:T(8,128)(2,1)S(1)}, u32[]{:S(2)}, u32[]{:S(2)}) collective-permute-start(bf16[2,512,256]{1,2,0:T(8,128)(2,1)S(1)} %bitcast.447), channel_id=1, source_target_pairs={{0,4},{4,0},{1,5},{5,1},{2,6},{6,2},{3,7},{7,3},{8,12},{12,8},{9,1... | collective-permute-start | bytes 1572872 | tf_op jit(solution)/shard_map/ppermute | solution.py:368
  162.1 70.2 %collective-permute-start.30 = (bf16[256,1024]{1,0:T(8,128)(2,1)S(1)}, bf16[256,1024]{1,0:T(8,128)(2,1)S(1)}, u32[]{:S(2)}, u32[]{:S(2)}) collective-permute-start(bf16[256,1024]{1,0:T(8,128)(2,1)S(1)} %copy-done.56), channel_id=1, source_target_pairs={{0,2},{1,3},{2,0},{3,1},{4,6},{5,7},{6,4},{7,5},{8,10},{9,11},{10,... | collective-permute-start | bytes 1572872 | tf_op jit(solution)/shard_map/ppermute | solution.py:371
  226.9 56.0 %collective-permute-start.19 = (bf16[768,512]{0,1:T(8,128)(2,1)S(1)}, bf16[768,512]{0,1:T(8,128)(2,1)S(1)}, u32[]{:S(2)}, u32[]{:S(2)}) collective-permute-start(bf16[768,512]{0,1:T(8,128)(2,1)S(1)} %constant_dynamic-update-slice_fusion.4), channel_id=1, source_target_pairs={{0,8},{8,0},{16,24},{24,16},{1,9},{9,1},{17,25},{25,17},{2,10},{10... | collective-permute-start | bytes 2359304 | tf_op jit(solution)/shard_map/ppermute | solution.py:377
  282.9 103.4 %collective-permute-start.39 = (bf16[768,1024]{1,0:T(8,128)(2,1)}, bf16[768,1024]{1,0:T(8,128)(2,1)S(1)}, u32[]{:S(2)}, u32[]{:S(2)}) collective-permute-start(bf16[768,1024]{1,0:T(8,128)(2,1)} %constant_dynamic-update-slice_fusion.10), channel_id=1, source_target_pairs={{0,8},{8,0},{16,24},{24,16},{1,9},{9,1},{17,25},{25,17},{2,10},{10... | collective-permute-start | bytes 4718600 | tf_op jit(solution)/shard_map/ppermute | solution.py:377
  291.3 39.5 %collective-permute-start.4 = (bf16[512,1024]{0,1:T(8,128)(2,1)S(1)}, bf16[512,1024]{0,1:T(8,128)(2,1)S(1)}, u32[]{:S(2)}, u32[]{:S(2)}) collective-permute-start(bf16[512,1024]{0,1:T(8,128)(2,1)S(1)} %fusion.6), channel_id=1, source_target_pairs={{0,4},{4,0},{1,5},{5,1},{2,6},{6,2},{3,7},{7,3},{8,12},{12,8},{9,1... | collective-permute-start | bytes 3145736 | tf_op jit(solution)/shard_map/ppermute | solution.py:368
  325.3 64.7 %collective-permute-start.40 = (bf16[768,1024]{1,0:T(8,128)(2,1)}, bf16[768,1024]{1,0:T(8,128)(2,1)S(1)}, u32[]{:S(2)}, u32[]{:S(2)}) collective-permute-start(bf16[768,1024]{1,0:T(8,128)(2,1)} %constant_dynamic-update-slice_fusion.10), channel_id=1, source_target_pairs={{0,16},{8,24},{16,0},{24,8},{1,17},{9,25},{17,1},{25,9},{2,18},{10... | collective-permute-start | bytes 4718600 | tf_op jit(solution)/shard_map/ppermute | solution.py:377
  328.4 85.7 %collective-permute-start.32 = (bf16[768,1024]{1,0:T(8,128)(2,1)}, bf16[768,1024]{1,0:T(8,128)(2,1)}, u32[]{:S(2)}, u32[]{:S(2)}) collective-permute-start(bf16[768,1024]{1,0:T(8,128)(2,1)} %constant_dynamic-update-slice_fusion.7), channel_id=1, source_target_pairs={{0,8},{8,0},{16,24},{24,16},{1,9},{9,1},{17,25},{25,17},{2,10},{10... | collective-permute-start | bytes 4718600 | tf_op jit(solution)/shard_map/ppermute | solution.py:377
  330.9 49.9 %collective-permute-start.21 = (bf16[384,512]{0,1:T(8,128)(2,1)}, bf16[384,512]{0,1:T(8,128)(2,1)}, u32[]{:S(2)}, u32[]{:S(2)}) collective-permute-start(bf16[384,512]{0,1:T(8,128)(2,1)} %slice.1112), channel_id=1, source_target_pairs={{0,16},{8,24},{16,0},{24,8},{1,17},{9,25},{17,1},{25,9},{2,18},{10... | collective-permute-start | bytes 1179656 | tf_op jit(solution)/shard_map/ppermute | solution.py:377
  335.6 45.8 %collective-permute-start.22 = (bf16[384,512]{0,1:T(8,128)(2,1)}, bf16[384,512]{0,1:T(8,128)(2,1)}, u32[]{:S(2)}, u32[]{:S(2)}) collective-permute-start(bf16[384,512]{0,1:T(8,128)(2,1)} %slice.1113), channel_id=1, source_target_pairs={{0,8},{8,0},{16,24},{24,16},{1,9},{9,1},{17,25},{25,17},{2,10},{10... | collective-permute-start | bytes 1179656 | tf_op jit(solution)/shard_map/ppermute | solution.py:377
  390.0 45.3 %collective-permute-start.41 = (bf16[384,1024]{1,0:T(8,128)(2,1)}, bf16[384,1024]{1,0:T(8,128)(2,1)}, u32[]{:S(2)}, u32[]{:S(2)}) collective-permute-start(bf16[384,1024]{1,0:T(8,128)(2,1)} %slice.1132), channel_id=1, source_target_pairs={{0,16},{8,24},{16,0},{24,8},{1,17},{9,25},{17,1},{25,9},{2,18},{10... | collective-permute-start | bytes 2359304 | tf_op jit(solution)/shard_map/ppermute | solution.py:377
  392.5 42.9 %collective-permute-start.42 = (bf16[384,1024]{1,0:T(8,128)(2,1)}, bf16[384,1024]{1,0:T(8,128)(2,1)}, u32[]{:S(2)}, u32[]{:S(2)}) collective-permute-start(bf16[384,1024]{1,0:T(8,128)(2,1)} %slice.1133), channel_id=1, source_target_pairs={{0,8},{8,0},{16,24},{24,16},{1,9},{9,1},{17,25},{25,17},{2,10},{10... | collective-permute-start | bytes 2359304 | tf_op jit(solution)/shard_map/ppermute | solution.py:377
  396.1 55.5 %collective-permute-start.15 = (bf16[512,1024]{0,1:T(8,128)(2,1)}, bf16[512,1024]{0,1:T(8,128)(2,1)}, u32[]{:S(2)}, u32[]{:S(2)}) collective-permute-start(bf16[512,1024]{0,1:T(8,128)(2,1)} %add_convert_fusion.6), channel_id=1, source_target_pairs={{0,4},{4,0},{1,5},{5,1},{2,6},{6,2},{3,7},{7,3},{8,12},{12,8},{9,1... | collective-permute-start | bytes 3145736 | tf_op jit(solution)/shard_map/ppermute | solution.py:368
  609.7 122.9 %collective-permute-start.101 = (bf16[2,512,1024]{2,1,0:T(8,128)(2,1)}, bf16[2,512,1024]{2,1,0:T(8,128)(2,1)}, u32[]{:S(2)}, u32[]{:S(2)}) collective-permute-start(bf16[2,512,1024]{2,1,0:T(8,128)(2,1)} %pad_maximum_fusion.5), channel_id=1, source_target_pairs={{0,8},{8,0},{16,24},{24,16},{1,9},{9,1},{17,25},{25,17},{2,10},{10... | collective-permute-start | bytes 6291464 | tf_op jit(solution)/shard_map/ppermute | solution.py:377
  611.2 122.0 %collective-permute-start.104 = (bf16[2,512,1024]{2,1,0:T(8,128)(2,1)}, bf16[2,512,1024]{2,1,0:T(8,128)(2,1)}, u32[]{:S(2)}, u32[]{:S(2)}) collective-permute-start(bf16[2,512,1024]{2,1,0:T(8,128)(2,1)} %stack.322), channel_id=1, source_target_pairs={{0,16},{8,24},{16,0},{24,8},{1,17},{9,25},{17,1},{25,9},{2,18},{10... | collective-permute-start | bytes 6291464 | tf_op jit(solution)/shard_map/ppermute | solution.py:377
  640.3 96.6 %collective-permute-start.90 = (bf16[2,512,1024]{2,1,0:T(8,128)(2,1)}, bf16[2,512,1024]{2,1,0:T(8,128)(2,1)}, u32[]{:S(2)}, u32[]{:S(2)}) collective-permute-start(bf16[2,512,1024]{2,1,0:T(8,128)(2,1)} %pad_maximum_fusion.3), channel_id=1, source_target_pairs={{0,8},{8,0},{16,24},{24,16},{1,9},{9,1},{17,25},{25,17},{2,10},{10... | collective-permute-start | bytes 6291464 | tf_op jit(solution)/shard_map/ppermute | solution.py:377
  668.9 69.5 %collective-permute-start.93 = (bf16[2,512,1024]{2,1,0:T(8,128)(2,1)}, bf16[2,512,1024]{2,1,0:T(8,128)(2,1)S(1)}, u32[]{:S(2)}, u32[]{:S(2)}) collective-permute-start(bf16[2,512,1024]{2,1,0:T(8,128)(2,1)} %stack.315), channel_id=1, source_target_pairs={{0,16},{8,24},{16,0},{24,8},{1,17},{9,25},{17,1},{25,9},{2,18},{10... | collective-permute-start | bytes 6291464 | tf_op jit(solution)/shard_map/ppermute | solution.py:377
  738.4 43.0 %collective-permute-start.105 = (bf16[512,1024]{1,0:T(8,128)(2,1)}, bf16[512,1024]{1,0:T(8,128)(2,1)}, u32[]{:S(2)}, u32[]{:S(2)}) collective-permute-start(bf16[512,1024]{1,0:T(8,128)(2,1)} %get-tuple-element.230), channel_id=1, source_target_pairs={{0,8},{8,0},{16,24},{24,16},{1,9},{9,1},{17,25},{25,17},{2,10},{10... | collective-permute-start | bytes 3145736 | tf_op jit(solution)/shard_map/ppermute | solution.py:377
  743.5 43.3 %collective-permute-start.91 = (bf16[512,1024]{1,0:T(8,128)(2,1)}, bf16[512,1024]{1,0:T(8,128)(2,1)}, u32[]{:S(2)}, u32[]{:S(2)}) collective-permute-start(bf16[512,1024]{1,0:T(8,128)(2,1)} %get-tuple-element.235), channel_id=1, source_target_pairs={{0,16},{8,24},{16,0},{24,8},{1,17},{9,25},{17,1},{25,9},{2,18},{10... | collective-permute-start | bytes 3145736 | tf_op jit(solution)/shard_map/ppermute | solution.py:377
  759.0 44.3 %collective-permute-start.94 = (bf16[512,1024]{1,0:T(8,128)(2,1)}, bf16[512,1024]{1,0:T(8,128)(2,1)S(1)}, u32[]{:S(2)}, u32[]{:S(2)}) collective-permute-start(bf16[512,1024]{1,0:T(8,128)(2,1)} %get-tuple-element.236), channel_id=1, source_target_pairs={{0,8},{8,0},{16,24},{24,16},{1,9},{9,1},{17,25},{25,17},{2,10},{10... | collective-permute-start | bytes 3145736 | tf_op jit(solution)/shard_map/ppermute | solution.py:377
  761.7 131.5 %collective-permute-start.56 = (bf16[512,1024]{0,1:T(8,128)(2,1)S(1)}, bf16[512,1024]{0,1:T(8,128)(2,1)S(1)}, u32[]{:S(2)}, u32[]{:S(2)}) collective-permute-start(bf16[512,1024]{0,1:T(8,128)(2,1)S(1)} %copy-done.90), channel_id=1, source_target_pairs={{0,4},{4,0},{1,5},{5,1},{2,6},{6,2},{3,7},{7,3},{8,12},{12,8},{9,1... | collective-permute-start | bytes 3145736 | tf_op jit(solution)/shard_map/ppermute | solution.py:368
  765.5 40.3 %collective-permute-start.65 = (bf16[512,256]{1,0:T(8,128)(2,1)S(1)}, bf16[512,256]{1,0:T(8,128)(2,1)S(1)}, u32[]{:S(2)}, u32[]{:S(2)}) collective-permute-start(bf16[512,256]{1,0:T(8,128)(2,1)S(1)} %get-tuple-element.312), channel_id=1, source_target_pairs={{0,1},{1,2},{2,3},{3,0},{4,5},{5,6},{6,7},{7,4},{8,9},{9,10},{10,1... | collective-permute-start | bytes 786440 | tf_op jit(solution)/shard_map/ppermute | solution.py:374
  786.8 55.8 %collective-permute-start.106 = (bf16[256,1024]{1,0:T(8,128)(2,1)S(1)}, bf16[256,1024]{1,0:T(8,128)(2,1)S(1)}, u32[]{:S(2)}, u32[]{:S(2)}) collective-permute-start(bf16[256,1024]{1,0:T(8,128)(2,1)S(1)} %get-tuple-element.256), channel_id=1, source_target_pairs={{0,2},{1,3},{2,0},{3,1},{4,6},{5,7},{6,4},{7,5},{8,10},{9,11},{10,... | collective-permute-start | bytes 1572872 | tf_op jit(solution)/shard_map/ppermute | solution.py:374
  803.2 40.8 %collective-permute-start.107 = (bf16[256,1024]{1,0:T(8,128)(2,1)S(1)}, bf16[256,1024]{1,0:T(8,128)(2,1)S(1)}, u32[]{:S(2)}, u32[]{:S(2)}) collective-permute-start(bf16[256,1024]{1,0:T(8,128)(2,1)S(1)} %get-tuple-element.257), channel_id=1, source_target_pairs={{0,3},{1,0},{2,1},{3,2},{4,7},{5,4},{6,5},{7,6},{8,11},{9,8},{10,9... | collective-permute-start | bytes 1572872 | tf_op jit(solution)/shard_map/ppermute | solution.py:374
  842.6 47.4 %collective-permute-start.96 = (bf16[256,1024]{1,0:T(8,128)(2,1)S(1)}, bf16[256,1024]{1,0:T(8,128)(2,1)S(1)}, u32[]{:S(2)}, u32[]{:S(2)}) collective-permute-start(bf16[256,1024]{1,0:T(8,128)(2,1)S(1)} %get-tuple-element.259), channel_id=1, source_target_pairs={{0,3},{1,0},{2,1},{3,2},{4,7},{5,4},{6,5},{7,6},{8,11},{9,8},{10,9... | collective-permute-start | bytes 1572872 | tf_op jit(solution)/shard_map/ppermute | solution.py:374
  844.1 47.3 %collective-permute-start.92 = (bf16[256,1024]{1,0:T(8,128)(2,1)S(1)}, bf16[256,1024]{1,0:T(8,128)(2,1)S(1)}, u32[]{:S(2)}, u32[]{:S(2)}) collective-permute-start(bf16[256,1024]{1,0:T(8,128)(2,1)S(1)} %slice.1253), channel_id=1, source_target_pairs={{0,1},{1,2},{2,3},{3,0},{4,5},{5,6},{6,7},{7,4},{8,9},{9,10},{10,1... | collective-permute-start | bytes 1572872 | tf_op jit(solution)/shard_map/ppermute | solution.py:374
  846.5 192.5 %collective-permute-start.82 = (bf16[2,512,512]{1,2,0:T(8,128)(2,1)}, bf16[2,512,512]{1,2,0:T(8,128)(2,1)}, u32[]{:S(2)}, u32[]{:S(2)}) collective-permute-start(bf16[2,512,512]{1,2,0:T(8,128)(2,1)} %pad_maximum_fusion.39), channel_id=1, source_target_pairs={{0,16},{8,24},{16,0},{24,8},{1,17},{9,25},{17,1},{25,9},{2,18},{10... | collective-permute-start | bytes 3145736 | tf_op jit(solution)/shard_map/ppermute | solution.py:377
  877.5 157.4 %collective-permute-start.108 = (bf16[256,1024]{1,0:T(8,128)(2,1)}, bf16[256,1024]{1,0:T(8,128)(2,1)}, u32[]{:S(2)}, u32[]{:S(2)}) collective-permute-start(bf16[256,1024]{1,0:T(8,128)(2,1)} %add_convert_fusion.8), channel_id=1, source_target_pairs={{0,8},{8,0},{16,24},{24,16},{1,9},{9,1},{17,25},{25,17},{2,10},{10... | collective-permute-start | bytes 1572872 | tf_op jit(solution)/shard_map/ppermute | solution.py:377
  890.1 147.3 %collective-permute-start.109 = (bf16[256,1024]{1,0:T(8,128)(2,1)}, bf16[256,1024]{1,0:T(8,128)(2,1)}, u32[]{:S(2)}, u32[]{:S(2)}) collective-permute-start(bf16[256,1024]{1,0:T(8,128)(2,1)} %add_convert_fusion.8), channel_id=1, source_target_pairs={{0,16},{8,24},{16,0},{24,8},{1,17},{9,25},{17,1},{25,9},{2,18},{10... | collective-permute-start | bytes 1572872 | tf_op jit(solution)/shard_map/ppermute | solution.py:377
  892.5 147.8 %collective-permute-start.98 = (bf16[256,1024]{1,0:T(8,128)(2,1)}, bf16[256,1024]{1,0:T(8,128)(2,1)}, u32[]{:S(2)}, u32[]{:S(2)}) collective-permute-start(bf16[256,1024]{1,0:T(8,128)(2,1)} %add_convert_fusion.9), channel_id=1, source_target_pairs={{0,16},{8,24},{16,0},{24,8},{1,17},{9,25},{17,1},{25,9},{2,18},{10... | collective-permute-start | bytes 1572872 | tf_op jit(solution)/shard_map/ppermute | solution.py:377
  893.2 150.0 %collective-permute-start.97 = (bf16[256,1024]{1,0:T(8,128)(2,1)}, bf16[256,1024]{1,0:T(8,128)(2,1)}, u32[]{:S(2)}, u32[]{:S(2)}) collective-permute-start(bf16[256,1024]{1,0:T(8,128)(2,1)} %add_convert_fusion.9), channel_id=1, source_target_pairs={{0,8},{8,0},{16,24},{24,16},{1,9},{9,1},{17,25},{25,17},{2,10},{10... | collective-permute-start | bytes 1572872 | tf_op jit(solution)/shard_map/ppermute | solution.py:377
  1035.0 40.9 %collective-permute-start.80 = (bf16[512,512]{0,1:T(8,128)(2,1)S(1)}, bf16[512,512]{0,1:T(8,128)(2,1)S(1)}, u32[]{:S(2)}, u32[]{:S(2)}) collective-permute-start(bf16[512,512]{0,1:T(8,128)(2,1)S(1)} %copy-done.104), channel_id=1, source_target_pairs={{0,16},{8,24},{16,0},{24,8},{1,17},{9,25},{17,1},{25,9},{2,18},{10... | collective-permute-start | bytes 1572872 | tf_op jit(solution)/shard_map/ppermute | solution.py:377
  1043.3 65.3 %collective-permute-start.68 = (bf16[2,512,512]{1,2,0:T(8,128)(2,1)}, bf16[2,512,512]{1,2,0:T(8,128)(2,1)}, u32[]{:S(2)}, u32[]{:S(2)}) collective-permute-start(bf16[2,512,512]{1,2,0:T(8,128)(2,1)} %pad_maximum_fusion.30), channel_id=1, source_target_pairs={{0,8},{8,0},{16,24},{24,16},{1,9},{9,1},{17,25},{25,17},{2,10},{10... | collective-permute-start | bytes 3145736 | tf_op jit(solution)/shard_map/ppermute | solution.py:377
  1071.5 46.2 %collective-permute-start.58 = (bf16[512,1024]{0,1:T(8,128)(2,1)}, bf16[512,1024]{0,1:T(8,128)(2,1)}, u32[]{:S(2)}, u32[]{:S(2)}) collective-permute-start(bf16[512,1024]{0,1:T(8,128)(2,1)} %dynamic-slice_convert_fusion.1), channel_id=1, source_target_pairs={{0,4},{4,0},{1,5},{5,1},{2,6},{6,2},{3,7},{7,3},{8,12},{12,8},{9,1... | collective-permute-start | bytes 3145736 | tf_op jit(solution)/shard_map/ppermute | solution.py:368
  1099.2 81.7 %collective-permute-start.57 = (bf16[512,1024]{0,1:T(8,128)(2,1)}, bf16[512,1024]{0,1:T(8,128)(2,1)}, u32[]{:S(2)}, u32[]{:S(2)}) collective-permute-start(bf16[512,1024]{0,1:T(8,128)(2,1)} %dynamic-slice_convert_fusion.2), channel_id=1, source_target_pairs={{0,4},{4,0},{1,5},{5,1},{2,6},{6,2},{3,7},{7,3},{8,12},{12,8},{9,1... | collective-permute-start | bytes 3145736 | tf_op jit(solution)/shard_map/ppermute | solution.py:368
  1111.6 47.2 %collective-permute-start.71 = (bf16[2,512,512]{1,2,0:T(8,128)(2,1)}, bf16[2,512,512]{1,2,0:T(8,128)(2,1)}, u32[]{:S(2)}, u32[]{:S(2)}) collective-permute-start(bf16[2,512,512]{1,2,0:T(8,128)(2,1)} %pad_maximum_fusion.32), channel_id=1, source_target_pairs={{0,16},{8,24},{16,0},{24,8},{1,17},{9,25},{17,1},{25,9},{2,18},{10... | collective-permute-start | bytes 3145736 | tf_op jit(solution)/shard_map/ppermute | solution.py:377
  1114.5 97.8 %collective-permute-start.69 = (bf16[512,512]{0,1:T(8,128)(2,1)}, bf16[512,512]{0,1:T(8,128)(2,1)}, u32[]{:S(2)}, u32[]{:S(2)}) collective-permute-start(bf16[512,512]{0,1:T(8,128)(2,1)} %get-tuple-element.292), channel_id=1, source_target_pairs={{0,16},{8,24},{16,0},{24,8},{1,17},{9,25},{17,1},{25,9},{2,18},{10... | collective-permute-start | bytes 1572872 | tf_op jit(solution)/shard_map/ppermute | solution.py:377
  1161.3 51.0 %collective-permute-start.72 = (bf16[512,512]{0,1:T(8,128)(2,1)}, bf16[512,512]{0,1:T(8,128)(2,1)}, u32[]{:S(2)}, u32[]{:S(2)}) collective-permute-start(bf16[512,512]{0,1:T(8,128)(2,1)} %fusion.37), channel_id=1, source_target_pairs={{0,8},{8,0},{16,24},{24,16},{1,9},{9,1},{17,25},{25,17},{2,10},{10... | collective-permute-start | bytes 1572872 | tf_op jit(solution)/shard_map/ppermute | solution.py:377
  1217.3 63.2 %collective-permute-start.63 = (bf16[2,512,256]{2,1,0:T(8,128)(2,1)S(1)}, bf16[2,512,256]{2,1,0:T(8,128)(2,1)S(1)}, u32[]{:S(2)}, u32[]{:S(2)}) collective-permute-start(bf16[2,512,256]{2,1,0:T(8,128)(2,1)S(1)} %get-tuple-element.316), channel_id=1, source_target_pairs={{0,4},{4,0},{1,5},{5,1},{2,6},{6,2},{3,7},{7,3},{8,12},{12,8},{9,1... | collective-permute-start | bytes 1572872 | tf_op jit(solution)/shard_map/ppermute | solution.py:368
  1237.2 43.5 %collective-permute-start.75 = (bf16[256,512]{0,1:T(8,128)(2,1)S(1)}, bf16[256,512]{0,1:T(8,128)(2,1)S(1)}, u32[]{:S(2)}, u32[]{:S(2)}) collective-permute-start(bf16[256,512]{0,1:T(8,128)(2,1)S(1)} %add_convert_fusion.11), channel_id=1, source_target_pairs={{0,8},{8,0},{16,24},{24,16},{1,9},{9,1},{17,25},{25,17},{2,10},{10... | collective-permute-start | bytes 786440 | tf_op jit(solution)/shard_map/ppermute | solution.py:377
  1237.9 45.2 %collective-permute-start.76 = (bf16[256,512]{0,1:T(8,128)(2,1)S(1)}, bf16[256,512]{0,1:T(8,128)(2,1)S(1)}, u32[]{:S(2)}, u32[]{:S(2)}) collective-permute-start(bf16[256,512]{0,1:T(8,128)(2,1)S(1)} %add_convert_fusion.11), channel_id=1, source_target_pairs={{0,16},{8,24},{16,0},{24,8},{1,17},{9,25},{17,1},{25,9},{2,18},{10... | collective-permute-start | bytes 786440 | tf_op jit(solution)/shard_map/ppermute | solution.py:377
  (300 other events, 5389.2 us)

commit v2 on v1

--- a/solution.py
+++ b/solution.py
@@ -344,12 +344,407 @@
     )(dz, dz.T, f.T, w1, w2, act, slope)
 
 
-def norm_forward(stream, gain, bias):
-    center = jnp.mean(stream, axis=1, keepdims=True)
-    spread = jnp.mean(stream * stream, axis=1, keepdims=True) - center * center
+MESH = pl.DeviceIdType.MESH
+ANYWHERE = pl.BlockSpec(memory_space=pl.ANY)
+IN_VMEM = pl.BlockSpec(memory_space=pltpu.VMEM)
+
+
+def here():
+    return lax.axis_index("dp"), lax.axis_index("row"), lax.axis_index("col")
+
+
+def meet(partners):
+    barrier = pltpu.get_barrier_semaphore()
+    for partner in partners:
+        pl.semaphore_signal(barrier, inc=1, device_id=partner, device_id_type=MESH)
+    pl.semaphore_wait(barrier, len(partners))
+
+
+def remote(src, dst, sends, recvs, device):
+    return pltpu.make_async_remote_copy(
+        src_ref=src, dst_ref=dst, send_sem=sends, recv_sem=recvs, device_id=device,
+        device_id_type=MESH,
+    )
+
+
+def start_kernel(
+    tokens, encoder, vec_f, vec_c, *refs, n_col,
+):
+    weights, (x_ext, enc, all_f, all_c), full = refs[:8], refs[8:12], refs[12:20]
+    zeros, w_send, w_recv, w_own, t_send, t_recv, e_send, e_recv, v_send, v_recv, z_sem = refs[20:]
+    dp, row, col = here()
+    part = lax.rem(dp, PARTS)
+    twin = (dp, 1 - row, col)
+    flip = [
+        dp + 1 - 2 * lax.rem(dp, 2),
+        dp + 2 - 4 * lax.rem(dp // 2, 2),
+    ]
+    by_x, by_y = (flip[0], row, col), (flip[1], row, col)
+    part_x, part_y = lax.rem(flip[0], PARTS), lax.rem(flip[1], PARTS)
+    shift = [lax.rem(col + k, n_col) for k in range(n_col)]
+    group = [(dp, r, c) for r in (row, 1 - row) for c in shift][1:]
+    meet(group + [by_x, by_y])
+
+    wide = tokens.shape[1]
+    deep = n_col * wide
+    rest = deep - wide
+
+    def chunk(index, size):
+        return pl.ds(pl.multiple_of(index * size, size), size)
+
+    def weight_z(i, k):
+        w, to = weights[i], (dp, row, lax.rem(col + n_col - k, n_col))
+        if i % 4 < 3:
+            size = w.shape[1] // PARTS
+            src = w.at[:, chunk(part, size)]
+            dst = full[i].at[pl.ds(k * wide, wide), chunk(part, size)]
+        else:
+            size = w.shape[0] // PARTS
+            src = w.at[chunk(part, size), :]
+            dst = full[i].at[chunk(part, size), pl.ds(k * wide, wide)]
+        return remote(src, dst, w_send.at[i, k - 1], w_recv.at[i, k - 1], to)
+
+    def weight_own(i):
+        w = weights[i]
+        place = full[i].at[pl.ds(0, wide), :] if i % 4 < 3 else full[i].at[:, pl.ds(0, wide)]
+        return pltpu.make_async_copy(w, place, w_own.at[i])
+
+    def weight_part(i, which, begin, size):
+        if i % 4 < 3:
+            return full[i].at[pl.ds(begin, size), chunk(which, weights[i].shape[1] // PARTS)]
+        return full[i].at[chunk(which, weights[i].shape[0] // PARTS), pl.ds(begin, size)]
+
+    def weight_plane(i, stage):
+        half = rest // 2
+        which, begin, size, to = [
+            (part, wide, rest, by_x),
+            (part, wide, rest, by_y),
+            (part_x, wide, half, by_y),
+            (part_y, wide + half, half, by_x),
+        ][stage]
+        ref = weight_part(i, which, begin, size)
+        return remote(ref, ref, w_send.at[i, 3 + stage], w_recv.at[i, 3 + stage], to)
+
+    def token_piece(j, slot):
+        rows = tokens.shape[0] // n_col
+        to_col = 2 * row + j // 2 + (1 - slot)
+        k = lax.rem(col + n_col - lax.rem(to_col, n_col), n_col)
+        src = tokens.at[pl.ds(j * rows, rows), :]
+        dst = x_ext.at[slot, :, chunk(k, wide)]
+        local = (row == j % 2) & (col == to_col)
+        valid = to_col < n_col
+        return src, dst, k, local, valid, (dp, j % 2, to_col)
+
+    def send_tokens(slot):
+        for j in range(n_col):
+            src, dst, k, local, valid, to = token_piece(j, slot)
+
+            @pl.when(valid & local)
+            def _():
+                pltpu.make_async_copy(src, dst, t_recv.at[slot, k]).start()
+
+            @pl.when(valid & jnp.logical_not(local))
+            def _():
+                remote(src, dst, t_send.at[slot, j], t_recv.at[slot, k], to).start()
+
+    def enc_z(k):
+        ref = enc.at[chunk(row, encoder.shape[0]), pl.ds(k * wide, wide)]
+        to = (dp, row, lax.rem(col + n_col - k, n_col))
+        return remote(encoder, ref, e_send.at[0, k], e_recv.at[0, k], to)
+
+    def enc_twin(k):
+        ref = enc.at[chunk(row, encoder.shape[0]), pl.ds(k * wide, wide)]
+        return remote(encoder if k == 0 else ref, ref, e_send.at[1, k], e_recv.at[1, k], twin)
+
+    def vectors(k):
+        to = (dp, row, lax.rem(col + n_col - k, n_col))
+        return [
+            remote(vec_f, all_f.at[:, pl.ds(k * wide, wide)], v_send.at[0, k], v_recv.at[0, k], to),
+            remote(vec_c, all_c.at[col], v_send.at[1, k], v_recv.at[1, k], to),
+        ]
+
+    own_vectors = [
+        pltpu.make_async_copy(vec_f, all_f.at[:, pl.ds(0, wide)], v_recv.at[0, 0]),
+        pltpu.make_async_copy(vec_c, all_c.at[col], v_recv.at[1, 0]),
+        pltpu.make_async_copy(
+            encoder, enc.at[chunk(row, encoder.shape[0]), pl.ds(0, wide)], e_recv.at[0, 0]
+        ),
+    ]
+    ks = range(1, n_col)
+    for i in range(4):
+        for k in ks:
+            weight_z(i, k).start()
+    send_tokens(1)
+    for k in ks:
+        for copy in vectors(k):
+            copy.start()
+    for i in range(4, 8):
+        for k in ks:
+            weight_z(i, k).start()
+    send_tokens(0)
+    enc_twin(0).start()
+    for k in ks:
+        enc_z(k).start()
+    for i in range(8):
+        weight_own(i).start()
+    for copy in own_vectors:
+        copy.start()
+
+    @pl.when(col == 0)
+    def _():
+        zeros[...] = jnp.zeros_like(zeros)
+        clear = pltpu.make_async_copy(zeros, x_ext.at[0], z_sem)
+        clear.start()
+        clear.wait()
+
+    for base in (0, 4):
+        for i in range(base, base + 4):
+            for k in ks:
+                weight_z(i, k).wait_recv()
+            weight_plane(i, 0).start()
+            weight_plane(i, 1).start()
+        for i in range(base, base + 4):
+            weight_plane(i, 0).wait_recv()
+            weight_plane(i, 2).start()
+            weight_plane(i, 1).wait_recv()
+            weight_plane(i, 3).start()
+    for k in ks:
+        enc_z(k).wait_recv()
+        enc_twin(k).start()
+    for i in range(8):
+        weight_plane(i, 2).wait_recv()
+        weight_plane(i, 3).wait_recv()
+        weight_own(i).wait()
+        for k in ks:
+            weight_z(i, k).wait_send()
+        for stage in range(4):
+            weight_plane(i, stage).wait_send()
+    for copy in own_vectors:
+        copy.wait()
+    for k in ks:
+        for copy in vectors(k):
+            copy.wait()
+        enc_z(k).wait_send()
+    for k in range(n_col):
+        enc_twin(k).wait()
+    for slot in (1, 0):
+        for j in range(n_col):
+            src, dst, k, local, valid, to = token_piece(j, slot)
+
+            @pl.when(valid & jnp.logical_not(local))
+            def _():
+                remote(src, dst, t_send.at[slot, j], t_recv.at[slot, k], to).wait_send()
+
+        for k in range(n_col):
+            rows = tokens.shape[0] // n_col
+            came = pltpu.make_async_copy(
+                tokens.at[pl.ds(0, rows), :],
+                x_ext.at[slot, :, pl.ds(k * wide, wide)],
+                t_recv.at[slot, k],
+            )
+            if slot == 1:
+                came.wait()
+            else:
+
+                @pl.when(col > 0)
+                def _():
+                    came.wait()
+
+
+def start(tokens, encoder, vec_f, vec_c, weights, n_col):
+    wide = tokens.shape[1]
+    deep = n_col * wide
+    rows = tokens.shape[0] // n_col
+    shapes = [
+        jax.ShapeDtypeStruct((2, rows, deep), low),
+        jax.ShapeDtypeStruct((2 * encoder.shape[0], deep), low),
+        jax.ShapeDtypeStruct((vec_f.shape[0], deep), f32),
+        jax.ShapeDtypeStruct((n_col,) + vec_c.shape, f32),
+    ]
+    for i, w in enumerate(weights):
+        shapes.append(
+            jax.ShapeDtypeStruct((deep, w.shape[1]) if i % 4 < 3 else (w.shape[0], deep), low)
+        )
+    dma = pltpu.SemaphoreType.DMA
+    return pl.pallas_call(
+        functools.partial(start_kernel, n_col=n_col),
+        in_specs=[ANYWHERE] * 12,
+        out_specs=[ANYWHERE] * 12,
+        out_shape=shapes,
+        scratch_shapes=[
+            pltpu.VMEM((rows, deep), low),
+            dma((8, 7)), dma((8, 7)), dma((8,)),
+            dma((2, n_col)), dma((2, n_col)),
+            dma((2, n_col)), dma((2, n_col)),
+            dma((2, n_col)), dma((2, n_col)),
+            dma,
+        ],
+        compiler_params=pltpu.CompilerParams(
+            collective_id=1, has_side_effects=True, vmem_limit_bytes=VMEM
+        ),
+        name="start",
+    )(tokens, encoder, vec_f, vec_c, *weights)
+
+
+def norm_rows(x):
+    center = jnp.mean(x, axis=1, keepdims=True)
+    spread = jnp.mean(x * x, axis=1, keepdims=True) - center * center
     scaling = lax.rsqrt(spread + norm_epsilon)
-    normed = (stream - center) * scaling
-    return (normed * gain + bias).astype(low), normed, scaling
+    return (x - center) * scaling, scaling
+
+
+CUT = 256
+
+
+def enter_kernel(x_ref, gain, shift, a_ref, sends, recvs):
+    dp, row, col = here()
+    twin = (dp, 1 - row, col)
+    meet([twin])
+    slots, rows = x_ref.shape[:2]
+
+    def place(slot):
+        return a_ref.at[slot, pl.ds(pl.multiple_of(row * rows, rows), rows), :]
+
+    copies = []
+    for slot in reversed(range(slots)):
+        for t in range(rows // CUT):
+            normed, _ = norm_rows(x_ref[slot, pl.ds(t * CUT, CUT), :].astype(f32))
+            begin = pl.multiple_of(row * rows + t * CUT, CUT)
+            a_ref[slot, pl.ds(begin, CUT), :] = (normed * gain[...] + shift[...]).astype(low)
+        copy = remote(place(slot), place(slot), sends.at[slot], recvs.at[slot], twin)
+        copy.start()
+        copies.append(copy)
+    for copy in copies:
+        copy.wait()
+
+
+def enter(x_ext, gain, shift, number):
+    slots, rows, deep = x_ext.shape
+    return pl.pallas_call(
+        enter_kernel,
+        in_specs=[IN_VMEM] * 3,
+        out_specs=IN_VMEM,
+        out_shape=jax.ShapeDtypeStruct((slots, 2 * rows, deep), low),
+        scratch_shapes=[pltpu.SemaphoreType.DMA((slots,)), pltpu.SemaphoreType.DMA((slots,))],
+        compiler_params=pltpu.CompilerParams(
+            collective_id=number, has_side_effects=True, vmem_limit_bytes=VMEM
+        ),
+        name="enter",
+    )(x_ext, gain[None], shift[None])
+
+
+def junction_kernel(*refs, kinds, mode):
+    dp, row, col = here()
+    twin = (dp, 1 - row, col)
+    meet([twin])
+    refs = list(refs)
+    sources = []
+    for kind in kinds:
+        sources.append((kind, refs.pop(0), refs.pop(0) if kind != "sum" else None))
+    if mode == "forward":
+        x_ref, bias, gain, shift, x_out, full, away, came, s1, r1, s2, r2 = refs
+    elif mode == "backward":
+        res_ref, x_ref, gain, dx_out, full, stats, away, came, s1, r1, s2, r2 = refs
+    else:
+        out, away, came, s1, r1 = refs
+    rows = came.shape[0]
+    cuts = rows // CUT
+
+    def partial(begin):
+        total = None
+        for kind, g, w in sources:
+            part = g[pl.ds(begin, CUT), :]
+            if kind == "sum":
+                part = part.astype(f32)
+            elif kind == "nt":
+                part = mm_nt(part, w[...])
+            else:
+                part = mm(part, w[...])
+            total = part if total is None else total + part
+        return total
+
+    sent = []
+    for t in range(cuts):
+        at = pl.ds(t * CUT, CUT)
+        away[at, :] = partial(pl.multiple_of((1 - row) * rows + t * CUT, CUT)).astype(low)
+        copy = remote(away.at[at, :], came.at[at, :], s1.at[t], r1.at[t], twin)
+        copy.start()
+        sent.append(copy)
+    gathered = []
+    sums = [0.0, 0.0, 0.0]
+    for t in range(cuts):
+        at = pl.ds(t * CUT, CUT)
+        begin = pl.multiple_of(row * rows + t * CUT, CUT)
+        own = partial(begin)
+        sent[t].wait_recv()
+        total = own + came[at, :].astype(f32)
+        if mode == "sum":
+            out[at, :] = total
+            continue
+        if mode == "forward":
+            x = x_ref[at, :].astype(f32) + (total + bias[...])
+            x_out[at, :] = x
+            normed, _ = norm_rows(x)
+            result = (normed * gain[...] + shift[...]).astype(low)
+        else:
+            normed, scaling = norm_rows(x_ref[at, :].astype(f32))
+            upstream = total * gain[...]
+            mean_up = jnp.mean(upstream, axis=1, keepdims=True)
+            mean_both = jnp.mean(upstream * normed, axis=1, keepdims=True)
+            dx = res_ref[at, :].astype(f32) + scaling * (upstream - mean_up - normed * mean_both)
+            dx_out[at, :] = dx
+            result = dx.astype(low)
+            for i, value in enumerate((total * normed, total, result.astype(f32))):
+                sums[i] = sums[i] + jnp.sum(value, axis=0, keepdims=True)
+        if full is None:
+            continue
+        full[pl.ds(begin, CUT), :] = result
+        place = full.at[pl.ds(begin, CUT), :]
+        copy = remote(place, place, s2.at[t], r2.at[t], twin)
+        copy.start()
+        gathered.append(copy)
+    if mode == "backward":
+        for i in range(3):
+            stats[i : i + 1, :] = sums[i]
+    for copy in sent:
+        copy.wait_send()
+    for copy in gathered:
+        copy.wait()
+
+
+def junction(mode, sources, others, number):
+    kinds = [x[0] for x in sources]
+    first = sources[0]
+    tokens = first[1].shape[0]
+    deep = first[1].shape[1]
+    if first[0] != "sum":
+        deep = first[2].shape[0 if first[0] == "nt" else 1]
+    rows = tokens // 2
+    flat = [x for source in sources for x in source[1:]]
+    dma = pltpu.SemaphoreType.DMA((rows // CUT,))
+    wide_rows = jax.ShapeDtypeStruct((rows, deep), f32)
+    every = jax.ShapeDtypeStruct((tokens, deep), low)
+    shapes = {
+        "forward": [wide_rows, every],
+        "backward": [wide_rows, every, jax.ShapeDtypeStruct((8, deep), f32)],
+        "sum": [wide_rows],
+    }[mode]
+    scratch = [pltpu.VMEM((rows, deep), low), pltpu.VMEM((rows, deep), low), dma, dma]
+    if mode != "sum":
+        scratch += [dma, dma]
+    args = flat + [x[None] if x.ndim == 1 else x for x in others]
+    out = pl.pallas_call(
+        functools.partial(junction_kernel, kinds=kinds, mode=mode),
+        in_specs=[IN_VMEM] * len(args),
+        out_specs=[IN_VMEM] * len(shapes),
+        out_shape=shapes,
+        scratch_shapes=scratch,
+        compiler_params=pltpu.CompilerParams(
+            collective_id=number, has_side_effects=True, vmem_limit_bytes=VMEM
+        ),
+        name="junction_" + mode,
+    )(*args)
+    return out if len(out) > 1 else out[0]
 
 
 def norm_backward(incoming, normed, scaling, gain):
@@ -481,49 +876,44 @@
                 bit *= 2
             return in_order(plane_gather(total.astype(low)))
 
-        feature_vectors = jnp.stack([
+        vec_f = jnp.stack([
             self_norm_gain, self_norm_bias, self_out_bias, cross_norm_gain, cross_norm_bias,
             cross_out_bias, hidden_norm_gain, hidden_norm_bias, hidden_out_bias,
         ])
-        column_vectors = jnp.concatenate(
+        vec_f = jnp.pad(vec_f, ((0, 7), (0, 0)))
+        vec_c = jnp.concatenate(
             [self_query_bias, self_value_bias, cross_query_bias, cross_value_bias, hidden_in_bias]
+        ).reshape(-1, 128)
+        vec_c = jnp.pad(vec_c, ((0, -vec_c.shape[0] % 8), (0, 0)))
+        weights = [
+            self_query, self_key, self_value, self_out,
+            cross_query, cross_key, cross_value, cross_out,
+        ]
+        x_ext, enc, vectors, columns, *full = start(
+            tokens, encoder, vec_f, vec_c, weights, n_col
         )
-        gathered = lax.all_gather(feature_vectors, "col", axis=0)
-        rolled = lax.dynamic_slice_in_dim(jnp.concatenate([gathered, gathered]), col, n_col, 0)
-        vectors = jnp.moveaxis(rolled, 0, 1).reshape(feature_vectors.shape[0], n_col * wide)
-        (gain1, shift1, out_bias1, gain2, shift2, out_bias2, gain3, shift3, out_bias3) = vectors
-        columns = lax.all_gather(column_vectors, "col", axis=0)
+        wq1, wk1, wv1, wo1, wq2, wk2, wv2, wo2 = full
+        (gain1, shift1, out_bias1, gain2, shift2, out_bias2, gain3, shift3, out_bias3) = vectors[:9]
+        size = self_query_bias.shape[0]
 
         def column_vector(start, size):
-            flat = columns[:, start : start + size].reshape(-1)
-            parts = flat.reshape(PARTS, -1)
-            return jnp.concatenate(
-                [
-                    lax.dynamic_index_in_dim(parts, place ^ j, 0, keepdims=False)
-                    for j in range(PARTS)
-                ]
-            )
-
-        size = self_query_bias.shape[0]
+            return columns.reshape(n_col, -1)[:, start : start + size].reshape(-1)
+
         q_bias1 = column_vector(0, size)
         v_bias1 = column_vector(size, size)
         q_bias2 = column_vector(2 * size, size)
         v_bias2 = column_vector(3 * size, size)
-        hidden_bias = column_vector(4 * size, hidden_in_bias.shape[0])
-
-        self_parts = weights_of([self_query, self_key, self_value, self_out.T])
-        cross_parts = weights_of([cross_query, cross_key, cross_value, cross_out.T])
+        hidden_bias = column_vector(4 * size, hidden_in_bias.shape[0]).reshape(PARTS, -1)
+        hidden_bias = jnp.stack(
+            [lax.dynamic_index_in_dim(hidden_bias, place ^ j, 0) for j in range(PARTS)]
+        )
+
+        hidden_in, hidden_out, cotangent, x_ext = lax.optimization_barrier(
+            (hidden_in, hidden_out, cotangent, x_ext)
+        )
         w1 = jnp.stack(weights_of([hidden_in]))
         w2 = jnp.stack(weights_of([hidden_out.T]))
         step = self_query.shape[1] // PARTS
-
-        def columns_of(parts, index):
-            return jnp.concatenate(
-                [p[:, index * step : (index + 1) * step] for p in parts], axis=1
-            )
-
-        wq1, wk1, wv1, wo1 = [columns_of(self_parts, i) for i in range(4)]
-        wq2, wk2, wv2, wo2 = [columns_of(cross_parts, i) for i in range(4)]
 
         dec_ids = doc_numbers(dec_lengths, SEQ_LEN)[0]
         src_ids = doc_numbers(src_lengths, ENC)[0]
@@ -532,47 +922,34 @@
         query_ids = key_ids[WIN:]
 
         scale = low(HEAD_DIM**-0.5)
-        stream = spread_rows(tokens).astype(f32)
-        a_own, normed1, scaling1 = norm_forward(stream, gain1, shift1)
-        a = row_gather(a_own)
-        before = lax.ppermute(a_own, "col", [(i, i + 1) for i in range(n_col - 1)])
-        before = jnp.concatenate([before[:, wide:], before[:, :wide]], axis=1)
-        a_ext = jnp.concatenate([row_gather(before), a], axis=0)
+        x0 = x_ext[1]
+        a_ext = enter(x_ext, gain1, shift1, 2).reshape(WIN + span, -1)
+        a = a_ext[WIN:]
         q1 = (mm(a, wq1) + q_bias1).astype(low) * scale
         k1 = mm(a_ext, wk1).astype(low)
         v1 = (mm(a_ext, wv1) + v_bias1).astype(low)
         o1, lse1 = attend(q1, k1, v1, query_ids, key_ids, True)
-        x1 = stream + (row_scatter(mm_nt(o1, wo1)) + out_bias1)
-
-        c_own, normed2, scaling2 = norm_forward(x1, gain2, shift2)
-        c = row_gather(c_own)
-        enc = row_gather(
-            jnp.concatenate(
-                [encoder] + [from_col(encoder, k) for k in range(1, n_col)], axis=1
-            )
-        )
+        x1, c = junction("forward", [("nn", o1, wo1)], [x0, out_bias1, gain2, shift2], 3)
+
         q2 = (mm(c, wq2) + q_bias2).astype(low) * scale
         k2 = mm(enc, wk2).astype(low)
         v2 = (mm(enc, wv2) + v_bias2).astype(low)
         o2, lse2 = attend(q2, k2, v2, query_ids, src_ids, False)
-        x2 = x1 + (row_scatter(mm_nt(o2, wo2)) + out_bias2)
-
-        f_own, normed3, scaling3 = norm_forward(x2, gain3, shift3)
-        f = row_gather(f_own)
-        act, slope, branch = hidden_forward(f, w1, hidden_bias.reshape(PARTS, 1, -1), w2)
-        layer_out = collect_rows((x2 + (row_scatter(branch) + out_bias3)).astype(low))
+        x2, f = junction("forward", [("nn", o2, wo2)], [x1, out_bias2, gain3, shift3], 4)
+
+        act, slope, branch = hidden_forward(f, w1, hidden_bias, w2)
+        layer_out = collect_rows(
+            (x2 + (junction("sum", [("sum", branch)], [], 5) + out_bias3)).astype(low)
+        )
 
         dz_own = spread_rows(cotangent)
         dz = row_gather(dz_own)
         g1, g2, hidden_bias_grad, df = hidden_backward(dz, f, w1, w2, act, slope)
         g1_parts = grads_of([g1[j] for j in range(PARTS)])
         g2_parts = grads_of([g2[j] for j in range(PARTS)])
-        back3, gain_grad3, shift_grad3 = norm_backward(row_scatter(df), normed3, scaling3, gain3)
-        dx2 = dz_own.astype(f32) + back3
-
-        dyc_own = dx2.astype(low)
-        dyc = row_gather(dyc_own)
-        doc = mm(dyc, wo2).astype(low)
+        dx2, dyc, stats3 = junction("backward", [("sum", df)], [dz_own, x2, gain3], 6)
+
+        doc = mm_nt(dyc, wo2).astype(low)
         dq2, dk2, dv2 = attend_back(q2, k2, v2, doc, o2, lse2, query_ids, src_ids, False)
         grads = [
             mm_tn(c, dq2).astype(low),
@@ -583,31 +960,35 @@
 
         def by_part(arrays):
             return [
-                jnp.concatenate([g[:, j * step : (j + 1) * step] for g in arrays], axis=1)
+                jnp.concatenate(
+                    [
+                        lax.dynamic_slice_in_dim(g, (place ^ j) * step, step, 1)
+                        for g in arrays
+                    ],
+                    axis=1,
+                )
                 for j in range(PARTS)
             ]
 
         cross_grads = grads_of(by_part(grads))
-        enc_back = row_scatter(mm_nt(dk2, wk2) + mm_nt(dv2, wv2))
+        enc_back = junction("sum", [("nt", dk2, wk2), ("nt", dv2, wv2)], [], 7)
         encoder_grad = enc_back[:, :wide]
         for k in range(1, n_col):
             encoder_grad = encoder_grad + to_col(
                 enc_back[:, k * wide : (k + 1) * wide].astype(low), k
             ).astype(f32)
-        back2, gain_grad2, shift_grad2 = norm_backward(
-            row_scatter(mm_nt(dq2, wq2)), normed2, scaling2, gain2
+        dx1, dy, stats2 = junction("backward", [("nt", dq2, wq2)], [dx2, x1, gain2], 8)
+
+        do = mm_nt(dy, wo1).astype(low)
+        dq1, dk1, dv1 = attend_back(q1, k1, v1, do, o1, lse1, query_ids, key_ids, True)
+        da_before = junction("sum", [("nt", dk1[:WIN], wk1), ("nt", dv1[:WIN], wv1)], [], 9)
+        da_after = lax.ppermute(
+            da_before.astype(low), "col", [(i + 1, i) for i in range(n_col - 1)]
         )
-        dx1 = dx2 + back2
-
-        dy_own = dx1.astype(low)
-        dy = row_gather(dy_own)
-        do = mm(dy, wo1).astype(low)
-        dq1, dk1, dv1 = attend_back(q1, k1, v1, do, o1, lse1, query_ids, key_ids, True)
-        da_ext = mm_nt(dk1, wk1) + mm_nt(dv1, wv1)
-        da_before = row_scatter(da_ext[:WIN]).astype(low)
-        da_after = lax.ppermute(da_before, "col", [(i + 1, i) for i in range(n_col - 1)])
         da_after = jnp.concatenate([da_after[:, -wide:], da_after[:, :-wide]], axis=1)
-        da = row_scatter(da_ext[WIN:] + mm_nt(dq1, wq1)) + da_after.astype(f32)
+        da = junction(
+            "sum", [("nt", dq1, wq1), ("nt", dk1[WIN:], wk1), ("nt", dv1[WIN:], wv1)], [], 10
+        ) + da_after.astype(f32)
         grads = [
             mm_tn(a, dq1).astype(low),
             mm_tn(a_ext, dk1).astype(low),
@@ -615,15 +996,16 @@
             mm_tn(dy, o1).astype(low),
         ]
         self_grads = grads_of(by_part(grads))
+        normed1, scaling1 = norm_rows(x0.astype(f32))
         back1, gain_grad1, shift_grad1 = norm_backward(da, normed1, scaling1, gain1)
         tokens_grad = collect_rows((dx1 + back1).astype(low)).astype(f32)
 
         def total(x):
             return jnp.sum(x, axis=0, dtype=f32)
 
-        feature_grads = jnp.stack([
-            gain_grad1, shift_grad1, total(dy_own), gain_grad2, shift_grad2, total(dyc_own),
-            gain_grad3, shift_grad3, total(dz_own),
+        feature_grads = jnp.concatenate([
+            jnp.stack([gain_grad1, shift_grad1]), stats2[2:3], stats2[:2], stats3[2:3], stats3[:2],
+            total(dz_own)[None],
         ])
         count = feature_grads.shape[0]
         chunks = jnp.moveaxis(feature_grads.reshape(count, n_col, wide), 1, 0)
@@ -635,9 +1017,9 @@
         column_grads = []
         for vector in (total(dq1), total(dv1), total(dq2), total(dv2), hidden_bias_grad):
             parts = vector.reshape(PARTS, -1)
-            column_grads.append(
-                jnp.concatenate(in_order([parts[j] for j in range(PARTS)])).reshape(n_col, -1)
-            )
+            if vector is hidden_bias_grad:
+                parts = jnp.stack(in_order([parts[j] for j in range(PARTS)]))
+            column_grads.append(parts.reshape(n_col, -1))
         column_grads = lax.psum(jnp.concatenate(column_grads, axis=1), ("dp", "col"))
         column_grads = lax.dynamic_index_in_dim(column_grads, col, 0, keepdims=False)
 

time: 1310 us -> 1200 us (0.916)
  Pallas kernels: 215 us -> 403 us
  waiting for transfers between devices: 404 us -> 299 us
  local copies, waits for them, and re-layouts: 170 us -> 102 us
  other arithmetic: 144 us -> 89.9 us
  blocking collectives: 163 us -> 136 us
  starting transfers between devices: 131 us -> 113 us
    pallas_call x0 -> x10, Pallas kernels: none -> 188 us  [the longest x1 109 us: start(): pl.pallas_call(functools.partial(start_kernel, n_col=n_col), in_specs=[AN...]
    ppermute x21 -> x9, waiting for transfers between devices: 102 us -> 38.2 us  [from_col(): return lax.ppermute(x, 'col', [(i, (i - k) % n_col) for i in range(n_col)])]
    all_gather x2 -> x0, blocking collectives: 53.2 us -> none  [the longest x1 40.6 us: local(): columns = lax.all_gather(column_vectors, 'col', axis=0)]
    ppermute x21, waiting for transfers between devices: 142 us -> 90.1 us  [to_col(): return lax.ppermute(x, 'col', [(i, (i + k) % n_col) for i in range(n_col)])]
    ppermute x48 -> x40, waiting for transfers between devices: 126 us -> 170 us  [across(): return lax.ppermute(x, 'dp', [(i, i ^ bit) for i in range(n_dp)])]
    unnamed x530 -> x246, local copies, waits for them, and re-layouts: 67.6 us -> 28.5 us
    ppermute x2 -> x1, waiting for transfers between devices: 34.9 us -> 0.01 us  [local(): lax.ppermute(da_before.astype(low), 'col', [(i + 1, i) for i in range(n_c...]
    psum x1, blocking collectives: 41.2 us -> 63 us  [local(): chunks = lax.psum(chunks, ('dp', 'row', 'col'))]
  transfers between devices with their start and end apart: 112 -> 75, of which waited for: 38 -> 25; matrix products, arithmetic and copies ran while one was open for 25% -> 14% of each run, Pallas kernels for 8% -> 8%
where the time goes in v2:
time: 1200 us; the launch traced here: 1190 us
  Pallas kernels  403 us (34%)
  waiting for transfers between devices  299 us (25%)
  blocking collectives  136 us (11%)
  starting transfers between devices  113 us (9%)
  local copies, waits for them, and re-layouts  102 us (8%)
  other arithmetic  89.9 us (7%)
  matrix products  48.5 us (4%)
    ppermute x40, waiting for transfers between devices, across(): return lax.ppermute(x, 'dp', [(i, i ^ bit) for i in range(n_dp)])  170 us
    pallas_call x1, Pallas kernels, start(): pl.pallas_call(functools.partial(start_kernel, n_col=n_col), in_specs=[AN...  109 us
    ppermute x21, waiting for transfers between devices, to_col(): return lax.ppermute(x, 'col', [(i, (i + k) % n_col) for i in range(n_col)])  90.1 us
    psum x1, blocking collectives, local(): lax.psum(jnp.concatenate(column_grads, axis=1), ('dp', 'col'))  72.9 us
    pallas_call x2, Pallas kernels, attend_back(): pl.pallas_call(functools.partial(attend_back_kernel, span=span, windowed=...  70.7 us
    pallas_call x8, Pallas kernels, junction(): pl.pallas_call(functools.partial(junction_kernel, kinds=kinds, mode=mode)...  70.1 us
    psum x1, blocking collectives, local(): chunks = lax.psum(chunks, ('dp', 'row', 'col'))  63 us
    pallas_call x1, Pallas kernels, hidden_backward(): pl.pallas_call(hidden_back_kernel, grid=grid, in_specs=[whole, turned, tu...  56 us
  transfers between devices with their start and end apart: 75, of which 25 were waited for; matrix products, arithmetic and copies ran while one was open for 14% of the time, Pallas kernels for 8%

profile of v2, /device:TPU:8, one launch (start us, length us, event | category | flops | bytes accessed | tf_op | source)
XLA Modules:
  0.0 1193.6 jit_solution(11813849196511291807)
XLA Ops:
  6.9 109.4 %start.1 = (bf16[2,512,1024]{2,1,0:T(8,128)(2,1)}, bf16[1024,1024]{1,0:T(8,128)(2,1)}, f32[16,1024]{1,0:T(8,128)}, f32[4,16,128]{2,1,0:T(8,128)}, bf16[1024,512]...) custom-call(bf16[2048,256]{1,0:T(8,128)(2,1)} %tokens.1, ...), custom_call_target="tpu_custom_call" | custom-call | tf_op jit(solution)/shard_map/start/pallas_call | solution.py:569
  120.9 12.1 %collective-permute-start.1 = (bf16[256,1024]{1,0:T(8,128)(2,1)}, bf16[256,1024]{1,0:T(8,128)(2,1)}, u32[]{:S(2)}, u32[]{:S(2)}) collective-permute-start(bf16[256,1024]{1,0:T(8,128)(2,1)} %get-tuple-element.233), channel_id=1, source_target_pairs={{0,2},{1,3},{2,0},{3,1},{4,6},{5,7},{6,4},{7,5},{8,10},{9,11},{10,... | collective-permute-start | bytes 1572872 | tf_op jit(solution)/shard_map/ppermute | solution.py:766
  145.0 8.7 enter.1
  153.8 4.0 fusion.22.q_ref
  157.8 3.7 convolution_convert_fusion.k_ref
  161.5 3.7 add_convert_fusion.v_ref
  165.2 27.8 %attend.2 = (bf16[1024,512]{1,0:T(8,128)(2,1)}, f32[4,8,1024]{2,1,0:T(8,128)}) custom-call(bf16[1024,512]{1,0:T(8,128)(2,1)} %fusion.22.q_ref, bf16[2048,512]{1,0:T(8,128)(2,1)} %convolution_convert_fusion.k_ref, bf16[2048,512]{1,0:T(8,128)(2,1)} %add_convert_fusion.v_ref, s32[1024,1]{1,0:T(8,128)} %copy.95.qid_ref, s32[1,2048]{1,0:T(1,128)} %bitcast.370), custom_call_target="tpu_custom_call" | custom-call | flops 10737418240 | bytes 4194304 | tf_op jit(solution)/shard_map/attend/pallas_call | solution.py:95
  193.1 9.7 junction_forward.2
  202.8 4.0 fusion.25.q_ref
  226.5 10.1 collective-permute-done.8
  238.9 20.1 %collective-permute-done.9 = bf16[256,1024]{1,0:T(8,128)(2,1)S(1)} collective-permute-done((bf16[256,1024]{1,0:T(8,128)(2,1)}, bf16[256,1024]{1,0:T(8,128)(2,1)S(1)}, u32[]{:S(2)}, u32[]{:S(2)}) %collective-permute-start.9) | collective-permute-done | bytes 524320 | tf_op jit(solution)/shard_map/ppermute | solution.py:766
  272.7 21.7 %attend.3 = (bf16[1024,512]{1,0:T(8,128)(2,1)}, f32[4,8,1024]{2,1,0:T(8,128)}) custom-call(bf16[1024,512]{1,0:T(8,128)(2,1)} %fusion.25.q_ref, bf16[1024,512]{1,0:T(8,128)(2,1)} %convolution_convert_fusion.8.k_ref, bf16[1024,512]{1,0:T(8,128)(2,1)} %add_convert_fusion.2.v_ref, s32[1024,1]{1,0:T(8,128)} %copy.95.qid_ref, s32[1,1024]{1,0:T(1,128)} %bitcast.373), custom_call_target="tpu_custom_call" | custom-call | flops 8589934592 | bytes 2097152 | tf_op jit(solution)/shard_map/attend/pallas_call | solution.py:95
  294.4 10.0 junction_forward.3
  304.4 4.1 copy.103
  326.2 13.0 %maximum_select_fusion.dz_ref = bf16[1024,1024]{1,0:T(8,128)(2,1)S(1)} fusion(bf16[512,1024]{1,0:T(8,128)(2,1)} %collective-permute-done.22, bf16[512,256]{1,0:T(8,128)(2,1)S(1)} %copy-done.72, bf16[512,256]{1,0:T(8,128)(2,1)S(1)} %copy-done.74, bf16[512,256]{1,0:T(8,128)(2,1)S(1)} %copy-done.76, bf16[512,256]{1,0:T(8,128)(2,1)S(1)} %get-tuple-element.299, ...), kind=kLoop, calls=%fused_computation.28 | loop fusion | flops 22020096 | bytes 4194305 | tf_op jit(solution)/shard_map/jit(_where)/select_n | solution.py:807
  354.4 4.0 pad_maximum_fusion.w1_ref
  358.4 4.0 collective-permute-done.13
  365.5 4.0 pad_maximum_fusion.1.w2_ref
  369.5 38.6 %hidden_forward.1 = (bf16[4,1024,1024]{2,1,0:T(8,128)(2,1)}, bf16[4,1024,1024]{2,1,0:T(8,128)(2,1)}, bf16[1024,1024]{1,0:T(8,128)(2,1)}) custom-call(bf16[1024,1024]{1,0:T(8,128)(2,1)} %get-tuple-element.88.f_ref, bf16[4,1024,1024]{2,1,0:T(8,128)(2,1)} %pad_maximum_fusion.w1_ref, f32[4,1,1024]{2,1,0:T(1,128)} %pad_maximum_fusion.24.b1_ref, ...), custom_call_target="tpu_custom_call" | custom-call | flops 17179869184 | bytes 33554432 | tf_op jit(solution)/shard_map/hidden_forward/pallas_call | solution.py:254
  408.1 56.0 %hidden_backward.1 = (bf16[4,1024,1024]{2,1,0:T(8,128)(2,1)}, bf16[4,1024,1024]{2,1,0:T(8,128)(2,1)}, f32[4,1,1024]{2,1,0:T(1,128)}, bf16[1024,1024]{1,0:T(8,128)(2,1)}) custom-call(bf16[1024,1024]{1,0:T(8,128)(2,1)} %copy-done.6, bf16[1024,1024]{1,0:T(8,128)(2,1)} %copy.104.dzt_ref, bf16[1024,1024]{1,0:T(8,128)(2,1)} %bitcast.352, ...), custom_call_target="tpu_custom_call" | custom-call | flops 34359738368 | bytes 67108864 | tf_op jit(solution)/shard_map/hidden_backward/pallas_call | solution.py:325
  464.1 10.2 junction_backward.2
  474.3 3.9 convolution_convert_fusion.7.do_ref
  478.2 32.2 %attend_back.2 = (bf16[1024,512]{1,0:T(8,128)(2,1)}, bf16[1024,512]{1,0:T(8,128)(2,1)}, bf16[1024,512]{1,0:T(8,128)(2,1)}) custom-call(bf16[1024,512]{1,0:T(8,128)(2,1)} %fusion.25.q_ref, bf16[1024,512]{1,0:T(8,128)(2,1)} %convolution_convert_fusion.8.k_ref, bf16[1024,512]{1,0:T(8,128)(2,1)} %add_convert_fusion.2.v_ref, ...), custom_call_target="tpu_custom_call" | custom-call | flops 21474836480 | bytes 4194304 | tf_op jit(solution)/shard_map/attend_back/pallas_call | solution.py:183
  510.5 11.5 junction_backward.3
  528.9 7.2 junction_sum.7
  545.5 38.5 %attend_back.3 = (bf16[1024,512]{1,0:T(8,128)(2,1)}, bf16[2048,512]{1,0:T(8,128)(2,1)}, bf16[2048,512]{1,0:T(8,128)(2,1)}) custom-call(bf16[1024,512]{1,0:T(8,128)(2,1)} %fusion.22.q_ref, bf16[2048,512]{1,0:T(8,128)(2,1)} %convolution_convert_fusion.k_ref, bf16[2048,512]{1,0:T(8,128)(2,1)} %add_convert_fusion.v_ref, ...), custom_call_target="tpu_custom_call" | custom-call | flops 26843545600 | bytes 8388608 | tf_op jit(solution)/shard_map/attend_back/pallas_call | solution.py:183
  584.0 5.1 convolution_convert_fusion.9
  604.7 5.9 junction_sum.4
  617.4 4.2 collective-permute-start.15
  621.8 7.2 junction_sum.6
  655.7 8.4 junction_sum.5
  664.1 72.9 %psum.15 = f32[4,1536]{1,0:T(4,128)S(1)} all-reduce(f32[4,1536]{1,0:T(4,128)S(1)} %constant_dynamic-update-slice_fusion.14), channel_id=1, replica_groups=mesh['dp'=4,'row'=2,'col'=4] {'dp','col'}, use_global_device_ids=true, to_apply=%region_16.17 | all-reduce | flops 6144 | bytes 49152 | tf_op jit(solution)/shard_map/psum | solution.py:1023
  739.4 6.2 collective-permute-start.28
  765.2 13.5 %collective-permute-done.42 = bf16[2,512,512]{1,2,0:T(8,128)(2,1)} collective-permute-done((bf16[2,512,512]{1,2,0:T(8,128)(2,1)}, bf16[2,512,512]{1,2,0:T(8,128)(2,1)}, u32[]{:S(2)}, u32[]{:S(2)}) %collective-permute-start.42) | collective-permute-done | bytes 1048608 | tf_op jit(solution)/shard_map/ppermute | solution.py:772
  781.0 20.2 %collective-permute-done.31 = bf16[2,512,512]{1,2,0:T(8,128)(2,1)} collective-permute-done((bf16[2,512,512]{1,2,0:T(8,128)(2,1)}, bf16[2,512,512]{1,2,0:T(8,128)(2,1)}, u32[]{:S(2)}, u32[]{:S(2)}) %collective-permute-start.31) | collective-permute-done | bytes 1048608 | tf_op jit(solution)/shard_map/ppermute | solution.py:772
  811.4 30.1 %collective-permute-done.43 = bf16[512,512]{0,1:T(8,128)(2,1)S(1)} collective-permute-done((bf16[512,512]{0,1:T(8,128)(2,1)S(1)}, bf16[512,512]{0,1:T(8,128)(2,1)S(1)}, u32[]{:S(2)}, u32[]{:S(2)}) %collective-permute-start.43) | collective-permute-done | bytes 524320 | tf_op jit(solution)/shard_map/ppermute | solution.py:772
  844.4 63.0 %psum.14 = f32[4,9,256]{2,0,1:T(4,128)S(1)} all-reduce(f32[4,9,256]{2,0,1:T(4,128)S(1)} %fusion.52), channel_id=1, replica_groups=mesh['dp'=4,'row'=2,'col'=4] {'dp','row','col'}, use_global_device_ids=true, to_apply=%region_11.12 | all-reduce | flops 9216 | bytes 73728 | tf_op jit(solution)/shard_map/psum | solution.py:1015
  919.5 48.3 %collective-permute-done.35 = bf16[512,512]{0,1:T(8,128)(2,1)S(1)} collective-permute-done((bf16[512,512]{0,1:T(8,128)(2,1)S(1)}, bf16[512,512]{0,1:T(8,128)(2,1)S(1)}, u32[]{:S(2)}, u32[]{:S(2)}) %collective-permute-start.35) | collective-permute-done | bytes 524320 | tf_op jit(solution)/shard_map/ppermute | solution.py:772
  973.4 9.9 collective-permute-done.44
  988.8 4.2 collective-permute-done.37
  998.7 26.0 %collective-permute-done.50 = bf16[256,512]{0,1:T(8,128)(2,1)S(1)} collective-permute-done((bf16[256,512]{0,1:T(8,128)(2,1)S(1)}, bf16[256,512]{0,1:T(8,128)(2,1)S(1)}, u32[]{:S(2)}, u32[]{:S(2)}) %collective-permute-start.50) | collective-permute-done | bytes 262176 | tf_op jit(solution)/shard_map/ppermute | solution.py:772
  1033.1 16.5 %collective-permute-done.38 = bf16[256,512]{0,1:T(8,128)(2,1)S(1)} collective-permute-done((bf16[256,512]{0,1:T(8,128)(2,1)S(1)}, bf16[256,512]{0,1:T(8,128)(2,1)S(1)}, u32[]{:S(2)}, u32[]{:S(2)}) %collective-permute-start.38) | collective-permute-done | bytes 262176 | tf_op jit(solution)/shard_map/ppermute | solution.py:772
  1056.4 9.4 collective-permute-start.70
  1075.2 22.5 %collective-permute-done.70 = bf16[256,1024]{1,0:T(8,128)(2,1)S(1)} collective-permute-done((bf16[256,1024]{1,0:T(8,128)(2,1)S(1)}, bf16[256,1024]{1,0:T(8,128)(2,1)S(1)}, u32[]{:S(2)}, u32[]{:S(2)}) %collective-permute-start.70) | collective-permute-done | bytes 524320 | tf_op jit(solution)/shard_map/ppermute | solution.py:769
  1099.9 30.6 %collective-permute-done.66 = bf16[256,1024]{1,0:T(8,128)(2,1)S(1)} collective-permute-done((bf16[256,1024]{1,0:T(8,128)(2,1)S(1)}, bf16[256,1024]{1,0:T(8,128)(2,1)S(1)}, u32[]{:S(2)}, u32[]{:S(2)}) %collective-permute-start.66) | collective-permute-done | bytes 524320 | tf_op jit(solution)/shard_map/ppermute | solution.py:769
  1133.7 10.4 collective-permute-done.59
  1144.1 8.8 collective-permute-done.55
  1185.3 5.6 copy.116
  (573 shorter events, 289.8 us)
Async XLA Ops:
  117.7 96.5 %collective-permute-start = (bf16[256,1024]{1,0:T(8,128)(2,1)}, bf16[256,1024]{1,0:T(8,128)(2,1)S(1)}, u32[]{:S(2)}, u32[]{:S(2)}) collective-permute-start(bf16[256,1024]{1,0:T(8,128)(2,1)} %get-tuple-element.233), channel_id=1, source_target_pairs={{0,3},{1,0},{2,1},{3,2},{4,7},{5,4},{6,5},{7,6},{8,11},{9,8},{10,9... | collective-permute-start | bytes 1572872 | tf_op jit(solution)/shard_map/ppermute | solution.py:766
  120.9 99.0 %collective-permute-start.1 = (bf16[256,1024]{1,0:T(8,128)(2,1)}, bf16[256,1024]{1,0:T(8,128)(2,1)}, u32[]{:S(2)}, u32[]{:S(2)}) collective-permute-start(bf16[256,1024]{1,0:T(8,128)(2,1)} %get-tuple-element.233), channel_id=1, source_target_pairs={{0,2},{1,3},{2,0},{3,1},{4,6},{5,7},{6,4},{7,5},{8,10},{9,11},{10,... | collective-permute-start | bytes 1572872 | tf_op jit(solution)/shard_map/ppermute | solution.py:766
  133.0 90.3 %collective-permute-start.2 = (bf16[256,1024]{1,0:T(8,128)(2,1)}, bf16[256,1024]{1,0:T(8,128)(2,1)}, u32[]{:S(2)}, u32[]{:S(2)}) collective-permute-start(bf16[256,1024]{1,0:T(8,128)(2,1)} %get-tuple-element.233), channel_id=1, source_target_pairs={{0,1},{1,2},{2,3},{3,0},{4,5},{5,6},{6,7},{7,4},{8,9},{9,10},{10,1... | collective-permute-start | bytes 1572872 | tf_op jit(solution)/shard_map/ppermute | solution.py:766
  137.3 80.6 %collective-permute-start.7 = (bf16[256,1024]{1,0:T(8,128)(2,1)}, bf16[256,1024]{1,0:T(8,128)(2,1)}, u32[]{:S(2)}, u32[]{:S(2)}) collective-permute-start(bf16[256,1024]{1,0:T(8,128)(2,1)} %get-tuple-element.229), channel_id=1, source_target_pairs={{0,3},{1,0},{2,1},{3,2},{4,7},{5,4},{6,5},{7,6},{8,11},{9,8},{10,9... | collective-permute-start | bytes 1572872 | tf_op jit(solution)/shard_map/ppermute | solution.py:766
  141.4 70.8 %collective-permute-start.18 = (bf16[2,512,256]{2,1,0:T(8,128)(2,1)}, bf16[2,512,256]{2,1,0:T(8,128)(2,1)}, u32[]{:S(2)}, u32[]{:S(2)}) collective-permute-start(bf16[2,512,256]{2,1,0:T(8,128)(2,1)} %get-tuple-element.304), channel_id=1, source_target_pairs={{0,4},{4,0},{1,5},{5,1},{2,6},{6,2},{3,7},{7,3},{8,12},{12,8},{9,1... | collective-permute-start | bytes 1572872 | tf_op jit(solution)/shard_map/ppermute | solution.py:763
  214.2 44.8 %collective-permute-start.9 = (bf16[256,1024]{1,0:T(8,128)(2,1)}, bf16[256,1024]{1,0:T(8,128)(2,1)S(1)}, u32[]{:S(2)}, u32[]{:S(2)}) collective-permute-start(bf16[256,1024]{1,0:T(8,128)(2,1)} %get-tuple-element.229), channel_id=1, source_target_pairs={{0,1},{1,2},{2,3},{3,0},{4,5},{5,6},{6,7},{7,4},{8,9},{9,10},{10,1... | collective-permute-start | bytes 1572872 | tf_op jit(solution)/shard_map/ppermute | solution.py:766
  217.9 46.7 %collective-permute-start.21 = (bf16[512,256]{1,0:T(8,128)(2,1)S(1)}, bf16[512,256]{1,0:T(8,128)(2,1)S(1)}, u32[]{:S(2)}, u32[]{:S(2)}) collective-permute-start(bf16[512,256]{1,0:T(8,128)(2,1)S(1)} %get-tuple-element.300), channel_id=1, source_target_pairs={{0,1},{1,2},{2,3},{3,0},{4,5},{5,6},{6,7},{7,4},{8,9},{9,10},{10,1... | collective-permute-start | bytes 786440 | tf_op jit(solution)/shard_map/ppermute | solution.py:766
  220.0 49.4 %collective-permute-start.20 = (bf16[512,256]{1,0:T(8,128)(2,1)S(1)}, bf16[512,256]{1,0:T(8,128)(2,1)S(1)}, u32[]{:S(2)}, u32[]{:S(2)}) collective-permute-start(bf16[512,256]{1,0:T(8,128)(2,1)S(1)} %get-tuple-element.301), channel_id=1, source_target_pairs={{0,2},{1,3},{2,0},{3,1},{4,6},{5,7},{6,4},{7,5},{8,10},{9,11},{10,... | collective-permute-start | bytes 786440 | tf_op jit(solution)/shard_map/ppermute | solution.py:766
  223.3 48.9 %collective-permute-start.19 = (bf16[512,256]{1,0:T(8,128)(2,1)S(1)}, bf16[512,256]{1,0:T(8,128)(2,1)S(1)}, u32[]{:S(2)}, u32[]{:S(2)}) collective-permute-start(bf16[512,256]{1,0:T(8,128)(2,1)S(1)} %get-tuple-element.302), channel_id=1, source_target_pairs={{0,3},{1,0},{2,1},{3,2},{4,7},{5,4},{6,5},{7,6},{8,11},{9,8},{10,9... | collective-permute-start | bytes 786440 | tf_op jit(solution)/shard_map/ppermute | solution.py:766
  236.6 82.4 %collective-permute-start.4 = (bf16[768,1024]{1,0:T(8,128)(2,1)}, bf16[768,1024]{1,0:T(8,128)(2,1)}, u32[]{:S(2)}, u32[]{:S(2)}) collective-permute-start(bf16[768,1024]{1,0:T(8,128)(2,1)} %constant_dynamic-update-slice_fusion.1), channel_id=1, source_target_pairs={{0,16},{8,24},{16,0},{24,8},{1,17},{9,25},{17,1},{25,9},{2,18},{10... | collective-permute-start | bytes 4718600 | tf_op jit(solution)/shard_map/ppermute | solution.py:772
  259.1 63.5 %collective-permute-start.3 = (bf16[768,1024]{1,0:T(8,128)(2,1)}, bf16[768,1024]{1,0:T(8,128)(2,1)}, u32[]{:S(2)}, u32[]{:S(2)}) collective-permute-start(bf16[768,1024]{1,0:T(8,128)(2,1)} %constant_dynamic-update-slice_fusion.1), channel_id=1, source_target_pairs={{0,8},{8,0},{16,24},{24,16},{1,9},{9,1},{17,25},{25,17},{2,10},{10... | collective-permute-start | bytes 4718600 | tf_op jit(solution)/shard_map/ppermute | solution.py:772
  264.6 77.5 %collective-permute-start.11 = (bf16[768,1024]{1,0:T(8,128)(2,1)}, bf16[768,1024]{1,0:T(8,128)(2,1)}, u32[]{:S(2)}, u32[]{:S(2)}) collective-permute-start(bf16[768,1024]{1,0:T(8,128)(2,1)} %constant_dynamic-update-slice_fusion.4), channel_id=1, source_target_pairs={{0,16},{8,24},{16,0},{24,8},{1,17},{9,25},{17,1},{25,9},{2,18},{10... | collective-permute-start | bytes 4718600 | tf_op jit(solution)/shard_map/ppermute | solution.py:772
  269.4 74.5 %collective-permute-start.10 = (bf16[768,1024]{1,0:T(8,128)(2,1)}, bf16[768,1024]{1,0:T(8,128)(2,1)}, u32[]{:S(2)}, u32[]{:S(2)}) collective-permute-start(bf16[768,1024]{1,0:T(8,128)(2,1)} %constant_dynamic-update-slice_fusion.4), channel_id=1, source_target_pairs={{0,8},{8,0},{16,24},{24,16},{1,9},{9,1},{17,25},{25,17},{2,10},{10... | collective-permute-start | bytes 4718600 | tf_op jit(solution)/shard_map/ppermute | solution.py:772
  272.5 53.7 %collective-permute-start.22 = (bf16[512,1024]{1,0:T(8,128)(2,1)S(1)}, bf16[512,1024]{1,0:T(8,128)(2,1)}, u32[]{:S(2)}, u32[]{:S(2)}) collective-permute-start(bf16[512,1024]{1,0:T(8,128)(2,1)S(1)} %get-tuple-element.201.refs_1_), channel_id=1, source_target_pairs={{0,4},{4,0},{1,5},{5,1},{2,6},{6,2},{3,7},{7,3},{8,12},{12,8},{9,1... | collective-permute-start | bytes 3145736 | tf_op jit(solution)/shard_map/ppermute | solution.py:763
  321.1 31.2 %collective-permute-start.6 = (bf16[384,1024]{1,0:T(8,128)(2,1)}, bf16[384,1024]{1,0:T(8,128)(2,1)}, u32[]{:S(2)}, u32[]{:S(2)}) collective-permute-start(bf16[384,1024]{1,0:T(8,128)(2,1)} %slice.721), channel_id=1, source_target_pairs={{0,8},{8,0},{16,24},{24,16},{1,9},{9,1},{17,25},{25,17},{2,10},{10... | collective-permute-start | bytes 2359304 | tf_op jit(solution)/shard_map/ppermute | solution.py:772
  324.7 27.7 %collective-permute-start.5 = (bf16[384,1024]{1,0:T(8,128)(2,1)}, bf16[384,1024]{1,0:T(8,128)(2,1)}, u32[]{:S(2)}, u32[]{:S(2)}) collective-permute-start(bf16[384,1024]{1,0:T(8,128)(2,1)} %slice.720), channel_id=1, source_target_pairs={{0,16},{8,24},{16,0},{24,8},{1,17},{9,25},{17,1},{25,9},{2,18},{10... | collective-permute-start | bytes 2359304 | tf_op jit(solution)/shard_map/ppermute | solution.py:772
  614.6 123.1 %collective-permute-start.14 = (bf16[512,256]{1,0:T(8,128)(2,1)}, bf16[512,256]{1,0:T(8,128)(2,1)}, u32[]{:S(2)}, u32[]{:S(2)}) collective-permute-start(bf16[512,256]{1,0:T(8,128)(2,1)} %get-tuple-element.311), channel_id=1, source_target_pairs={{0,1},{1,2},{2,3},{3,0},{4,5},{5,6},{6,7},{7,4},{8,9},{9,10},{10,1... | collective-permute-start | bytes 786440 | tf_op jit(solution)/shard_map/ppermute | solution.py:769
  617.4 121.9 %collective-permute-start.15 = (bf16[512,256]{1,0:T(8,128)(2,1)}, bf16[512,256]{1,0:T(8,128)(2,1)}, u32[]{:S(2)}, u32[]{:S(2)}) collective-permute-start(bf16[512,256]{1,0:T(8,128)(2,1)} %get-tuple-element.310), channel_id=1, source_target_pairs={{0,2},{1,3},{2,0},{3,1},{4,6},{5,7},{6,4},{7,5},{8,10},{9,11},{10,... | collective-permute-start | bytes 786440 | tf_op jit(solution)/shard_map/ppermute | solution.py:769
  621.6 125.6 %collective-permute-start.16 = (bf16[512,256]{1,0:T(8,128)(2,1)}, bf16[512,256]{1,0:T(8,128)(2,1)}, u32[]{:S(2)}, u32[]{:S(2)}) collective-permute-start(bf16[512,256]{1,0:T(8,128)(2,1)} %get-tuple-element.309), channel_id=1, source_target_pairs={{0,3},{1,0},{2,1},{3,2},{4,7},{5,4},{6,5},{7,6},{8,11},{9,8},{10,9... | collective-permute-start | bytes 786440 | tf_op jit(solution)/shard_map/ppermute | solution.py:769
  631.9 126.5 %collective-permute-start.23 = (bf16[512,1024]{1,0:T(8,128)(2,1)}, bf16[512,1024]{1,0:T(8,128)(2,1)}, u32[]{:S(2)}, u32[]{:S(2)}) collective-permute-start(bf16[512,1024]{1,0:T(8,128)(2,1)} %convert_element_type.218), channel_id=1, source_target_pairs={{1,0},{2,1},{3,2},{5,4},{6,5},{7,6},{9,8},{10,9},{11,10},{13,12},{... | collective-permute-start | bytes 3145736 | tf_op jit(solution)/shard_map/ppermute | solution.py:985
  636.4 116.0 %collective-permute-start.30 = (bf16[512,256]{1,0:T(8,128)(2,1)}, bf16[512,256]{1,0:T(8,128)(2,1)S(1)}, u32[]{:S(2)}, u32[]{:S(2)}) collective-permute-start(bf16[512,256]{1,0:T(8,128)(2,1)} %get-tuple-element.291), channel_id=1, source_target_pairs={{0,3},{1,0},{2,1},{3,2},{4,7},{5,4},{6,5},{7,6},{8,11},{9,8},{10,9... | collective-permute-start | bytes 786440 | tf_op jit(solution)/shard_map/ppermute | solution.py:769
  752.4 48.7 %collective-permute-start.31 = (bf16[2,512,512]{1,2,0:T(8,128)(2,1)}, bf16[2,512,512]{1,2,0:T(8,128)(2,1)}, u32[]{:S(2)}, u32[]{:S(2)}) collective-permute-start(bf16[2,512,512]{1,2,0:T(8,128)(2,1)} %pad_maximum_fusion.13), channel_id=1, source_target_pairs={{0,8},{8,0},{16,24},{24,16},{1,9},{9,1},{17,25},{25,17},{2,10},{10... | collective-permute-start | bytes 3145736 | tf_op jit(solution)/shard_map/ppermute | solution.py:772
  754.4 162.9 %collective-permute-start.64 = (bf16[2,512,1024]{2,1,0:T(8,128)(2,1)}, bf16[2,512,1024]{2,1,0:T(8,128)(2,1)}, u32[]{:S(2)}, u32[]{:S(2)}) collective-permute-start(bf16[2,512,1024]{2,1,0:T(8,128)(2,1)} %pad_maximum_fusion.4), channel_id=1, source_target_pairs={{0,8},{8,0},{16,24},{24,16},{1,9},{9,1},{17,25},{25,17},{2,10},{10... | collective-permute-start | bytes 6291464 | tf_op jit(solution)/shard_map/ppermute | solution.py:772
  755.4 163.0 %collective-permute-start.67 = (bf16[2,512,1024]{2,1,0:T(8,128)(2,1)}, bf16[2,512,1024]{2,1,0:T(8,128)(2,1)}, u32[]{:S(2)}, u32[]{:S(2)}) collective-permute-start(bf16[2,512,1024]{2,1,0:T(8,128)(2,1)} %stack.296), channel_id=1, source_target_pairs={{0,16},{8,24},{16,0},{24,8},{1,17},{9,25},{17,1},{25,9},{2,18},{10... | collective-permute-start | bytes 6291464 | tf_op jit(solution)/shard_map/ppermute | solution.py:772
  764.7 39.4 %collective-permute-start.24 = (bf16[512,256]{1,0:T(8,128)(2,1)}, bf16[512,256]{1,0:T(8,128)(2,1)S(1)}, u32[]{:S(2)}, u32[]{:S(2)}) collective-permute-start(bf16[512,256]{1,0:T(8,128)(2,1)} %get-tuple-element.298), channel_id=1, source_target_pairs={{0,1},{1,2},{2,3},{3,0},{4,5},{5,6},{6,7},{7,4},{8,9},{9,10},{10,1... | collective-permute-start | bytes 786440 | tf_op jit(solution)/shard_map/ppermute | solution.py:769
  804.1 37.5 %collective-permute-start.45 = (bf16[2,512,512]{1,2,0:T(8,128)(2,1)S(1)}, bf16[2,512,512]{1,2,0:T(8,128)(2,1)S(1)}, u32[]{:S(2)}, u32[]{:S(2)}) collective-permute-start(bf16[2,512,512]{1,2,0:T(8,128)(2,1)S(1)} %pad_maximum_fusion.22), channel_id=1, source_target_pairs={{0,16},{8,24},{16,0},{24,8},{1,17},{9,25},{17,1},{25,9},{2,18},{10... | collective-permute-start | bytes 3145736 | tf_op jit(solution)/shard_map/ppermute | solution.py:772
  805.9 35.6 %collective-permute-start.43 = (bf16[512,512]{0,1:T(8,128)(2,1)S(1)}, bf16[512,512]{0,1:T(8,128)(2,1)S(1)}, u32[]{:S(2)}, u32[]{:S(2)}) collective-permute-start(bf16[512,512]{0,1:T(8,128)(2,1)S(1)} %get-tuple-element.244), channel_id=1, source_target_pairs={{0,16},{8,24},{16,0},{24,8},{1,17},{9,25},{17,1},{25,9},{2,18},{10... | collective-permute-start | bytes 1572872 | tf_op jit(solution)/shard_map/ppermute | solution.py:772
  808.7 103.5 %collective-permute-start.34 = (bf16[2,512,512]{1,2,0:T(8,128)(2,1)}, bf16[2,512,512]{1,2,0:T(8,128)(2,1)}, u32[]{:S(2)}, u32[]{:S(2)}) collective-permute-start(bf16[2,512,512]{1,2,0:T(8,128)(2,1)} %pad_maximum_fusion.15), channel_id=1, source_target_pairs={{0,16},{8,24},{16,0},{24,8},{1,17},{9,25},{17,1},{25,9},{2,18},{10... | collective-permute-start | bytes 3145736 | tf_op jit(solution)/shard_map/ppermute | solution.py:772
  841.6 68.3 %collective-permute-start.32 = (bf16[512,512]{0,1:T(8,128)(2,1)}, bf16[512,512]{0,1:T(8,128)(2,1)}, u32[]{:S(2)}, u32[]{:S(2)}) collective-permute-start(bf16[512,512]{0,1:T(8,128)(2,1)} %get-tuple-element.270), channel_id=1, source_target_pairs={{0,16},{8,24},{16,0},{24,8},{1,17},{9,25},{17,1},{25,9},{2,18},{10... | collective-permute-start | bytes 1572872 | tf_op jit(solution)/shard_map/ppermute | solution.py:772
  844.3 69.5 %collective-permute-start.46 = (bf16[512,512]{0,1:T(8,128)(2,1)}, bf16[512,512]{0,1:T(8,128)(2,1)}, u32[]{:S(2)}, u32[]{:S(2)}) collective-permute-start(bf16[512,512]{0,1:T(8,128)(2,1)} %fusion.38), channel_id=1, source_target_pairs={{0,8},{8,0},{16,24},{24,16},{1,9},{9,1},{17,25},{25,17},{2,10},{10... | collective-permute-start | bytes 1572872 | tf_op jit(solution)/shard_map/ppermute | solution.py:772
  910.0 86.4 %collective-permute-start.53 = (bf16[2,512,1024]{2,1,0:T(8,128)(2,1)S(1)}, bf16[2,512,1024]{2,1,0:T(8,128)(2,1)S(1)}, u32[]{:S(2)}, u32[]{:S(2)}) collective-permute-start(bf16[2,512,1024]{2,1,0:T(8,128)(2,1)S(1)} %copy-done.31), channel_id=1, source_target_pairs={{0,8},{8,0},{16,24},{24,16},{1,9},{9,1},{17,25},{25,17},{2,10},{10... | collective-permute-start | bytes 6291464 | tf_op jit(solution)/shard_map/ppermute | solution.py:772
  912.2 86.0 %collective-permute-start.56 = (bf16[2,512,1024]{2,1,0:T(8,128)(2,1)S(1)}, bf16[2,512,1024]{2,1,0:T(8,128)(2,1)S(1)}, u32[]{:S(2)}, u32[]{:S(2)}) collective-permute-start(bf16[2,512,1024]{2,1,0:T(8,128)(2,1)S(1)} %copy-done.30), channel_id=1, source_target_pairs={{0,16},{8,24},{16,0},{24,8},{1,17},{9,25},{17,1},{25,9},{2,18},{10... | collective-permute-start | bytes 6291464 | tf_op jit(solution)/shard_map/ppermute | solution.py:772
  913.8 54.1 %collective-permute-start.35 = (bf16[512,512]{0,1:T(8,128)(2,1)S(1)}, bf16[512,512]{0,1:T(8,128)(2,1)S(1)}, u32[]{:S(2)}, u32[]{:S(2)}) collective-permute-start(bf16[512,512]{0,1:T(8,128)(2,1)S(1)} %fusion.44), channel_id=1, source_target_pairs={{0,8},{8,0},{16,24},{24,16},{1,9},{9,1},{17,25},{25,17},{2,10},{10... | collective-permute-start | bytes 1572872 | tf_op jit(solution)/shard_map/ppermute | solution.py:772
  917.3 52.8 %collective-permute-start.48 = (bf16[256,512]{0,1:T(8,128)(2,1)S(1)}, bf16[256,512]{0,1:T(8,128)(2,1)S(1)}, u32[]{:S(2)}, u32[]{:S(2)}) collective-permute-start(bf16[256,512]{0,1:T(8,128)(2,1)S(1)} %get-tuple-element.313), channel_id=1, source_target_pairs={{0,3},{1,0},{2,1},{3,2},{4,7},{5,4},{6,5},{7,6},{8,11},{9,8},{10,9... | collective-permute-start | bytes 786440 | tf_op jit(solution)/shard_map/ppermute | solution.py:769
  918.4 53.2 %collective-permute-start.47 = (bf16[256,512]{0,1:T(8,128)(2,1)S(1)}, bf16[256,512]{0,1:T(8,128)(2,1)S(1)}, u32[]{:S(2)}, u32[]{:S(2)}) collective-permute-start(bf16[256,512]{0,1:T(8,128)(2,1)S(1)} %get-tuple-element.312), channel_id=1, source_target_pairs={{0,2},{1,3},{2,0},{3,1},{4,6},{5,7},{6,4},{7,5},{8,10},{9,11},{10,... | collective-permute-start | bytes 786440 | tf_op jit(solution)/shard_map/ppermute | solution.py:769
  993.0 56.9 %collective-permute-start.65 = (bf16[512,1024]{1,0:T(8,128)(2,1)S(1)}, bf16[512,1024]{1,0:T(8,128)(2,1)S(1)}, u32[]{:S(2)}, u32[]{:S(2)}) collective-permute-start(bf16[512,1024]{1,0:T(8,128)(2,1)S(1)} %get-tuple-element.204), channel_id=1, source_target_pairs={{0,16},{8,24},{16,0},{24,8},{1,17},{9,25},{17,1},{25,9},{2,18},{10... | collective-permute-start | bytes 3145736 | tf_op jit(solution)/shard_map/ppermute | solution.py:772
  994.2 58.7 %collective-permute-start.68 = (bf16[512,1024]{1,0:T(8,128)(2,1)S(1)}, bf16[512,1024]{1,0:T(8,128)(2,1)S(1)}, u32[]{:S(2)}, u32[]{:S(2)}) collective-permute-start(bf16[512,1024]{1,0:T(8,128)(2,1)S(1)} %get-tuple-element.205), channel_id=1, source_target_pairs={{0,8},{8,0},{16,24},{24,16},{1,9},{9,1},{17,25},{25,17},{2,10},{10... | collective-permute-start | bytes 3145736 | tf_op jit(solution)/shard_map/ppermute | solution.py:772
  995.9 28.9 %collective-permute-start.50 = (bf16[256,512]{0,1:T(8,128)(2,1)S(1)}, bf16[256,512]{0,1:T(8,128)(2,1)S(1)}, u32[]{:S(2)}, u32[]{:S(2)}) collective-permute-start(bf16[256,512]{0,1:T(8,128)(2,1)S(1)} %add_convert_fusion.7), channel_id=1, source_target_pairs={{0,16},{8,24},{16,0},{24,8},{1,17},{9,25},{17,1},{25,9},{2,18},{10... | collective-permute-start | bytes 786440 | tf_op jit(solution)/shard_map/ppermute | solution.py:772
  996.3 29.5 %collective-permute-start.49 = (bf16[256,512]{0,1:T(8,128)(2,1)S(1)}, bf16[256,512]{0,1:T(8,128)(2,1)S(1)}, u32[]{:S(2)}, u32[]{:S(2)}) collective-permute-start(bf16[256,512]{0,1:T(8,128)(2,1)S(1)} %add_convert_fusion.7), channel_id=1, source_target_pairs={{0,8},{8,0},{16,24},{24,16},{1,9},{9,1},{17,25},{25,17},{2,10},{10... | collective-permute-start | bytes 786440 | tf_op jit(solution)/shard_map/ppermute | solution.py:772
  998.2 31.8 %collective-permute-start.39 = (bf16[256,512]{0,1:T(8,128)(2,1)S(1)}, bf16[256,512]{0,1:T(8,128)(2,1)S(1)}, u32[]{:S(2)}, u32[]{:S(2)}) collective-permute-start(bf16[256,512]{0,1:T(8,128)(2,1)S(1)} %add_convert_fusion.8), channel_id=1, source_target_pairs={{0,16},{8,24},{16,0},{24,8},{1,17},{9,25},{17,1},{25,9},{2,18},{10... | collective-permute-start | bytes 786440 | tf_op jit(solution)/shard_map/ppermute | solution.py:772
  1024.7 31.0 %collective-permute-start.54 = (bf16[512,1024]{1,0:T(8,128)(2,1)S(1)}, bf16[512,1024]{1,0:T(8,128)(2,1)S(1)}, u32[]{:S(2)}, u32[]{:S(2)}) collective-permute-start(bf16[512,1024]{1,0:T(8,128)(2,1)S(1)} %get-tuple-element.210), channel_id=1, source_target_pairs={{0,16},{8,24},{16,0},{24,8},{1,17},{9,25},{17,1},{25,9},{2,18},{10... | collective-permute-start | bytes 3145736 | tf_op jit(solution)/shard_map/ppermute | solution.py:772
  1025.8 30.5 %collective-permute-start.57 = (bf16[512,1024]{1,0:T(8,128)(2,1)S(1)}, bf16[512,1024]{1,0:T(8,128)(2,1)S(1)}, u32[]{:S(2)}, u32[]{:S(2)}) collective-permute-start(bf16[512,1024]{1,0:T(8,128)(2,1)S(1)} %get-tuple-element.211), channel_id=1, source_target_pairs={{0,8},{8,0},{16,24},{24,16},{1,9},{9,1},{17,25},{25,17},{2,10},{10... | collective-permute-start | bytes 3145736 | tf_op jit(solution)/shard_map/ppermute | solution.py:772
  1056.4 41.3 %collective-permute-start.70 = (bf16[256,1024]{1,0:T(8,128)(2,1)S(1)}, bf16[256,1024]{1,0:T(8,128)(2,1)S(1)}, u32[]{:S(2)}, u32[]{:S(2)}) collective-permute-start(bf16[256,1024]{1,0:T(8,128)(2,1)S(1)} %get-tuple-element.235), channel_id=1, source_target_pairs={{0,3},{1,0},{2,1},{3,2},{4,7},{5,4},{6,5},{7,6},{8,11},{9,8},{10,9... | collective-permute-start | bytes 1572872 | tf_op jit(solution)/shard_map/ppermute | solution.py:769
  1066.2 33.7 %collective-permute-start.69 = (bf16[256,1024]{1,0:T(8,128)(2,1)S(1)}, bf16[256,1024]{1,0:T(8,128)(2,1)S(1)}, u32[]{:S(2)}, u32[]{:S(2)}) collective-permute-start(bf16[256,1024]{1,0:T(8,128)(2,1)S(1)} %get-tuple-element.234), channel_id=1, source_target_pairs={{0,2},{1,3},{2,0},{3,1},{4,6},{5,7},{6,4},{7,5},{8,10},{9,11},{10,... | collective-permute-start | bytes 1572872 | tf_op jit(solution)/shard_map/ppermute | solution.py:769
  1066.3 64.2 %collective-permute-start.66 = (bf16[256,1024]{1,0:T(8,128)(2,1)S(1)}, bf16[256,1024]{1,0:T(8,128)(2,1)S(1)}, u32[]{:S(2)}, u32[]{:S(2)}) collective-permute-start(bf16[256,1024]{1,0:T(8,128)(2,1)S(1)} %slice.819), channel_id=1, source_target_pairs={{0,1},{1,2},{2,3},{3,0},{4,5},{5,6},{6,7},{7,4},{8,9},{9,10},{10,1... | collective-permute-start | bytes 1572872 | tf_op jit(solution)/shard_map/ppermute | solution.py:769
  1067.9 76.2 %collective-permute-start.59 = (bf16[256,1024]{1,0:T(8,128)(2,1)S(1)}, bf16[256,1024]{1,0:T(8,128)(2,1)S(1)}, u32[]{:S(2)}, u32[]{:S(2)}) collective-permute-start(bf16[256,1024]{1,0:T(8,128)(2,1)S(1)} %get-tuple-element.237), channel_id=1, source_target_pairs={{0,3},{1,0},{2,1},{3,2},{4,7},{5,4},{6,5},{7,6},{8,11},{9,8},{10,9... | collective-permute-start | bytes 1572872 | tf_op jit(solution)/shard_map/ppermute | solution.py:769
  1068.6 75.5 %collective-permute-start.58 = (bf16[256,1024]{1,0:T(8,128)(2,1)S(1)}, bf16[256,1024]{1,0:T(8,128)(2,1)S(1)}, u32[]{:S(2)}, u32[]{:S(2)}) collective-permute-start(bf16[256,1024]{1,0:T(8,128)(2,1)S(1)} %get-tuple-element.236), channel_id=1, source_target_pairs={{0,2},{1,3},{2,0},{3,1},{4,6},{5,7},{6,4},{7,5},{8,10},{9,11},{10,... | collective-permute-start | bytes 1572872 | tf_op jit(solution)/shard_map/ppermute | solution.py:769
  1097.7 55.2 %collective-permute-start.55 = (bf16[256,1024]{1,0:T(8,128)(2,1)S(1)}, bf16[256,1024]{1,0:T(8,128)(2,1)S(1)}, u32[]{:S(2)}, u32[]{:S(2)}) collective-permute-start(bf16[256,1024]{1,0:T(8,128)(2,1)S(1)} %slice.809), channel_id=1, source_target_pairs={{0,1},{1,2},{2,3},{3,0},{4,5},{5,6},{6,7},{7,4},{8,9},{9,10},{10,1... | collective-permute-start | bytes 1572872 | tf_op jit(solution)/shard_map/ppermute | solution.py:769
  (137 other events, 1625.5 us)

commit v3 on v2

--- a/solution.py
+++ b/solution.py
@@ -41,6 +41,35 @@
 
 def mm_tn(a, b):
     return lax.dot_general(a, b, (((0,), (0,)), ((), ())), preferred_element_type=f32)
+
+
+MESH = pl.DeviceIdType.MESH
+ANYWHERE = pl.BlockSpec(memory_space=pl.ANY)
+IN_VMEM = pl.BlockSpec(memory_space=pltpu.VMEM)
+
+
+def here():
+    return lax.axis_index("dp"), lax.axis_index("row"), lax.axis_index("col")
+
+
+def meet(partners):
+    barrier = pltpu.get_barrier_semaphore()
+    for partner in partners:
+        pl.semaphore_signal(barrier, inc=1, device_id=partner, device_id_type=MESH)
+    pl.semaphore_wait(barrier, len(partners))
+
+
+def remote(src, dst, sends, recvs, device):
+    return pltpu.make_async_remote_copy(
+        src_ref=src, dst_ref=dst, send_sem=sends, recv_sem=recvs, device_id=device,
+        device_id_type=MESH,
+    )
+
+
+def plane():
+    dp, row, col = here()
+    flips = [dp + b - 2 * b * lax.rem(dp // b, 2) for b in (1, 2)]
+    return (flips[0], row, col), (flips[1], row, col)
 
 
 def head_masks():
@@ -112,27 +141,35 @@
         ],
         scratch_shapes=[pltpu.VMEM((rows, span), f32)],
         compiler_params=pltpu.CompilerParams(vmem_limit_bytes=VMEM),
-        cost_estimate=pl.CostEstimate(
-            flops=16 * tokens * span * width, bytes_accessed=4 * keys * width, transcendentals=0
-        ),
         name="attend",
     )(q, k, v, qid[:, None], kid[None, :])
 
 
-def attend_back_kernel(
-    q_ref, k_ref, v_ref, do_ref, o_ref, lse_ref, qid_ref, kid_ref, dq_ref, dk_ref, dv_ref,
-    bias, dk_sum, dv_sum, *, span, windowed,
-):
+def attend_back_kernel(*refs, span, windowed, rider, n_ins, n_outs):
+    refs = list(refs)
+    q_ref, k_ref, v_ref, do_ref, o_ref, lse_ref, qid_ref, kid_ref = refs[:8]
+    rider_refs = refs[8 : 8 + n_ins]
+    refs = refs[8 + n_ins :]
+    dq_ref, dk_ref, dv_ref = refs[:3]
+    rider_refs += refs[3 : 3 + n_outs]
+    bias, dk_sum, dv_sum = refs[3 + n_outs : 6 + n_outs]
+    rider_refs += refs[6 + n_outs :]
     rows = q_ref.shape[0]
     pairs = q_ref.shape[1] // PAIR
     step = pl.program_id(0)
     start = pl.multiple_of(step * rows, rows) if windowed else 0
     keys = pl.ds(start, span)
+    begin, middle, end = rider(*rider_refs)
 
     @pl.when(step == 0)
     def _():
+        begin()
         dk_sum[...] = jnp.zeros_like(dk_sum)
         dv_sum[...] = jnp.zeros_like(dv_sum)
+
+    @pl.when(step == 1)
+    def _():
+        middle()
 
     allowed = kid_ref[keys, :] == qid_ref[...]
     if windowed:
@@ -170,9 +207,10 @@
     def _():
         dk_ref[...] = dk_sum[...].astype(low)
         dv_ref[...] = dv_sum[...].astype(low)
-
-
-def attend_back(q, k, v, do, o, lse, qid, kid, windowed):
+        end()
+
+
+def attend_back(q, k, v, do, o, lse, qid, kid, windowed, rider, riding, shapes, scratch, number):
     tokens, width = q.shape
     keys = k.shape[0]
     pairs = width // PAIR
@@ -181,7 +219,10 @@
     by_row = pl.BlockSpec((rows, width), lambda i: (i, 0))
     whole = pl.BlockSpec((keys, width), lambda i: (0, 0))
     return pl.pallas_call(
-        functools.partial(attend_back_kernel, span=span, windowed=windowed),
+        functools.partial(
+            attend_back_kernel, span=span, windowed=windowed, rider=rider, n_ins=len(riding),
+            n_outs=len(shapes),
+        ),
         grid=(tokens // rows,),
         in_specs=[
             by_row,
@@ -192,24 +233,125 @@
             pl.BlockSpec((pairs, 8, rows), lambda i: (0, 0, i)),
             pl.BlockSpec((1, rows), lambda i: (0, i)),
             pl.BlockSpec((keys, 1), lambda i: (0, 0)),
-        ],
-        out_specs=[by_row, whole, whole],
+        ]
+        + [ANYWHERE] * len(riding),
+        out_specs=[by_row, whole, whole] + [ANYWHERE] * len(shapes),
         out_shape=[
             jax.ShapeDtypeStruct((tokens, width), low),
             jax.ShapeDtypeStruct((keys, width), low),
             jax.ShapeDtypeStruct((keys, width), low),
-        ],
+        ]
+        + [jax.ShapeDtypeStruct(*x) for x in shapes],
         scratch_shapes=[
             pltpu.VMEM((span, rows), f32),
             pltpu.VMEM((keys, width), f32),
             pltpu.VMEM((keys, width), f32),
-        ],
-        compiler_params=pltpu.CompilerParams(vmem_limit_bytes=VMEM),
-        cost_estimate=pl.CostEstimate(
-            flops=40 * tokens * span * width, bytes_accessed=8 * keys * width, transcendentals=0
+        ]
+        + scratch,
+        compiler_params=pltpu.CompilerParams(
+            vmem_limit_bytes=VMEM, collective_id=number, has_side_effects=True
         ),
         name="attend_back",
-    )(q, k, v, do, o, lse, qid[None, :], kid[:, None])
+    )(q, k, v, do, o, lse, qid[None, :], kid[:, None], *riding)
+
+
+def first_rider(
+    g1, g2, got_a, got_b, back_a, back_b, far_a, far_b,
+    load, mid, l_s, s_s, r_s,
+):
+    by_x, by_y = plane()
+    half = back_a.shape[0]
+    up, down = pl.ds(0, half), pl.ds(half, half)
+    loads = [
+        pltpu.make_async_copy(src, load.at[i], l_s.at[i])
+        for i, src in enumerate((g1.at[2, up, :], got_a.at[0], g1.at[1, down, :], got_b.at[0]))
+    ]
+    hops = [
+        remote(g2.at[3, up, :], far_a, s_s.at[0], r_s.at[0], by_x),
+        remote(g2.at[3, down, :], far_b, s_s.at[1], r_s.at[1], by_y),
+        remote(mid.at[0], back_a, s_s.at[2], r_s.at[2], by_y),
+        remote(mid.at[1], back_b, s_s.at[3], r_s.at[3], by_x),
+    ]
+
+    def begin():
+        meet([by_x, by_y])
+        for copy in loads + hops[:2]:
+            copy.start()
+
+    def middle():
+        for i in range(2):
+            loads[2 * i].wait()
+            loads[2 * i + 1].wait()
+            mid[i] = (load[2 * i].astype(f32) + load[2 * i + 1].astype(f32)).astype(low)
+            hops[2 + i].start()
+
+    def end():
+        for copy in hops:
+            copy.wait()
+
+    return begin, middle, end
+
+
+def second_rider(
+    g1, g2, got_a, got_b, back_a, back_b, far_a, far_b,
+    near_a, near_b, far_back_a, far_back_b, z_got, own,
+    load, mid, load_z, out_z, l_s, lz_s, s_s, r_s, z_s, z_r, o_s,
+    *, n_col,
+):
+    dp, row, col = here()
+    by_x, by_y = plane()
+    half = back_a.shape[0]
+    wide = own.shape[0]
+    up, down = pl.ds(0, half), pl.ds(half, half)
+    loads = [
+        pltpu.make_async_copy(src, load.at[i], l_s.at[i])
+        for i, src in enumerate((g2.at[2, up, :], far_a, g2.at[1, down, :], far_b))
+    ]
+    loads_z = []
+    for i, (source, got, back) in enumerate(((up, got_a, back_a), (down, got_b, back_b))):
+        for n, src in enumerate((g1.at[0, source, :], got.at[1], back)):
+            loads_z.append(
+                pltpu.make_async_copy(src, load_z.at[n, source, :], lz_s.at[i, n])
+            )
+    hops = [
+        remote(g2.at[1, up, :], near_a, s_s.at[0], r_s.at[0], by_x),
+        remote(g2.at[2, down, :], near_b, s_s.at[1], r_s.at[1], by_y),
+        remote(mid.at[0], far_back_a, s_s.at[2], r_s.at[2], by_y),
+        remote(mid.at[1], far_back_b, s_s.at[3], r_s.at[3], by_x),
+    ]
+    cols = [(dp, row, lax.rem(col + k, n_col)) for k in range(n_col)]
+    over = [
+        remote(out_z.at[k], z_got.at[k - 1], z_s.at[k - 1], z_r.at[k - 1], cols[k])
+        for k in range(1, n_col)
+    ]
+    keep = pltpu.make_async_copy(out_z.at[0], own, o_s)
+
+    def begin():
+        meet([by_x, by_y] + cols[1:])
+        for copy in loads + loads_z + hops[:2]:
+            copy.start()
+
+    def middle():
+        for i in range(2):
+            loads[2 * i].wait()
+            loads[2 * i + 1].wait()
+            mid[i] = (load[2 * i].astype(f32) + load[2 * i + 1].astype(f32)).astype(low)
+            hops[2 + i].start()
+        for copy in loads_z:
+            copy.wait()
+        for k in list(range(1, n_col)) + [0]:
+            at = pl.ds(k * wide, wide)
+            value = load_z[0, at, :].astype(f32) + load_z[1, at, :].astype(f32)
+            out_z[k] = (value + load_z[2, at, :].astype(f32)).astype(low)
+            if k:
+                over[k - 1].start()
+        keep.start()
+
+    def end():
+        for copy in hops + over + [keep]:
+            copy.wait()
+
+    return begin, middle, end
 
 
 ROOT = 0.7978845608028654
@@ -268,24 +410,24 @@
         ],
         scratch_shapes=[pltpu.VMEM((tokens, width), f32)],
         compiler_params=pltpu.CompilerParams(vmem_limit_bytes=VMEM),
-        cost_estimate=pl.CostEstimate(
-            flops=4 * tokens * width * parts * inner,
-            bytes_accessed=8 * width * parts * inner,
-            transcendentals=0,
-        ),
         name="hidden_forward",
     )(f, w1, b1, w2)
 
 
 def hidden_back_kernel(
     dz_ref, dzt_ref, ft_ref, w1_ref, w2_ref, act_ref, slope_ref,
-    g1_ref, g2_ref, gb_ref, df_ref, dh_low, total,
+    g1_ref, g2_ref, gb_ref, df_ref, got_a, got_b, dh_low, total, away_a, away_b, s_s, r_s,
 ):
-    step = pl.program_id(0) * pl.num_programs(1) + pl.program_id(1)
-    last = pl.num_programs(0) * pl.num_programs(1) - 1
+    inner, inners = pl.program_id(1), pl.num_programs(1)
+    order = pl.program_id(0)
+    step = order * inners + inner
+    last = pl.num_programs(0) * inners - 1
+    by_x, by_y = plane()
+    half = got_a.shape[1]
 
     @pl.when(step == 0)
     def _():
+        meet([by_x, by_y])
         total[...] = jnp.zeros_like(total)
 
     gb_ref[...] = jnp.zeros_like(gb_ref)
@@ -308,63 +450,77 @@
 
     lax.fori_loop(0, ft_ref.shape[0] // 256, one_grad, 0)
 
+    block = g1_ref.shape[2]
+    lanes = pl.ds(pl.multiple_of(inner * block, block), block)
+
+    def hop(which, slot):
+        away, got, to = [(away_a, got_a, by_x), (away_b, got_b, by_y)][which]
+        return remote(
+            away.at[slot], got.at[slot], s_s.at[which, slot], r_s.at[which, slot], to
+        )
+
+    for at, which, slot in ((0, 0, 0), (0, 1, 0), (1, 0, 1), (2, 1, 1)):
+
+        @pl.when(order == at)
+        def _():
+            away = (away_a, away_b)[which]
+            away[slot, :, lanes] = g1_ref[0, which * half : (which + 1) * half, :]
+
+        @pl.when((order == at) & (inner == inners - 1))
+        def _():
+            hop(which, slot).start()
+
     @pl.when(step == last)
     def _():
         df_ref[...] = total[...].astype(low)
-
-
-def hidden_backward(dz, f, w1, w2, act, slope):
+        for which in range(2):
+            for slot in range(2):
+                hop(which, slot).wait()
+
+
+def hidden_backward(dz, f, w1, w2, act, slope, number):
     parts, width, inner = w1.shape
     tokens = f.shape[0]
     block = min(512, inner)
     grid = (parts, inner // block)
-    weight = pl.BlockSpec((1, width, block), lambda j, n: (j, 0, n))
-    active = pl.BlockSpec((1, tokens, block), lambda j, n: (j, 0, n))
+
+    def number_of(j):
+        return jnp.where(j == 0, parts - 1, jnp.where(j == parts - 1, 0, j))
+
+    weight = pl.BlockSpec((1, width, block), lambda j, n: (number_of(j), 0, n))
+    active = pl.BlockSpec((1, tokens, block), lambda j, n: (number_of(j), 0, n))
     whole = pl.BlockSpec((tokens, width), lambda j, n: (0, 0))
     turned = pl.BlockSpec((width, tokens), lambda j, n: (0, 0))
+    landing = jax.ShapeDtypeStruct((2, width // 2, inner), low)
     return pl.pallas_call(
         hidden_back_kernel,
         grid=grid,
         in_specs=[whole, turned, turned, weight, weight, active, active],
-        out_specs=[weight, weight, pl.BlockSpec((1, 1, block), lambda j, n: (j, 0, n)), whole],
+        out_specs=[
+            weight, weight, pl.BlockSpec((1, 1, block), lambda j, n: (number_of(j), 0, n)), whole,
+            ANYWHERE, ANYWHERE,
+        ],
         out_shape=[
             jax.ShapeDtypeStruct(w1.shape, low),
             jax.ShapeDtypeStruct(w1.shape, low),
             jax.ShapeDtypeStruct((parts, 1, inner), f32),
             jax.ShapeDtypeStruct((tokens, width), low),
+            landing,
+            landing,
         ],
-        scratch_shapes=[pltpu.VMEM((tokens, block), low), pltpu.VMEM((tokens, width), f32)],
-        compiler_params=pltpu.CompilerParams(vmem_limit_bytes=VMEM),
-        cost_estimate=pl.CostEstimate(
-            flops=8 * tokens * width * parts * inner,
-            bytes_accessed=16 * width * parts * inner,
-            transcendentals=0,
+        scratch_shapes=[
+            pltpu.VMEM((tokens, block), low),
+            pltpu.VMEM((tokens, width), f32),
+            pltpu.VMEM(landing.shape, low),
+            pltpu.VMEM(landing.shape, low),
+            pltpu.SemaphoreType.DMA((2, 2)),
+            pltpu.SemaphoreType.DMA((2, 2)),
+        ],
+        compiler_params=pltpu.CompilerParams(
+            vmem_limit_bytes=VMEM, collective_id=number, has_side_effects=True
         ),
         name="hidden_backward",
     )(dz, dz.T, f.T, w1, w2, act, slope)
-
-
-MESH = pl.DeviceIdType.MESH
-ANYWHERE = pl.BlockSpec(memory_space=pl.ANY)
-IN_VMEM = pl.BlockSpec(memory_space=pltpu.VMEM)
-
-
-def here():
-    return lax.axis_index("dp"), lax.axis_index("row"), lax.axis_index("col")
-
-
-def meet(partners):
-    barrier = pltpu.get_barrier_semaphore()
-    for partner in partners:
-        pl.semaphore_signal(barrier, inc=1, device_id=partner, device_id_type=MESH)
-    pl.semaphore_wait(barrier, len(partners))
-
-
-def remote(src, dst, sends, recvs, device):
-    return pltpu.make_async_remote_copy(
-        src_ref=src, dst_ref=dst, send_sem=sends, recv_sem=recvs, device_id=device,
-        device_id_type=MESH,
-    )
 
 
 def start_kernel(
@@ -747,6 +903,323 @@
     return out if len(out) > 1 else out[0]
 
 
+def finish_kernel(
+    ga, gb, small, enc_in, tg, g2, near_a, near_b, far_back_a, far_back_b, z_got, own1,
+    full, hidden_full, small_out, enc_out, tg_out,
+    load, load_own, load_got, h_out, h_in, l_s, lo_s, hz_s, hz_r, h_extra, hx_s, hx_r, hg_s, hg_r,
+    first, second, mid, zout, zin, tot, enc_got, s_cur, s_got, s_z, extra,
+    f_s, f_r, m_s, m_r, z_s, z_r, g_s, g_r, e_s, e_r, s_s, s_r, sz_s, sz_r, t_s, t_r, x_s, x_r,
+    *, n_col, n_dp,
+):
+    dp, row, col = here()
+    part = lax.rem(dp, PARTS)
+    twin = (dp, 1 - row, col)
+    bits = [1 << b for b in range(n_dp.bit_length() - 1)]
+    flips = [dp + b - 2 * b * lax.rem(dp // b, 2) for b in bits]
+    by_bit = [(f, row, col) for f in flips]
+    shift = [lax.rem(col + k, n_col) for k in range(n_col)]
+    group = [(dp, r, c) for r in (row, 1 - row) for c in shift][1:]
+    meet(group + by_bit)
+    wide = enc_out.shape[1]
+    ks = range(1, n_col)
+    ways = [(ga, 0, (1, 3), 2), (gb, 1, (2, 3), 1)]
+    h_half = near_a.shape[0]
+    loads = []
+    for i, sources in enumerate(((near_a, far_back_a), (near_b, far_back_b))):
+        at = pl.ds(i * h_half, h_half)
+        for n, src in enumerate((g2.at[0, at, :],) + sources):
+            loads.append(pltpu.make_async_copy(src, load.at[n, at, :], l_s.at[i, n]))
+    loads_own = [
+        pltpu.make_async_copy(own1, load_own, lo_s.at[0]),
+        pltpu.make_async_copy(z_got, load_got, lo_s.at[1]),
+    ]
+
+    def hidden_hop(k):
+        return remote(h_out.at[k], h_in.at[k - 1], hz_s.at[k - 1], hz_r.at[k - 1], z_to(k))
+
+    def hidden_total(k):
+        at = rows(k)
+        value = load[0, at, :].astype(f32) + load[1, at, :].astype(f32)
+        return value + load[2, at, :].astype(f32)
+
+    def other_bits(value, g, store, s_x, r_x):
+        for i in range(len(bits) - 2):
+            store[g, i, 0] = value.astype(low)
+            copy = remote(
+                store.at[g, i, 0], store.at[g, i, 1], s_x.at[g, i], r_x.at[g, i], by_bit[2 + i]
+            )
+            copy.start()
+            copy.wait()
+            value = value + store[g, i, 1].astype(f32)
+        return value
+
+    def rows(q):
+        return pl.ds(q * wide, wide)
+
+    def z_to(k):
+        return (dp, row, shift[k])
+
+    def hop(g, a, q):
+        src, way, away, _ = ways[g]
+        return remote(
+            src.at[away[a], rows(q), :], first.at[g, a, rows(q), :], f_s.at[g, a, q],
+            f_r.at[g, a, q], by_bit[way],
+        )
+
+    def hop2(g, q):
+        ref = mid.at[g, rows(q), :]
+        return remote(
+            ref, second.at[g, rows(q), :], m_s.at[g, q], m_r.at[g, q], by_bit[1 - ways[g][1]]
+        )
+
+    def z_hop(g, q):
+        return remote(zout.at[g, q - 1], zin.at[g, q - 1], z_s.at[g, q - 1], z_r.at[g, q - 1], z_to(q))
+
+    def enc_hop(k):
+        src = enc_in.at[:, pl.ds(k * wide, wide)]
+        return remote(src, enc_got.at[k - 1], e_s.at[k - 1], e_r.at[k - 1], z_to(k))
+
+    partners = [twin] + by_bit
+
+    def small_hop(i):
+        return remote(s_cur.at[i], s_got.at[i], s_s.at[i], s_r.at[i], partners[i])
+
+    def small_z(k):
+        return remote(s_cur.at[len(partners), k], s_z.at[k - 1], sz_s.at[k - 1], sz_r.at[k - 1], z_to(k))
+
+    def small_step(i):
+        if i == 0:
+            s_cur[0] = small[...]
+        elif i <= len(partners):
+            small_hop(i - 1).wait_recv()
+            got = s_got[i - 1]
+            if i == 1:
+                lane = lax.broadcasted_iota(jnp.int32, got.shape, 2)
+                got = jnp.where(lane < wide, got, 0.0)
+            s_cur[i] = s_cur[i - 1] + got
+        if i < len(partners):
+            small_hop(i).start()
+        elif i == len(partners):
+            for k in ks:
+                small_z(k).start()
+        else:
+            value = s_cur[len(partners), 0]
+            for k in ks:
+                small_z(k).wait_recv()
+                value = value + s_z[k - 1]
+            small_out[...] = value
+
+    t_rows = tg.shape[0]
+    home = col // 2
+    at_home = 2 * lax.rem(col, 2) + row
+
+    def tg_hop(k):
+        src = tg.at[:, pl.ds(k * wide, wide)]
+        dst = tg_out.at[pl.ds(pl.multiple_of(at_home * t_rows, t_rows), t_rows), :]
+        return src, dst, (dp, home, shift[k])
+
+    part_x, part_y = lax.rem(flips[0], PARTS), lax.rem(flips[1], PARTS)
+    half = wide // 2
+
+    def plane_hop(full, g, stage, sends, recvs):
+        which, begin, size, way = [
+            (part, 0, wide, 0), (part, 0, wide, 1), (part_x, 0, half, 1), (part_y, half, half, 0),
+        ][stage]
+        ref = full.at[g, which, pl.ds(begin, size), :]
+        return remote(ref, ref, sends.at[g, stage], recvs.at[g, stage], by_bit[way])
+
+    def plane_to(g, stage):
+        return plane_hop(full, g, stage, g_s, g_r)
+
+    def hidden_plane(g, stage):
+        return plane_hop(hidden_full, g, stage, hg_s, hg_r)
+
+    small_step(0)
+    for copy in loads + loads_own:
+        copy.start()
+    for q in range(n_col):
+        for g in range(2):
+            hop(g, 1, q).start()
+    for k in ks:
+        enc_hop(k).start()
+    for q in range(n_col):
+        for g in range(2):
+            hop(g, 0, q).start()
+    for k in range(n_col):
+        src, dst, to = tg_hop(k)
+        if k == 0:
+
+            @pl.when(home == row)
+            def _():
+                pltpu.make_async_copy(src, dst, t_r.at[at_home]).start()
+
+            @pl.when(home != row)
+            def _():
+                remote(src, dst, t_s.at[k], t_r.at[at_home], to).start()
+        else:
+            remote(src, dst, t_s.at[k], t_r.at[at_home], to).start()
+    for copy in loads:
+        copy.wait()
+    for k in ks:
+        h_out[k] = hidden_total(k).astype(low)
+        hidden_hop(k).start()
+    for copy in loads_own:
+        copy.wait()
+    value = load_own[...].astype(f32)
+    for k in ks:
+        value = value + load_got[k - 1].astype(f32)
+    hidden_full[0, part] = other_bits(value, 0, h_extra, hx_s, hx_r).astype(low)
+    hidden_plane(0, 0).start()
+    hidden_plane(0, 1).start()
+    done = 1
+    for q in range(n_col):
+        for g in range(2):
+            src, _, _, keep = ways[g]
+            hop(g, 1, q).wait_recv()
+            value = src[keep, rows(q), :].astype(f32) + first[g, 1, rows(q), :].astype(f32)
+            mid[g, rows(q), :] = value.astype(low)
+            hop2(g, q).start()
+        if done < len(partners) + 2:
+            small_step(done)
+            done += 1
+    for q in (1, 2, 3, 0):
+        for g in range(2):
+            src = ways[g][0]
+            hop(g, 0, q).wait_recv()
+            hop2(g, q).wait_recv()
+            value = src[0, rows(q), :].astype(f32) + first[g, 0, rows(q), :].astype(f32)
+            value = value + second[g, rows(q), :].astype(f32)
+            if q:
+                zout[g, q - 1] = value.astype(low)
+                z_hop(g, q).start()
+            else:
+                tot[g] = value
+        if done < len(partners) + 2:
+            small_step(done)
+            done += 1
+    for stage in range(2):
+        hidden_plane(0, stage).wait_recv()
+        hidden_plane(0, 2 + stage).start()
+    value = enc_in[:, pl.ds(0, wide)].astype(f32)
+    for k in ks:
+        enc_hop(k).wait_recv()
+        value = value + enc_got[k - 1].astype(f32)
+    enc_out[...] = value
+    while done < len(partners) + 2:
+        small_step(done)
+        done += 1
+    for g in range(2):
+        value = tot[g]
+        for q in ks:
+            z_hop(g, q).wait_recv()
+            value = value + zin[g, q - 1].astype(f32)
+        value = other_bits(value, g, extra, x_s, x_r)
+        full[g, part] = value.astype(low)
+    for g in range(2):
+        plane_to(g, 0).start()
+        plane_to(g, 1).start()
+    value = hidden_total(0)
+    for k in ks:
+        hidden_hop(k).wait_recv()
+        value = value + h_in[k - 1].astype(f32)
+    hidden_full[1, part] = other_bits(value, 1, h_extra, hx_s, hx_r).astype(low)
+    hidden_plane(1, 0).start()
+    hidden_plane(1, 1).start()
+    for g in range(2):
+        for stage in range(2):
+            plane_to(g, stage).wait_recv()
+            plane_to(g, 2 + stage).start()
+    for stage in range(2):
+        hidden_plane(1, stage).wait_recv()
+        hidden_plane(1, 2 + stage).start()
+    for k in ks:
+        hidden_hop(k).wait_send()
+    for g in range(2):
+        for ways_out in (plane_to, hidden_plane):
+            ways_out(g, 2).wait_recv()
+            ways_out(g, 3).wait_recv()
+            for stage in range(4):
+                ways_out(g, stage).wait_send()
+        for q in range(n_col):
+            hop(g, 0, q).wait_send()
+            hop(g, 1, q).wait_send()
+            hop2(g, q).wait_send()
+            if q:
+                z_hop(g, q).wait_send()
+    for k in ks:
+        enc_hop(k).wait_send()
+        small_z(k).wait_send()
+    for i in range(len(partners)):
+        small_hop(i).wait_send()
+    for k in range(n_col):
+        src, dst, to = tg_hop(k)
+
+        @pl.when((home != row) | (k > 0))
+        def _():
+            remote(src, dst, t_s.at[k], t_r.at[at_home], to).wait_send()
+
+        place = tg_out.at[pl.ds(k * t_rows, t_rows), :]
+        pltpu.make_async_copy(src, place, t_r.at[k]).wait()
+
+
+def finish(ga, gb, small, enc_in, tg, riding, n_col, n_dp):
+    parts, deep, columns = ga.shape
+    wide = deep // n_col
+    steps = n_dp.bit_length()
+    sd, vm, dma = jax.ShapeDtypeStruct, pltpu.VMEM, pltpu.SemaphoreType.DMA
+    more = max(n_dp.bit_length() - 3, 1)
+    others = n_col - 1
+    hidden = riding[0].shape[2]
+    return pl.pallas_call(
+        functools.partial(finish_kernel, n_col=n_col, n_dp=n_dp),
+        in_specs=[IN_VMEM] * 4 + [ANYWHERE] * 8,
+        out_specs=[IN_VMEM] * 4 + [ANYWHERE],
+        out_shape=[
+            sd((2, parts, wide, columns), low),
+            sd((2, parts, wide, hidden), low),
+            sd(small.shape[1:], f32),
+            sd((enc_in.shape[0], wide), f32),
+            sd((n_col * tg.shape[0], wide), low),
+        ],
+        scratch_shapes=[
+            vm((3, deep, hidden), low),
+            vm((wide, hidden), low),
+            vm((others, wide, hidden), low),
+            vm((n_col, wide, hidden), low),
+            vm((others, wide, hidden), low),
+            dma((2, 3)), dma((2,)),
+            dma((others,)), dma((others,)),
+            vm((2, more, 2, wide, hidden), low),
+            dma((2, more)), dma((2, more)),
+            dma((2, 4)), dma((2, 4)),
+            vm((2, 2, deep, columns), low),
+            vm((2, deep, columns), low),
+            vm((2, deep, columns), low),
+            vm((2, others, wide, columns), low),
+            vm((2, others, wide, columns), low),
+            vm((2, wide, columns), f32),
+            vm((others, enc_in.shape[0], wide), low),
+            vm((steps + 1,) + small.shape, f32),
+            vm((steps,) + small.shape, f32),
+            vm((others,) + small.shape[1:], f32),
+            vm((2, more, 2, wide, columns), low),
+            dma((2, 2, n_col)), dma((2, 2, n_col)),
+            dma((2, n_col)), dma((2, n_col)),
+            dma((2, others)), dma((2, others)),
+            dma((2, 4)), dma((2, 4)),
+            dma((others,)), dma((others,)),
+            dma((steps,)), dma((steps,)),
+            dma((others,)), dma((others,)),
+            dma((n_col,)), dma((n_col,)),
+            dma((2, more)), dma((2, more)),
+        ],
+        compiler_params=pltpu.CompilerParams(
+            collective_id=20, has_side_effects=True, vmem_limit_bytes=VMEM
+        ),
+        name="finish",
+    )(ga, gb, small, enc_in, tg, *riding)
+
+
 def norm_backward(incoming, normed, scaling, gain):
     gain_grad = jnp.sum(incoming * normed, axis=0)
     bias_grad = jnp.sum(incoming, axis=0)
@@ -776,17 +1249,6 @@
         by_x, by_y = across(x, 1), across(x, 2)
         far = jnp.concatenate([across(by_x[:half], 2), across(by_y[half:], 1)], axis=0)
         return [x, by_x, by_y, far]
-
-    def plane_scatter(parts):
-        half = parts[0].shape[0] // 2
-        a, b = [p[:half] for p in parts], [p[half:] for p in parts]
-        got = across(jnp.stack([a[1], a[3]]), 1)
-        a0, a2 = a[0] + got[0], a[2] + got[1]
-        got = across(jnp.stack([b[2], b[3]]), 2)
-        b0, b1 = b[0] + got[0], b[1] + got[1]
-        a0 = a0 + across(a2, 2)
-        b0 = b0 + across(b1, 1)
-        return jnp.concatenate([a0, b0], axis=0)
 
     def local(
         tokens, encoder, cotangent, dec_lengths, src_lengths,
@@ -864,17 +1326,6 @@
                 jnp.concatenate([own(j), part], axis=0)
                 for j, part in enumerate(plane_gather(rest))
             ]
-
-        def grads_of(parts):
-            mine = plane_scatter(parts)
-            total = mine[:wide].astype(f32)
-            for k in range(1, n_col):
-                total = total + to_col(mine[k * wide : (k + 1) * wide], k).astype(f32)
-            bit = PARTS
-            while bit < n_dp:
-                total = total + across(total.astype(low), bit).astype(f32)
-                bit *= 2
-            return in_order(plane_gather(total.astype(low)))
 
         vec_f = jnp.stack([
             self_norm_gain, self_norm_bias, self_out_bias, cross_norm_gain, cross_norm_bias,
@@ -944,13 +1395,24 @@
 
         dz_own = spread_rows(cotangent)
         dz = row_gather(dz_own)
-        g1, g2, hidden_bias_grad, df = hidden_backward(dz, f, w1, w2, act, slope)
-        g1_parts = grads_of([g1[j] for j in range(PARTS)])
-        g2_parts = grads_of([g2[j] for j in range(PARTS)])
+        g1, g2, hidden_bias_grad, df, got_a, got_b = hidden_backward(
+            dz, f, w1, w2, act, slope, 11
+        )
+        inner = g1.shape[2]
+        half = g1.shape[1] // 2
+        dma, one = pltpu.SemaphoreType.DMA, ((half, inner), low)
         dx2, dyc, stats3 = junction("backward", [("sum", df)], [dz_own, x2, gain3], 6)
 
         doc = mm_nt(dyc, wo2).astype(low)
-        dq2, dk2, dv2 = attend_back(q2, k2, v2, doc, o2, lse2, query_ids, src_ids, False)
+        dq2, dk2, dv2, back_a, back_b, far_a, far_b = attend_back(
+            q2, k2, v2, doc, o2, lse2, query_ids, src_ids, False,
+            first_rider, [g1, g2, got_a, got_b], [one] * 4,
+            [
+                pltpu.VMEM((4, half, inner), low), pltpu.VMEM((2, half, inner), low),
+                dma((4,)), dma((4,)), dma((4,)),
+            ],
+            12,
+        )
         grads = [
             mm_tn(c, dq2).astype(low),
             mm_tn(enc, dk2).astype(low),
@@ -970,17 +1432,24 @@
                 for j in range(PARTS)
             ]
 
-        cross_grads = grads_of(by_part(grads))
+        cross_grads = jnp.stack(by_part(grads))
         enc_back = junction("sum", [("nt", dk2, wk2), ("nt", dv2, wv2)], [], 7)
-        encoder_grad = enc_back[:, :wide]
-        for k in range(1, n_col):
-            encoder_grad = encoder_grad + to_col(
-                enc_back[:, k * wide : (k + 1) * wide].astype(low), k
-            ).astype(f32)
         dx1, dy, stats2 = junction("backward", [("nt", dq2, wq2)], [dx2, x1, gain2], 8)
 
         do = mm_nt(dy, wo1).astype(low)
-        dq1, dk1, dv1 = attend_back(q1, k1, v1, do, o1, lse1, query_ids, key_ids, True)
+        dq1, dk1, dv1, near_a, near_b, far_back_a, far_back_b, z_got, own1 = attend_back(
+            q1, k1, v1, do, o1, lse1, query_ids, key_ids, True,
+            functools.partial(second_rider, n_col=n_col),
+            [g1, g2, got_a, got_b, back_a, back_b, far_a, far_b],
+            [one] * 4 + [((n_col - 1, wide, inner), low), ((wide, inner), low)],
+            [
+                pltpu.VMEM((4, half, inner), low), pltpu.VMEM((2, half, inner), low),
+                pltpu.VMEM((3, 2 * half, inner), low), pltpu.VMEM((n_col, wide, inner), low),
+                dma((4,)), dma((2, 3)), dma((4,)), dma((4,)),
+                dma((n_col - 1,)), dma((n_col - 1,)), dma,
+            ],
+            13,
+        )
         da_before = junction("sum", [("nt", dk1[:WIN], wk1), ("nt", dv1[:WIN], wv1)], [], 9)
         da_after = lax.ppermute(
             da_before.astype(low), "col", [(i + 1, i) for i in range(n_col - 1)]
@@ -995,11 +1464,9 @@
             mm_tn(a_ext, dv1).astype(low),
             mm_tn(dy, o1).astype(low),
         ]
-        self_grads = grads_of(by_part(grads))
+        self_grads = jnp.stack(by_part(grads))
         normed1, scaling1 = norm_rows(x0.astype(f32))
         back1, gain_grad1, shift_grad1 = norm_backward(da, normed1, scaling1, gain1)
-        tokens_grad = collect_rows((dx1 + back1).astype(low)).astype(f32)
-
         def total(x):
             return jnp.sum(x, axis=0, dtype=f32)
 
@@ -1007,21 +1474,36 @@
             jnp.stack([gain_grad1, shift_grad1]), stats2[2:3], stats2[:2], stats3[2:3], stats3[:2],
             total(dz_own)[None],
         ])
-        count = feature_grads.shape[0]
-        chunks = jnp.moveaxis(feature_grads.reshape(count, n_col, wide), 1, 0)
-        chunks = lax.dynamic_slice_in_dim(
-            jnp.concatenate([chunks, chunks]), (n_col - col) % n_col, n_col, 0
-        )
-        chunks = lax.psum(chunks, ("dp", "row", "col"))
-        feature_grads = lax.dynamic_index_in_dim(chunks, col, 0, keepdims=False)
+        feature_grads = jnp.moveaxis(feature_grads.reshape(-1, n_col, wide), 1, 0)
         column_grads = []
         for vector in (total(dq1), total(dv1), total(dq2), total(dv2), hidden_bias_grad):
             parts = vector.reshape(PARTS, -1)
             if vector is hidden_bias_grad:
                 parts = jnp.stack(in_order([parts[j] for j in range(PARTS)]))
             column_grads.append(parts.reshape(n_col, -1))
-        column_grads = lax.psum(jnp.concatenate(column_grads, axis=1), ("dp", "col"))
-        column_grads = lax.dynamic_index_in_dim(column_grads, col, 0, keepdims=False)
+        column_grads = jnp.concatenate(column_grads, axis=1).reshape(n_col, -1, 128)
+        column_grads = lax.dynamic_slice_in_dim(
+            jnp.concatenate([column_grads, column_grads]), col, n_col, 0
+        )
+        lines = -(-max(feature_grads.shape[1], column_grads.shape[1]) // 8) * 8
+        small = jnp.concatenate(
+            [
+                jnp.pad(x, ((0, 0), (0, lines - x.shape[1]), (0, 0)))
+                for x in (feature_grads, column_grads)
+            ],
+            axis=2,
+        )
+        sums, hidden_sums, small, encoder_grad, tokens_grad = finish(
+            cross_grads, self_grads, small, enc_back.astype(low), (dx1 + back1).astype(low),
+            [g2, near_a, near_b, far_back_a, far_back_b, z_got, own1],
+            n_col, n_dp,
+        )
+        g1_parts, g2_parts = [[hidden_sums[i, j] for j in range(PARTS)] for i in range(2)]
+        tokens_grad = tokens_grad.astype(f32)
+        cross_grads = [sums[0, i] for i in range(PARTS)]
+        self_grads = [sums[1, i] for i in range(PARTS)]
+        feature_grads = small[:, :wide]
+        column_grads = small[:, wide:].reshape(-1)
 
         def whole(parts, index=None):
             if index is not None:
@@ -1053,7 +1535,7 @@
             feature_grads[6],
             feature_grads[7],
             whole(g1_parts),
-            column_grads[4 * size :],
+            column_grads[4 * size : 4 * size + hidden_in_bias.shape[0]],
             whole(g2_parts).T,
             feature_grads[8],
         )

time: 1200 us -> 943 us (0.79)
  waiting for transfers between devices: 299 us -> 32.1 us
  Pallas kernels: 403 us -> 643 us
  blocking collectives: 136 us -> 0 us
  starting transfers between devices: 113 us -> 55.8 us
  local copies, waits for them, and re-layouts: 102 us -> 79.7 us
  other arithmetic: 89.9 us -> 73.4 us
    pallas_call x0 -> x1, Pallas kernels: none -> 184 us  [finish(): pl.pallas_call(functools.partial(finish_kernel, n_col=n_col, n_dp=n_dp),...]
    ppermute x40 -> x8, waiting for transfers between devices: 170 us -> 5.74 us  [across(): return lax.ppermute(x, 'dp', [(i, i ^ bit) for i in range(n_dp)])]
    psum x2 -> x0, blocking collectives: 136 us -> none  [the longest x1 72.9 us: local(): lax.psum(jnp.concatenate(column_grads, axis=1), ('dp', 'col'))]
    ppermute x21 -> x3, waiting for transfers between devices: 90.1 us -> 0.01 us  [to_col(): return lax.ppermute(x, 'col', [(i, (i + k) % n_col) for i in range(n_col)])]
    pallas_call x2, Pallas kernels: 70.7 us -> 115 us  [attend_back(): pl.pallas_call(functools.partial(attend_back_kernel, span=span, windowed=...]
    ppermute x40 -> x8, starting transfers between devices: 47.7 us -> 10.2 us  [across(): return lax.ppermute(x, 'dp', [(i, i ^ bit) for i in range(n_dp)])]
    ppermute x21 -> x3, starting transfers between devices: 38.2 us -> 4.21 us  [to_col(): return lax.ppermute(x, 'col', [(i, (i + k) % n_col) for i in range(n_col)])]
    ppermute x9, starting transfers between devices: 23.5 us -> 38.8 us  [from_col(): return lax.ppermute(x, 'col', [(i, (i - k) % n_col) for i in range(n_col)])]
  transfers between devices with their start and end apart: 75 -> 24, of which waited for: 25 -> 5; matrix products, arithmetic and copies ran while one was open for 14% -> 12% of each run, Pallas kernels for 8% -> 11%
where the time goes in v3:
time: 943 us; the launch traced here: 934 us
  Pallas kernels  643 us (68%)
  local copies, waits for them, and re-layouts  79.7 us (8%)
  other arithmetic  73.4 us (8%)
  starting transfers between devices  55.8 us (6%)
  matrix products  47.8 us (5%)
  waiting for transfers between devices  32.1 us (3%)
    pallas_call x1, Pallas kernels, finish(): pl.pallas_call(functools.partial(finish_kernel, n_col=n_col, n_dp=n_dp),...  184 us
    pallas_call x2, Pallas kernels, attend_back(): pl.pallas_call(functools.partial(attend_back_kernel, span=span, windowed=...  115 us
    pallas_call x1, Pallas kernels, start(): pl.pallas_call(functools.partial(start_kernel, n_col=n_col), in_specs=[AN...  109 us
    pallas_call x8, Pallas kernels, junction(): pl.pallas_call(functools.partial(junction_kernel, kinds=kinds, mode=mode)...  69.7 us
    pallas_call x1, Pallas kernels, hidden_backward(): pl.pallas_call(hidden_back_kernel, grid=grid, in_specs=[whole, turned, tu...  68 us
    pallas_call x2, Pallas kernels, attend(): pl.pallas_call(functools.partial(attend_kernel, span=span, windowed=windo...  49.2 us
    ppermute x9, starting transfers between devices, from_col(): return lax.ppermute(x, 'col', [(i, (i - k) % n_col) for i in range(n_col)])  38.8 us
    pallas_call x1, Pallas kernels, hidden_forward(): pl.pallas_call(hidden_kernel, grid=grid, in_specs=[pl.BlockSpec((tokens,...  38.6 us
  transfers between devices with their start and end apart: 24, of which 5 were waited for; matrix products, arithmetic and copies ran while one was open for 12% of the time, Pallas kernels for 11%

profile of v3, /device:TPU:8, one launch (start us, length us, event | category | flops | bytes accessed | tf_op | source)
XLA Modules:
  0.0 934.3 jit_solution(8349951170012962053)
XLA Ops:
  6.9 109.4 %start.1 = (bf16[2,512,1024]{2,1,0:T(8,128)(2,1)}, bf16[1024,1024]{1,0:T(8,128)(2,1)}, f32[16,1024]{1,0:T(8,128)}, f32[4,16,128]{2,1,0:T(8,128)}, bf16[1024,512]...) custom-call(bf16[2048,256]{1,0:T(8,128)(2,1)} %tokens.1, ...), custom_call_target="tpu_custom_call" | custom-call | tf_op jit(solution)/shard_map/start/pallas_call | solution.py:725
  117.7 3.2 collective-permute-start
  120.9 12.1 %collective-permute-start.1 = (bf16[256,1024]{1,0:T(8,128)(2,1)}, bf16[256,1024]{1,0:T(8,128)(2,1)}, u32[]{:S(2)}, u32[]{:S(2)}) collective-permute-start(bf16[256,1024]{1,0:T(8,128)(2,1)} %get-tuple-element.263), channel_id=1, source_target_pairs={{0,2},{1,3},{2,0},{3,1},{4,6},{5,7},{6,4},{7,5},{8,10},{9,11},{10,... | collective-permute-start | bytes 1572872 | tf_op jit(solution)/shard_map/ppermute | solution.py:1239
  133.0 2.9 copy.102
  145.0 8.7 enter.1
  153.8 4.0 fusion.22.q_ref.refs_0_
  157.8 3.7 convolution_convert_fusion.k_ref.refs_1_
  161.5 3.7 add_convert_fusion.v_ref.refs_2_
  165.3 27.5 %attend.2 = (bf16[1024,512]{1,0:T(8,128)(2,1)}, f32[4,8,1024]{2,1,0:T(8,128)}) custom-call(bf16[1024,512]{1,0:T(8,128)(2,1)} %fusion.22.q_ref.refs_0_, bf16[2048,512]{1,0:T(8,128)(2,1)} %convolution_convert_fusion.k_ref.refs_1_, bf16[2048,512]{1,0:T(8,128)(2,1)} %add_convert_fusion.v_ref.refs_2_, s32[1024,1]{1,0:T(8,128)} %copy.100.qid_ref, s32[1,2048]{1,0:T(1,128)} %bitcast.262), custom_call_target="tpu_custom_call" | custom-call | tf_op jit(solution)/shard_map/attend/pallas_call | solution.py:124
  192.7 9.6 %junction_forward.2 = (f32[512,1024]{1,0:T(8,128)}, bf16[1024,1024]{1,0:T(8,128)(2,1)}) custom-call(bf16[1024,512]{1,0:T(8,128)(2,1)} %get-tuple-element.94.refs_0_.refs_4_, bf16[512,1024]{1,0:T(8,128)(2,1)} %get-tuple-element.95.refs_1_, bf16[512,1024]{1,0:T(8,128)(2,1)} %slice_bitcast_fusion.refs_2_, f32[1,1024]{1,0:T(1,128)} %get-tuple-element.346.refs_3_, ...), custom_call_target="tpu_custom_call" | custom-call | tf_op jit(solution)/shard_map/junction_forward/pallas_call | solution.py:892
  202.4 4.0 fusion.25.q_ref.refs_0_
  212.5 2.8 collective-permute-start.9
  223.9 11.6 %collective-permute-done.8 = bf16[256,1024]{1,0:T(8,128)(2,1)S(1)} collective-permute-done((bf16[256,1024]{1,0:T(8,128)(2,1)}, bf16[256,1024]{1,0:T(8,128)(2,1)S(1)}, u32[]{:S(2)}, u32[]{:S(2)}) %collective-permute-start.8) | collective-permute-done | bytes 524320 | tf_op jit(solution)/shard_map/ppermute | solution.py:1239
  235.5 3.3 collective-permute-start.20
  238.8 8.0 collective-permute-done.9
  246.7 14.7 %collective-permute-start.19 = (bf16[512,256]{1,0:T(8,128)(2,1)S(1)}, bf16[512,256]{1,0:T(8,128)(2,1)S(1)}, u32[]{:S(2)}, u32[]{:S(2)}) collective-permute-start(bf16[512,256]{1,0:T(8,128)(2,1)S(1)} %get-tuple-element.299), channel_id=1, source_target_pairs={{0,3},{1,0},{2,1},{3,2},{4,7},{5,4},{6,5},{7,6},{8,11},{9,8},{10,9... | collective-permute-start | bytes 786440 | tf_op jit(solution)/shard_map/ppermute | solution.py:1239
  268.0 6.7 collective-permute-done.19
  276.0 21.7 %attend.3 = (bf16[1024,512]{1,0:T(8,128)(2,1)}, f32[4,8,1024]{2,1,0:T(8,128)}) custom-call(bf16[1024,512]{1,0:T(8,128)(2,1)} %fusion.25.q_ref.refs_0_, bf16[1024,512]{1,0:T(8,128)(2,1)} %convolution_convert_fusion.8.k_ref.refs_1_, bf16[1024,512]{1,0:T(8,128)(2,1)} %add_convert_fusion.2.v_ref.refs_2_, s32[1024,1]{1,0:T(8,128)} %copy.100.qid_ref, ...), custom_call_target="tpu_custom_call" | custom-call | tf_op jit(solution)/shard_map/attend/pallas_call | solution.py:124
  297.7 9.7 %junction_forward.3 = (f32[512,1024]{1,0:T(8,128)}, bf16[1024,1024]{1,0:T(8,128)(2,1)}) custom-call(bf16[1024,512]{1,0:T(8,128)(2,1)} %get-tuple-element.101.refs_0_.refs_4_, bf16[512,1024]{1,0:T(8,128)(2,1)} %get-tuple-element.102.refs_1_, f32[512,1024]{1,0:T(8,128)} %get-tuple-element.103.refs_2_.refs_3_, f32[1,1024]{1,0:T(1,128)} %get-tuple-element.343.refs_3_, ...), custom_call_target="tpu_custom_call" | custom-call | tf_op jit(solution)/shard_map/junction_forward/pallas_call | solution.py:892
  307.5 4.1 copy.109
  315.1 3.1 maximum_bitcast_fusion
  318.2 2.7 maximum_bitcast_fusion.4
  328.3 13.0 %maximum_select_fusion.dz_ref = bf16[1024,1024]{1,0:T(8,128)(2,1)S(1)} fusion(bf16[512,1024]{1,0:T(8,128)(2,1)} %collective-permute-done.22, bf16[512,256]{1,0:T(8,128)(2,1)S(1)} %copy-done.46, bf16[512,256]{1,0:T(8,128)(2,1)S(1)} %copy-done.48, bf16[512,256]{1,0:T(8,128)(2,1)S(1)} %copy-done.50, bf16[512,256]{1,0:T(8,128)(2,1)S(1)} %get-tuple-element.296, ...), kind=kLoop, calls=%fused_computation.30 | loop fusion | flops 22020096 | bytes 4194305 | tf_op jit(solution)/shard_map/jit(_where)/select_n | solution.py:1269
  341.3 3.0 copy.110.dzt_ref
  356.7 3.9 pad_maximum_fusion.w1_ref
  360.6 4.2 collective-permute-done.13
  368.0 3.9 pad_maximum_fusion.1.w2_ref
  371.8 38.6 %hidden_forward.1 = (bf16[4,1024,1024]{2,1,0:T(8,128)(2,1)}, bf16[4,1024,1024]{2,1,0:T(8,128)(2,1)}, bf16[1024,1024]{1,0:T(8,128)(2,1)}) custom-call(bf16[1024,1024]{1,0:T(8,128)(2,1)} %get-tuple-element.105.f_ref, bf16[4,1024,1024]{2,1,0:T(8,128)(2,1)} %pad_maximum_fusion.w1_ref, f32[4,1,1024]{2,1,0:T(1,128)} %pad_maximum_fusion.6.b1_ref, ...), custom_call_target="tpu_custom_call" | custom-call | tf_op jit(solution)/shard_map/hidden_forward/pallas_call | solution.py:396
  410.5 68.0 %hidden_backward.1 = (bf16[4,1024,1024]{2,1,0:T(8,128)(2,1)}, bf16[4,1024,1024]{2,1,0:T(8,128)(2,1)}, f32[4,1,1024]{2,1,0:T(1,128)}, bf16[1024,1024]{1,0:T(8,128...) custom-call(bf16[1024,1024]{1,0:T(8,128)(2,1)} %copy-done, bf16[1024,1024]{1,0:T(8,128)(2,1)} %copy.110.dzt_ref, ...), custom_call_target="tpu_custom_call" | custom-call | tf_op jit(solution)/shard_map/hidden_backward/pallas_call | solution.py:495
  478.5 10.2 %junction_backward.2 = (f32[512,1024]{1,0:T(8,128)}, bf16[1024,1024]{1,0:T(8,128)(2,1)}, f32[8,1024]{1,0:T(8,128)}) custom-call(bf16[1024,1024]{1,0:T(8,128)(2,1)} %get-tuple-element.112.refs_0_, bf16[512,1024]{1,0:T(8,128)(2,1)} %copy-done.14, f32[512,1024]{1,0:T(8,128)} %get-tuple-element.104.refs_2_, f32[1,1024]{1,0:T(1,128)} %get-tuple-element.342.refs_4_.refs_3_), custom_call_target="tpu_custom_call" | custom-call | tf_op jit(solution)/shard_map/junction_backward/pallas_call | solution.py:892
  488.7 4.0 convolution_convert_fusion.3
  494.9 52.1 %attend_back.2 = (bf16[1024,512]{1,0:T(8,128)(2,1)}, bf16[1024,512]{1,0:T(8,128)(2,1)}, bf16[1024,512]{1,0:T(8,128)(2,1)}, bf16[512,1024]{1,0:T(8,128)(2,1)}, bf...) custom-call(bf16[1024,512]{1,0:T(8,128)(2,1)} %fusion.25.q_ref.refs_0_, ...), custom_call_target="tpu_custom_call" | custom-call | tf_op jit(solution)/shard_map/attend_back/pallas_call | solution.py:221
  547.1 3.5 convolution_convert_fusion.6
  550.6 11.1 %junction_backward.3 = (f32[512,1024]{1,0:T(8,128)}, bf16[1024,1024]{1,0:T(8,128)(2,1)}, f32[8,1024]{1,0:T(8,128)}) custom-call(bf16[1024,512]{1,0:T(8,128)(2,1)} %get-tuple-element.119.refs_0_, bf16[1024,512]{1,0:T(8,128)(2,1)} %get-tuple-element.97.refs_1_, f32[512,1024]{1,0:T(8,128)} %get-tuple-element.122.refs_2_, ...), custom_call_target="tpu_custom_call" | custom-call | tf_op jit(solution)/shard_map/junction_backward/pallas_call | solution.py:892
  561.7 4.0 convolution_convert_fusion.1
  568.0 63.3 %attend_back.3 = (bf16[1024,512]{1,0:T(8,128)(2,1)}, bf16[2048,512]{1,0:T(8,128)(2,1)}, bf16[2048,512]{1,0:T(8,128)(2,1)}, bf16[512,1024]{1,0:T(8,128)(2,1)}, bf...) custom-call(bf16[1024,512]{1,0:T(8,128)(2,1)} %fusion.22.q_ref.refs_, ...), custom_call_target="tpu_custom_call" | custom-call | tf_op jit(solution)/shard_map/attend_back/pallas_call | solution.py:221
  631.3 3.6 fusion.17
  647.0 5.9 junction_sum.4
  661.6 7.1 junction_sum.6
  668.8 2.9 convert_element_type.157
  688.7 7.2 junction_sum.7
  695.9 2.7 convert_element_type.165.enc_in
  698.6 8.9 junction_sum.5
  716.7 3.7 fusion.9.tg
  720.4 184.5 %finish.1 = (bf16[2,4,256,512]{3,2,1,0:T(8,128)(2,1)}, bf16[2,4,256,1024]{3,2,1,0:T(8,128)(2,1)}, f32[16,384]{1,0:T(8,128)}, f32[512,256]{1,0:T(8,128)}, bf16[2048,256]{1,0:T(8,128)(2,1)}) custom-call(bf16[4,1024,512]{2,1,0:T(8,128)(2,1)} %pad_maximum_fusion.2.ga, bf16[4,1024,512]{2,1,0:T(8,128)(2,1)} %pad_maximum_fusion.3.gb, ...), custom_call_target="tpu_custom_call" | custom-call | tf_op jit(solution)/shard_map/finish/pallas_call | solution.py:1173
  909.1 2.7 convert_element_type.167
  915.1 2.6 slice_bitcast_fusion.4
  920.2 5.6 copy.123
  (315 shorter events, 134.9 us)
Async XLA Ops:
  0.7 115.7 %copy-start.21 = (bf16[256,4096]{1,0:T(8,128)(2,1)S(1)}, bf16[256,4096]{1,0:T(8,128)(2,1)}, u32[]{:S(2)}) copy-start(bf16[256,4096]{1,0:T(8,128)(2,1)} %param.54) | copy-start | bytes 6291460
  117.7 93.3 %collective-permute-start = (bf16[256,1024]{1,0:T(8,128)(2,1)}, bf16[256,1024]{1,0:T(8,128)(2,1)S(1)}, u32[]{:S(2)}, u32[]{:S(2)}) collective-permute-start(bf16[256,1024]{1,0:T(8,128)(2,1)} %get-tuple-element.263), channel_id=1, source_target_pairs={{0,3},{1,0},{2,1},{3,2},{4,7},{5,4},{6,5},{7,6},{8,11},{9,8},{10,9... | collective-permute-start | bytes 1572872 | tf_op jit(solution)/shard_map/ppermute | solution.py:1239
  120.9 91.6 %collective-permute-start.1 = (bf16[256,1024]{1,0:T(8,128)(2,1)}, bf16[256,1024]{1,0:T(8,128)(2,1)}, u32[]{:S(2)}, u32[]{:S(2)}) collective-permute-start(bf16[256,1024]{1,0:T(8,128)(2,1)} %get-tuple-element.263), channel_id=1, source_target_pairs={{0,2},{1,3},{2,0},{3,1},{4,6},{5,7},{6,4},{7,5},{8,10},{9,11},{10,... | collective-permute-start | bytes 1572872 | tf_op jit(solution)/shard_map/ppermute | solution.py:1239
  133.0 84.2 %collective-permute-start.2 = (bf16[256,1024]{1,0:T(8,128)(2,1)}, bf16[256,1024]{1,0:T(8,128)(2,1)}, u32[]{:S(2)}, u32[]{:S(2)}) collective-permute-start(bf16[256,1024]{1,0:T(8,128)(2,1)} %get-tuple-element.263), channel_id=1, source_target_pairs={{0,1},{1,2},{2,3},{3,0},{4,5},{5,6},{6,7},{7,4},{8,9},{9,10},{10,1... | collective-permute-start | bytes 1572872 | tf_op jit(solution)/shard_map/ppermute | solution.py:1239
  137.3 6.7 copy-start.1
  137.3 86.3 %collective-permute-start.7 = (bf16[256,1024]{1,0:T(8,128)(2,1)}, bf16[256,1024]{1,0:T(8,128)(2,1)}, u32[]{:S(2)}, u32[]{:S(2)}) collective-permute-start(bf16[256,1024]{1,0:T(8,128)(2,1)} %get-tuple-element.259), channel_id=1, source_target_pairs={{0,3},{1,0},{2,1},{3,2},{4,7},{5,4},{6,5},{7,6},{8,11},{9,8},{10,9... | collective-permute-start | bytes 1572872 | tf_op jit(solution)/shard_map/ppermute | solution.py:1239
  141.4 79.2 %collective-permute-start.18 = (bf16[2,512,256]{2,1,0:T(8,128)(2,1)}, bf16[2,512,256]{2,1,0:T(8,128)(2,1)}, u32[]{:S(2)}, u32[]{:S(2)}) collective-permute-start(bf16[2,512,256]{2,1,0:T(8,128)(2,1)} %get-tuple-element.301), channel_id=1, source_target_pairs={{0,4},{4,0},{1,5},{5,1},{2,6},{6,2},{3,7},{7,3},{8,12},{12,8},{9,1... | collective-permute-start | bytes 1572872 | tf_op jit(solution)/shard_map/ppermute | solution.py:1236
  143.0 10.8 %copy-start.60 = (s32[1024]{0:T(1024)}, s32[1024]{0:T(1024)S(1)}, u32[]{:S(2)}) copy-start(s32[1024]{0:T(1024)S(1)} %pad_dynamic-slice_fusion.2) | copy-start | bytes 12292
  145.0 8.7 copy-start.51
  192.7 9.7 %copy-start.38 = (bf16[1024,512]{1,0:T(8,128)(2,1)S(1)}, bf16[1024,512]{1,0:T(8,128)(2,1)}, u32[]{:S(2)}) copy-start(bf16[1024,512]{1,0:T(8,128)(2,1)} %get-tuple-element.97.refs_1_) | copy-start | bytes 3145732
  211.1 12.4 %copy-start.23 = (bf16[256,1024]{1,0:T(8,128)(2,1)}, bf16[256,1024]{1,0:T(8,128)(2,1)S(1)}, u32[]{:S(2)}) copy-start(bf16[256,1024]{1,0:T(8,128)(2,1)S(1)} %collective-permute-done) | copy-start | bytes 1572868
  211.1 24.4 %collective-permute-start.8 = (bf16[256,1024]{1,0:T(8,128)(2,1)}, bf16[256,1024]{1,0:T(8,128)(2,1)S(1)}, u32[]{:S(2)}, u32[]{:S(2)}) collective-permute-start(bf16[256,1024]{1,0:T(8,128)(2,1)} %get-tuple-element.259), channel_id=1, source_target_pairs={{0,2},{1,3},{2,0},{3,1},{4,6},{5,7},{6,4},{7,5},{8,10},{9,11},{10,... | collective-permute-start | bytes 1572872 | tf_op jit(solution)/shard_map/ppermute | solution.py:1239
  212.5 34.3 %collective-permute-start.9 = (bf16[256,1024]{1,0:T(8,128)(2,1)}, bf16[256,1024]{1,0:T(8,128)(2,1)S(1)}, u32[]{:S(2)}, u32[]{:S(2)}) collective-permute-start(bf16[256,1024]{1,0:T(8,128)(2,1)} %get-tuple-element.259), channel_id=1, source_target_pairs={{0,1},{1,2},{2,3},{3,0},{4,5},{5,6},{6,7},{7,4},{8,9},{9,10},{10,1... | collective-permute-start | bytes 1572872 | tf_op jit(solution)/shard_map/ppermute | solution.py:1239
  219.1 101.9 %collective-permute-start.4 = (bf16[768,1024]{1,0:T(8,128)(2,1)}, bf16[768,1024]{1,0:T(8,128)(2,1)}, u32[]{:S(2)}, u32[]{:S(2)}) collective-permute-start(bf16[768,1024]{1,0:T(8,128)(2,1)} %constant_dynamic-update-slice_fusion.1), channel_id=1, source_target_pairs={{0,16},{8,24},{16,0},{24,8},{1,17},{9,25},{17,1},{25,9},{2,18},{10... | collective-permute-start | bytes 4718600 | tf_op jit(solution)/shard_map/ppermute | solution.py:1245
  220.6 104.0 %collective-permute-start.3 = (bf16[768,1024]{1,0:T(8,128)(2,1)}, bf16[768,1024]{1,0:T(8,128)(2,1)}, u32[]{:S(2)}, u32[]{:S(2)}) collective-permute-start(bf16[768,1024]{1,0:T(8,128)(2,1)} %constant_dynamic-update-slice_fusion.1), channel_id=1, source_target_pairs={{0,8},{8,0},{16,24},{24,16},{1,9},{9,1},{17,25},{25,17},{2,10},{10... | collective-permute-start | bytes 4718600 | tf_op jit(solution)/shard_map/ppermute | solution.py:1245
  223.6 41.4 %collective-permute-start.21 = (bf16[512,256]{1,0:T(8,128)(2,1)S(1)}, bf16[512,256]{1,0:T(8,128)(2,1)S(1)}, u32[]{:S(2)}, u32[]{:S(2)}) collective-permute-start(bf16[512,256]{1,0:T(8,128)(2,1)S(1)} %get-tuple-element.297), channel_id=1, source_target_pairs={{0,1},{1,2},{2,3},{3,0},{4,5},{5,6},{6,7},{7,4},{8,9},{9,10},{10,1... | collective-permute-start | bytes 786440 | tf_op jit(solution)/shard_map/ppermute | solution.py:1239
  235.5 39.4 %copy-start.24 = (bf16[256,1024]{1,0:T(8,128)(2,1)}, bf16[256,1024]{1,0:T(8,128)(2,1)S(1)}, u32[]{:S(2)}) copy-start(bf16[256,1024]{1,0:T(8,128)(2,1)S(1)} %collective-permute-done.8) | copy-start | bytes 1572868
  235.5 31.0 %collective-permute-start.20 = (bf16[512,256]{1,0:T(8,128)(2,1)S(1)}, bf16[512,256]{1,0:T(8,128)(2,1)S(1)}, u32[]{:S(2)}, u32[]{:S(2)}) collective-permute-start(bf16[512,256]{1,0:T(8,128)(2,1)S(1)} %get-tuple-element.298), channel_id=1, source_target_pairs={{0,2},{1,3},{2,0},{3,1},{4,6},{5,7},{6,4},{7,5},{8,10},{9,11},{10,... | collective-permute-start | bytes 786440 | tf_op jit(solution)/shard_map/ppermute | solution.py:1239
  246.7 28.2 %copy-start.26 = (bf16[256,1024]{1,0:T(8,128)(2,1)}, bf16[256,1024]{1,0:T(8,128)(2,1)S(1)}, u32[]{:S(2)}) copy-start(bf16[256,1024]{1,0:T(8,128)(2,1)S(1)} %collective-permute-done.9) | copy-start | bytes 1572868
  246.7 27.9 %collective-permute-start.19 = (bf16[512,256]{1,0:T(8,128)(2,1)S(1)}, bf16[512,256]{1,0:T(8,128)(2,1)S(1)}, u32[]{:S(2)}, u32[]{:S(2)}) collective-permute-start(bf16[512,256]{1,0:T(8,128)(2,1)S(1)} %get-tuple-element.299), channel_id=1, source_target_pairs={{0,3},{1,0},{2,1},{3,2},{4,7},{5,4},{6,5},{7,6},{8,11},{9,8},{10,9... | collective-permute-start | bytes 786440 | tf_op jit(solution)/shard_map/ppermute | solution.py:1239
  264.9 10.0 %copy-start.45 = (bf16[512,256]{1,0:T(8,128)(2,1)}, bf16[512,256]{1,0:T(8,128)(2,1)S(1)}, u32[]{:S(2)}) copy-start(bf16[512,256]{1,0:T(8,128)(2,1)S(1)} %collective-permute-done.21) | copy-start | bytes 786436
  264.9 79.4 %collective-permute-start.11 = (bf16[768,1024]{1,0:T(8,128)(2,1)}, bf16[768,1024]{1,0:T(8,128)(2,1)}, u32[]{:S(2)}, u32[]{:S(2)}) collective-permute-start(bf16[768,1024]{1,0:T(8,128)(2,1)} %constant_dynamic-update-slice_fusion.4), channel_id=1, source_target_pairs={{0,16},{8,24},{16,0},{24,8},{1,17},{9,25},{17,1},{25,9},{2,18},{10... | collective-permute-start | bytes 4718600 | tf_op jit(solution)/shard_map/ppermute | solution.py:1245
  266.5 8.6 copy-start.47
  266.5 79.7 %collective-permute-start.10 = (bf16[768,1024]{1,0:T(8,128)(2,1)}, bf16[768,1024]{1,0:T(8,128)(2,1)}, u32[]{:S(2)}, u32[]{:S(2)}) collective-permute-start(bf16[768,1024]{1,0:T(8,128)(2,1)} %constant_dynamic-update-slice_fusion.4), channel_id=1, source_target_pairs={{0,8},{8,0},{16,24},{24,16},{1,9},{9,1},{17,25},{25,17},{2,10},{10... | collective-permute-start | bytes 4718600 | tf_op jit(solution)/shard_map/ppermute | solution.py:1245
  274.9 32.5 %copy-start.14 = (bf16[512,1024]{1,0:T(8,128)(2,1)}, bf16[512,1024]{1,0:T(8,128)(2,1)S(1)}, u32[]{:S(2)}) copy-start(bf16[512,1024]{1,0:T(8,128)(2,1)S(1)} %get-tuple-element.235.refs_1_) | copy-start | bytes 3145732
  275.0 53.3 %collective-permute-start.22 = (bf16[512,1024]{1,0:T(8,128)(2,1)S(1)}, bf16[512,1024]{1,0:T(8,128)(2,1)}, u32[]{:S(2)}, u32[]{:S(2)}) collective-permute-start(bf16[512,1024]{1,0:T(8,128)(2,1)S(1)} %get-tuple-element.235.refs_1_), channel_id=1, source_target_pairs={{0,4},{4,0},{1,5},{5,1},{2,6},{6,2},{3,7},{7,3},{8,12},{12,8},{9,1... | collective-permute-start | bytes 3145736 | tf_op jit(solution)/shard_map/ppermute | solution.py:1236
  307.5 7.2 copy-start.2
  320.9 7.3 copy-start.46
  320.9 7.3 copy-start.48
  321.0 7.3 copy-start.50
  323.1 31.5 %collective-permute-start.6 = (bf16[384,1024]{1,0:T(8,128)(2,1)}, bf16[384,1024]{1,0:T(8,128)(2,1)}, u32[]{:S(2)}, u32[]{:S(2)}) collective-permute-start(bf16[384,1024]{1,0:T(8,128)(2,1)} %slice.439), channel_id=1, source_target_pairs={{0,8},{8,0},{16,24},{24,16},{1,9},{9,1},{17,25},{25,17},{2,10},{10... | collective-permute-start | bytes 2359304 | tf_op jit(solution)/shard_map/ppermute | solution.py:1245
  326.7 27.9 %collective-permute-start.5 = (bf16[384,1024]{1,0:T(8,128)(2,1)}, bf16[384,1024]{1,0:T(8,128)(2,1)}, u32[]{:S(2)}, u32[]{:S(2)}) collective-permute-start(bf16[384,1024]{1,0:T(8,128)(2,1)} %slice.438), channel_id=1, source_target_pairs={{0,16},{8,24},{16,0},{24,8},{1,17},{9,25},{17,1},{25,9},{2,18},{10... | collective-permute-start | bytes 2359304 | tf_op jit(solution)/shard_map/ppermute | solution.py:1245
  345.6 19.3 %collective-permute-start.13 = (bf16[384,1024]{1,0:T(8,128)(2,1)S(1)}, bf16[384,1024]{1,0:T(8,128)(2,1)S(1)}, u32[]{:S(2)}, u32[]{:S(2)}) collective-permute-start(bf16[384,1024]{1,0:T(8,128)(2,1)S(1)} %slice.442), channel_id=1, source_target_pairs={{0,8},{8,0},{16,24},{24,16},{1,9},{9,1},{17,25},{25,17},{2,10},{10... | collective-permute-start | bytes 2359304 | tf_op jit(solution)/shard_map/ppermute | solution.py:1245
  347.3 19.0 %collective-permute-start.12 = (bf16[384,1024]{1,0:T(8,128)(2,1)S(1)}, bf16[384,1024]{1,0:T(8,128)(2,1)S(1)}, u32[]{:S(2)}, u32[]{:S(2)}) collective-permute-start(bf16[384,1024]{1,0:T(8,128)(2,1)S(1)} %slice.441), channel_id=1, source_target_pairs={{0,16},{8,24},{16,0},{24,8},{1,17},{9,25},{17,1},{25,9},{2,18},{10... | collective-permute-start | bytes 2359304 | tf_op jit(solution)/shard_map/ppermute | solution.py:1245
  356.7 9.7 %copy-start.29 = (bf16[256,1024]{1,0:T(8,128)(2,1)S(1)}, bf16[256,1024]{1,0:T(8,128)(2,1)}, u32[]{:S(2)}) copy-start(bf16[256,1024]{1,0:T(8,128)(2,1)} %get-tuple-element.257) | copy-start | bytes 1572868
  478.4 10.2 %copy-start.9 = (bf16[1024,512]{1,0:T(8,128)(2,1)S(1)}, bf16[1024,512]{1,0:T(8,128)(2,1)}, u32[]{:S(2)}) copy-start(bf16[1024,512]{1,0:T(8,128)(2,1)} %get-tuple-element.101.refs_0_.refs_4_) | copy-start | bytes 3145732
  494.9 52.1 %copy-start.68 = (bf16[1024,1024]{1,0:T(8,128)(2,1)S(1)}, bf16[1024,1024]{1,0:T(8,128)(2,1)}, u32[]{:S(2)}) copy-start(bf16[1024,1024]{1,0:T(8,128)(2,1)} %get-tuple-element.96) | copy-start | bytes 6291460
  550.6 11.1 %copy-start.10 = (bf16[1024,512]{1,0:T(8,128)(2,1)S(1)}, bf16[1024,512]{1,0:T(8,128)(2,1)}, u32[]{:S(2)}) copy-start(bf16[1024,512]{1,0:T(8,128)(2,1)} %get-tuple-element.94.refs_0_.refs_4_) | copy-start | bytes 3145732
  568.0 63.3 %copy-start.12 = (bf16[2,1024,1024]{2,1,0:T(8,128)(2,1)S(1)}, bf16[2,1024,1024]{2,1,0:T(8,128)(2,1)}, u32[]{:S(2)}) copy-start(bf16[2,1024,1024]{2,1,0:T(8,128)(2,1)} %enter.1) | copy-start | bytes 12582916
  656.1 26.4 %collective-permute-start.14 = (bf16[512,256]{1,0:T(8,128)(2,1)}, bf16[512,256]{1,0:T(8,128)(2,1)}, u32[]{:S(2)}, u32[]{:S(2)}) collective-permute-start(bf16[512,256]{1,0:T(8,128)(2,1)} %get-tuple-element.307), channel_id=1, source_target_pairs={{0,1},{1,2},{2,3},{3,0},{4,5},{5,6},{6,7},{7,4},{8,9},{9,10},{10,1... | collective-permute-start | bytes 786440 | tf_op jit(solution)/shard_map/ppermute | solution.py:1242
  656.1 27.3 %collective-permute-start.15 = (bf16[512,256]{1,0:T(8,128)(2,1)}, bf16[512,256]{1,0:T(8,128)(2,1)}, u32[]{:S(2)}, u32[]{:S(2)}) collective-permute-start(bf16[512,256]{1,0:T(8,128)(2,1)} %get-tuple-element.306), channel_id=1, source_target_pairs={{0,2},{1,3},{2,0},{3,1},{4,6},{5,7},{6,4},{7,5},{8,10},{9,11},{10,... | collective-permute-start | bytes 786440 | tf_op jit(solution)/shard_map/ppermute | solution.py:1242
  658.4 26.1 %collective-permute-start.16 = (bf16[512,256]{1,0:T(8,128)(2,1)}, bf16[512,256]{1,0:T(8,128)(2,1)}, u32[]{:S(2)}, u32[]{:S(2)}) collective-permute-start(bf16[512,256]{1,0:T(8,128)(2,1)} %get-tuple-element.305), channel_id=1, source_target_pairs={{0,3},{1,0},{2,1},{3,2},{4,7},{5,4},{6,5},{7,6},{8,11},{9,8},{10,9... | collective-permute-start | bytes 786440 | tf_op jit(solution)/shard_map/ppermute | solution.py:1242
  671.7 40.6 %collective-permute-start.23 = (bf16[512,1024]{1,0:T(8,128)(2,1)}, bf16[512,1024]{1,0:T(8,128)(2,1)}, u32[]{:S(2)}, u32[]{:S(2)}) collective-permute-start(bf16[512,1024]{1,0:T(8,128)(2,1)} %convert_element_type.157), channel_id=1, source_target_pairs={{1,0},{2,1},{3,2},{5,4},{6,5},{7,6},{9,8},{10,9},{11,10},{13,12},{... | collective-permute-start | bytes 3145736 | tf_op jit(solution)/shard_map/ppermute | solution.py:1454
  685.6 25.5 %collective-permute-start.17 = (bf16[2,512,256]{2,1,0:T(8,128)(2,1)S(1)}, bf16[2,512,256]{2,1,0:T(8,128)(2,1)S(1)}, u32[]{:S(2)}, u32[]{:S(2)}) collective-permute-start(bf16[2,512,256]{2,1,0:T(8,128)(2,1)S(1)} %get-tuple-element.304), channel_id=1, source_target_pairs={{0,4},{4,0},{1,5},{5,1},{2,6},{6,2},{3,7},{7,3},{8,12},{12,8},{9,1... | collective-permute-start | bytes 1572872 | tf_op jit(solution)/shard_map/ppermute | solution.py:1236
  698.6 8.9 copy-start.52
  698.6 8.9 copy-start.53
  698.6 8.9 copy-start.54
  904.9 6.9 copy-start.20
  (49 other events, 158.7 us)

commit v4 on v3

--- a/solution.py
+++ b/solution.py
@@ -66,6 +66,48 @@
     )
 
 
+def home_hop(rows, home, sends, recvs, n_col, k):
+    dp, row, col = here()
+    wide, count = home.shape[1], rows.shape[0]
+    to_row, at = col // 2, 2 * lax.rem(col, 2) + row
+    src = rows.at[:, pl.ds(k * wide, wide)]
+    dst = home.at[pl.ds(pl.multiple_of(at * count, count), count), :]
+    copy = remote(src, dst, sends.at[k], recvs.at[at], (dp, to_row, lax.rem(col + k, n_col)))
+    return copy, pltpu.make_async_copy(src, dst, recvs.at[at]), to_row == row
+
+
+def send_home(rows, home, sends, recvs, n_col):
+    for k in range(n_col):
+        away, here_copy, same = home_hop(rows, home, sends, recvs, n_col, k)
+        if k:
+            away.start()
+            continue
+
+        @pl.when(same)
+        def _():
+            here_copy.start()
+
+        @pl.when(jnp.logical_not(same))
+        def _():
+            away.start()
+
+
+def wait_home(rows, home, sends, recvs, n_col):
+    wide, count = home.shape[1], rows.shape[0]
+    for k in range(n_col):
+        away, _, same = home_hop(rows, home, sends, recvs, n_col, k)
+        if k:
+            away.wait_send()
+        else:
+
+            @pl.when(jnp.logical_not(same))
+            def _():
+                away.wait_send()
+
+        src = rows.at[:, pl.ds(k * wide, wide)]
+        pltpu.make_async_copy(src, home.at[pl.ds(k * count, count), :], recvs.at[k]).wait()
+
+
 def plane():
     dp, row, col = here()
     flips = [dp + b - 2 * b * lax.rem(dp // b, 2) for b in (1, 2)]
@@ -78,10 +120,27 @@
     return first.astype(low), (1.0 - first).astype(low), lane < HEAD_DIM
 
 
-def attend_kernel(q_ref, k_ref, v_ref, qid_ref, kid_ref, o_ref, lse_ref, bias, *, span, windowed):
+def attend_kernel(*refs, span, windowed, rider, n_ins, n_outs):
+    refs = list(refs)
+    q_ref, k_ref, v_ref, qid_ref, kid_ref = refs[:5]
+    rider_refs = refs[5 : 5 + n_ins]
+    refs = refs[5 + n_ins :]
+    o_ref, lse_ref = refs[:2]
+    rider_refs += refs[2 : 2 + n_outs]
+    bias = refs[2 + n_outs]
+    rider_refs += refs[3 + n_outs :]
     rows = q_ref.shape[0]
     pairs = q_ref.shape[1] // PAIR
-    start = pl.program_id(0) * rows if windowed else 0
+    step = pl.program_id(0)
+    if rider is not None:
+        hooks = rider(*rider_refs)
+        for at, hook in hooks:
+
+            @pl.when(step == at)
+            def _():
+                hook()
+
+    start = step * rows if windowed else 0
     if windowed:
         start = pl.multiple_of(start, rows)
     allowed = qid_ref[...] == kid_ref[0:1, pl.ds(start, span)]
@@ -114,15 +173,31 @@
 
     lax.fori_loop(0, pairs, one_pair, 0)
 
-
-def attend(q, k, v, qid, kid, windowed):
+    if rider is not None:
+
+        @pl.when(step == pl.num_programs(0) - 1)
+        def _():
+            hooks.end()
+
+
+class Hooks(list):
+    end = None
+
+
+def attend(q, k, v, qid, kid, windowed, rider=None, riding=(), shapes=(), scratch=(), number=0):
     tokens, width = q.shape
     keys = k.shape[0]
     pairs = width // PAIR
     rows = QUERY_ROWS
     span = WIN + rows if windowed else keys
+    params = dict(vmem_limit_bytes=VMEM)
+    if rider is not None:
+        params.update(collective_id=number, has_side_effects=True)
     return pl.pallas_call(
-        functools.partial(attend_kernel, span=span, windowed=windowed),
+        functools.partial(
+            attend_kernel, span=span, windowed=windowed, rider=rider, n_ins=len(riding),
+            n_outs=len(shapes),
+        ),
         grid=(tokens // rows,),
         in_specs=[
             pl.BlockSpec((rows, width), lambda i: (i, 0)),
@@ -130,19 +205,84 @@
             pl.BlockSpec((keys, width), lambda i: (0, 0)),
             pl.BlockSpec((rows, 1), lambda i: (i, 0)),
             pl.BlockSpec((1, keys), lambda i: (0, 0)),
-        ],
+        ]
+        + [pl.BlockSpec(x.shape, lambda i: (0, 0)) for x in riding],
         out_specs=[
             pl.BlockSpec((rows, width), lambda i: (i, 0)),
             pl.BlockSpec((pairs, 8, rows), lambda i: (0, 0, i)),
-        ],
+        ]
+        + [ANYWHERE] * len(shapes),
         out_shape=[
             jax.ShapeDtypeStruct((tokens, width), low),
             jax.ShapeDtypeStruct((pairs, 8, tokens), f32),
-        ],
-        scratch_shapes=[pltpu.VMEM((rows, span), f32)],
-        compiler_params=pltpu.CompilerParams(vmem_limit_bytes=VMEM),
+        ]
+        + [jax.ShapeDtypeStruct(*x) for x in shapes],
+        scratch_shapes=[pltpu.VMEM((rows, span), f32)] + list(scratch),
+        compiler_params=pltpu.CompilerParams(**params),
         name="attend",
-    )(q, k, v, qid[:, None], kid[None, :])
+    )(q, k, v, qid[:, None], kid[None, :], *riding)
+
+
+def cross_rider(*refs, n_col):
+    raw, slices, full = refs[:4], refs[4:8], refs[8:12]
+    w_s, w_r, own_s = refs[12:]
+    dp, row, col = here()
+    part = lax.rem(dp, PARTS)
+    part_x, part_y = part + 1 - 2 * lax.rem(part, 2), part + 2 - 4 * (part // 2)
+    by_x, by_y = plane()
+    wide = raw[0].shape[0]
+    rest = (n_col - 1) * wide
+    half = rest // 2
+
+    def spot(i, which, begin, size):
+        if i < 3:
+            count = raw[i].shape[1] // PARTS
+            return full[i].at[pl.ds(begin, size), pl.ds(pl.multiple_of(which * count, count), count)]
+        count = raw[i].shape[0] // PARTS
+        return full[i].at[pl.ds(pl.multiple_of(which * count, count), count), pl.ds(begin, size)]
+
+    def hop(i, stage):
+        which, begin, size, to = [
+            (part, wide, rest, by_x), (part, wide, rest, by_y),
+            (part_x, wide, half, by_y), (part_y, wide + half, half, by_x),
+        ][stage]
+        dst = spot(i, which, begin, size)
+        return remote(slices[i] if stage < 2 else dst, dst, w_s.at[i, stage], w_r.at[i, stage], to)
+
+    def own(i):
+        place = full[i].at[pl.ds(0, wide), :] if i < 3 else full[i].at[:, pl.ds(0, wide)]
+        return [
+            pltpu.make_async_copy(raw[i], place, own_s.at[i, 0]),
+            pltpu.make_async_copy(slices[i], spot(i, part, wide, rest), own_s.at[i, 1]),
+        ]
+
+    def begin():
+        meet([by_x, by_y])
+        for i in range(4):
+            hop(i, 0).start()
+            hop(i, 1).start()
+        for i in range(4):
+            for copy in own(i):
+                copy.start()
+
+    def later():
+        for i in range(4):
+            for stage in range(2):
+                hop(i, stage).wait_recv()
+                hop(i, 2 + stage).start()
+
+    def end():
+        for i in range(4):
+            hop(i, 2).wait_recv()
+            hop(i, 3).wait_recv()
+            for stage in range(4):
+                hop(i, stage).wait_send()
+            for copy in own(i):
+                copy.wait()
+
+    hooks = Hooks([(0, begin), (2, later)])
+    hooks.end = end
+    return hooks
 
 
 def attend_back_kernel(*refs, span, windowed, rider, n_ins, n_outs):
@@ -166,10 +306,6 @@
         begin()
         dk_sum[...] = jnp.zeros_like(dk_sum)
         dv_sum[...] = jnp.zeros_like(dv_sum)
-
-    @pl.when(step == 1)
-    def _():
-        middle()
 
     allowed = kid_ref[keys, :] == qid_ref[...]
     if windowed:
@@ -199,6 +335,11 @@
         dk_sum[keys, lanes] += dk
         dv_sum[keys, lanes] += dv
         dq_ref[:, lanes] = (jnp.where(is_first, dqs[0], dqs[1]) * HEAD_DIM**-0.5).astype(low)
+
+        @pl.when((step == 0) & (p == 0))
+        def _():
+            middle()
+
         return carry
 
     lax.fori_loop(0, pairs, one_pair, 0)
@@ -358,13 +499,47 @@
 CUBE = 0.044715
 
 
-def hidden_kernel(f_ref, w1_ref, b1_ref, w2_ref, act_ref, slope_ref, out_ref, total):
+def hidden_kernel(
+    f_ref, w1_ref, b1_ref, w2_ref, x_ref, bias, cot, act_ref, slope_ref, out_ref, dz,
+    total, away, came, s_s, s_r, c_s, c_r, d_s, d_r,
+    *, n_col,
+):
     step = pl.program_id(0) * pl.num_programs(1) + pl.program_id(1)
     last = pl.num_programs(0) * pl.num_programs(1) - 1
+    dp, row, col = here()
+    twin = (dp, 1 - row, col)
+    wide = cot.shape[1]
+    rows_here = cot.shape[0] // n_col
+
+    def cot_piece(j):
+        to_col = 2 * row + j // 2
+        k = lax.rem(col + n_col - to_col, n_col)
+        src = cot.at[pl.ds(j * rows_here, rows_here), :]
+        dst = dz.at[j % 2, :, pl.ds(pl.multiple_of(k * wide, wide), wide)]
+        local = (row == j % 2) & (col == to_col)
+        return src, dst, k, local, (dp, j % 2, to_col)
+
+    def cot_twin(k):
+        ref = dz.at[row, :, pl.ds(k * wide, wide)]
+        return remote(ref, ref, d_s.at[k], d_r.at[k], twin)
 
     @pl.when(step == 0)
     def _():
         total[...] = jnp.zeros_like(total)
+        group = [
+            (dp, r, lax.rem(col + k, n_col)) for r in (row, 1 - row) for k in range(n_col)
+        ]
+        meet(group[1:])
+        for j in range(n_col):
+            src, dst, k, local, to = cot_piece(j)
+
+            @pl.when(local)
+            def _():
+                pltpu.make_async_copy(src, dst, c_r.at[k]).start()
+
+            @pl.when(jnp.logical_not(local))
+            def _():
+                remote(src, dst, c_s.at[j], c_r.at[k], to).start()
 
     def one_part(t, carry):
         rows = pl.ds(pl.multiple_of(t * 256, 256), 256)
@@ -381,42 +556,89 @@
 
     lax.fori_loop(0, f_ref.shape[0] // 256, one_part, 0)
 
+    @pl.when(step == last - 1)
+    def _():
+        for k in range(n_col):
+            pltpu.make_async_copy(
+                cot.at[pl.ds(0, rows_here), :], dz.at[row, :, pl.ds(k * wide, wide)], c_r.at[k]
+            ).wait()
+            cot_twin(k).start()
+
     @pl.when(step == last)
     def _():
-        out_ref[...] = total[...].astype(low)
-
-
-def hidden_forward(f, w1, b1, w2):
+        rows = came.shape[0]
+        sent = []
+        for t in range(rows // CUT):
+            at = pl.ds(t * CUT, CUT)
+            begin = pl.multiple_of((1 - row) * rows + t * CUT, CUT)
+            away[at, :] = total[pl.ds(begin, CUT), :].astype(low)
+            copy = remote(away.at[at, :], came.at[at, :], s_s.at[t], s_r.at[t], twin)
+            copy.start()
+            sent.append(copy)
+        for t in range(rows // CUT):
+            at = pl.ds(t * CUT, CUT)
+            begin = pl.multiple_of(row * rows + t * CUT, CUT)
+            sent[t].wait()
+            branch = total[pl.ds(begin, CUT), :] + came[at, :].astype(f32)
+            out_ref[at, :] = (x_ref[at, :] + (branch + bias[...])).astype(low)
+        for j in range(n_col):
+            src, dst, k, local, to = cot_piece(j)
+
+            @pl.when(jnp.logical_not(local))
+            def _():
+                remote(src, dst, c_s.at[j], c_r.at[k], to).wait_send()
+
+        for k in range(n_col):
+            cot_twin(k).wait()
+
+
+def hidden_forward(f, w1, b1, w2, x, bias, cotangent, n_col, number):
     parts, width, inner = w1.shape
     tokens = f.shape[0]
     block = min(512, inner)
     grid = (parts, inner // block)
     weight = pl.BlockSpec((1, width, block), lambda j, n: (j, 0, n))
     active = pl.BlockSpec((1, tokens, block), lambda j, n: (j, 0, n))
+    rows = tokens // 2
+    dma = pltpu.SemaphoreType.DMA
+    half = pl.BlockSpec((rows, width), lambda j, n: (0, 0))
     return pl.pallas_call(
-        hidden_kernel,
+        functools.partial(hidden_kernel, n_col=n_col),
         grid=grid,
         in_specs=[
             pl.BlockSpec((tokens, width), lambda j, n: (0, 0)),
             weight,
             pl.BlockSpec((1, 1, block), lambda j, n: (j, 0, n)),
             weight,
+            half,
+            pl.BlockSpec((1, width), lambda j, n: (0, 0)),
+            pl.BlockSpec(cotangent.shape, lambda j, n: (0, 0)),
         ],
-        out_specs=[active, active, pl.BlockSpec((tokens, width), lambda j, n: (0, 0))],
+        out_specs=[active, active, half, ANYWHERE],
         out_shape=[
             jax.ShapeDtypeStruct((parts, tokens, inner), low),
             jax.ShapeDtypeStruct((parts, tokens, inner), low),
-            jax.ShapeDtypeStruct((tokens, width), low),
+            jax.ShapeDtypeStruct((rows, width), low),
+            jax.ShapeDtypeStruct((2, rows, width), low),
         ],
-        scratch_shapes=[pltpu.VMEM((tokens, width), f32)],
-        compiler_params=pltpu.CompilerParams(vmem_limit_bytes=VMEM),
+        scratch_shapes=[
+            pltpu.VMEM((tokens, width), f32),
+            pltpu.VMEM((rows, width), low),
+            pltpu.VMEM((rows, width), low),
+            dma((rows // CUT,)), dma((rows // CUT,)),
+            dma((n_col,)), dma((n_col,)), dma((n_col,)), dma((n_col,)),
+        ],
+        compiler_params=pltpu.CompilerParams(
+            vmem_limit_bytes=VMEM, collective_id=number, has_side_effects=True
+        ),
         name="hidden_forward",
-    )(f, w1, b1, w2)
+    )(f, w1, b1, w2, x, bias[None], cotangent)
 
 
 def hidden_back_kernel(
-    dz_ref, dzt_ref, ft_ref, w1_ref, w2_ref, act_ref, slope_ref,
-    g1_ref, g2_ref, gb_ref, df_ref, got_a, got_b, dh_low, total, away_a, away_b, s_s, r_s,
+    dz_ref, dzt_ref, ft_ref, w1_ref, w2_ref, act_ref, slope_ref, rows_out,
+    g1_ref, g2_ref, gb_ref, df_ref, got_a, got_b, home, dh_low, total, away_a, away_b, s_s, r_s,
+    h_s, h_r, *, n_col,
 ):
     inner, inners = pl.program_id(1), pl.num_programs(1)
     order = pl.program_id(0)
@@ -424,11 +646,16 @@
     last = pl.num_programs(0) * inners - 1
     by_x, by_y = plane()
     half = got_a.shape[1]
+    dp, row, col = here()
 
     @pl.when(step == 0)
     def _():
-        meet([by_x, by_y])
+        group = [
+            (dp, r, lax.rem(col + k, n_col)) for r in (row, 1 - row) for k in range(n_col)
+        ]
+        meet(group[1:] + [by_x, by_y])
         total[...] = jnp.zeros_like(total)
+        send_home(rows_out, home, h_s, h_r, n_col)
 
     gb_ref[...] = jnp.zeros_like(gb_ref)
 
@@ -453,10 +680,12 @@
     block = g1_ref.shape[2]
     lanes = pl.ds(pl.multiple_of(inner * block, block), block)
 
-    def hop(which, slot):
+    def hop(which, slot, n):
         away, got, to = [(away_a, got_a, by_x), (away_b, got_b, by_y)][which]
+        at = pl.ds(n * block, block)
         return remote(
-            away.at[slot], got.at[slot], s_s.at[which, slot], r_s.at[which, slot], to
+            away.at[slot, :, at], got.at[slot, :, at], s_s.at[which, slot, n],
+            r_s.at[which, slot, n], to,
         )
 
     for at, which, slot in ((0, 0, 0), (0, 1, 0), (1, 0, 1), (2, 1, 1)):
@@ -466,19 +695,23 @@
             away = (away_a, away_b)[which]
             away[slot, :, lanes] = g1_ref[0, which * half : (which + 1) * half, :]
 
-        @pl.when((order == at) & (inner == inners - 1))
-        def _():
-            hop(which, slot).start()
+        for n in range(got_a.shape[2] // block):
+
+            @pl.when((order == at) & (inner == n))
+            def _():
+                hop(which, slot, n).start()
 
     @pl.when(step == last)
     def _():
         df_ref[...] = total[...].astype(low)
         for which in range(2):
             for slot in range(2):
-                hop(which, slot).wait()
-
-
-def hidden_backward(dz, f, w1, w2, act, slope, number):
+                for n in range(got_a.shape[2] // block):
+                    hop(which, slot, n).wait()
+        wait_home(rows_out, home, h_s, h_r, n_col)
+
+
+def hidden_backward(dz, f, w1, w2, act, slope, rows_out, n_col, number):
     parts, width, inner = w1.shape
     tokens = f.shape[0]
     block = min(512, inner)
@@ -493,12 +726,13 @@
     turned = pl.BlockSpec((width, tokens), lambda j, n: (0, 0))
     landing = jax.ShapeDtypeStruct((2, width // 2, inner), low)
     return pl.pallas_call(
-        hidden_back_kernel,
+        functools.partial(hidden_back_kernel, n_col=n_col),
         grid=grid,
-        in_specs=[whole, turned, turned, weight, weight, active, active],
+        in_specs=[whole, turned, turned, weight, weight, active, active]
+        + [pl.BlockSpec(rows_out.shape, lambda j, n: (0, 0))],
         out_specs=[
             weight, weight, pl.BlockSpec((1, 1, block), lambda j, n: (number_of(j), 0, n)), whole,
-            ANYWHERE, ANYWHERE,
+            ANYWHERE, ANYWHERE, ANYWHERE,
         ],
         out_shape=[
             jax.ShapeDtypeStruct(w1.shape, low),
@@ -507,27 +741,31 @@
             jax.ShapeDtypeStruct((tokens, width), low),
             landing,
             landing,
+            jax.ShapeDtypeStruct((n_col * rows_out.shape[0], width // n_col), low),
         ],
         scratch_shapes=[
             pltpu.VMEM((tokens, block), low),
             pltpu.VMEM((tokens, width), f32),
             pltpu.VMEM(landing.shape, low),
             pltpu.VMEM(landing.shape, low),
-            pltpu.SemaphoreType.DMA((2, 2)),
-            pltpu.SemaphoreType.DMA((2, 2)),
+            pltpu.SemaphoreType.DMA((2, 2, inner // block)),
+            pltpu.SemaphoreType.DMA((2, 2, inner // block)),
+            pltpu.SemaphoreType.DMA((n_col,)),
+            pltpu.SemaphoreType.DMA((n_col,)),
         ],
         compiler_params=pltpu.CompilerParams(
             vmem_limit_bytes=VMEM, collective_id=number, has_side_effects=True
         ),
         name="hidden_backward",
-    )(dz, dz.T, f.T, w1, w2, act, slope)
+    )(dz, dz.T, f.T, w1, w2, act, slope, rows_out)
 
 
 def start_kernel(
     tokens, encoder, vec_f, vec_c, *refs, n_col,
 ):
     weights, (x_ext, enc, all_f, all_c), full = refs[:8], refs[8:12], refs[12:20]
-    zeros, w_send, w_recv, w_own, t_send, t_recv, e_send, e_recv, v_send, v_recv, z_sem = refs[20:]
+    (zeros, w_send, w_recv, w_own, t_send, t_recv, v_send, v_recv, z_sem, z_send, z_recv, e_send,
+     e_recv, o_sem) = refs[20:]
     dp, row, col = here()
     part = lax.rem(dp, PARTS)
     twin = (dp, 1 - row, col)
@@ -548,17 +786,71 @@
     def chunk(index, size):
         return pl.ds(pl.multiple_of(index * size, size), size)
 
-    def weight_z(i, k):
-        w, to = weights[i], (dp, row, lax.rem(col + n_col - k, n_col))
+    to_right, to_left = (dp, row, lax.rem(col + 1, n_col)), (dp, row, lax.rem(col + n_col - 1, n_col))
+
+    def weight_chunk(i, k):
+        w = weights[i]
         if i % 4 < 3:
-            size = w.shape[1] // PARTS
-            src = w.at[:, chunk(part, size)]
-            dst = full[i].at[pl.ds(k * wide, wide), chunk(part, size)]
-        else:
-            size = w.shape[0] // PARTS
-            src = w.at[chunk(part, size), :]
-            dst = full[i].at[chunk(part, size), pl.ds(k * wide, wide)]
-        return remote(src, dst, w_send.at[i, k - 1], w_recv.at[i, k - 1], to)
+            return full[i].at[pl.ds(k * wide, wide), chunk(part, w.shape[1] // PARTS)]
+        return full[i].at[chunk(part, w.shape[0] // PARTS), pl.ds(k * wide, wide)]
+
+    def weight_slice(i):
+        w = weights[i]
+        if i % 4 < 3:
+            return w.at[:, chunk(part, w.shape[1] // PARTS)]
+        return w.at[chunk(part, w.shape[0] // PARTS), :]
+
+    def enc_chunk(k):
+        return enc.at[chunk(row, encoder.shape[0]), pl.ds(k * wide, wide)]
+
+    def piece(i, k):
+        if i == 8:
+            return enc_chunk(k)
+        if i < 4:
+            return weight_chunk(i, k)
+        if i % 4 < 3:
+            return full[i].at[pl.ds((k - 1) * wide, wide), :]
+        return full[i].at[:, pl.ds((k - 1) * wide, wide)]
+
+    def own_piece(i):
+        return encoder if i == 8 else weight_slice(i)
+
+    def enc_twin(k):
+        return remote(own_piece(8) if k == 0 else enc_chunk(k), enc_chunk(k), e_send.at[k],
+                      e_recv.at[k], twin)
+
+    def rightward(i, h):
+        src = own_piece(i) if h == 1 else piece(i, n_col + 1 - h)
+        k = n_col - h
+        return remote(src, piece(i, k), z_send.at[i, 0, h - 1], z_recv.at[i, k - 1], to_right)
+
+    def leftward(i, h):
+        src = own_piece(i) if h == 1 else piece(i, h - 1)
+        return remote(src, piece(i, h), z_send.at[i, 1, h - 1], z_recv.at[i, h - 1], to_left)
+
+    def right_valid(h):
+        return (col >= h - 1) & (col < n_col - 1)
+
+    def left_valid(h):
+        return (col <= n_col - h) & (col > 0)
+
+    def send_along(i, h):
+        @pl.when(right_valid(h))
+        def _():
+            rightward(i, h).start()
+
+        @pl.when(left_valid(h))
+        def _():
+            leftward(i, h).start()
+
+    def take(i, h):
+        @pl.when(col >= h)
+        def _():
+            rightward(i, h).wait_recv()
+
+        @pl.when(col < n_col - h)
+        def _():
+            leftward(i, h).wait_recv()
 
     def weight_own(i):
         w = weights[i]
@@ -579,7 +871,7 @@
             (part_y, wide + half, half, by_x),
         ][stage]
         ref = weight_part(i, which, begin, size)
-        return remote(ref, ref, w_send.at[i, 3 + stage], w_recv.at[i, 3 + stage], to)
+        return remote(ref, ref, w_send.at[i, stage], w_recv.at[i, stage], to)
 
     def token_piece(j, slot):
         rows = tokens.shape[0] // n_col
@@ -603,15 +895,6 @@
             def _():
                 remote(src, dst, t_send.at[slot, j], t_recv.at[slot, k], to).start()
 
-    def enc_z(k):
-        ref = enc.at[chunk(row, encoder.shape[0]), pl.ds(k * wide, wide)]
-        to = (dp, row, lax.rem(col + n_col - k, n_col))
-        return remote(encoder, ref, e_send.at[0, k], e_recv.at[0, k], to)
-
-    def enc_twin(k):
-        ref = enc.at[chunk(row, encoder.shape[0]), pl.ds(k * wide, wide)]
-        return remote(encoder if k == 0 else ref, ref, e_send.at[1, k], e_recv.at[1, k], twin)
-
     def vectors(k):
         to = (dp, row, lax.rem(col + n_col - k, n_col))
         return [
@@ -620,31 +903,27 @@
         ]
 
     own_vectors = [
+        pltpu.make_async_copy(encoder, enc_chunk(0), o_sem),
         pltpu.make_async_copy(vec_f, all_f.at[:, pl.ds(0, wide)], v_recv.at[0, 0]),
         pltpu.make_async_copy(vec_c, all_c.at[col], v_recv.at[1, 0]),
-        pltpu.make_async_copy(
-            encoder, enc.at[chunk(row, encoder.shape[0]), pl.ds(0, wide)], e_recv.at[0, 0]
-        ),
     ]
     ks = range(1, n_col)
-    for i in range(4):
-        for k in ks:
-            weight_z(i, k).start()
-    send_tokens(1)
+    for i in range(9):
+        send_along(i, 1)
     for k in ks:
         for copy in vectors(k):
             copy.start()
-    for i in range(4, 8):
-        for k in ks:
-            weight_z(i, k).start()
-    send_tokens(0)
-    enc_twin(0).start()
-    for k in ks:
-        enc_z(k).start()
-    for i in range(8):
+    for i in range(4):
         weight_own(i).start()
     for copy in own_vectors:
         copy.start()
+    enc_twin(0).start()
+    for h in (1, 2):
+        for i in range(9):
+            take(i, h)
+            send_along(i, h + 1)
+    send_tokens(1)
+    send_tokens(0)
 
     @pl.when(col == 0)
     def _():
@@ -653,36 +932,43 @@
         clear.start()
         clear.wait()
 
-    for base in (0, 4):
-        for i in range(base, base + 4):
-            for k in ks:
-                weight_z(i, k).wait_recv()
+    for i in range(8):
+        take(i, 3)
+        if i < 4:
             weight_plane(i, 0).start()
             weight_plane(i, 1).start()
-        for i in range(base, base + 4):
-            weight_plane(i, 0).wait_recv()
-            weight_plane(i, 2).start()
-            weight_plane(i, 1).wait_recv()
-            weight_plane(i, 3).start()
+    take(8, 3)
     for k in ks:
-        enc_z(k).wait_recv()
         enc_twin(k).start()
-    for i in range(8):
+    for i in range(4):
+        weight_plane(i, 0).wait_recv()
+        weight_plane(i, 2).start()
+        weight_plane(i, 1).wait_recv()
+        weight_plane(i, 3).start()
+    for i in range(4):
         weight_plane(i, 2).wait_recv()
         weight_plane(i, 3).wait_recv()
         weight_own(i).wait()
-        for k in ks:
-            weight_z(i, k).wait_send()
         for stage in range(4):
             weight_plane(i, stage).wait_send()
+    for k in range(n_col):
+        enc_twin(k).wait()
+    for i in range(9):
+        for h in ks:
+
+            @pl.when(right_valid(h))
+            def _():
+                rightward(i, h).wait_send()
+
+            @pl.when(left_valid(h))
+            def _():
+                leftward(i, h).wait_send()
+
     for copy in own_vectors:
         copy.wait()
     for k in ks:
         for copy in vectors(k):
             copy.wait()
-        enc_z(k).wait_send()
-    for k in range(n_col):
-        enc_twin(k).wait()
     for slot in (1, 0):
         for j in range(n_col):
             src, dst, k, local, valid, to = token_piece(j, slot)
@@ -718,22 +1004,22 @@
         jax.ShapeDtypeStruct((n_col,) + vec_c.shape, f32),
     ]
     for i, w in enumerate(weights):
-        shapes.append(
-            jax.ShapeDtypeStruct((deep, w.shape[1]) if i % 4 < 3 else (w.shape[0], deep), low)
-        )
+        at, length, size = (0, deep, w.shape[1]) if i % 4 < 3 else (1, deep, w.shape[0])
+        if i >= 4:
+            length, size = deep - wide, size // PARTS
+        shapes.append(jax.ShapeDtypeStruct((size, length) if at else (length, size), low))
     dma = pltpu.SemaphoreType.DMA
     return pl.pallas_call(
         functools.partial(start_kernel, n_col=n_col),
-        in_specs=[ANYWHERE] * 12,
+        in_specs=[IN_VMEM] * 12,
         out_specs=[ANYWHERE] * 12,
         out_shape=shapes,
         scratch_shapes=[
             pltpu.VMEM((rows, deep), low),
-            dma((8, 7)), dma((8, 7)), dma((8,)),
+            dma((4, 4)), dma((4, 4)), dma((4,)),
             dma((2, n_col)), dma((2, n_col)),
             dma((2, n_col)), dma((2, n_col)),
-            dma((2, n_col)), dma((2, n_col)),
-            dma,
+            dma, dma((9, 2, n_col - 1)), dma((9, n_col - 1)), dma((n_col,)), dma((n_col,)), dma,
         ],
         compiler_params=pltpu.CompilerParams(
             collective_id=1, has_side_effects=True, vmem_limit_bytes=VMEM
@@ -750,6 +1036,7 @@
 
 
 CUT = 256
+N_COL = 4
 
 
 def enter_kernel(x_ref, gain, shift, a_ref, sends, recvs):
@@ -801,6 +1088,9 @@
         x_ref, bias, gain, shift, x_out, full, away, came, s1, r1, s2, r2 = refs
     elif mode == "backward":
         res_ref, x_ref, gain, dx_out, full, stats, away, came, s1, r1, s2, r2 = refs
+    elif mode == "last":
+        res_ref, x_ref, gain, after, dx_out, stats, away, came, s1, r1 = refs
+        full = None
     else:
         out, away, came, s1, r1 = refs
     rows = came.shape[0]
@@ -827,7 +1117,7 @@
         copy.start()
         sent.append(copy)
     gathered = []
-    sums = [0.0, 0.0, 0.0]
+    sums = [0.0] * 4
     for t in range(cuts):
         at = pl.ds(t * CUT, CUT)
         begin = pl.multiple_of(row * rows + t * CUT, CUT)
@@ -835,8 +1125,13 @@
         sent[t].wait_recv()
         total = own + came[at, :].astype(f32)
         if mode == "sum":
-            out[at, :] = total
+            out[at, :] = total.astype(low)
             continue
+        if mode == "last":
+            deep = after.shape[1]
+            wide = deep // N_COL
+            moved = [after[at, pl.ds(deep - wide, wide)], after[at, pl.ds(0, deep - wide)]]
+            total = total + jnp.concatenate(moved, axis=1).astype(f32)
         if mode == "forward":
             x = x_ref[at, :].astype(f32) + (total + bias[...])
             x_out[at, :] = x
@@ -847,10 +1142,11 @@
             upstream = total * gain[...]
             mean_up = jnp.mean(upstream, axis=1, keepdims=True)
             mean_both = jnp.mean(upstream * normed, axis=1, keepdims=True)
-            dx = res_ref[at, :].astype(f32) + scaling * (upstream - mean_up - normed * mean_both)
-            dx_out[at, :] = dx
+            res = res_ref[at if res_ref.shape[0] == rows else pl.ds(begin, CUT), :].astype(f32)
+            dx = res + scaling * (upstream - mean_up - normed * mean_both)
+            dx_out[at, :] = dx.astype(dx_out.dtype)
             result = dx.astype(low)
-            for i, value in enumerate((total * normed, total, result.astype(f32))):
+            for i, value in enumerate((total * normed, total, result.astype(f32), res)):
                 sums[i] = sums[i] + jnp.sum(value, axis=0, keepdims=True)
         if full is None:
             continue
@@ -859,8 +1155,8 @@
         copy = remote(place, place, s2.at[t], r2.at[t], twin)
         copy.start()
         gathered.append(copy)
-    if mode == "backward":
-        for i in range(3):
+    if mode in ("backward", "last"):
+        for i in range(4):
             stats[i : i + 1, :] = sums[i]
     for copy in sent:
         copy.wait_send()
@@ -883,10 +1179,11 @@
     shapes = {
         "forward": [wide_rows, every],
         "backward": [wide_rows, every, jax.ShapeDtypeStruct((8, deep), f32)],
-        "sum": [wide_rows],
+        "last": [jax.ShapeDtypeStruct((rows, deep), low), jax.ShapeDtypeStruct((8, deep), f32)],
+        "sum": [jax.ShapeDtypeStruct((rows, deep), low)],
     }[mode]
     scratch = [pltpu.VMEM((rows, deep), low), pltpu.VMEM((rows, deep), low), dma, dma]
-    if mode != "sum":
+    if mode in ("forward", "backward"):
         scratch += [dma, dma]
     args = flat + [x[None] if x.ndim == 1 else x for x in others]
     out = pl.pallas_call(
@@ -920,9 +1217,10 @@
     shift = [lax.rem(col + k, n_col) for k in range(n_col)]
     group = [(dp, r, c) for r in (row, 1 - row) for c in shift][1:]
     meet(group + by_bit)
-    wide = enc_out.shape[1]
+    wide = ga.shape[1] // n_col
     ks = range(1, n_col)
-    ways = [(ga, 0, (1, 3), 2), (gb, 1, (2, 3), 1)]
+    part_x, part_y, part_xy = part + 1 - 2 * lax.rem(part, 2), part + 2 - 4 * (part // 2), 3 - part
+    ways = [(ga, 0, (part_x, part_xy), part_y), (gb, 1, (part_y, part_xy), part_x)]
     h_half = near_a.shape[0]
     loads = []
     for i, sources in enumerate(((near_a, far_back_a), (near_b, far_back_b))):
@@ -1009,16 +1307,6 @@
                 value = value + s_z[k - 1]
             small_out[...] = value
 
-    t_rows = tg.shape[0]
-    home = col // 2
-    at_home = 2 * lax.rem(col, 2) + row
-
-    def tg_hop(k):
-        src = tg.at[:, pl.ds(k * wide, wide)]
-        dst = tg_out.at[pl.ds(pl.multiple_of(at_home * t_rows, t_rows), t_rows), :]
-        return src, dst, (dp, home, shift[k])
-
-    part_x, part_y = lax.rem(flips[0], PARTS), lax.rem(flips[1], PARTS)
     half = wide // 2
 
     def plane_hop(full, g, stage, sends, recvs):
@@ -1040,29 +1328,24 @@
     for q in range(n_col):
         for g in range(2):
             hop(g, 1, q).start()
-    for k in ks:
-        enc_hop(k).start()
-    for q in range(n_col):
-        for g in range(2):
-            hop(g, 0, q).start()
-    for k in range(n_col):
-        src, dst, to = tg_hop(k)
-        if k == 0:
-
-            @pl.when(home == row)
-            def _():
-                pltpu.make_async_copy(src, dst, t_r.at[at_home]).start()
-
-            @pl.when(home != row)
-            def _():
-                remote(src, dst, t_s.at[k], t_r.at[at_home], to).start()
-        else:
-            remote(src, dst, t_s.at[k], t_r.at[at_home], to).start()
     for copy in loads:
         copy.wait()
     for k in ks:
         h_out[k] = hidden_total(k).astype(low)
         hidden_hop(k).start()
+    small_step(1)
+    done = 2
+    for q in range(n_col):
+        for g in range(2):
+            src, _, _, keep = ways[g]
+            hop(g, 1, q).wait_recv()
+            value = src[keep, rows(q), :].astype(f32) + first[g, 1, rows(q), :].astype(f32)
+            mid[g, rows(q), :] = value.astype(low)
+            hop2(g, q).start()
+            hop(g, 0, q).start()
+        if done < len(partners) + 2:
+            small_step(done)
+            done += 1
     for copy in loads_own:
         copy.wait()
     value = load_own[...].astype(f32)
@@ -1071,23 +1354,12 @@
     hidden_full[0, part] = other_bits(value, 0, h_extra, hx_s, hx_r).astype(low)
     hidden_plane(0, 0).start()
     hidden_plane(0, 1).start()
-    done = 1
     for q in range(n_col):
-        for g in range(2):
-            src, _, _, keep = ways[g]
-            hop(g, 1, q).wait_recv()
-            value = src[keep, rows(q), :].astype(f32) + first[g, 1, rows(q), :].astype(f32)
-            mid[g, rows(q), :] = value.astype(low)
-            hop2(g, q).start()
-        if done < len(partners) + 2:
-            small_step(done)
-            done += 1
-    for q in (1, 2, 3, 0):
         for g in range(2):
             src = ways[g][0]
             hop(g, 0, q).wait_recv()
             hop2(g, q).wait_recv()
-            value = src[0, rows(q), :].astype(f32) + first[g, 0, rows(q), :].astype(f32)
+            value = src[part, rows(q), :].astype(f32) + first[g, 0, rows(q), :].astype(f32)
             value = value + second[g, rows(q), :].astype(f32)
             if q:
                 zout[g, q - 1] = value.astype(low)
@@ -1097,14 +1369,20 @@
         if done < len(partners) + 2:
             small_step(done)
             done += 1
-    for stage in range(2):
-        hidden_plane(0, stage).wait_recv()
-        hidden_plane(0, 2 + stage).start()
-    value = enc_in[:, pl.ds(0, wide)].astype(f32)
+    send_home(tg, tg_out, t_s, t_r, n_col)
     for k in ks:
-        enc_hop(k).wait_recv()
-        value = value + enc_got[k - 1].astype(f32)
-    enc_out[...] = value
+        enc_hop(k).start()
+    value = hidden_total(0)
+    for k in ks:
+        hidden_hop(k).wait_recv()
+        value = value + h_in[k - 1].astype(f32)
+    hidden_full[1, part] = other_bits(value, 1, h_extra, hx_s, hx_r).astype(low)
+    hidden_plane(1, 0).start()
+    hidden_plane(1, 1).start()
+    for g in range(2):
+        for stage in range(2):
+            hidden_plane(g, stage).wait_recv()
+            hidden_plane(g, 2 + stage).start()
     while done < len(partners) + 2:
         small_step(done)
         done += 1
@@ -1115,27 +1393,22 @@
             value = value + zin[g, q - 1].astype(f32)
         value = other_bits(value, g, extra, x_s, x_r)
         full[g, part] = value.astype(low)
-    for g in range(2):
         plane_to(g, 0).start()
         plane_to(g, 1).start()
-    value = hidden_total(0)
-    for k in ks:
-        hidden_hop(k).wait_recv()
-        value = value + h_in[k - 1].astype(f32)
-    hidden_full[1, part] = other_bits(value, 1, h_extra, hx_s, hx_r).astype(low)
-    hidden_plane(1, 0).start()
-    hidden_plane(1, 1).start()
     for g in range(2):
         for stage in range(2):
             plane_to(g, stage).wait_recv()
             plane_to(g, 2 + stage).start()
-    for stage in range(2):
-        hidden_plane(1, stage).wait_recv()
-        hidden_plane(1, 2 + stage).start()
+    value = enc_in[:, pl.ds(0, wide)].astype(f32)
+    for k in ks:
+        enc_hop(k).wait()
+        value = value + enc_got[k - 1].astype(f32)
+    enc_out[...] = value
     for k in ks:
         hidden_hop(k).wait_send()
+        small_z(k).wait_send()
     for g in range(2):
-        for ways_out in (plane_to, hidden_plane):
+        for ways_out in (hidden_plane, plane_to):
             ways_out(g, 2).wait_recv()
             ways_out(g, 3).wait_recv()
             for stage in range(4):
@@ -1146,20 +1419,9 @@
             hop2(g, q).wait_send()
             if q:
                 z_hop(g, q).wait_send()
-    for k in ks:
-        enc_hop(k).wait_send()
-        small_z(k).wait_send()
     for i in range(len(partners)):
         small_hop(i).wait_send()
-    for k in range(n_col):
-        src, dst, to = tg_hop(k)
-
-        @pl.when((home != row) | (k > 0))
-        def _():
-            remote(src, dst, t_s.at[k], t_r.at[at_home], to).wait_send()
-
-        place = tg_out.at[pl.ds(k * t_rows, t_rows), :]
-        pltpu.make_async_copy(src, place, t_r.at[k]).wait()
+    wait_home(tg, tg_out, t_s, t_r, n_col)
 
 
 def finish(ga, gb, small, enc_in, tg, riding, n_col, n_dp):
@@ -1172,7 +1434,7 @@
     hidden = riding[0].shape[2]
     return pl.pallas_call(
         functools.partial(finish_kernel, n_col=n_col, n_dp=n_dp),
-        in_specs=[IN_VMEM] * 4 + [ANYWHERE] * 8,
+        in_specs=[IN_VMEM] * 5 + [ANYWHERE] * 7,
         out_specs=[IN_VMEM] * 4 + [ANYWHERE],
         out_shape=[
             sd((2, parts, wide, columns), low),
@@ -1220,35 +1482,86 @@
     )(ga, gb, small, enc_in, tg, *riding)
 
 
-def norm_backward(incoming, normed, scaling, gain):
-    gain_grad = jnp.sum(incoming * normed, axis=0)
-    bias_grad = jnp.sum(incoming, axis=0)
-    upstream = incoming * gain
-    mean_up = jnp.mean(upstream, axis=1, keepdims=True)
-    mean_both = jnp.mean(upstream * normed, axis=1, keepdims=True)
-    return scaling * (upstream - mean_up - normed * mean_both), gain_grad, bias_grad
+def column_grads_kernel(*refs, pairs, firsts):
+    count = len(pairs)
+    firsts_refs, others = refs[:firsts], refs[firsts : firsts + count]
+    out, sums = refs[firsts + count :]
+    size = out.shape[2] // count
+    for i, (which, begin) in enumerate(pairs):
+        a, b = firsts_refs[which], others[i]
+        value = mm_tn(a[pl.ds(begin, b.shape[0]), :], b[...]).astype(low)
+        for p in range(out.shape[0]):
+            out[p, :, i * size : (i + 1) * size] = value[:, p * size : (p + 1) * size]
+
+    @pl.when(pl.program_id(0) == 0)
+    def _():
+        for i in range(count):
+            sums[i : i + 1, :] = jnp.sum(others[i][...].astype(f32), axis=0, keepdims=True)
+
+
+def column_grads_of(firsts, pairs, others):
+    deep, width = firsts[0].shape[1], others[0].shape[1]
+    block = 256
+    return pl.pallas_call(
+        functools.partial(column_grads_kernel, pairs=pairs, firsts=len(firsts)),
+        grid=(deep // block,),
+        in_specs=[pl.BlockSpec((x.shape[0], block), lambda i: (0, i)) for x in firsts]
+        + [pl.BlockSpec(x.shape, lambda i: (0, 0)) for x in others],
+        out_specs=[
+            pl.BlockSpec((PARTS, block, width), lambda i: (0, i, 0)),
+            pl.BlockSpec((8, width), lambda i: (0, 0)),
+        ],
+        out_shape=[
+            jax.ShapeDtypeStruct((PARTS, deep, width), low),
+            jax.ShapeDtypeStruct((8, width), f32),
+        ],
+        compiler_params=pltpu.CompilerParams(vmem_limit_bytes=VMEM),
+        name="column_grads",
+    )(*firsts, *others)
+
+
+def unpack_kernel(sums, hidden, *outs):
+    size = sums.shape[3] // 4
+    for g in range(2):
+        for i in range(4):
+            value = sums[g, 0, :, i * size : (i + 1) * size].astype(f32)
+            outs[4 * g + i][...] = value if i < 3 else jnp.transpose(value)
+    outs[8][...] = hidden[0, 0].astype(f32)
+    outs[9][...] = jnp.transpose(hidden[1, 0].astype(f32))
+
+
+def unpack(sums, hidden):
+    _, parts, wide, columns = sums.shape
+    inner = hidden.shape[3]
+    size = columns // 4
+    into = (pl.BlockSpec((wide, size), lambda p: (0, p)), (wide, parts * size))
+    out_of = (pl.BlockSpec((size, wide), lambda p: (p, 0)), (parts * size, wide))
+    layouts = [into, into, into, out_of] * 2 + [
+        (pl.BlockSpec((wide, inner), lambda p: (0, p)), (wide, parts * inner)),
+        (pl.BlockSpec((inner, wide), lambda p: (p, 0)), (parts * inner, wide)),
+    ]
+    return pl.pallas_call(
+        unpack_kernel,
+        grid=(parts,),
+        in_specs=[
+            pl.BlockSpec((2, 1, wide, columns), lambda p: (0, p, 0, 0)),
+            pl.BlockSpec((2, 1, wide, inner), lambda p: (0, p, 0, 0)),
+        ],
+        out_specs=[x[0] for x in layouts],
+        out_shape=[jax.ShapeDtypeStruct(x[1], f32) for x in layouts],
+        compiler_params=pltpu.CompilerParams(vmem_limit_bytes=VMEM),
+        name="unpack",
+    )(sums, hidden)
 
 
 def build_local(mesh):
     n_dp, n_col = mesh.shape["dp"], mesh.shape["col"]
 
-    def swap(x):
-        return lax.ppermute(x, "row", [(0, 1), (1, 0)])
-
     def from_col(x, k):
         return lax.ppermute(x, "col", [(i, (i - k) % n_col) for i in range(n_col)])
 
-    def to_col(x, k):
-        return lax.ppermute(x, "col", [(i, (i + k) % n_col) for i in range(n_col)])
-
     def across(x, bit):
         return lax.ppermute(x, "dp", [(i, i ^ bit) for i in range(n_dp)])
-
-    def plane_gather(x):
-        half = x.shape[0] // 2
-        by_x, by_y = across(x, 1), across(x, 2)
-        far = jnp.concatenate([across(by_x[:half], 2), across(by_y[half:], 1)], axis=0)
-        return [x, by_x, by_y, far]
 
     def local(
         tokens, encoder, cotangent, dec_lengths, src_lengths,
@@ -1265,46 +1578,6 @@
         chunk = tokens.shape[0] // n_col
         span = 2 * chunk
 
-        def by_row(own, other):
-            return jnp.where(
-                row == 0,
-                jnp.concatenate([own, other], axis=0),
-                jnp.concatenate([other, own], axis=0),
-            )
-
-        def row_gather(own):
-            return by_row(own, swap(own))
-
-        def row_scatter(partial):
-            half = partial.shape[0] // 2
-            away = lax.dynamic_slice_in_dim(partial, (1 - row) * half, half, 0)
-            mine = lax.dynamic_slice_in_dim(partial, row * half, half, 0)
-            return mine.astype(f32) + swap(away.astype(low)).astype(f32)
-
-        def spread_rows(x):
-            cut = x.reshape(2, 2, chunk, wide)
-            own = lax.dynamic_index_in_dim(cut, row, 1, keepdims=False)
-            other = swap(lax.dynamic_index_in_dim(cut, 1 - row, 1, keepdims=False))
-            every = by_row(own, other)
-            pieces = []
-            for k in range(n_col):
-                piece = lax.dynamic_index_in_dim(every, (col - k) % n_col, 0, keepdims=False)
-                pieces.append(from_col(piece, k) if k else piece)
-            return jnp.concatenate(pieces, axis=1)
-
-        def collect_rows(x):
-            every = jnp.zeros((n_col, chunk, wide), x.dtype)
-            for k in range(n_col):
-                piece = x[:, k * wide : (k + 1) * wide]
-                piece = to_col(piece, k) if k else piece
-                every = lax.dynamic_update_index_in_dim(every, piece, (col - k) % n_col, 0)
-            own = lax.dynamic_slice_in_dim(every, 2 * row, 2, 0)
-            other = swap(lax.dynamic_slice_in_dim(every, 2 * (1 - row), 2, 0))
-            both = jnp.where(
-                row == 0, jnp.stack([own, other], axis=1), jnp.stack([other, own], axis=1)
-            )
-            return both.reshape(n_col * chunk, wide)
-
         def in_order(parts):
             stacked = jnp.stack(parts)
             return [
@@ -1312,20 +1585,17 @@
                 for i in range(PARTS)
             ]
 
-        def weights_of(arrays):
-            def own(j):
-                cuts = []
-                for w in arrays:
-                    size = w.shape[1] // PARTS
-                    cuts.append(lax.dynamic_slice_in_dim(w, (place ^ j) * size, size, 1))
-                return jnp.concatenate(cuts, axis=1)
-
-            mine = own(0)
-            rest = jnp.concatenate([from_col(mine, k) for k in range(1, n_col)], axis=0)
-            return [
-                jnp.concatenate([own(j), part], axis=0)
-                for j, part in enumerate(plane_gather(rest))
-            ]
+        def own_columns(w, j):
+            size = w.shape[1] // PARTS
+            return lax.dynamic_slice_in_dim(w, (place ^ j) * size, size, 1)
+
+        def along_col(w):
+            return [from_col(own_columns(w, 0), k) for k in range(1, n_col)]
+
+        def whole_weight(w, parts):
+            return jnp.stack(
+                [jnp.concatenate([own_columns(w, j), p], axis=0) for j, p in enumerate(parts)]
+            )
 
         vec_f = jnp.stack([
             self_norm_gain, self_norm_bias, self_out_bias, cross_norm_gain, cross_norm_bias,
@@ -1340,10 +1610,8 @@
             self_query, self_key, self_value, self_out,
             cross_query, cross_key, cross_value, cross_out,
         ]
-        x_ext, enc, vectors, columns, *full = start(
-            tokens, encoder, vec_f, vec_c, weights, n_col
-        )
-        wq1, wk1, wv1, wo1, wq2, wk2, wv2, wo2 = full
+        x_ext, enc, vectors, columns, *full = start(tokens, encoder, vec_f, vec_c, weights, n_col)
+        wq1, wk1, wv1, wo1 = full[:4]
         (gain1, shift1, out_bias1, gain2, shift2, out_bias2, gain3, shift3, out_bias3) = vectors[:9]
         size = self_query_bias.shape[0]
 
@@ -1359,12 +1627,9 @@
             [lax.dynamic_index_in_dim(hidden_bias, place ^ j, 0) for j in range(PARTS)]
         )
 
-        hidden_in, hidden_out, cotangent, x_ext = lax.optimization_barrier(
-            (hidden_in, hidden_out, cotangent, x_ext)
-        )
-        w1 = jnp.stack(weights_of([hidden_in]))
-        w2 = jnp.stack(weights_of([hidden_out.T]))
-        step = self_query.shape[1] // PARTS
+        hidden_in, x_ext = lax.optimization_barrier((hidden_in, x_ext))
+        hidden_out_t = hidden_out.T
+        pieces1 = along_col(hidden_in)
 
         dec_ids = doc_numbers(dec_lengths, SEQ_LEN)[0]
         src_ids = doc_numbers(src_lengths, ENC)[0]
@@ -1376,32 +1641,53 @@
         x0 = x_ext[1]
         a_ext = enter(x_ext, gain1, shift1, 2).reshape(WIN + span, -1)
         a = a_ext[WIN:]
+        hidden_out_t, a_ext = lax.optimization_barrier((hidden_out_t, a_ext))
+        pieces2 = along_col(hidden_out_t)
         q1 = (mm(a, wq1) + q_bias1).astype(low) * scale
         k1 = mm(a_ext, wk1).astype(low)
         v1 = (mm(a_ext, wv1) + v_bias1).astype(low)
-        o1, lse1 = attend(q1, k1, v1, query_ids, key_ids, True)
+        dma = pltpu.SemaphoreType.DMA
+        o1, lse1, wq2, wk2, wv2, wo2 = attend(
+            q1, k1, v1, query_ids, key_ids, True,
+            functools.partial(cross_rider, n_col=n_col),
+            weights[4:] + full[4:],
+            [(x.shape, low) for x in full[:4]],
+            [dma((4, 4)), dma((4, 4)), dma((4, 2))],
+            14,
+        )
+        pieces1, o1 = lax.optimization_barrier((pieces1, o1))
+        rest1 = jnp.concatenate(pieces1, axis=0)
+        near1 = [across(rest1, 1), across(rest1, 2)]
+        pieces2, o1 = lax.optimization_barrier((pieces2, o1))
+        rest2 = jnp.concatenate(pieces2, axis=0)
+        near2 = [across(rest2, 1), across(rest2, 2)]
         x1, c = junction("forward", [("nn", o1, wo1)], [x0, out_bias1, gain2, shift2], 3)
 
+        near1, c = lax.optimization_barrier((near1, c))
+        half = rest1.shape[0] // 2
+        far1 = [across(near1[0][:half], 2), across(near1[1][half:], 1)]
         q2 = (mm(c, wq2) + q_bias2).astype(low) * scale
         k2 = mm(enc, wk2).astype(low)
         v2 = (mm(enc, wv2) + v_bias2).astype(low)
         o2, lse2 = attend(q2, k2, v2, query_ids, src_ids, False)
+        near2, o2 = lax.optimization_barrier((near2, o2))
+        far2 = [across(near2[0][:half], 2), across(near2[1][half:], 1)]
         x2, f = junction("forward", [("nn", o2, wo2)], [x1, out_bias2, gain3, shift3], 4)
-
-        act, slope, branch = hidden_forward(f, w1, hidden_bias, w2)
-        layer_out = collect_rows(
-            (x2 + (junction("sum", [("sum", branch)], [], 5) + out_bias3)).astype(low)
+        w1 = whole_weight(hidden_in, [rest1, *near1, jnp.concatenate(far1)])
+        w2 = whole_weight(hidden_out_t, [rest2, *near2, jnp.concatenate(far2)])
+
+        act, slope, rows_out, dz = hidden_forward(
+            f, w1, hidden_bias, w2, x2, out_bias3, cotangent, n_col, 5
         )
-
-        dz_own = spread_rows(cotangent)
-        dz = row_gather(dz_own)
-        g1, g2, hidden_bias_grad, df, got_a, got_b = hidden_backward(
-            dz, f, w1, w2, act, slope, 11
+        dz = dz.reshape(span, -1)
+
+        g1, g2, hidden_bias_grad, df, got_a, got_b, layer_out = hidden_backward(
+            dz, f, w1, w2, act, slope, rows_out, n_col, 11
         )
         inner = g1.shape[2]
         half = g1.shape[1] // 2
-        dma, one = pltpu.SemaphoreType.DMA, ((half, inner), low)
-        dx2, dyc, stats3 = junction("backward", [("sum", df)], [dz_own, x2, gain3], 6)
+        one = ((half, inner), low)
+        dx2, dyc, stats3 = junction("backward", [("sum", df)], [dz, x2, gain3], 6)
 
         doc = mm_nt(dyc, wo2).astype(low)
         dq2, dk2, dv2, back_a, back_b, far_a, far_b = attend_back(
@@ -1413,31 +1699,16 @@
             ],
             12,
         )
-        grads = [
-            mm_tn(c, dq2).astype(low),
-            mm_tn(enc, dk2).astype(low),
-            mm_tn(enc, dv2).astype(low),
-            mm_tn(dyc, o2).astype(low),
-        ]
-
-        def by_part(arrays):
-            return [
-                jnp.concatenate(
-                    [
-                        lax.dynamic_slice_in_dim(g, (place ^ j) * step, step, 1)
-                        for g in arrays
-                    ],
-                    axis=1,
-                )
-                for j in range(PARTS)
-            ]
-
-        cross_grads = jnp.stack(by_part(grads))
+        cross_grads, cross_columns = column_grads_of(
+            [c, enc, dyc], [(0, 0), (1, 0), (1, 0), (2, 0)], [dq2, dk2, dv2, o2]
+        )
         enc_back = junction("sum", [("nt", dk2, wk2), ("nt", dv2, wv2)], [], 7)
         dx1, dy, stats2 = junction("backward", [("nt", dq2, wq2)], [dx2, x1, gain2], 8)
 
         do = mm_nt(dy, wo1).astype(low)
-        dq1, dk1, dv1, near_a, near_b, far_back_a, far_back_b, z_got, own1 = attend_back(
+        (
+            dq1, dk1, dv1, near_a, near_b, far_back_a, far_back_b, z_got, own1
+        ) = attend_back(
             q1, k1, v1, do, o1, lse1, query_ids, key_ids, True,
             functools.partial(second_rider, n_col=n_col),
             [g1, g2, got_a, got_b, back_a, back_b, far_a, far_b],
@@ -1451,36 +1722,27 @@
             13,
         )
         da_before = junction("sum", [("nt", dk1[:WIN], wk1), ("nt", dv1[:WIN], wv1)], [], 9)
-        da_after = lax.ppermute(
-            da_before.astype(low), "col", [(i + 1, i) for i in range(n_col - 1)]
+        da_after = lax.ppermute(da_before, "col", [(i + 1, i) for i in range(n_col - 1)])
+        self_grads, self_columns = column_grads_of(
+            [a_ext, dy], [(0, WIN), (0, 0), (0, 0), (1, 0)], [dq1, dk1, dv1, o1]
         )
-        da_after = jnp.concatenate([da_after[:, -wide:], da_after[:, :-wide]], axis=1)
-        da = junction(
-            "sum", [("nt", dq1, wq1), ("nt", dk1[WIN:], wk1), ("nt", dv1[WIN:], wv1)], [], 10
-        ) + da_after.astype(f32)
-        grads = [
-            mm_tn(a, dq1).astype(low),
-            mm_tn(a_ext, dk1).astype(low),
-            mm_tn(a_ext, dv1).astype(low),
-            mm_tn(dy, o1).astype(low),
-        ]
-        self_grads = jnp.stack(by_part(grads))
-        normed1, scaling1 = norm_rows(x0.astype(f32))
-        back1, gain_grad1, shift_grad1 = norm_backward(da, normed1, scaling1, gain1)
-        def total(x):
-            return jnp.sum(x, axis=0, dtype=f32)
+        x0_grad, stats1 = junction(
+            "last",
+            [("nt", dq1, wq1), ("nt", dk1[WIN:], wk1), ("nt", dv1[WIN:], wv1)],
+            [dx1, x0, gain1, da_after],
+            10,
+        )
 
         feature_grads = jnp.concatenate([
-            jnp.stack([gain_grad1, shift_grad1]), stats2[2:3], stats2[:2], stats3[2:3], stats3[:2],
-            total(dz_own)[None],
+            stats1[:2], stats2[2:3], stats2[:2], stats3[2:3], stats3[:2], stats3[3:4],
         ])
         feature_grads = jnp.moveaxis(feature_grads.reshape(-1, n_col, wide), 1, 0)
         column_grads = []
-        for vector in (total(dq1), total(dv1), total(dq2), total(dv2), hidden_bias_grad):
-            parts = vector.reshape(PARTS, -1)
-            if vector is hidden_bias_grad:
-                parts = jnp.stack(in_order([parts[j] for j in range(PARTS)]))
-            column_grads.append(parts.reshape(n_col, -1))
+        for vector in (self_columns[0], self_columns[2], cross_columns[0], cross_columns[2]):
+            column_grads.append(vector.reshape(n_col, -1))
+        column_grads.append(
+            jnp.stack(in_order([hidden_bias_grad[j] for j in range(PARTS)])).reshape(n_col, -1)
+        )
         column_grads = jnp.concatenate(column_grads, axis=1).reshape(n_col, -1, 128)
         column_grads = lax.dynamic_slice_in_dim(
             jnp.concatenate([column_grads, column_grads]), col, n_col, 0
@@ -1494,21 +1756,14 @@
             axis=2,
         )
         sums, hidden_sums, small, encoder_grad, tokens_grad = finish(
-            cross_grads, self_grads, small, enc_back.astype(low), (dx1 + back1).astype(low),
+            cross_grads, self_grads, small, enc_back, x0_grad,
             [g2, near_a, near_b, far_back_a, far_back_b, z_got, own1],
             n_col, n_dp,
         )
-        g1_parts, g2_parts = [[hidden_sums[i, j] for j in range(PARTS)] for i in range(2)]
+        grads = unpack(sums, hidden_sums)
         tokens_grad = tokens_grad.astype(f32)
-        cross_grads = [sums[0, i] for i in range(PARTS)]
-        self_grads = [sums[1, i] for i in range(PARTS)]
         feature_grads = small[:, :wide]
         column_grads = small[:, wide:].reshape(-1)
-
-        def whole(parts, index=None):
-            if index is not None:
-                parts = [p[:, index * step : (index + 1) * step] for p in parts]
-            return jnp.concatenate(parts, axis=1).astype(f32)
 
         return (
             layer_out,
@@ -1516,27 +1771,27 @@
             encoder_grad,
             feature_grads[0],
             feature_grads[1],
-            whole(self_grads, 0),
-            whole(self_grads, 1),
-            whole(self_grads, 2),
+            grads[4],
+            grads[5],
+            grads[6],
             column_grads[:size],
             column_grads[size : 2 * size],
-            whole(self_grads, 3).T,
+            grads[7],
             feature_grads[2],
             feature_grads[3],
             feature_grads[4],
-            whole(cross_grads, 0),
-            whole(cross_grads, 1),
-            whole(cross_grads, 2),
+            grads[0],
+            grads[1],
+            grads[2],
             column_grads[2 * size : 3 * size],
             column_grads[3 * size : 4 * size],
-            whole(cross_grads, 3).T,
+            grads[3],
             feature_grads[5],
             feature_grads[6],
             feature_grads[7],
-            whole(g1_parts),
+            grads[8],
             column_grads[4 * size : 4 * size + hidden_in_bias.shape[0]],
-            whole(g2_parts).T,
+            grads[9],
             feature_grads[8],
         )
 

time: 943 us -> 793 us (0.84)
  other arithmetic: 73.4 us -> 24.7 us
  starting transfers between devices: 55.8 us -> 32.8 us
  Pallas kernels: 643 us -> 621 us
  local copies, waits for them, and re-layouts: 79.7 us -> 59.6 us
  waiting for transfers between devices: 32.1 us -> 13.4 us
  matrix products: 47.8 us -> 30.9 us
    pallas_call x1, Pallas kernels: 184 us -> 156 us  [finish(): pl.pallas_call(functools.partial(finish_kernel, n_col=n_col, n_dp=n_dp),...]
    dot_general x8 -> x0, matrix products: 23.4 us -> none  [mm_tn(): lax.dot_general(a, b, (((0,), (0,)), ((), ())), preferred_element_type=f32)]
    ppermute x9 -> x6, waiting for transfers between devices: 26.3 us -> 6.82 us  [from_col(): return lax.ppermute(x, 'col', [(i, (i - k) % n_col) for i in range(n_col)])]
    convert_element_type x11 -> x0, other arithmetic: 18.9 us -> none  [the longest x7 7.47 us: whole(): return jnp.concatenate(parts, axis=1).astype(f32)]
    ppermute x9 -> x6, starting transfers between devices: 38.8 us -> 21.8 us  [from_col(): return lax.ppermute(x, 'col', [(i, (i - k) % n_col) for i in range(n_col)])]
    select_n x3 -> x0, other arithmetic: 15.6 us -> none  [the longest x2 14.4 us: by_row(): jnp.where(row == 0, jnp.concatenate([own, other], axis=0), jnp.concatenat...]
    pallas_call x2, Pallas kernels: 49.2 us -> 59.6 us  [attend(): pl.pallas_call(functools.partial(attend_kernel, span=span, windowed=windo...]
    unnamed x163 -> x78, local copies, waits for them, and re-layouts: 23.1 us -> 14.6 us
  transfers between devices with their start and end apart: 24 -> 15, of which waited for: 5 -> 5; matrix products, arithmetic and copies ran while one was open for 12% -> 9% of each run, Pallas kernels for 11% -> 15%
where the time goes in v4:
time: 793 us; the launch traced here: 784 us
  Pallas kernels  621 us (78%)
  local copies, waits for them, and re-layouts  59.6 us (8%)
  starting transfers between devices  32.8 us (4%)
  matrix products  30.9 us (4%)
  other arithmetic  24.7 us (3%)
  waiting for transfers between devices  13.4 us (2%)
    pallas_call x1, Pallas kernels, finish(): pl.pallas_call(functools.partial(finish_kernel, n_col=n_col, n_dp=n_dp),...  156 us
    pallas_call x2, Pallas kernels, attend_back(): pl.pallas_call(functools.partial(attend_back_kernel, span=span, windowed=...  111 us
    pallas_call x1, Pallas kernels, start(): pl.pallas_call(functools.partial(start_kernel, n_col=n_col), in_specs=[IN...  77.5 us
    pallas_call x7, Pallas kernels, junction(): pl.pallas_call(functools.partial(junction_kernel, kinds=kinds, mode=mode)...  66.1 us
    pallas_call x1, Pallas kernels, hidden_backward(): pl.pallas_call(functools.partial(hidden_back_kernel, n_col=n_col), grid=g...  65.4 us
    pallas_call x2, Pallas kernels, attend(): pl.pallas_call(functools.partial(attend_kernel, span=span, windowed=windo...  59.6 us
    pallas_call x1, Pallas kernels, hidden_forward(): pl.pallas_call(functools.partial(hidden_kernel, n_col=n_col), grid=grid,...  44.9 us
    dot_general x6, matrix products, mm(): lax.dot_general(a, b, (((1,), (0,)), ((), ())), preferred_element_type=f32)  23.2 us
  transfers between devices with their start and end apart: 15, of which 5 were waited for; matrix products, arithmetic and copies ran while one was open for 9% of the time, Pallas kernels for 15%

profile of v4, /device:TPU:8, one launch (start us, length us, event | category | flops | bytes accessed | tf_op | source)
XLA Modules:
  0.0 783.9 jit_solution(8377499597230573817)
XLA Ops:
  6.9 77.5 %start.1 = (bf16[2,512,1024]{2,1,0:T(8,128)(2,1)}, bf16[1024,1024]{1,0:T(8,128)(2,1)}, f32[16,1024]{1,0:T(8,128)}, f32[4,16,128]{2,1,0:T(8,128)}, bf16[1024,512]...) custom-call(bf16[2048,256]{1,0:T(8,128)(2,1)} %tokens.1, ...), custom_call_target="tpu_custom_call" | custom-call | tf_op jit(solution)/shard_map/start/pallas_call | solution.py:1012
  85.9 5.8 collective-permute-start.3
  91.7 8.8 %collective-permute-start.4 = (bf16[256,1024]{1,0:T(8,128)(2,1)}, bf16[256,1024]{1,0:T(8,128)(2,1)}, u32[]{:S(2)}, u32[]{:S(2)}) collective-permute-start(bf16[256,1024]{1,0:T(8,128)(2,1)} %get-tuple-element.230), channel_id=1, source_target_pairs={{0,2},{1,3},{2,0},{3,1},{4,6},{5,7},{6,4},{7,5},{8,10},{9,11},{10,... | collective-permute-start | bytes 1572872 | tf_op jit(solution)/shard_map/ppermute | solution.py:1561
  100.5 2.9 collective-permute-start.5
  104.0 2.9 copy.67
  106.9 10.0 %enter.1 = bf16[2,1024,1024]{2,1,0:T(8,128)(2,1)} custom-call(bf16[2,512,1024]{2,1,0:T(8,128)(2,1)} %get-tuple-element.124.x_ref, f32[1,1024]{1,0:T(1,128)} %get-tuple-element.239.gain.refs_8_, f32[1,1024]{1,0:T(1,128)} %get-tuple-element.238.shift), custom_call_target="tpu_custom_call" | custom-call | tf_op jit(solution)/shard_map/enter/pallas_call | solution.py:1066
  120.3 6.0 convolution_convert_fusion.refs_1_
  126.3 3.7 add_convert_fusion.refs_2_
  130.8 3.8 fusion.5.refs_0_
  134.6 2.6 collective-permute-start.2
  138.4 37.7 %attend.2 = (bf16[1024,512]{1,0:T(8,128)(2,1)}, f32[4,8,1024]{2,1,0:T(8,128)}, bf16[1024,512]{1,0:T(8,128)(2,1)}, bf16[1024,512]{1,0:T(8,128)(2,1)}, bf16[1024,5...) custom-call(bf16[1024,512]{1,0:T(8,128)(2,1)} %fusion.5.refs_0_, bf16[2048,512]{1,0:T(8,128)(2,1)} %convolution_convert_fusion.refs_1_, ...), custom_call_target="tpu_custom_call" | custom-call | tf_op jit(solution)/shard_map/attend/pallas_call | solution.py:196
  183.9 6.8 collective-permute-done.2
  201.5 3.6 convolution_convert_fusion.3.refs_1_
  205.0 2.3 add_convert_fusion.1.refs_2_
  207.3 9.9 %junction_forward.2 = (f32[512,1024]{1,0:T(8,128)}, bf16[1024,1024]{1,0:T(8,128)(2,1)}) custom-call(bf16[1024,512]{1,0:T(8,128)(2,1)} %get-tuple-element.145.refs_0_.refs_4_.refs_5_, bf16[512,1024]{1,0:T(8,128)(2,1)} %get-tuple-element.146.refs_1_, bf16[512,1024]{1,0:T(8,128)(2,1)} %slice_bitcast_fusion.refs_2_.refs_7_, ...), custom_call_target="tpu_custom_call" | custom-call | tf_op jit(solution)/shard_map/junction_forward/pallas_call | solution.py:1189
  217.2 2.3 collective-permute-done.8
  220.1 3.8 fusion.8.refs_0_
  223.9 21.9 %attend.3 = (bf16[1024,512]{1,0:T(8,128)(2,1)}, f32[4,8,1024]{2,1,0:T(8,128)}) custom-call(bf16[1024,512]{1,0:T(8,128)(2,1)} %fusion.8.refs_0_, bf16[1024,512]{1,0:T(8,128)(2,1)} %convolution_convert_fusion.3.refs_1_, bf16[1024,512]{1,0:T(8,128)(2,1)} %add_convert_fusion.1.refs_2_, s32[1024,1]{1,0:T(8,128)} %copy.68.refs_3_, s32[1,1024]{1,0:T(1,128)} %bitcast.129), custom_call_target="tpu_custom_call" | custom-call | tf_op jit(solution)/shard_map/attend/pallas_call | solution.py:196
  245.8 3.5 collective-permute-done.6
  249.5 2.1 slice.180
  253.1 2.1 slice.181
  255.7 2.7 maximum_bitcast_fusion.4
  260.1 2.1 slice.177
  263.7 2.1 slice.178
  266.3 9.7 %junction_forward.3 = (f32[512,1024]{1,0:T(8,128)}, bf16[1024,1024]{1,0:T(8,128)(2,1)}) custom-call(bf16[1024,512]{1,0:T(8,128)(2,1)} %get-tuple-element.154.refs_0_.refs_4_.refs_6_, bf16[512,1024]{1,0:T(8,128)(2,1)} %get-tuple-element.155.refs_1_, f32[512,1024]{1,0:T(8,128)} %get-tuple-element.156.refs_2_.refs_3_, f32[1,1024]{1,0:T(1,128)} %get-tuple-element.234.refs_3_, ...), custom_call_target="tpu_custom_call" | custom-call | tf_op jit(solution)/shard_map/junction_forward/pallas_call | solution.py:1189
  276.1 4.0 copy.70
  280.1 2.4 maximum_bitcast_fusion.5
  282.6 2.4 maximum_bitcast_fusion.1
  287.1 3.9 pad_maximum_fusion.1.w2_ref
  292.6 3.9 pad_maximum_fusion.w1_ref
  296.4 44.9 %hidden_forward.1 = (bf16[4,1024,1024]{2,1,0:T(8,128)(2,1)}, bf16[4,1024,1024]{2,1,0:T(8,128)(2,1)}, bf16[512,1024]{1,0:T(8,128)(2,1)}, bf16[2,512,1024]{2,1,0:T(8,128)(2,1)}) custom-call(bf16[1024,1024]{1,0:T(8,128)(2,1)} %get-tuple-element.157.f_ref, bf16[4,1024,1024]{2,1,0:T(8,128)(2,1)} %pad_maximum_fusion.w1_ref, ...), custom_call_target="tpu_custom_call" | custom-call | tf_op jit(solution)/shard_map/hidden_forward/pallas_call | solution.py:605
  341.3 3.9 copy.71.dzt_ref
  345.3 65.4 %hidden_backward.1 = (bf16[4,1024,1024]{2,1,0:T(8,128)(2,1)}, bf16[4,1024,1024]{2,1,0:T(8,128)(2,1)}, f32[4,1,1024]{2,1,0:T(1,128)}, bf16[1024,1024]{1,0:T(8,128...) custom-call(bf16[1024,1024]{1,0:T(8,128)(2,1)} %bitcast.113, ...), custom_call_target="tpu_custom_call" | custom-call | tf_op jit(solution)/shard_map/hidden_backward/pallas_call | solution.py:728
  410.7 10.7 %junction_backward.2 = (f32[512,1024]{1,0:T(8,128)}, bf16[1024,1024]{1,0:T(8,128)(2,1)}, f32[8,1024]{1,0:T(8,128)}) custom-call(bf16[1024,1024]{1,0:T(8,128)(2,1)} %get-tuple-element.168.refs_0_, bf16[1024,1024]{1,0:T(8,128)(2,1)} %bitcast.114, f32[512,1024]{1,0:T(8,128)} %get-tuple-element.162.x_ref.refs_2_, f32[1,1024]{1,0:T(1,128)} %get-tuple-element.233.refs_4_.refs_3_), custom_call_target="tpu_custom_call" | custom-call | tf_op jit(solution)/shard_map/junction_backward/pallas_call | solution.py:1189
  421.5 3.8 convolution_convert_fusion.2.refs_3_
  425.3 51.8 %attend_back.2 = (bf16[1024,512]{1,0:T(8,128)(2,1)}, bf16[1024,512]{1,0:T(8,128)(2,1)}, bf16[1024,512]{1,0:T(8,128)(2,1)}, bf16[512,1024]{1,0:T(8,128)(2,1)}, bf...) custom-call(bf16[1024,512]{1,0:T(8,128)(2,1)} %fusion.8.refs_0_, ...), custom_call_target="tpu_custom_call" | custom-call | tf_op jit(solution)/shard_map/attend_back/pallas_call | solution.py:362
  477.1 11.2 %junction_backward.3 = (f32[512,1024]{1,0:T(8,128)}, bf16[1024,1024]{1,0:T(8,128)(2,1)}, f32[8,1024]{1,0:T(8,128)}) custom-call(bf16[1024,512]{1,0:T(8,128)(2,1)} %get-tuple-element.175.refs_3_.refs_0_, bf16[1024,512]{1,0:T(8,128)(2,1)} %get-tuple-element.149.refs_1_, f32[512,1024]{1,0:T(8,128)} %get-tuple-element.179.refs_2_, ...), custom_call_target="tpu_custom_call" | custom-call | tf_op jit(solution)/shard_map/junction_backward/pallas_call | solution.py:1189
  488.3 3.8 convolution_convert_fusion.1.refs_3_
  492.2 58.8 %attend_back.3 = (bf16[1024,512]{1,0:T(8,128)(2,1)}, bf16[2048,512]{1,0:T(8,128)(2,1)}, bf16[2048,512]{1,0:T(8,128)(2,1)}, bf16[512,1024]{1,0:T(8,128)(2,1)}, bf...) custom-call(bf16[1024,512]{1,0:T(8,128)(2,1)} %fusion.5.refs_0_, ...), custom_call_target="tpu_custom_call" | custom-call | tf_op jit(solution)/shard_map/attend_back/pallas_call | solution.py:362
  550.9 3.2 fusion.14
  555.6 6.8 junction_sum.2
  564.3 12.8 %column_grads.3 = (bf16[4,1024,512]{2,1,0:T(8,128)(2,1)}, f32[8,512]{1,0:T(8,128)}) custom-call(bf16[2048,1024]{1,0:T(8,128)(2,1)} %bitcast.116, bf16[1024,1024]{1,0:T(8,128)(2,1)} %get-tuple-element.180.refs_1_, bf16[1024,512]{1,0:T(8,128)(2,1)} %get-tuple-element.186.refs_2_.refs_0_, bf16[2048,512]{1,0:T(8,128)(2,1)} %get-tuple-element.187.refs_3_, ...), custom_call_target="tpu_custom_call" | custom-call | tf_op jit(solution)/shard_map/column_grads/pallas_call | solution.py:1505
  577.9 10.4 %column_grads.2 = (bf16[4,1024,512]{2,1,0:T(8,128)(2,1)}, f32[8,512]{1,0:T(8,128)}) custom-call(bf16[1024,1024]{1,0:T(8,128)(2,1)} %get-tuple-element.148.refs_0_, bf16[1024,1024]{1,0:T(8,128)(2,1)} %get-tuple-element.150.refs_1_, bf16[1024,1024]{1,0:T(8,128)(2,1)} %get-tuple-element.169.refs_2_, bf16[1024,512]{1,0:T(8,128)(2,1)} %get-tuple-element.175.refs_3_.refs_0_, ...), custom_call_target="tpu_custom_call" | custom-call | tf_op jit(solution)/shard_map/column_grads/pallas_call | solution.py:1505
  589.1 6.8 junction_sum.3.enc_in
  598.6 10.9 %junction_last.1 = (bf16[512,1024]{1,0:T(8,128)(2,1)}, f32[8,1024]{1,0:T(8,128)}) custom-call(bf16[1024,512]{1,0:T(8,128)(2,1)} %get-tuple-element.186.refs_2_.refs_0_, bf16[1024,512]{1,0:T(8,128)(2,1)} %get-tuple-element.128.refs_1_, bf16[1024,512]{1,0:T(8,128)(2,1)} %get-tuple-element.222.refs_2_, bf16[1024,512]{1,0:T(8,128)(2,1)} %get-tuple-element.131.refs_1_.refs_3_, ...), custom_call_target="tpu_custom_call" | custom-call | tf_op jit(solution)/shard_map/junction_last/pallas_call | solution.py:1189
  611.1 155.5 %finish.1 = (bf16[2,4,256,512]{3,2,1,0:T(8,128)(2,1)}, bf16[2,4,256,1024]{3,2,1,0:T(8,128)(2,1)}, f32[16,384]{1,0:T(8,128)}, f32[512,256]{1,0:T(8,128)}, bf16[2048,256]{1,0:T(8,128)(2,1)}) custom-call(bf16[4,1024,512]{2,1,0:T(8,128)(2,1)} %get-tuple-element.178.ga, bf16[4,1024,512]{2,1,0:T(8,128)(2,1)} %get-tuple-element.189.gb, ...), custom_call_target="tpu_custom_call" | custom-call | tf_op jit(solution)/shard_map/finish/pallas_call | solution.py:1435
  770.8 2.7 convert_element_type.67
  773.6 7.8 unpack.1
  (147 shorter events, 57.6 us)
Async XLA Ops:
  0.7 83.8 %copy-start.7 = (bf16[256,4096]{1,0:T(8,128)(2,1)S(1)}, bf16[256,4096]{1,0:T(8,128)(2,1)}, u32[]{:S(2)}) copy-start(bf16[256,4096]{1,0:T(8,128)(2,1)} %param.54) | copy-start | bytes 6291460
  84.5 18.9 %copy-start.26 = (f32[16,1024]{1,0:T(8,128)S(1)}, f32[16,1024]{1,0:T(8,128)}, u32[]{:S(2)}) copy-start(f32[16,1024]{1,0:T(8,128)} %get-tuple-element.125) | copy-start | bytes 196612
  85.9 48.8 %collective-permute-start.3 = (bf16[256,1024]{1,0:T(8,128)(2,1)}, bf16[256,1024]{1,0:T(8,128)(2,1)}, u32[]{:S(2)}, u32[]{:S(2)}) collective-permute-start(bf16[256,1024]{1,0:T(8,128)(2,1)} %get-tuple-element.230), channel_id=1, source_target_pairs={{0,3},{1,0},{2,1},{3,2},{4,7},{5,4},{6,5},{7,6},{8,11},{9,8},{10,9... | collective-permute-start | bytes 1572872 | tf_op jit(solution)/shard_map/ppermute | solution.py:1561
  91.7 84.6 %collective-permute-start.4 = (bf16[256,1024]{1,0:T(8,128)(2,1)}, bf16[256,1024]{1,0:T(8,128)(2,1)}, u32[]{:S(2)}, u32[]{:S(2)}) collective-permute-start(bf16[256,1024]{1,0:T(8,128)(2,1)} %get-tuple-element.230), channel_id=1, source_target_pairs={{0,2},{1,3},{2,0},{3,1},{4,6},{5,7},{6,4},{7,5},{8,10},{9,11},{10,... | collective-permute-start | bytes 1572872 | tf_op jit(solution)/shard_map/ppermute | solution.py:1561
  100.5 75.8 %collective-permute-start.5 = (bf16[256,1024]{1,0:T(8,128)(2,1)}, bf16[256,1024]{1,0:T(8,128)(2,1)}, u32[]{:S(2)}, u32[]{:S(2)}) collective-permute-start(bf16[256,1024]{1,0:T(8,128)(2,1)} %get-tuple-element.230), channel_id=1, source_target_pairs={{0,1},{1,2},{2,3},{3,0},{4,5},{5,6},{6,7},{7,4},{8,9},{9,10},{10,1... | collective-permute-start | bytes 1572872 | tf_op jit(solution)/shard_map/ppermute | solution.py:1561
  116.9 3.2 copy-start.25
  117.0 3.2 copy-start.29
  117.0 3.4 copy-start.4
  118.3 65.5 %collective-permute-start = (bf16[256,1024]{1,0:T(8,128)(2,1)}, bf16[256,1024]{1,0:T(8,128)(2,1)S(1)}, u32[]{:S(2)}, u32[]{:S(2)}) collective-permute-start(bf16[256,1024]{1,0:T(8,128)(2,1)} %get-tuple-element.226), channel_id=1, source_target_pairs={{0,3},{1,0},{2,1},{3,2},{4,7},{5,4},{6,5},{7,6},{8,11},{9,8},{10,9... | collective-permute-start | bytes 1572872 | tf_op jit(solution)/shard_map/ppermute | solution.py:1561
  118.4 65.5 %collective-permute-start.1 = (bf16[256,1024]{1,0:T(8,128)(2,1)}, bf16[256,1024]{1,0:T(8,128)(2,1)S(1)}, u32[]{:S(2)}, u32[]{:S(2)}) collective-permute-start(bf16[256,1024]{1,0:T(8,128)(2,1)} %get-tuple-element.226), channel_id=1, source_target_pairs={{0,2},{1,3},{2,0},{3,1},{4,6},{5,7},{6,4},{7,5},{8,10},{9,11},{10,... | collective-permute-start | bytes 1572872 | tf_op jit(solution)/shard_map/ppermute | solution.py:1561
  120.3 6.0 copy-start
  120.3 6.0 copy-start.5
  126.3 4.5 copy-start.14
  130.8 7.4 copy-start.30
  134.6 56.1 %collective-permute-start.2 = (bf16[256,1024]{1,0:T(8,128)(2,1)}, bf16[256,1024]{1,0:T(8,128)(2,1)}, u32[]{:S(2)}, u32[]{:S(2)}) collective-permute-start(bf16[256,1024]{1,0:T(8,128)(2,1)} %get-tuple-element.226), channel_id=1, source_target_pairs={{0,1},{1,2},{2,3},{3,0},{4,5},{5,6},{6,7},{7,4},{8,9},{9,10},{10,1... | collective-permute-start | bytes 1572872 | tf_op jit(solution)/shard_map/ppermute | solution.py:1561
  137.2 38.9 %copy-start.23 = (s32[1024]{0:T(1024)}, s32[1024]{0:T(1024)S(1)}, u32[]{:S(2)}) copy-start(s32[1024]{0:T(1024)S(1)} %pad_dynamic-slice_fusion.2) | copy-start | bytes 12292
  176.2 21.1 %copy-start.24 = (s32[1024]{0:T(1024)}, s32[1024]{0:T(1024)S(1)}, u32[]{:S(2)}) copy-start(s32[1024]{0:T(1024)S(1)} %convert_reduce_fusion.1) | copy-start | bytes 12292
  181.9 16.5 %copy-start.22 = (s32[2048]{0:T(1024)S(1)}, s32[2048]{0:T(1024)}, u32[]{:S(2)}) copy-start(s32[2048]{0:T(1024)} %pad_dynamic-slice_fusion.3) | copy-start | bytes 24580
  181.9 37.6 %collective-permute-start.8 = (bf16[768,1024]{1,0:T(8,128)(2,1)}, bf16[768,1024]{1,0:T(8,128)(2,1)}, u32[]{:S(2)}, u32[]{:S(2)}) collective-permute-start(bf16[768,1024]{1,0:T(8,128)(2,1)} %constant_dynamic-update-slice_fusion.4), channel_id=1, source_target_pairs={{0,8},{8,0},{16,24},{24,16},{1,9},{9,1},{17,25},{25,17},{2,10},{10... | collective-permute-start | bytes 4718600 | tf_op jit(solution)/shard_map/ppermute | solution.py:1564
  182.4 37.7 %collective-permute-start.9 = (bf16[768,1024]{1,0:T(8,128)(2,1)}, bf16[768,1024]{1,0:T(8,128)(2,1)}, u32[]{:S(2)}, u32[]{:S(2)}) collective-permute-start(bf16[768,1024]{1,0:T(8,128)(2,1)} %constant_dynamic-update-slice_fusion.4), channel_id=1, source_target_pairs={{0,16},{8,24},{16,0},{24,8},{1,17},{9,25},{17,1},{25,9},{2,18},{10... | collective-permute-start | bytes 4718600 | tf_op jit(solution)/shard_map/ppermute | solution.py:1564
  191.5 8.8 %copy-start.3 = (bf16[2,512,1024]{2,1,0:T(8,128)(2,1)S(1)}, bf16[2,512,1024]{2,1,0:T(8,128)(2,1)}, u32[]{:S(2)}) copy-start(bf16[2,512,1024]{2,1,0:T(8,128)(2,1)} %get-tuple-element.124.x_ref) | copy-start | bytes 6291460
  194.2 55.0 %collective-permute-start.6 = (bf16[768,1024]{1,0:T(8,128)(2,1)}, bf16[768,1024]{1,0:T(8,128)(2,1)}, u32[]{:S(2)}, u32[]{:S(2)}) collective-permute-start(bf16[768,1024]{1,0:T(8,128)(2,1)} %constant_dynamic-update-slice_fusion.1), channel_id=1, source_target_pairs={{0,8},{8,0},{16,24},{24,16},{1,9},{9,1},{17,25},{25,17},{2,10},{10... | collective-permute-start | bytes 4718600 | tf_op jit(solution)/shard_map/ppermute | solution.py:1564
  195.7 53.8 %collective-permute-start.7 = (bf16[768,1024]{1,0:T(8,128)(2,1)}, bf16[768,1024]{1,0:T(8,128)(2,1)}, u32[]{:S(2)}, u32[]{:S(2)}) collective-permute-start(bf16[768,1024]{1,0:T(8,128)(2,1)} %constant_dynamic-update-slice_fusion.1), channel_id=1, source_target_pairs={{0,16},{8,24},{16,0},{24,8},{1,17},{9,25},{17,1},{25,9},{2,18},{10... | collective-permute-start | bytes 4718600 | tf_op jit(solution)/shard_map/ppermute | solution.py:1564
  199.7 1.7 copy-start.6
  201.5 3.6 copy-start.15
  207.3 12.8 %copy-start.20 = (bf16[1024,512]{1,0:T(8,128)(2,1)S(1)}, bf16[1024,512]{1,0:T(8,128)(2,1)}, u32[]{:S(2)}) copy-start(bf16[1024,512]{1,0:T(8,128)(2,1)} %get-tuple-element.149.refs_1_) | copy-start | bytes 3145732
  251.6 33.4 %collective-permute-start.12 = (bf16[384,1024]{1,0:T(8,128)(2,1)}, bf16[384,1024]{1,0:T(8,128)(2,1)}, u32[]{:S(2)}, u32[]{:S(2)}) collective-permute-start(bf16[384,1024]{1,0:T(8,128)(2,1)} %slice.180), channel_id=1, source_target_pairs={{0,16},{8,24},{16,0},{24,8},{1,17},{9,25},{17,1},{25,9},{2,18},{10... | collective-permute-start | bytes 2359304 | tf_op jit(solution)/shard_map/ppermute | solution.py:1564
  255.1 29.8 %collective-permute-start.13 = (bf16[384,1024]{1,0:T(8,128)(2,1)}, bf16[384,1024]{1,0:T(8,128)(2,1)}, u32[]{:S(2)}, u32[]{:S(2)}) collective-permute-start(bf16[384,1024]{1,0:T(8,128)(2,1)} %slice.181), channel_id=1, source_target_pairs={{0,8},{8,0},{16,24},{24,16},{1,9},{9,1},{17,25},{25,17},{2,10},{10... | collective-permute-start | bytes 2359304 | tf_op jit(solution)/shard_map/ppermute | solution.py:1564
  262.2 28.8 %collective-permute-start.10 = (bf16[384,1024]{1,0:T(8,128)(2,1)}, bf16[384,1024]{1,0:T(8,128)(2,1)}, u32[]{:S(2)}, u32[]{:S(2)}) collective-permute-start(bf16[384,1024]{1,0:T(8,128)(2,1)} %slice.177), channel_id=1, source_target_pairs={{0,16},{8,24},{16,0},{24,8},{1,17},{9,25},{17,1},{25,9},{2,18},{10... | collective-permute-start | bytes 2359304 | tf_op jit(solution)/shard_map/ppermute | solution.py:1564
  265.8 25.2 %collective-permute-start.11 = (bf16[384,1024]{1,0:T(8,128)(2,1)}, bf16[384,1024]{1,0:T(8,128)(2,1)}, u32[]{:S(2)}, u32[]{:S(2)}) collective-permute-start(bf16[384,1024]{1,0:T(8,128)(2,1)} %slice.178), channel_id=1, source_target_pairs={{0,8},{8,0},{16,24},{24,16},{1,9},{9,1},{17,25},{25,17},{2,10},{10... | collective-permute-start | bytes 2359304 | tf_op jit(solution)/shard_map/ppermute | solution.py:1564
  276.1 4.1 copy-start.10
  276.1 4.1 copy-start.11
  280.1 2.4 copy-start.8
  280.1 2.4 copy-start.9
  282.6 2.4 copy-start.13
  285.0 2.1 copy-start.2
  287.1 3.9 copy-start.12
  410.7 10.7 %copy-start.16 = (bf16[512,1024]{1,0:T(8,128)(2,1)S(1)}, bf16[512,1024]{1,0:T(8,128)(2,1)}, u32[]{:S(2)}) copy-start(bf16[512,1024]{1,0:T(8,128)(2,1)} %get-tuple-element.155.refs_1_) | copy-start | bytes 3145732
  477.1 11.2 %copy-start.18 = (bf16[512,1024]{1,0:T(8,128)(2,1)S(1)}, bf16[512,1024]{1,0:T(8,128)(2,1)}, u32[]{:S(2)}) copy-start(bf16[512,1024]{1,0:T(8,128)(2,1)} %get-tuple-element.146.refs_1_) | copy-start | bytes 3145732
  550.9 3.2 copy-start.1
  562.4 35.3 %collective-permute-start.14 = (bf16[512,1024]{1,0:T(8,128)(2,1)}, bf16[512,1024]{1,0:T(8,128)(2,1)S(1)}, u32[]{:S(2)}, u32[]{:S(2)}) collective-permute-start(bf16[512,1024]{1,0:T(8,128)(2,1)} %junction_sum.2), channel_id=1, source_target_pairs={{1,0},{2,1},{3,2},{5,4},{6,5},{7,6},{9,8},{10,9},{11,10},{13,12},{... | collective-permute-start | bytes 3145736 | tf_op jit(solution)/shard_map/ppermute | solution.py:1725
  589.1 8.4 %copy-start.28 = (f32[8,1024]{1,0:T(8,128)S(1)}, f32[8,1024]{1,0:T(8,128)}, u32[]{:S(2)}) copy-start(f32[8,1024]{1,0:T(8,128)} %get-tuple-element.193) | copy-start | bytes 98308
  589.1 8.4 %copy-start.27 = (f32[4,1,1024]{2,1,0:T(1,128)S(1)}, f32[4,1,1024]{2,1,0:T(1,128)}, u32[]{:S(2)}) copy-start(f32[4,1,1024]{2,1,0:T(1,128)} %get-tuple-element.196) | copy-start | bytes 49156
  597.7 1.0 copy-start.17
  773.6 7.8 copy-start.19
  781.4 1.3 copy-start.21

commit v5 on v4

--- a/solution.py
+++ b/solution.py
@@ -223,64 +223,56 @@
     )(q, k, v, qid[:, None], kid[None, :], *riding)
 
 
-def cross_rider(*refs, n_col):
-    raw, slices, full = refs[:4], refs[4:8], refs[8:12]
-    w_s, w_r, own_s = refs[12:]
+def cotangent_rider(cot, dz, c_s, c_r, d_s, d_r, *, n_col):
     dp, row, col = here()
-    part = lax.rem(dp, PARTS)
-    part_x, part_y = part + 1 - 2 * lax.rem(part, 2), part + 2 - 4 * (part // 2)
-    by_x, by_y = plane()
-    wide = raw[0].shape[0]
-    rest = (n_col - 1) * wide
-    half = rest // 2
-
-    def spot(i, which, begin, size):
-        if i < 3:
-            count = raw[i].shape[1] // PARTS
-            return full[i].at[pl.ds(begin, size), pl.ds(pl.multiple_of(which * count, count), count)]
-        count = raw[i].shape[0] // PARTS
-        return full[i].at[pl.ds(pl.multiple_of(which * count, count), count), pl.ds(begin, size)]
-
-    def hop(i, stage):
-        which, begin, size, to = [
-            (part, wide, rest, by_x), (part, wide, rest, by_y),
-            (part_x, wide, half, by_y), (part_y, wide + half, half, by_x),
-        ][stage]
-        dst = spot(i, which, begin, size)
-        return remote(slices[i] if stage < 2 else dst, dst, w_s.at[i, stage], w_r.at[i, stage], to)
-
-    def own(i):
-        place = full[i].at[pl.ds(0, wide), :] if i < 3 else full[i].at[:, pl.ds(0, wide)]
-        return [
-            pltpu.make_async_copy(raw[i], place, own_s.at[i, 0]),
-            pltpu.make_async_copy(slices[i], spot(i, part, wide, rest), own_s.at[i, 1]),
+    wide = cot.shape[1]
+    rows_here = cot.shape[0] // n_col
+
+    def piece(j):
+        to_col = 2 * row + j // 2
+        k = lax.rem(col + n_col - to_col, n_col)
+        src = cot.at[pl.ds(j * rows_here, rows_here), :]
+        dst = dz.at[j % 2, :, pl.ds(pl.multiple_of(k * wide, wide), wide)]
+        local = (row == j % 2) & (col == to_col)
+        return src, dst, k, local, (dp, j % 2, to_col)
+
+    def to_twin(k):
+        ref = dz.at[row, :, pl.ds(k * wide, wide)]
+        return remote(ref, ref, d_s.at[k], d_r.at[k], (dp, 1 - row, col))
+
+    def begin():
+        group = [
+            (dp, r, lax.rem(col + k, n_col)) for r in (row, 1 - row) for k in range(n_col)
         ]
-
-    def begin():
-        meet([by_x, by_y])
-        for i in range(4):
-            hop(i, 0).start()
-            hop(i, 1).start()
-        for i in range(4):
-            for copy in own(i):
-                copy.start()
-
-    def later():
-        for i in range(4):
-            for stage in range(2):
-                hop(i, stage).wait_recv()
-                hop(i, 2 + stage).start()
+        meet(group[1:])
+        for j in range(n_col):
+            src, dst, k, local, to = piece(j)
+
+            @pl.when(local)
+            def _():
+                pltpu.make_async_copy(src, dst, c_r.at[k]).start()
+
+            @pl.when(jnp.logical_not(local))
+            def _():
+                remote(src, dst, c_s.at[j], c_r.at[k], to).start()
 
     def end():
-        for i in range(4):
-            hop(i, 2).wait_recv()
-            hop(i, 3).wait_recv()
-            for stage in range(4):
-                hop(i, stage).wait_send()
-            for copy in own(i):
-                copy.wait()
-
-    hooks = Hooks([(0, begin), (2, later)])
+        for k in range(n_col):
+            pltpu.make_async_copy(
+                cot.at[pl.ds(0, rows_here), :], dz.at[row, :, pl.ds(k * wide, wide)], c_r.at[k]
+            ).wait()
+            to_twin(k).start()
+        for j in range(n_col):
+            src, dst, k, local, to = piece(j)
+
+            @pl.when(jnp.logical_not(local))
+            def _():
+                remote(src, dst, c_s.at[j], c_r.at[k], to).wait_send()
+
+        for k in range(n_col):
+            to_twin(k).wait()
+
+    hooks = Hooks([(0, begin)])
     hooks.end = end
     return hooks
 
@@ -499,51 +491,87 @@
 CUBE = 0.044715
 
 
-def hidden_kernel(
-    f_ref, w1_ref, b1_ref, w2_ref, x_ref, bias, cot, act_ref, slope_ref, out_ref, dz,
-    total, away, came, s_s, s_r, c_s, c_r, d_s, d_r,
-    *, n_col,
-):
-    step = pl.program_id(0) * pl.num_programs(1) + pl.program_id(1)
-    last = pl.num_programs(0) * pl.num_programs(1) - 1
+ORDER = (3, 1, 2, 0)
+
+
+def part_numbers():
+    part = lax.rem(lax.axis_index("dp"), PARTS)
+    return part, part + 1 - 2 * lax.rem(part, 2), part + 2 - 4 * (part // 2), PARTS - 1 - part
+
+
+def weight_copies(own, rest, j, n, to, sem):
+    wide, block = own.shape[0], to.shape[1]
+    inner = rest.shape[1]
+    begin = pl.multiple_of(part_numbers()[j] * inner + n * block, block)
+    return [
+        pltpu.make_async_copy(own.at[:, pl.ds(begin, block)], to.at[pl.ds(0, wide), :], sem),
+        pltpu.make_async_copy(
+            rest.at[:, pl.ds(pl.multiple_of(n * block, block), block)],
+            to.at[pl.ds(wide, rest.shape[0]), :],
+            sem,
+        ),
+    ]
+
+
+def hidden_kernel(*refs, numbers, opening, closing):
+    count = len(numbers)
+    refs = list(refs)
+
+    def take(n):
+        got, refs[:n] = refs[:n], []
+        return got
+
+    f_ref, b1_ref, own1, own2 = take(4)
+    rest1, rest2 = take(count), take(count)
+    if not opening:
+        (sum_in,) = take(1)
+    if closing:
+        x_ref, bias = take(2)
+    act_ref, slope_ref = take(2)
+    (out_ref,) = take(1)
+    total, w1, w2, w_sem = take(4)
+    step, steps = pl.program_id(0), pl.num_programs(0)
     dp, row, col = here()
     twin = (dp, 1 - row, col)
-    wide = cot.shape[1]
-    rows_here = cot.shape[0] // n_col
-
-    def cot_piece(j):
-        to_col = 2 * row + j // 2
-        k = lax.rem(col + n_col - to_col, n_col)
-        src = cot.at[pl.ds(j * rows_here, rows_here), :]
-        dst = dz.at[j % 2, :, pl.ds(pl.multiple_of(k * wide, wide), wide)]
-        local = (row == j % 2) & (col == to_col)
-        return src, dst, k, local, (dp, j % 2, to_col)
-
-    def cot_twin(k):
-        ref = dz.at[row, :, pl.ds(k * wide, wide)]
-        return remote(ref, ref, d_s.at[k], d_r.at[k], twin)
+    block = w1.shape[2]
+    blocks = rest1[0].shape[1] // block
+    slot = lax.rem(step, 2)
+
+    def fetch(s):
+        for i in range(count):
+
+            @pl.when(s // blocks == i)
+            def _():
+                n = lax.rem(s, blocks)
+                at = lax.rem(s, 2)
+                for copy in weight_copies(
+                    own1, rest1[i], numbers[i], n, w1.at[at], w_sem.at[0, at]
+                ) + weight_copies(own2, rest2[i], numbers[i], n, w2.at[at], w_sem.at[1, at]):
+                    copy.start()
+
+    if closing:
+        away, came, s_s, s_r = take(4)
 
     @pl.when(step == 0)
     def _():
-        total[...] = jnp.zeros_like(total)
-        group = [
-            (dp, r, lax.rem(col + k, n_col)) for r in (row, 1 - row) for k in range(n_col)
-        ]
-        meet(group[1:])
-        for j in range(n_col):
-            src, dst, k, local, to = cot_piece(j)
-
-            @pl.when(local)
-            def _():
-                pltpu.make_async_copy(src, dst, c_r.at[k]).start()
-
-            @pl.when(jnp.logical_not(local))
-            def _():
-                remote(src, dst, c_s.at[j], c_r.at[k], to).start()
+        fetch(step)
+        if opening:
+            total[...] = jnp.zeros_like(total)
+        else:
+            total[...] = sum_in[...]
+            if closing:
+                meet([twin])
+
+    @pl.when(step + 1 < steps)
+    def _():
+        fetch(step + 1)
+
+    for i, w in enumerate((w1, w2)):
+        pltpu.make_async_copy(w.at[slot], w.at[slot], w_sem.at[i, slot]).wait()
 
     def one_part(t, carry):
         rows = pl.ds(pl.multiple_of(t * 256, 256), 256)
-        h = mm(f_ref[rows, :], w1_ref[0]) + b1_ref[0]
+        h = mm(f_ref[rows, :], w1[slot]) + b1_ref[0]
         square = h * h
         bend = jnp.tanh(h * (ROOT + (ROOT * CUBE) * square))
         half = 0.5 + 0.5 * bend
@@ -551,99 +579,124 @@
         act_ref[0, rows, :] = act
         slope = half + (0.5 * h) * (1.0 - bend * bend) * (ROOT + (3.0 * ROOT * CUBE) * square)
         slope_ref[0, rows, :] = slope.astype(low)
-        total[rows, :] += mm_nt(act, w2_ref[0])
+        total[rows, :] += mm_nt(act, w2[slot])
         return carry
 
     lax.fori_loop(0, f_ref.shape[0] // 256, one_part, 0)
 
-    @pl.when(step == last - 1)
+    @pl.when(step == steps - 1)
     def _():
-        for k in range(n_col):
-            pltpu.make_async_copy(
-                cot.at[pl.ds(0, rows_here), :], dz.at[row, :, pl.ds(k * wide, wide)], c_r.at[k]
-            ).wait()
-            cot_twin(k).start()
-
-    @pl.when(step == last)
-    def _():
-        rows = came.shape[0]
-        sent = []
-        for t in range(rows // CUT):
-            at = pl.ds(t * CUT, CUT)
-            begin = pl.multiple_of((1 - row) * rows + t * CUT, CUT)
-            away[at, :] = total[pl.ds(begin, CUT), :].astype(low)
-            copy = remote(away.at[at, :], came.at[at, :], s_s.at[t], s_r.at[t], twin)
-            copy.start()
-            sent.append(copy)
-        for t in range(rows // CUT):
-            at = pl.ds(t * CUT, CUT)
-            begin = pl.multiple_of(row * rows + t * CUT, CUT)
-            sent[t].wait()
-            branch = total[pl.ds(begin, CUT), :] + came[at, :].astype(f32)
-            out_ref[at, :] = (x_ref[at, :] + (branch + bias[...])).astype(low)
-        for j in range(n_col):
-            src, dst, k, local, to = cot_piece(j)
-
-            @pl.when(jnp.logical_not(local))
+        if not closing:
+            out_ref[...] = total[...]
+        else:
+            rows = came.shape[0]
+            sent = []
+            for t in range(rows // CUT):
+                at = pl.ds(t * CUT, CUT)
+                begin = pl.multiple_of((1 - row) * rows + t * CUT, CUT)
+                away[at, :] = total[pl.ds(begin, CUT), :].astype(low)
+                copy = remote(away.at[at, :], came.at[at, :], s_s.at[t], s_r.at[t], twin)
+                copy.start()
+                sent.append(copy)
+            for t in range(rows // CUT):
+                at = pl.ds(t * CUT, CUT)
+                begin = pl.multiple_of(row * rows + t * CUT, CUT)
+                sent[t].wait()
+                branch = total[pl.ds(begin, CUT), :] + came[at, :].astype(f32)
+                out_ref[at, :] = (x_ref[at, :] + (branch + bias[...])).astype(low)
+
+def hidden_forward(f, b1, own1, own2, rest1, rest2, numbers, number, sum_in=None, x=None, bias=None):
+    tokens, width = f.shape
+    inner = rest1[0].shape[1]
+    count = len(numbers)
+    block = min(512, inner)
+    blocks = inner // block
+    rows = tokens // 2
+    opening, closing = sum_in is None, x is not None
+    dma = pltpu.SemaphoreType.DMA
+
+    def still(shape):
+        return pl.BlockSpec(shape, lambda s: (0,) * len(shape))
+
+    active = pl.BlockSpec((1, tokens, block), lambda s: (s // blocks, 0, lax.rem(s, blocks)))
+    args = [f, b1, own1, own2, *rest1, *rest2]
+    in_specs = [
+        still((tokens, width)),
+        pl.BlockSpec((1, 1, block), lambda s: (s // blocks, 0, lax.rem(s, blocks))),
+    ] + [ANYWHERE] * (2 + 2 * count)
+    out_specs = [active, active]
+    out_shape = [jax.ShapeDtypeStruct((count, tokens, inner), low)] * 2
+    scratch = [
+        pltpu.VMEM((tokens, width), f32),
+        pltpu.VMEM((2, width, block), low),
+        pltpu.VMEM((2, width, block), low),
+        dma((2, 2)),
+    ]
+    if not opening:
+        args.append(sum_in)
+        in_specs.append(still((tokens, width)))
+    if closing:
+        args += [x, bias[None]]
+        in_specs += [still((rows, width)), still((1, width))]
+        out_shape.append(jax.ShapeDtypeStruct((rows, width), low))
+        scratch += [pltpu.VMEM((rows, width), low), pltpu.VMEM((rows, width), low)]
+        scratch += [dma((rows // CUT,)), dma((rows // CUT,))]
+    else:
+        out_shape.append(jax.ShapeDtypeStruct((tokens, width), f32))
+    out_specs.append(still(out_shape[-1].shape))
+    params = dict(vmem_limit_bytes=VMEM)
+    if closing:
+        params.update(collective_id=number, has_side_effects=True)
+    return pl.pallas_call(
+        functools.partial(
+            hidden_kernel, numbers=numbers, opening=opening, closing=closing
+        ),
+        grid=(count * blocks,),
+        in_specs=in_specs,
+        out_specs=out_specs,
+        out_shape=out_shape,
+        scratch_shapes=scratch,
+        compiler_params=pltpu.CompilerParams(**params),
+        name="hidden_forward",
+    )(*args)
+
+
+def hidden_back_kernel(
+    dz_ref, dzt_ref, ft_ref, rows_out, own1, own2, *refs, n_col, places,
+):
+    rest1, rest2 = refs[:PARTS], refs[PARTS : 2 * PARTS]
+    calls = 1 + max(p[0] for p in places)
+    acts, slopes = refs[2 * PARTS : 2 * PARTS + calls], refs[2 * PARTS + calls : 2 * (PARTS + calls)]
+    (
+        g1_ref, g2_ref, gb_ref, df_ref, got_a, got_b, home, dh_low, total, away_a, away_b, s_s,
+        r_s, h_s, h_r, w1, w2, act_ref, slope_ref, w_sem,
+    ) = refs[2 * (PARTS + calls) :]
+    block = g1_ref.shape[2]
+    inners = rest1[0].shape[1] // block
+    step = pl.program_id(0)
+    last = pl.num_programs(0) - 1
+    order, inner = step // inners, lax.rem(step, inners)
+    slot = lax.rem(step, 2)
+
+    def fetch(s):
+        for i, j in enumerate(ORDER):
+
+            @pl.when(s // inners == i)
             def _():
-                remote(src, dst, c_s.at[j], c_r.at[k], to).wait_send()
-
-        for k in range(n_col):
-            cot_twin(k).wait()
-
-
-def hidden_forward(f, w1, b1, w2, x, bias, cotangent, n_col, number):
-    parts, width, inner = w1.shape
-    tokens = f.shape[0]
-    block = min(512, inner)
-    grid = (parts, inner // block)
-    weight = pl.BlockSpec((1, width, block), lambda j, n: (j, 0, n))
-    active = pl.BlockSpec((1, tokens, block), lambda j, n: (j, 0, n))
-    rows = tokens // 2
-    dma = pltpu.SemaphoreType.DMA
-    half = pl.BlockSpec((rows, width), lambda j, n: (0, 0))
-    return pl.pallas_call(
-        functools.partial(hidden_kernel, n_col=n_col),
-        grid=grid,
-        in_specs=[
-            pl.BlockSpec((tokens, width), lambda j, n: (0, 0)),
-            weight,
-            pl.BlockSpec((1, 1, block), lambda j, n: (j, 0, n)),
-            weight,
-            half,
-            pl.BlockSpec((1, width), lambda j, n: (0, 0)),
-            pl.BlockSpec(cotangent.shape, lambda j, n: (0, 0)),
-        ],
-        out_specs=[active, active, half, ANYWHERE],
-        out_shape=[
-            jax.ShapeDtypeStruct((parts, tokens, inner), low),
-            jax.ShapeDtypeStruct((parts, tokens, inner), low),
-            jax.ShapeDtypeStruct((rows, width), low),
-            jax.ShapeDtypeStruct((2, rows, width), low),
-        ],
-        scratch_shapes=[
-            pltpu.VMEM((tokens, width), f32),
-            pltpu.VMEM((rows, width), low),
-            pltpu.VMEM((rows, width), low),
-            dma((rows // CUT,)), dma((rows // CUT,)),
-            dma((n_col,)), dma((n_col,)), dma((n_col,)), dma((n_col,)),
-        ],
-        compiler_params=pltpu.CompilerParams(
-            vmem_limit_bytes=VMEM, collective_id=number, has_side_effects=True
-        ),
-        name="hidden_forward",
-    )(f, w1, b1, w2, x, bias[None], cotangent)
-
-
-def hidden_back_kernel(
-    dz_ref, dzt_ref, ft_ref, w1_ref, w2_ref, act_ref, slope_ref, rows_out,
-    g1_ref, g2_ref, gb_ref, df_ref, got_a, got_b, home, dh_low, total, away_a, away_b, s_s, r_s,
-    h_s, h_r, *, n_col,
-):
-    inner, inners = pl.program_id(1), pl.num_programs(1)
-    order = pl.program_id(0)
-    step = order * inners + inner
-    last = pl.num_programs(0) * inners - 1
+                n, at = lax.rem(s, inners), lax.rem(s, 2)
+                lanes = pl.ds(pl.multiple_of(n * block, block), block)
+                call, index = places[j]
+                copies = weight_copies(own1, rest1[j], j, n, w1.at[at], w_sem.at[0, at])
+                copies += weight_copies(own2, rest2[j], j, n, w2.at[at], w_sem.at[1, at])
+                for src, to, k in ((acts, act_ref, 2), (slopes, slope_ref, 3)):
+                    copies.append(
+                        pltpu.make_async_copy(
+                            src[call].at[index, :, lanes], to.at[at], w_sem.at[k, at]
+                        )
+                    )
+                for copy in copies:
+                    copy.start()
+
     by_x, by_y = plane()
     half = got_a.shape[1]
     dp, row, col = here()
@@ -656,28 +709,34 @@
         meet(group[1:] + [by_x, by_y])
         total[...] = jnp.zeros_like(total)
         send_home(rows_out, home, h_s, h_r, n_col)
+        fetch(step)
+
+    @pl.when(step < last)
+    def _():
+        fetch(step + 1)
 
     gb_ref[...] = jnp.zeros_like(gb_ref)
+    for i, w in enumerate((w1, w2, act_ref, slope_ref)):
+        pltpu.make_async_copy(w.at[slot], w.at[slot], w_sem.at[i, slot]).wait()
 
     def one_part(t, carry):
         rows = pl.ds(pl.multiple_of(t * 256, 256), 256)
-        dh = (mm(dz_ref[rows, :], w2_ref[0]) * slope_ref[0, rows, :].astype(f32)).astype(low)
+        dh = (mm(dz_ref[rows, :], w2[slot]) * slope_ref[slot, rows, :].astype(f32)).astype(low)
         dh_low[rows, :] = dh
         gb_ref[0] += jnp.sum(dh.astype(f32), axis=0, keepdims=True)
-        total[rows, :] += mm_nt(dh, w1_ref[0])
+        total[rows, :] += mm_nt(dh, w1[slot])
         return carry
 
     lax.fori_loop(0, dz_ref.shape[0] // 256, one_part, 0)
 
     def one_grad(t, carry):
         rows = pl.ds(pl.multiple_of(t * 256, 256), 256)
-        g2_ref[0, rows, :] = mm(dzt_ref[rows, :], act_ref[0]).astype(low)
+        g2_ref[0, rows, :] = mm(dzt_ref[rows, :], act_ref[slot]).astype(low)
         g1_ref[0, rows, :] = mm(ft_ref[rows, :], dh_low[...]).astype(low)
         return carry
 
     lax.fori_loop(0, ft_ref.shape[0] // 256, one_grad, 0)
 
-    block = g1_ref.shape[2]
     lanes = pl.ds(pl.multiple_of(inner * block, block), block)
 
     def hop(which, slot, n):
@@ -711,53 +770,65 @@
         wait_home(rows_out, home, h_s, h_r, n_col)
 
 
-def hidden_backward(dz, f, w1, w2, act, slope, rows_out, n_col, number):
-    parts, width, inner = w1.shape
-    tokens = f.shape[0]
+def hidden_backward(dz, f, own1, own2, rest1, rest2, acts, slopes, places, rows_out, n_col, number):
+    tokens, width = f.shape
+    inner = rest1[0].shape[1]
     block = min(512, inner)
-    grid = (parts, inner // block)
-
-    def number_of(j):
-        return jnp.where(j == 0, parts - 1, jnp.where(j == parts - 1, 0, j))
-
-    weight = pl.BlockSpec((1, width, block), lambda j, n: (number_of(j), 0, n))
-    active = pl.BlockSpec((1, tokens, block), lambda j, n: (number_of(j), 0, n))
-    whole = pl.BlockSpec((tokens, width), lambda j, n: (0, 0))
-    turned = pl.BlockSpec((width, tokens), lambda j, n: (0, 0))
+    blocks = inner // block
+
+    def number_of(s):
+        j = s // blocks
+        return jnp.where(j == 0, PARTS - 1, jnp.where(j == PARTS - 1, 0, j))
+
+    def still(shape):
+        return pl.BlockSpec(shape, lambda s: (0,) * len(shape))
+
+    weight = pl.BlockSpec((1, width, block), lambda s: (number_of(s), 0, lax.rem(s, blocks)))
     landing = jax.ShapeDtypeStruct((2, width // 2, inner), low)
+    grad = jax.ShapeDtypeStruct((PARTS, width, inner), low)
+    vm, dma = pltpu.VMEM, pltpu.SemaphoreType.DMA
     return pl.pallas_call(
-        functools.partial(hidden_back_kernel, n_col=n_col),
-        grid=grid,
-        in_specs=[whole, turned, turned, weight, weight, active, active]
-        + [pl.BlockSpec(rows_out.shape, lambda j, n: (0, 0))],
+        functools.partial(hidden_back_kernel, n_col=n_col, places=places),
+        grid=(PARTS * blocks,),
+        in_specs=[still((tokens, width)), still((width, tokens)), still((width, tokens))]
+        + [still(rows_out.shape)]
+        + [ANYWHERE] * (2 + 2 * PARTS + 2 * len(acts)),
         out_specs=[
-            weight, weight, pl.BlockSpec((1, 1, block), lambda j, n: (number_of(j), 0, n)), whole,
+            weight,
+            weight,
+            pl.BlockSpec((1, 1, block), lambda s: (number_of(s), 0, lax.rem(s, blocks))),
+            still((tokens, width)),
             ANYWHERE, ANYWHERE, ANYWHERE,
         ],
         out_shape=[
-            jax.ShapeDtypeStruct(w1.shape, low),
-            jax.ShapeDtypeStruct(w1.shape, low),
-            jax.ShapeDtypeStruct((parts, 1, inner), f32),
+            grad,
+            grad,
+            jax.ShapeDtypeStruct((PARTS, 1, inner), f32),
             jax.ShapeDtypeStruct((tokens, width), low),
             landing,
             landing,
             jax.ShapeDtypeStruct((n_col * rows_out.shape[0], width // n_col), low),
         ],
         scratch_shapes=[
-            pltpu.VMEM((tokens, block), low),
-            pltpu.VMEM((tokens, width), f32),
-            pltpu.VMEM(landing.shape, low),
-            pltpu.VMEM(landing.shape, low),
-            pltpu.SemaphoreType.DMA((2, 2, inner // block)),
-            pltpu.SemaphoreType.DMA((2, 2, inner // block)),
-            pltpu.SemaphoreType.DMA((n_col,)),
-            pltpu.SemaphoreType.DMA((n_col,)),
+            vm((tokens, block), low),
+            vm((tokens, width), f32),
+            vm(landing.shape, low),
+            vm(landing.shape, low),
+            dma((2, 2, blocks)),
+            dma((2, 2, blocks)),
+            dma((n_col,)),
+            dma((n_col,)),
+            vm((2, width, block), low),
+            vm((2, width, block), low),
+            vm((2, tokens, block), low),
+            vm((2, tokens, block), low),
+            dma((4, 2)),
         ],
         compiler_params=pltpu.CompilerParams(
             vmem_limit_bytes=VMEM, collective_id=number, has_side_effects=True
         ),
         name="hidden_backward",
-    )(dz, dz.T, f.T, w1, w2, act, slope, rows_out)
+    )(dz, dz.T, f.T, rows_out, own1, own2, *rest1, *rest2, *acts, *slopes)
 
 
 def start_kernel(
@@ -806,11 +877,7 @@
     def piece(i, k):
         if i == 8:
             return enc_chunk(k)
-        if i < 4:
-            return weight_chunk(i, k)
-        if i % 4 < 3:
-            return full[i].at[pl.ds((k - 1) * wide, wide), :]
-        return full[i].at[:, pl.ds((k - 1) * wide, wide)]
+        return weight_chunk(i, k)
 
     def own_piece(i):
         return encoder if i == 8 else weight_slice(i)
@@ -908,21 +975,28 @@
         pltpu.make_async_copy(vec_c, all_c.at[col], v_recv.at[1, 0]),
     ]
     ks = range(1, n_col)
-    for i in range(9):
+    for i in range(8):
         send_along(i, 1)
     for k in ks:
         for copy in vectors(k):
             copy.start()
-    for i in range(4):
+    for i in range(8):
         weight_own(i).start()
     for copy in own_vectors:
         copy.start()
     enc_twin(0).start()
     for h in (1, 2):
-        for i in range(9):
+        for i in range(8):
             take(i, h)
             send_along(i, h + 1)
+    send_along(8, 1)
     send_tokens(1)
+    for i in range(8):
+        take(i, 3)
+        weight_plane(i, 0).start()
+        weight_plane(i, 1).start()
+    take(8, 1)
+    send_along(8, 2)
     send_tokens(0)
 
     @pl.when(col == 0)
@@ -933,19 +1007,17 @@
         clear.wait()
 
     for i in range(8):
-        take(i, 3)
-        if i < 4:
-            weight_plane(i, 0).start()
-            weight_plane(i, 1).start()
-    take(8, 3)
-    for k in ks:
-        enc_twin(k).start()
-    for i in range(4):
         weight_plane(i, 0).wait_recv()
         weight_plane(i, 2).start()
         weight_plane(i, 1).wait_recv()
         weight_plane(i, 3).start()
-    for i in range(4):
+        if i == 3:
+            take(8, 2)
+            send_along(8, 3)
+    take(8, 3)
+    for k in ks:
+        enc_twin(k).start()
+    for i in range(8):
         weight_plane(i, 2).wait_recv()
         weight_plane(i, 3).wait_recv()
         weight_own(i).wait()
@@ -1004,10 +1076,9 @@
         jax.ShapeDtypeStruct((n_col,) + vec_c.shape, f32),
     ]
     for i, w in enumerate(weights):
-        at, length, size = (0, deep, w.shape[1]) if i % 4 < 3 else (1, deep, w.shape[0])
-        if i >= 4:
-            length, size = deep - wide, size // PARTS
-        shapes.append(jax.ShapeDtypeStruct((size, length) if at else (length, size), low))
+        shapes.append(
+            jax.ShapeDtypeStruct((deep, w.shape[1]) if i % 4 < 3 else (w.shape[0], deep), low)
+        )
     dma = pltpu.SemaphoreType.DMA
     return pl.pallas_call(
         functools.partial(start_kernel, n_col=n_col),
@@ -1016,7 +1087,7 @@
         out_shape=shapes,
         scratch_shapes=[
             pltpu.VMEM((rows, deep), low),
-            dma((4, 4)), dma((4, 4)), dma((4,)),
+            dma((8, 4)), dma((8, 4)), dma((8,)),
             dma((2, n_col)), dma((2, n_col)),
             dma((2, n_col)), dma((2, n_col)),
             dma, dma((9, 2, n_col - 1)), dma((9, n_col - 1)), dma((n_col,)), dma((n_col,)), dma,
@@ -1036,7 +1107,6 @@
 
 
 CUT = 256
-N_COL = 4
 
 
 def enter_kernel(x_ref, gain, shift, a_ref, sends, recvs):
@@ -1088,9 +1158,6 @@
         x_ref, bias, gain, shift, x_out, full, away, came, s1, r1, s2, r2 = refs
     elif mode == "backward":
         res_ref, x_ref, gain, dx_out, full, stats, away, came, s1, r1, s2, r2 = refs
-    elif mode == "last":
-        res_ref, x_ref, gain, after, dx_out, stats, away, came, s1, r1 = refs
-        full = None
     else:
         out, away, came, s1, r1 = refs
     rows = came.shape[0]
@@ -1127,11 +1194,6 @@
         if mode == "sum":
             out[at, :] = total.astype(low)
             continue
-        if mode == "last":
-            deep = after.shape[1]
-            wide = deep // N_COL
-            moved = [after[at, pl.ds(deep - wide, wide)], after[at, pl.ds(0, deep - wide)]]
-            total = total + jnp.concatenate(moved, axis=1).astype(f32)
         if mode == "forward":
             x = x_ref[at, :].astype(f32) + (total + bias[...])
             x_out[at, :] = x
@@ -1148,14 +1210,12 @@
             result = dx.astype(low)
             for i, value in enumerate((total * normed, total, result.astype(f32), res)):
                 sums[i] = sums[i] + jnp.sum(value, axis=0, keepdims=True)
-        if full is None:
-            continue
         full[pl.ds(begin, CUT), :] = result
         place = full.at[pl.ds(begin, CUT), :]
         copy = remote(place, place, s2.at[t], r2.at[t], twin)
         copy.start()
         gathered.append(copy)
-    if mode in ("backward", "last"):
+    if mode == "backward":
         for i in range(4):
             stats[i : i + 1, :] = sums[i]
     for copy in sent:
@@ -1179,7 +1239,6 @@
     shapes = {
         "forward": [wide_rows, every],
         "backward": [wide_rows, every, jax.ShapeDtypeStruct((8, deep), f32)],
-        "last": [jax.ShapeDtypeStruct((rows, deep), low), jax.ShapeDtypeStruct((8, deep), f32)],
         "sum": [jax.ShapeDtypeStruct((rows, deep), low)],
     }[mode]
     scratch = [pltpu.VMEM((rows, deep), low), pltpu.VMEM((rows, deep), low), dma, dma]
@@ -1200,82 +1259,383 @@
     return out if len(out) > 1 else out[0]
 
 
-def finish_kernel(
-    ga, gb, small, enc_in, tg, g2, near_a, near_b, far_back_a, far_back_b, z_got, own1,
-    full, hidden_full, small_out, enc_out, tg_out,
-    load, load_own, load_got, h_out, h_in, l_s, lo_s, hz_s, hz_r, h_extra, hx_s, hx_r, hg_s, hg_r,
-    first, second, mid, zout, zin, tot, enc_got, s_cur, s_got, s_z, extra,
-    f_s, f_r, m_s, m_r, z_s, z_r, g_s, g_r, e_s, e_r, s_s, s_r, sz_s, sz_r, t_s, t_r, x_s, x_r,
+def plane_copies(full, part, parts, by_x, by_y, sends, recvs):
+    size = full.shape[1]
+    half = size // 2
+
+    def copy(stage):
+        which, begin, count, to = [
+            (part, 0, size, by_x), (part, 0, size, by_y),
+            (parts[1], 0, half, by_y), (parts[2], half, half, by_x),
+        ][stage]
+        ref = full.at[which, pl.ds(begin, count), :]
+        return remote(ref, ref, sends.at[stage], recvs.at[stage], to)
+
+    return copy
+
+
+class LineSum:
+    def __init__(self, buf, in_l, in_r, sends, recvs, cols):
+        self.buf, self.in_l, self.in_r, self.sends, self.recvs = buf, in_l, in_r, sends, recvs
+        self.cols, self.n, self.col = cols, len(cols), lax.axis_index("col")
+
+    def right(self, d):
+        return remote(
+            self.buf.at[d - 1], self.in_l.at[d - 1], self.sends.at[0, d - 1],
+            self.recvs.at[0, d - 1], self.cols[1],
+        )
+
+    def left(self, d):
+        return remote(
+            self.buf.at[self.n - d - 1], self.in_r.at[d - 1], self.sends.at[1, d - 1],
+            self.recvs.at[1, d - 1], self.cols[self.n - 1],
+        )
+
+    def add(self, k, got):
+        self.buf[k - 1] = (self.buf[k - 1].astype(f32) + got.astype(f32)).astype(low)
+
+    def begin(self):
+        @pl.when(self.col == 0)
+        def _():
+            self.in_l[0] = jnp.zeros(self.in_l.shape[1:], low)
+            for d in range(self.n - 1, 0, -1):
+                self.right(d).start()
+
+        @pl.when(self.col == self.n - 1)
+        def _():
+            self.in_r[0] = jnp.zeros(self.in_r.shape[1:], low)
+            for d in range(self.n - 1, 0, -1):
+                self.left(d).start()
+
+    def go(self, d):
+        @pl.when((self.col > 0) & (self.col <= self.n - 1 - d))
+        def _():
+            self.right(d + 1).wait_recv()
+            self.add(d, self.in_l[d])
+            self.right(d).start()
+
+        @pl.when((self.col < self.n - 1) & (self.col >= d))
+        def _():
+            self.left(d + 1).wait_recv()
+            self.add(self.n - d, self.in_r[d])
+            self.left(d).start()
+
+    def total(self, value):
+        @pl.when(self.col > 0)
+        def _():
+            self.right(1).wait_recv()
+
+        @pl.when(self.col < self.n - 1)
+        def _():
+            self.left(1).wait_recv()
+
+        return value + self.in_l[0].astype(f32) + self.in_r[0].astype(f32)
+
+    def end(self):
+        for d in range(1, self.n):
+
+            @pl.when(self.col <= self.n - 1 - d)
+            def _():
+                self.right(d).wait_send()
+
+            @pl.when(self.col >= d)
+            def _():
+                self.left(d).wait_send()
+
+
+def with_other_bits(value, store, which, sends, recvs, partners):
+    for i, partner in enumerate(partners):
+        store[i, 0] = value.astype(low)
+        copy = remote(
+            store.at[i, 0], store.at[i, 1 + which], sends.at[which, i], recvs.at[which, i], partner
+        )
+        copy.start()
+        copy.wait()
+        value = value + store[i, 1 + which].astype(f32)
+    return value
+
+
+def bit_partners(n_dp):
+    dp, row, col = here()
+    bits = [1 << b for b in range(n_dp.bit_length() - 1)]
+    return [(dp + b - 2 * b * lax.rem(dp // b, 2), row, col) for b in bits]
+
+
+def fold_kernel(
+    dq, dk, dv, a_ext, dy, o, wq, wk, wv, res, x0, gain, ga,
+    g2, near_a, near_b, far_back_a, far_back_b, z_got, own1,
+    gb, sums, tg, stats, a_sum, hidden0, q_own,
+    load, load_own, load_got, h_out, h_l, h_r, first, second, mid, away_b, came_b, away_l, came_l,
+    da_got, extra,
+    l_s, lo_s, hz_s, hz_r, f_s, f_r, m_s, m_r, b_s, b_r, c_s, c_r, d_s, d_r, g_s, g_r, x_s, x_r,
     *, n_col, n_dp,
 ):
     dp, row, col = here()
-    part = lax.rem(dp, PARTS)
+    parts = part_numbers()
+    part = parts[0]
+    by_bit = bit_partners(n_dp)
+    by_x, by_y = by_bit[:2]
     twin = (dp, 1 - row, col)
-    bits = [1 << b for b in range(n_dp.bit_length() - 1)]
-    flips = [dp + b - 2 * b * lax.rem(dp // b, 2) for b in bits]
-    by_bit = [(f, row, col) for f in flips]
-    shift = [lax.rem(col + k, n_col) for k in range(n_col)]
-    group = [(dp, r, c) for r in (row, 1 - row) for c in shift][1:]
-    meet(group + by_bit)
-    wide = ga.shape[1] // n_col
+    cols = [(dp, row, lax.rem(col + k, n_col)) for k in range(n_col)]
+    left = cols[n_col - 1]
+    meet([twin] + by_bit + cols[1:])
     ks = range(1, n_col)
-    part_x, part_y, part_xy = part + 1 - 2 * lax.rem(part, 2), part + 2 - 4 * (part // 2), 3 - part
-    ways = [(ga, 0, (part_x, part_xy), part_y), (gb, 1, (part_y, part_xy), part_x)]
-    h_half = near_a.shape[0]
+    deep = tg.shape[1]
+    wide = deep // n_col
+    half = near_a.shape[0]
+    rows = tg.shape[0]
+    cuts = rows // CUT
+    window = dk.shape[0] - dq.shape[0]
+
+    def at(q):
+        return pl.ds(q * wide, wide)
+
     loads = []
     for i, sources in enumerate(((near_a, far_back_a), (near_b, far_back_b))):
-        at = pl.ds(i * h_half, h_half)
-        for n, src in enumerate((g2.at[0, at, :],) + sources):
-            loads.append(pltpu.make_async_copy(src, load.at[n, at, :], l_s.at[i, n]))
+        spot = pl.ds(i * half, half)
+        for n, src in enumerate((g2.at[0, spot, :],) + sources):
+            loads.append(pltpu.make_async_copy(src, load.at[n, spot, :], l_s.at[i, n]))
     loads_own = [
         pltpu.make_async_copy(own1, load_own, lo_s.at[0]),
         pltpu.make_async_copy(z_got, load_got, lo_s.at[1]),
     ]
 
-    def hidden_hop(k):
-        return remote(h_out.at[k], h_in.at[k - 1], hz_s.at[k - 1], hz_r.at[k - 1], z_to(k))
+    def hop(which, q):
+        source = ga.at[parts[3] if which else parts[1], at(q), :]
+        return remote(source, first.at[which, at(q), :], f_s.at[which, q], f_r.at[which, q], by_x)
+
+    def hop2(q):
+        return remote(mid.at[at(q), :], second.at[at(q), :], m_s.at[q], m_r.at[q], by_y)
+
+    line = LineSum(h_out, h_l, h_r, hz_s, hz_r, cols)
 
     def hidden_total(k):
-        at = rows(k)
-        value = load[0, at, :].astype(f32) + load[1, at, :].astype(f32)
-        return value + load[2, at, :].astype(f32)
-
-    def other_bits(value, g, store, s_x, r_x):
-        for i in range(len(bits) - 2):
-            store[g, i, 0] = value.astype(low)
-            copy = remote(
-                store.at[g, i, 0], store.at[g, i, 1], s_x.at[g, i], r_x.at[g, i], by_bit[2 + i]
-            )
-            copy.start()
-            copy.wait()
-            value = value + store[g, i, 1].astype(f32)
-        return value
+        value = load[0, at(k), :].astype(f32) + load[1, at(k), :].astype(f32)
+        return value + load[2, at(k), :].astype(f32)
+
+    for copy in loads + loads_own:
+        copy.start()
+    for which in (1, 0):
+        for q in range(n_col):
+            hop(which, q).start()
+
+    for copy in loads:
+        copy.wait()
+    for k in ks:
+        h_out[k - 1] = hidden_total(k).astype(low)
+    line.begin()
+
+    def before(begin):
+        spot = pl.ds(begin, CUT)
+        return mm_nt(dk[spot, :], wk[...]) + mm_nt(dv[spot, :], wv[...])
+
+    def exchange(away, came, sends, recvs, t):
+        spot = pl.ds(t * CUT, CUT)
+        return remote(away.at[spot, :], came.at[spot, :], sends.at[t], recvs.at[t], twin)
+
+    for t in range(cuts):
+        spot = pl.ds(t * CUT, CUT)
+        away_b[spot, :] = before(pl.multiple_of((1 - row) * rows + t * CUT, CUT)).astype(low)
+        exchange(away_b, came_b, b_s, b_r, t).start()
+    for t in range(cuts):
+        spot = pl.ds(t * CUT, CUT)
+        own = before(pl.multiple_of(row * rows + t * CUT, CUT))
+        exchange(away_b, came_b, b_s, b_r, t).wait_recv()
+        came_b[spot, :] = (own + came_b[spot, :].astype(f32)).astype(low)
+    da_hop = remote(came_b, da_got, d_s, d_r, left)
+
+    @pl.when(col > 0)
+    def _():
+        da_hop.start()
+
+    @pl.when(col == n_col - 1)
+    def _():
+        da_got[...] = jnp.zeros_like(da_got)
+
+    for q in range(n_col):
+        hop(1, q).wait_recv()
+        value = ga[parts[2], at(q), :].astype(f32) + first[1, at(q), :].astype(f32)
+        mid[at(q), :] = value.astype(low)
+        hop2(q).start()
+    for copy in loads_own:
+        copy.wait()
+    value = load_own[...].astype(f32)
+    for k in ks:
+        value = value + load_got[k - 1].astype(f32)
+    value = with_other_bits(value, extra, 0, x_s, x_r, by_bit[2:])
+    hidden0[part] = value.astype(low)
+    spread = plane_copies(hidden0, part, parts, by_x, by_y, g_s, g_r)
+    spread(0).start()
+    spread(1).start()
+
+    line.go(2)
+
+    def last(begin):
+        spot = pl.ds(begin, CUT)
+        later = pl.ds(window + begin, CUT)
+        value = mm_nt(dq[spot, :], wq[...]) + mm_nt(dk[later, :], wk[...])
+        return value + mm_nt(dv[later, :], wv[...])
+
+    for t in range(cuts):
+        spot = pl.ds(t * CUT, CUT)
+        away_l[spot, :] = last(pl.multiple_of((1 - row) * rows + t * CUT, CUT)).astype(low)
+        exchange(away_l, came_l, c_s, c_r, t).start()
+
+    size = gb.shape[2] // 4
+    pairs = ((window, dq), (0, dk), (0, dv), (None, o))
+
+    def one_block(i, carry):
+        lanes = pl.ds(pl.multiple_of(i * wide, wide), wide)
+        for n, (begin, other) in enumerate(pairs):
+            source = dy[:, lanes] if begin is None else a_ext[pl.ds(begin, other.shape[0]), lanes]
+            value = mm_tn(source, other[...]).astype(low)
+            for p in range(PARTS):
+                gb[p, lanes, n * size : (n + 1) * size] = value[:, p * size : (p + 1) * size]
+        return carry
+
+    lax.fori_loop(0, n_col, one_block, 0)
+    line.go(1)
+    for n, (_, other) in enumerate(pairs):
+        sums[n : n + 1, :] = jnp.sum(other[...].astype(f32), axis=0, keepdims=True)
+
+    @pl.when(col < n_col - 1)
+    def _():
+        da_hop.wait_recv()
+
+    totals = [0.0, 0.0]
+    for t in range(cuts):
+        spot = pl.ds(t * CUT, CUT)
+        own = last(pl.multiple_of(row * rows + t * CUT, CUT))
+        exchange(away_l, came_l, c_s, c_r, t).wait_recv()
+        total = own + came_l[spot, :].astype(f32)
+        after = [da_got[spot, pl.ds(deep - wide, wide)], da_got[spot, pl.ds(0, deep - wide)]]
+        total = total + jnp.concatenate(after, axis=1).astype(f32)
+        normed, scaling = norm_rows(x0[spot, :].astype(f32))
+        upstream = total * gain[...]
+        mean_up = jnp.mean(upstream, axis=1, keepdims=True)
+        mean_both = jnp.mean(upstream * normed, axis=1, keepdims=True)
+        dx = res[spot, :] + scaling * (upstream - mean_up - normed * mean_both)
+        tg[spot, :] = dx.astype(low)
+        for i, value in enumerate((total * normed, total)):
+            totals[i] = totals[i] + jnp.sum(value, axis=0, keepdims=True)
+    for i in range(2):
+        stats[i : i + 1, :] = totals[i]
+    for stage in range(2):
+        spread(stage).wait_recv()
+        spread(2 + stage).start()
+    for q in range(n_col):
+        hop(0, q).wait_recv()
+        hop2(q).wait_recv()
+        value = ga[part, at(q), :].astype(f32) + first[0, at(q), :].astype(f32)
+        a_sum[at(q), :] = (value + second[at(q), :].astype(f32)).astype(low)
+    value = line.total(hidden_total(0))
+    value = with_other_bits(value, extra, 1, x_s, x_r, by_bit[2:])
+    q_own[...] = value.astype(low)
+    spread(2).wait_recv()
+    spread(3).wait_recv()
+    for stage in range(4):
+        spread(stage).wait_send()
+    line.end()
+    for q in range(n_col):
+        hop(0, q).wait_send()
+        hop(1, q).wait_send()
+        hop2(q).wait_send()
+    for t in range(cuts):
+        exchange(away_b, came_b, b_s, b_r, t).wait_send()
+        exchange(away_l, came_l, c_s, c_r, t).wait_send()
+
+    @pl.when(col > 0)
+    def _():
+        da_hop.wait_send()
+
+
+def fold(dq, dk, dv, a_ext, dy, o, weights, res, x0, gain, ga, riding, n_col, n_dp):
+    sd, vm, dma = jax.ShapeDtypeStruct, pltpu.VMEM, pltpu.SemaphoreType.DMA
+    rows, deep = x0.shape
+    wide = deep // n_col
+    columns, hidden = ga.shape[2], riding[0].shape[2]
+    others, cuts = n_col - 1, rows // CUT
+    more = max(n_dp.bit_length() - 3, 1)
+    by_rows = vm((rows, deep), low)
+    return pl.pallas_call(
+        functools.partial(fold_kernel, n_col=n_col, n_dp=n_dp),
+        in_specs=[IN_VMEM] * 13 + [ANYWHERE] * 7,
+        out_specs=[IN_VMEM] * 7,
+        out_shape=[
+            sd(ga.shape, low),
+            sd((8, dq.shape[1]), f32),
+            sd((rows, deep), low),
+            sd((8, deep), f32),
+            sd((deep, columns), low),
+            sd((PARTS, wide, hidden), low),
+            sd((wide, hidden), low),
+        ],
+        scratch_shapes=[
+            vm((3, deep, hidden), low),
+            vm((wide, hidden), low),
+            vm((others, wide, hidden), low),
+            vm((others, wide, hidden), low),
+            vm((others, wide, hidden), low),
+            vm((others, wide, hidden), low),
+            vm((2, deep, columns), low),
+            vm((deep, columns), low),
+            vm((deep, columns), low),
+            by_rows, by_rows, by_rows, by_rows, by_rows,
+            vm((more, 3, wide, hidden), low),
+            dma((2, 3)), dma((2,)),
+            dma((2, others)), dma((2, others)),
+            dma((2, n_col)), dma((2, n_col)),
+            dma((n_col,)), dma((n_col,)),
+            dma((cuts,)), dma((cuts,)), dma((cuts,)), dma((cuts,)),
+            dma, dma,
+            dma((4,)), dma((4,)),
+            dma((2, more)), dma((2, more)),
+        ],
+        compiler_params=pltpu.CompilerParams(
+            collective_id=21, has_side_effects=True, vmem_limit_bytes=60 * 1024 * 1024
+        ),
+        name="fold",
+    )(dq, dk, dv, a_ext, dy, o, *weights, res, x0, gain[None], ga, *riding)
+
+
+def finish_kernel(
+    gb, a_sum, q_own, small, enc_in, tg,
+    full_a, full_b, hidden1, small_out, enc_out, tg_out,
+    first, second, mid, za, za_l, za_r, zb, zb_l, zb_r, enc_got, s_cur, s_got, s_z, extra,
+    f_s, f_r, m_s, m_r, za_s, za_t, zb_s, zb_t, g_s, g_r, e_s, e_r, s_s, s_r, sz_s, sz_r, t_s, t_r, x_s, x_r,
+    *, n_col, n_dp,
+):
+    dp, row, col = here()
+    parts = part_numbers()
+    part = parts[0]
+    by_bit = bit_partners(n_dp)
+    by_x, by_y = by_bit[:2]
+    twin = (dp, 1 - row, col)
+    cols = [(dp, row, lax.rem(col + k, n_col)) for k in range(n_col)]
+    meet([twin] + [(dp, 1 - row, c[2]) for c in cols[1:]] + cols[1:] + by_bit)
+    wide = gb.shape[1] // n_col
+    ks = range(1, n_col)
 
     def rows(q):
         return pl.ds(q * wide, wide)
 
-    def z_to(k):
-        return (dp, row, shift[k])
-
-    def hop(g, a, q):
-        src, way, away, _ = ways[g]
-        return remote(
-            src.at[away[a], rows(q), :], first.at[g, a, rows(q), :], f_s.at[g, a, q],
-            f_r.at[g, a, q], by_bit[way],
-        )
-
-    def hop2(g, q):
-        ref = mid.at[g, rows(q), :]
-        return remote(
-            ref, second.at[g, rows(q), :], m_s.at[g, q], m_r.at[g, q], by_bit[1 - ways[g][1]]
-        )
-
-    def z_hop(g, q):
-        return remote(zout.at[g, q - 1], zin.at[g, q - 1], z_s.at[g, q - 1], z_r.at[g, q - 1], z_to(q))
+    def hop(which, q):
+        to, side = (by_y, 2) if 2 * q < n_col else (by_x, 1)
+        source = gb.at[parts[3] if which else parts[side], rows(q), :]
+        return remote(source, first.at[which, rows(q), :], f_s.at[which, q], f_r.at[which, q], to)
+
+    def hop2(q):
+        to = by_x if 2 * q < n_col else by_y
+        return remote(mid.at[rows(q), :], second.at[rows(q), :], m_s.at[q], m_r.at[q], to)
+
+    turns = [q for pair in zip(range(n_col // 2), range(n_col // 2, n_col)) for q in pair]
+
+    line_a = LineSum(za, za_l, za_r, za_s, za_t, cols)
+    line_b = LineSum(zb, zb_l, zb_r, zb_s, zb_t, cols)
 
     def enc_hop(k):
         src = enc_in.at[:, pl.ds(k * wide, wide)]
-        return remote(src, enc_got.at[k - 1], e_s.at[k - 1], e_r.at[k - 1], z_to(k))
+        return remote(src, enc_got.at[k - 1], e_s.at[k - 1], e_r.at[k - 1], cols[k])
 
     partners = [twin] + by_bit
 
@@ -1283,7 +1643,9 @@
         return remote(s_cur.at[i], s_got.at[i], s_s.at[i], s_r.at[i], partners[i])
 
     def small_z(k):
-        return remote(s_cur.at[len(partners), k], s_z.at[k - 1], sz_s.at[k - 1], sz_r.at[k - 1], z_to(k))
+        return remote(
+            s_cur.at[len(partners), k], s_z.at[k - 1], sz_s.at[k - 1], sz_r.at[k - 1], cols[k]
+        )
 
     def small_step(i):
         if i == 0:
@@ -1307,168 +1669,120 @@
                 value = value + s_z[k - 1]
             small_out[...] = value
 
-    half = wide // 2
-
-    def plane_hop(full, g, stage, sends, recvs):
-        which, begin, size, way = [
-            (part, 0, wide, 0), (part, 0, wide, 1), (part_x, 0, half, 1), (part_y, half, half, 0),
-        ][stage]
-        ref = full.at[g, which, pl.ds(begin, size), :]
-        return remote(ref, ref, sends.at[g, stage], recvs.at[g, stage], by_bit[way])
-
-    def plane_to(g, stage):
-        return plane_hop(full, g, stage, g_s, g_r)
-
-    def hidden_plane(g, stage):
-        return plane_hop(hidden_full, g, stage, hg_s, hg_r)
+    spread_q = plane_copies(hidden1, part, parts, by_x, by_y, g_s.at[0], g_r.at[0])
+    spread_a = plane_copies(full_a, part, parts, by_x, by_y, g_s.at[1], g_r.at[1])
+    spread_b = plane_copies(full_b, part, parts, by_x, by_y, g_s.at[2], g_r.at[2])
 
     small_step(0)
-    for copy in loads + loads_own:
-        copy.start()
-    for q in range(n_col):
-        for g in range(2):
-            hop(g, 1, q).start()
-    for copy in loads:
-        copy.wait()
-    for k in ks:
-        h_out[k] = hidden_total(k).astype(low)
-        hidden_hop(k).start()
-    small_step(1)
-    done = 2
-    for q in range(n_col):
-        for g in range(2):
-            src, _, _, keep = ways[g]
-            hop(g, 1, q).wait_recv()
-            value = src[keep, rows(q), :].astype(f32) + first[g, 1, rows(q), :].astype(f32)
-            mid[g, rows(q), :] = value.astype(low)
-            hop2(g, q).start()
-            hop(g, 0, q).start()
-        if done < len(partners) + 2:
-            small_step(done)
-            done += 1
-    for copy in loads_own:
-        copy.wait()
-    value = load_own[...].astype(f32)
-    for k in ks:
-        value = value + load_got[k - 1].astype(f32)
-    hidden_full[0, part] = other_bits(value, 0, h_extra, hx_s, hx_r).astype(low)
-    hidden_plane(0, 0).start()
-    hidden_plane(0, 1).start()
-    for q in range(n_col):
-        for g in range(2):
-            src = ways[g][0]
-            hop(g, 0, q).wait_recv()
-            hop2(g, q).wait_recv()
-            value = src[part, rows(q), :].astype(f32) + first[g, 0, rows(q), :].astype(f32)
-            value = value + second[g, rows(q), :].astype(f32)
-            if q:
-                zout[g, q - 1] = value.astype(low)
-                z_hop(g, q).start()
-            else:
-                tot[g] = value
-        if done < len(partners) + 2:
-            small_step(done)
-            done += 1
+    for q in ks:
+        za[q - 1] = a_sum[rows(q), :]
+    hidden1[part] = q_own[...]
+    for i in range(1, len(partners)):
+        small_step(i)
+    for q in turns:
+        hop(1, q).start()
+    small_step(len(partners))
+    line_a.begin()
     send_home(tg, tg_out, t_s, t_r, n_col)
+    spread_q(0).start()
+    for q in turns:
+        hop(1, q).wait_recv()
+        keep = parts[1] if 2 * q < n_col else parts[2]
+        value = gb[keep, rows(q), :].astype(f32) + first[1, rows(q), :].astype(f32)
+        mid[rows(q), :] = value.astype(low)
+        hop2(q).start()
+        hop(0, q).start()
+    spread_q(1).start()
+    for q in list(ks) + [0]:
+        hop(0, q).wait_recv()
+        hop2(q).wait_recv()
+        value = gb[part, rows(q), :].astype(f32) + first[0, rows(q), :].astype(f32)
+        value = value + second[rows(q), :].astype(f32)
+        if q:
+            zb[q - 1] = value.astype(low)
+    line_b.begin()
+    line_a.go(2)
+    line_b.go(2)
+    line_a.go(1)
+    line_b.go(1)
     for k in ks:
         enc_hop(k).start()
-    value = hidden_total(0)
-    for k in ks:
-        hidden_hop(k).wait_recv()
-        value = value + h_in[k - 1].astype(f32)
-    hidden_full[1, part] = other_bits(value, 1, h_extra, hx_s, hx_r).astype(low)
-    hidden_plane(1, 0).start()
-    hidden_plane(1, 1).start()
-    for g in range(2):
-        for stage in range(2):
-            hidden_plane(g, stage).wait_recv()
-            hidden_plane(g, 2 + stage).start()
-    while done < len(partners) + 2:
-        small_step(done)
-        done += 1
-    for g in range(2):
-        value = tot[g]
-        for q in ks:
-            z_hop(g, q).wait_recv()
-            value = value + zin[g, q - 1].astype(f32)
-        value = other_bits(value, g, extra, x_s, x_r)
-        full[g, part] = value.astype(low)
-        plane_to(g, 0).start()
-        plane_to(g, 1).start()
-    for g in range(2):
-        for stage in range(2):
-            plane_to(g, stage).wait_recv()
-            plane_to(g, 2 + stage).start()
+    for stage in range(2):
+        spread_q(stage).wait_recv()
+        spread_q(2 + stage).start()
+    value_a = line_a.total(a_sum[rows(0), :].astype(f32))
+    value_a = with_other_bits(value_a, extra, 0, x_s, x_r, by_bit[2:])
+    full_a[part] = value_a.astype(low)
+    spread_a(0).start()
+    spread_a(1).start()
+    value = line_b.total(value)
+    value = with_other_bits(value, extra, 1, x_s, x_r, by_bit[2:])
+    full_b[part] = value.astype(low)
+    spread_b(0).start()
+    spread_b(1).start()
+    for stage in range(2):
+        spread_a(stage).wait_recv()
+        spread_a(2 + stage).start()
+    small_step(len(partners) + 1)
+    for stage in range(2):
+        spread_b(stage).wait_recv()
+        spread_b(2 + stage).start()
     value = enc_in[:, pl.ds(0, wide)].astype(f32)
     for k in ks:
         enc_hop(k).wait()
         value = value + enc_got[k - 1].astype(f32)
     enc_out[...] = value
-    for k in ks:
-        hidden_hop(k).wait_send()
-        small_z(k).wait_send()
-    for g in range(2):
-        for ways_out in (hidden_plane, plane_to):
-            ways_out(g, 2).wait_recv()
-            ways_out(g, 3).wait_recv()
-            for stage in range(4):
-                ways_out(g, stage).wait_send()
-        for q in range(n_col):
-            hop(g, 0, q).wait_send()
-            hop(g, 1, q).wait_send()
-            hop2(g, q).wait_send()
-            if q:
-                z_hop(g, q).wait_send()
+    for spread in (spread_q, spread_a, spread_b):
+        spread(2).wait_recv()
+        spread(3).wait_recv()
+        for stage in range(4):
+            spread(stage).wait_send()
+    for q in range(n_col):
+        hop(0, q).wait_send()
+        hop(1, q).wait_send()
+        hop2(q).wait_send()
+        if q:
+            small_z(q).wait_send()
+    line_a.end()
+    line_b.end()
     for i in range(len(partners)):
         small_hop(i).wait_send()
     wait_home(tg, tg_out, t_s, t_r, n_col)
 
 
-def finish(ga, gb, small, enc_in, tg, riding, n_col, n_dp):
-    parts, deep, columns = ga.shape
-    wide = deep // n_col
+def finish(gb, a_sum, q_own, small, enc_in, tg, n_col, n_dp):
+    parts, deep, columns = gb.shape
+    wide, hidden = q_own.shape
     steps = n_dp.bit_length()
     sd, vm, dma = jax.ShapeDtypeStruct, pltpu.VMEM, pltpu.SemaphoreType.DMA
     more = max(n_dp.bit_length() - 3, 1)
     others = n_col - 1
-    hidden = riding[0].shape[2]
     return pl.pallas_call(
         functools.partial(finish_kernel, n_col=n_col, n_dp=n_dp),
-        in_specs=[IN_VMEM] * 5 + [ANYWHERE] * 7,
-        out_specs=[IN_VMEM] * 4 + [ANYWHERE],
+        in_specs=[IN_VMEM] * 6,
+        out_specs=[IN_VMEM] * 5 + [ANYWHERE],
         out_shape=[
-            sd((2, parts, wide, columns), low),
-            sd((2, parts, wide, hidden), low),
+            sd((parts, wide, columns), low),
+            sd((parts, wide, columns), low),
+            sd((parts, wide, hidden), low),
             sd(small.shape[1:], f32),
             sd((enc_in.shape[0], wide), f32),
             sd((n_col * tg.shape[0], wide), low),
         ],
         scratch_shapes=[
-            vm((3, deep, hidden), low),
-            vm((wide, hidden), low),
-            vm((others, wide, hidden), low),
-            vm((n_col, wide, hidden), low),
-            vm((others, wide, hidden), low),
-            dma((2, 3)), dma((2,)),
-            dma((others,)), dma((others,)),
-            vm((2, more, 2, wide, hidden), low),
-            dma((2, more)), dma((2, more)),
-            dma((2, 4)), dma((2, 4)),
-            vm((2, 2, deep, columns), low),
             vm((2, deep, columns), low),
-            vm((2, deep, columns), low),
-            vm((2, others, wide, columns), low),
-            vm((2, others, wide, columns), low),
-            vm((2, wide, columns), f32),
+            vm((deep, columns), low),
+            vm((deep, columns), low),
+            *[vm((others, wide, columns), low)] * 6,
             vm((others, enc_in.shape[0], wide), low),
             vm((steps + 1,) + small.shape, f32),
             vm((steps,) + small.shape, f32),
             vm((others,) + small.shape[1:], f32),
-            vm((2, more, 2, wide, columns), low),
-            dma((2, 2, n_col)), dma((2, 2, n_col)),
+            vm((more, 3, wide, columns), low),
             dma((2, n_col)), dma((2, n_col)),
-            dma((2, others)), dma((2, others)),
-            dma((2, 4)), dma((2, 4)),
+            dma((n_col,)), dma((n_col,)),
+            *[dma((2, others))] * 4,
+            dma((3, 4)), dma((3, 4)),
             dma((others,)), dma((others,)),
             dma((steps,)), dma((steps,)),
             dma((others,)), dma((others,)),
@@ -1479,7 +1793,7 @@
             collective_id=20, has_side_effects=True, vmem_limit_bytes=VMEM
         ),
         name="finish",
-    )(ga, gb, small, enc_in, tg, *riding)
+    )(gb, a_sum, q_own, small, enc_in, tg)
 
 
 def column_grads_kernel(*refs, pairs, firsts):
@@ -1520,19 +1834,19 @@
     )(*firsts, *others)
 
 
-def unpack_kernel(sums, hidden, *outs):
-    size = sums.shape[3] // 4
-    for g in range(2):
+def unpack_kernel(full_a, full_b, hidden0, hidden1, *outs):
+    size = full_a.shape[2] // 4
+    for g, full in enumerate((full_a, full_b)):
         for i in range(4):
-            value = sums[g, 0, :, i * size : (i + 1) * size].astype(f32)
+            value = full[0, :, i * size : (i + 1) * size].astype(f32)
             outs[4 * g + i][...] = value if i < 3 else jnp.transpose(value)
-    outs[8][...] = hidden[0, 0].astype(f32)
-    outs[9][...] = jnp.transpose(hidden[1, 0].astype(f32))
-
-
-def unpack(sums, hidden):
-    _, parts, wide, columns = sums.shape
-    inner = hidden.shape[3]
+    outs[8][...] = hidden0[0].astype(f32)
+    outs[9][...] = jnp.transpose(hidden1[0].astype(f32))
+
+
+def unpack(full_a, full_b, hidden0, hidden1):
+    parts, wide, columns = full_a.shape
+    inner = hidden0.shape[2]
     size = columns // 4
     into = (pl.BlockSpec((wide, size), lambda p: (0, p)), (wide, parts * size))
     out_of = (pl.BlockSpec((size, wide), lambda p: (p, 0)), (parts * size, wide))
@@ -1544,14 +1858,14 @@
         unpack_kernel,
         grid=(parts,),
         in_specs=[
-            pl.BlockSpec((2, 1, wide, columns), lambda p: (0, p, 0, 0)),
-            pl.BlockSpec((2, 1, wide, inner), lambda p: (0, p, 0, 0)),
+            pl.BlockSpec((1, wide, x.shape[2]), lambda p: (p, 0, 0))
+            for x in (full_a, full_b, hidden0, hidden1)
         ],
         out_specs=[x[0] for x in layouts],
         out_shape=[jax.ShapeDtypeStruct(x[1], f32) for x in layouts],
         compiler_params=pltpu.CompilerParams(vmem_limit_bytes=VMEM),
         name="unpack",
-    )(sums, hidden)
+    )(full_a, full_b, hidden0, hidden1)
 
 
 def build_local(mesh):
@@ -1592,11 +1906,6 @@
         def along_col(w):
             return [from_col(own_columns(w, 0), k) for k in range(1, n_col)]
 
-        def whole_weight(w, parts):
-            return jnp.stack(
-                [jnp.concatenate([own_columns(w, j), p], axis=0) for j, p in enumerate(parts)]
-            )
-
         vec_f = jnp.stack([
             self_norm_gain, self_norm_bias, self_out_bias, cross_norm_gain, cross_norm_bias,
             cross_out_bias, hidden_norm_gain, hidden_norm_bias, hidden_out_bias,
@@ -1611,7 +1920,7 @@
             cross_query, cross_key, cross_value, cross_out,
         ]
         x_ext, enc, vectors, columns, *full = start(tokens, encoder, vec_f, vec_c, weights, n_col)
-        wq1, wk1, wv1, wo1 = full[:4]
+        wq1, wk1, wv1, wo1, wq2, wk2, wv2, wo2 = full
         (gain1, shift1, out_bias1, gain2, shift2, out_bias2, gain3, shift3, out_bias3) = vectors[:9]
         size = self_query_bias.shape[0]
 
@@ -1647,42 +1956,46 @@
         k1 = mm(a_ext, wk1).astype(low)
         v1 = (mm(a_ext, wv1) + v_bias1).astype(low)
         dma = pltpu.SemaphoreType.DMA
-        o1, lse1, wq2, wk2, wv2, wo2 = attend(
-            q1, k1, v1, query_ids, key_ids, True,
-            functools.partial(cross_rider, n_col=n_col),
-            weights[4:] + full[4:],
-            [(x.shape, low) for x in full[:4]],
-            [dma((4, 4)), dma((4, 4)), dma((4, 2))],
-            14,
-        )
+        dma = pltpu.SemaphoreType.DMA
+        o1, lse1 = attend(q1, k1, v1, query_ids, key_ids, True)
         pieces1, o1 = lax.optimization_barrier((pieces1, o1))
         rest1 = jnp.concatenate(pieces1, axis=0)
         near1 = [across(rest1, 1), across(rest1, 2)]
-        pieces2, o1 = lax.optimization_barrier((pieces2, o1))
+        x1, c = junction("forward", [("nn", o1, wo1)], [x0, out_bias1, gain2, shift2], 3)
+
+        pieces2, c = lax.optimization_barrier((pieces2, c))
         rest2 = jnp.concatenate(pieces2, axis=0)
         near2 = [across(rest2, 1), across(rest2, 2)]
-        x1, c = junction("forward", [("nn", o1, wo1)], [x0, out_bias1, gain2, shift2], 3)
-
-        near1, c = lax.optimization_barrier((near1, c))
-        half = rest1.shape[0] // 2
-        far1 = [across(near1[0][:half], 2), across(near1[1][half:], 1)]
         q2 = (mm(c, wq2) + q_bias2).astype(low) * scale
         k2 = mm(enc, wk2).astype(low)
         v2 = (mm(enc, wv2) + v_bias2).astype(low)
-        o2, lse2 = attend(q2, k2, v2, query_ids, src_ids, False)
-        near2, o2 = lax.optimization_barrier((near2, o2))
-        far2 = [across(near2[0][:half], 2), across(near2[1][half:], 1)]
+        o2, lse2, dz = attend(
+            q2, k2, v2, query_ids, src_ids, False,
+            functools.partial(cotangent_rider, n_col=n_col), [cotangent],
+            [((2, chunk, n_col * wide), low)], [dma((n_col,))] * 4, 14,
+        )
+        near1, near2, o2 = lax.optimization_barrier((near1, near2, o2))
+        far1 = across(near1[0], 2)
+        far2 = across(near2[1], 1)
         x2, f = junction("forward", [("nn", o2, wo2)], [x1, out_bias2, gain3, shift3], 4)
-        w1 = whole_weight(hidden_in, [rest1, *near1, jnp.concatenate(far1)])
-        w2 = whole_weight(hidden_out_t, [rest2, *near2, jnp.concatenate(far2)])
-
-        act, slope, rows_out, dz = hidden_forward(
-            f, w1, hidden_bias, w2, x2, out_bias3, cotangent, n_col, 5
+        rests1, rests2 = [rest1, *near1], [rest2, *near2]
+        act0, slope0, part_sum = hidden_forward(
+            f, hidden_bias[:1], hidden_in, hidden_out_t, rests1[:1], rests2[:1], (0,), 0
+        )
+        rests1, rests2 = [rest1, *near1, far1], [rest2, *near2, far2]
+        act1, slope1, part_sum = hidden_forward(
+            f, hidden_bias[1:3], hidden_in, hidden_out_t, rests1[1:3], rests2[1:3], (1, 2), 0,
+            sum_in=part_sum,
+        )
+        act2, slope2, rows_out = hidden_forward(
+            f, hidden_bias[3:], hidden_in, hidden_out_t, rests1[3:], rests2[3:], (3,), 5,
+            sum_in=part_sum, x=x2, bias=out_bias3,
         )
         dz = dz.reshape(span, -1)
 
         g1, g2, hidden_bias_grad, df, got_a, got_b, layer_out = hidden_backward(
-            dz, f, w1, w2, act, slope, rows_out, n_col, 11
+            dz, f, hidden_in, hidden_out_t, rests1, rests2, [act0, act1, act2],
+            [slope0, slope1, slope2], ((0, 0), (1, 0), (1, 1), (2, 0)), rows_out, n_col, 11,
         )
         inner = g1.shape[2]
         half = g1.shape[1] // 2
@@ -1705,6 +2018,7 @@
         enc_back = junction("sum", [("nt", dk2, wk2), ("nt", dv2, wv2)], [], 7)
         dx1, dy, stats2 = junction("backward", [("nt", dq2, wq2)], [dx2, x1, gain2], 8)
 
+        cross_grads, enc_back, dy = lax.optimization_barrier((cross_grads, enc_back, dy))
         do = mm_nt(dy, wo1).astype(low)
         (
             dq1, dk1, dv1, near_a, near_b, far_back_a, far_back_b, z_got, own1
@@ -1721,16 +2035,9 @@
             ],
             13,
         )
-        da_before = junction("sum", [("nt", dk1[:WIN], wk1), ("nt", dv1[:WIN], wv1)], [], 9)
-        da_after = lax.ppermute(da_before, "col", [(i + 1, i) for i in range(n_col - 1)])
-        self_grads, self_columns = column_grads_of(
-            [a_ext, dy], [(0, WIN), (0, 0), (0, 0), (1, 0)], [dq1, dk1, dv1, o1]
-        )
-        x0_grad, stats1 = junction(
-            "last",
-            [("nt", dq1, wq1), ("nt", dk1[WIN:], wk1), ("nt", dv1[WIN:], wv1)],
-            [dx1, x0, gain1, da_after],
-            10,
+        gb, self_columns, x0_grad, stats1, a_sum, hidden0, q_own = fold(
+            dq1, dk1, dv1, a_ext, dy, o1, [wq1, wk1, wv1], dx1, x0, gain1, cross_grads,
+            [g2, near_a, near_b, far_back_a, far_back_b, z_got, own1], n_col, n_dp,
         )
 
         feature_grads = jnp.concatenate([
@@ -1755,12 +2062,10 @@
             ],
             axis=2,
         )
-        sums, hidden_sums, small, encoder_grad, tokens_grad = finish(
-            cross_grads, self_grads, small, enc_back, x0_grad,
-            [g2, near_a, near_b, far_back_a, far_back_b, z_got, own1],
-            n_col, n_dp,
+        full_a, full_b, hidden1, small, encoder_grad, tokens_grad = finish(
+            gb, a_sum, q_own, small, enc_back, x0_grad, n_col, n_dp
         )
-        grads = unpack(sums, hidden_sums)
+        grads = unpack(full_a, full_b, hidden0, hidden1)
         tokens_grad = tokens_grad.astype(f32)
         feature_grads = small[:, :wide]
         column_grads = small[:, wide:].reshape(-1)

time: 793 us -> 797 us (level)
  Pallas kernels: 621 us -> 647 us
  waiting for transfers between devices: 13.4 us -> 39.2 us
  other arithmetic: 24.7 us -> 5.15 us
  local copies, waits for them, and re-layouts: 59.6 us -> 42.7 us
  starting transfers between devices: 32.8 us -> 24.6 us
    pallas_call x3 -> x6, Pallas kernels: 118 us -> 207 us  [the longest x1 76.4 us: fold(): pl.pallas_call(functools.partial(fold_kernel, n_col=n_col, n_dp=n_dp), in...]
    pallas_call x1, Pallas kernels: 156 us -> 116 us  [finish(): pl.pallas_call(functools.partial(finish_kernel, n_col=n_col, n_dp=n_dp),...]
    another operation x8 -> x0, other arithmetic: 20.2 us -> none  [whole_weight(): jnp.stack([jnp.concatenate([own_columns(w, j), p], axis=0) for j, p in en...]
    pallas_call x7 -> x5, Pallas kernels: 66.1 us -> 47.8 us  [junction(): pl.pallas_call(functools.partial(junction_kernel, kinds=kinds, mode=mode)...]
    ppermute x8 -> x6, waiting for transfers between devices: 6.6 us -> 21.9 us  [across(): return lax.ppermute(x, 'dp', [(i, i ^ bit) for i in range(n_dp)])]
    pallas_call x2 -> x1, Pallas kernels: 23.2 us -> 10.2 us  [column_grads_of(): pl.pallas_call(functools.partial(column_grads_kernel, pairs=pairs, firsts...]
    slice x6 -> x0, local copies, waits for them, and re-layouts: 12.9 us -> none  [the longest x2 4.2 us: local(): far1 = [across(near1[0][:half], 2), across(near1[1][half:], 1)]]
    ppermute x6, waiting for transfers between devices: 6.82 us -> 17.3 us  [from_col(): return lax.ppermute(x, 'col', [(i, (i - k) % n_col) for i in range(n_col)])]
  transfers between devices with their start and end apart: 15 -> 12, of which waited for: 5 -> 5; matrix products, arithmetic and copies ran while one was open for 9% -> 6% of each run, Pallas kernels for 15% -> 16%
where the time goes in v5:
time: 797 us; the launch traced here: 788 us
  Pallas kernels  647 us (81%)
  local copies, waits for them, and re-layouts  42.7 us (5%)
  waiting for transfers between devices  39.2 us (5%)
  matrix products  27.8 us (3%)
  starting transfers between devices  24.6 us (3%)
    pallas_call x1, Pallas kernels, finish(): pl.pallas_call(functools.partial(finish_kernel, n_col=n_col, n_dp=n_dp),...  116 us
    pallas_call x2, Pallas kernels, attend_back(): pl.pallas_call(functools.partial(attend_back_kernel, span=span, windowed=...  112 us
    pallas_call x1, Pallas kernels, start(): pl.pallas_call(functools.partial(start_kernel, n_col=n_col), in_specs=[IN...  85.6 us
    pallas_call x1, Pallas kernels, fold(): pl.pallas_call(functools.partial(fold_kernel, n_col=n_col, n_dp=n_dp), in...  76.4 us
    pallas_call x1, Pallas kernels, hidden_backward(): pl.pallas_call(functools.partial(hidden_back_kernel, n_col=n_col, places=...  66.1 us
    pallas_call x2, Pallas kernels, attend(): pl.pallas_call(functools.partial(attend_kernel, span=span, windowed=windo...  59.3 us
    pallas_call x3, Pallas kernels, hidden_forward(): pl.pallas_call(functools.partial(hidden_kernel, numbers=numbers, opening=...  57.1 us
    pallas_call x5, Pallas kernels, junction(): pl.pallas_call(functools.partial(junction_kernel, kinds=kinds, mode=mode)...  47.8 us
  transfers between devices with their start and end apart: 12, of which 5 were waited for; matrix products, arithmetic and copies ran while one was open for 6% of the time, Pallas kernels for 16%

profile of v5, /device:TPU:8, one launch (start us, length us, event | category | flops | bytes accessed | tf_op | source)
XLA Modules:
  0.0 787.9 jit_solution(15550377698934638332)
XLA Ops:
  4.6 1.5 stack.63
  6.8 85.6 %start.1 = (bf16[2,512,1024]{2,1,0:T(8,128)(2,1)}, bf16[1024,1024]{1,0:T(8,128)(2,1)}, f32[16,1024]{1,0:T(8,128)}, f32[4,16,128]{2,1,0:T(8,128)}, bf16[1024,512]...) custom-call(bf16[2048,256]{1,0:T(8,128)(2,1)} %tokens.1, ...), custom_call_target="tpu_custom_call" | custom-call | tf_op jit(solution)/shard_map/start/pallas_call | solution.py:1083
  92.3 1.9 constant_dynamic-slice_fusion.4
  94.2 2.3 collective-permute-start.3
  96.5 9.4 %collective-permute-start.4 = (bf16[256,1024]{1,0:T(8,128)(2,1)}, bf16[256,1024]{1,0:T(8,128)(2,1)}, u32[]{:S(2)}, u32[]{:S(2)}) collective-permute-start(bf16[256,1024]{1,0:T(8,128)(2,1)} %constant_dynamic-slice_fusion.4), channel_id=1, source_target_pairs={{0,2},{1,3},{2,0},{3,1},{4,6},{5,7},{6,4},{7,5},{8,10},{9,11},{10,... | collective-permute-start | bytes 1572872 | tf_op jit(solution)/shard_map/ppermute | solution.py:1875
  105.9 2.9 collective-permute-start.5
  108.8 1.9 fusion.10
  110.7 2.9 copy.67
  113.6 9.3 %enter.1 = bf16[2,1024,1024]{2,1,0:T(8,128)(2,1)} custom-call(bf16[2,512,1024]{2,1,0:T(8,128)(2,1)} %get-tuple-element.132.x_ref, f32[1,1024]{1,0:T(1,128)} %get-tuple-element.243.gain, f32[1,1024]{1,0:T(1,128)} %get-tuple-element.242.shift), custom_call_target="tpu_custom_call" | custom-call | tf_op jit(solution)/shard_map/enter/pallas_call | solution.py:1136
  123.8 1.5 collective-permute-start.1
  125.5 4.0 fusion.5.refs_0_
  129.5 3.7 add_convert_fusion.refs_2_
  133.2 3.7 convolution_convert_fusion.refs_1_
  136.9 2.3 collective-permute-start.2
  141.0 27.6 %attend.2 = (bf16[1024,512]{1,0:T(8,128)(2,1)}, f32[4,8,1024]{2,1,0:T(8,128)}) custom-call(bf16[1024,512]{1,0:T(8,128)(2,1)} %fusion.5.refs_0_, bf16[2048,512]{1,0:T(8,128)(2,1)} %convolution_convert_fusion.refs_1_, bf16[2048,512]{1,0:T(8,128)(2,1)} %add_convert_fusion.refs_2_, s32[1024,1]{1,0:T(8,128)} %copy.68.refs_3_, s32[1,2048]{1,0:T(1,128)} %bitcast.111), custom_call_target="tpu_custom_call" | custom-call | tf_op jit(solution)/shard_map/attend/pallas_call | solution.py:196
  169.7 5.0 collective-permute-done.5
  174.7 9.4 %junction_forward.2 = (f32[512,1024]{1,0:T(8,128)}, bf16[1024,1024]{1,0:T(8,128)(2,1)}) custom-call(bf16[1024,512]{1,0:T(8,128)(2,1)} %get-tuple-element.142.refs_0_.refs_4_.o, bf16[512,1024]{1,0:T(8,128)(2,1)} %get-tuple-element.143.refs_1_, bf16[512,1024]{1,0:T(8,128)(2,1)} %slice_bitcast_fusion.refs_2_.x0, f32[1,1024]{1,0:T(1,128)} %get-tuple-element.241.refs_3_, ...), custom_call_target="tpu_custom_call" | custom-call | tf_op jit(solution)/shard_map/junction_forward/pallas_call | solution.py:1248
  184.1 1.9 collective-permute-done.1
  186.0 10.4 %collective-permute-done.2 = bf16[256,1024]{1,0:T(8,128)(2,1)S(1)} collective-permute-done((bf16[256,1024]{1,0:T(8,128)(2,1)}, bf16[256,1024]{1,0:T(8,128)(2,1)S(1)}, u32[]{:S(2)}, u32[]{:S(2)}) %collective-permute-start.2) | collective-permute-done | bytes 524320 | tf_op jit(solution)/shard_map/ppermute | solution.py:1875
  196.5 1.6 collective-permute-start.8
  198.1 1.5 collective-permute-start.9
  204.8 4.3 convolution_convert_fusion.3.refs_1_
  209.1 2.2 add_convert_fusion.1.refs_2_
  211.4 2.2 fusion.8.refs_0_
  213.6 31.7 %attend.3 = (bf16[1024,512]{1,0:T(8,128)(2,1)}, f32[4,8,1024]{2,1,0:T(8,128)}, bf16[2,512,1024]{2,1,0:T(8,128)(2,1)}) custom-call(bf16[1024,512]{1,0:T(8,128)(2,1)} %fusion.8.refs_0_, bf16[1024,512]{1,0:T(8,128)(2,1)} %convolution_convert_fusion.3.refs_1_, bf16[1024,512]{1,0:T(8,128)(2,1)} %add_convert_fusion.1.refs_2_, s32[1024,1]{1,0:T(8,128)} %copy.68.refs_3_, ...), custom_call_target="tpu_custom_call" | custom-call | tf_op jit(solution)/shard_map/attend/pallas_call | solution.py:196
  245.3 20.7 %collective-permute-done.6.refs_4_.refs_1_ = bf16[768,1024]{1,0:T(8,128)(2,1)} collective-permute-done((bf16[768,1024]{1,0:T(8,128)(2,1)S(1)}, bf16[768,1024]{1,0:T(8,128)(2,1)}, u32[]{:S(2)}, u32[]{:S(2)}) %collective-permute-start.6) | collective-permute-done | bytes 1572896 | tf_op jit(solution)/shard_map/ppermute | solution.py:1878
  267.2 1.5 collective-permute-start.10
  270.3 1.4 copy.73.refs_7_
  272.9 3.9 copy.71.dzt_ref
  276.8 9.7 %junction_forward.3 = (f32[512,1024]{1,0:T(8,128)}, bf16[1024,1024]{1,0:T(8,128)(2,1)}) custom-call(bf16[1024,512]{1,0:T(8,128)(2,1)} %get-tuple-element.158.refs_0_.refs_4_.refs_6_, bf16[512,1024]{1,0:T(8,128)(2,1)} %get-tuple-element.159.refs_1_, f32[512,1024]{1,0:T(8,128)} %get-tuple-element.160.refs_2_.refs_3_, f32[1,1024]{1,0:T(1,128)} %get-tuple-element.238.refs_3_, ...), custom_call_target="tpu_custom_call" | custom-call | tf_op jit(solution)/shard_map/junction_forward/pallas_call | solution.py:1248
  286.6 3.9 copy.70
  290.5 15.0 %hidden_forward.3 = (bf16[1,1024,1024]{2,1,0:T(8,128)(2,1)}, bf16[1,1024,1024]{2,1,0:T(8,128)(2,1)}, f32[1024,1024]{1,0:T(8,128)}) custom-call(bf16[1024,1024]{1,0:T(8,128)(2,1)} %get-tuple-element.161.refs_0_, f32[1,1,1024]{2,1,0:T(1,128)} %get-tuple-element.271.refs_1_, bf16[256,4096]{1,0:T(8,128)(2,1)} %own1, bf16[256,4096]{1,0:T(8,128)(2,1)} %bitcast.97, ...), custom_call_target="tpu_custom_call" | custom-call | tf_op jit(solution)/shard_map/hidden_forward/pallas_call | solution.py:650
  305.5 24.3 %hidden_forward.4 = (bf16[2,1024,1024]{2,1,0:T(8,128)(2,1)}, bf16[2,1024,1024]{2,1,0:T(8,128)(2,1)}, f32[1024,1024]{1,0:T(8,128)}) custom-call(bf16[1024,1024]{1,0:T(8,128)(2,1)} %get-tuple-element.161.refs_0_, f32[2,1,1024]{2,1,0:T(1,128)} %pad_maximum_fusion.1.refs_1_, bf16[256,4096]{1,0:T(8,128)(2,1)} %own1, bf16[256,4096]{1,0:T(8,128)(2,1)} %bitcast.98, ...), custom_call_target="tpu_custom_call" | custom-call | tf_op jit(solution)/shard_map/hidden_forward/pallas_call | solution.py:650
  331.5 17.9 %hidden_forward.5 = (bf16[1,1024,1024]{2,1,0:T(8,128)(2,1)}, bf16[1,1024,1024]{2,1,0:T(8,128)(2,1)}, bf16[512,1024]{1,0:T(8,128)(2,1)}) custom-call(bf16[1024,1024]{1,0:T(8,128)(2,1)} %get-tuple-element.161.refs_0_, f32[1,1,1024]{2,1,0:T(1,128)} %get-tuple-element.274.refs_1_, bf16[256,4096]{1,0:T(8,128)(2,1)} %own1, bf16[256,4096]{1,0:T(8,128)(2,1)} %bitcast.99, ...), custom_call_target="tpu_custom_call" | custom-call | tf_op jit(solution)/shard_map/hidden_forward/pallas_call | solution.py:650
  349.4 66.1 %hidden_backward.1 = (bf16[4,1024,1024]{2,1,0:T(8,128)(2,1)}, bf16[4,1024,1024]{2,1,0:T(8,128)(2,1)}, f32[4,1,1024]{2,1,0:T(1,128)}, bf16[1024,1024]{1,0:T(8,128...) custom-call(bf16[1024,1024]{1,0:T(8,128)(2,1)} %bitcast.102, ...), custom_call_target="tpu_custom_call" | custom-call | tf_op jit(solution)/shard_map/hidden_backward/pallas_call | solution.py:790
  415.5 10.7 %junction_backward.2 = (f32[512,1024]{1,0:T(8,128)}, bf16[1024,1024]{1,0:T(8,128)(2,1)}, f32[8,1024]{1,0:T(8,128)}) custom-call(bf16[1024,1024]{1,0:T(8,128)(2,1)} %get-tuple-element.177.refs_0_, bf16[1024,1024]{1,0:T(8,128)(2,1)} %bitcast.103, f32[512,1024]{1,0:T(8,128)} %get-tuple-element.168.refs_7_.refs_2_, f32[1,1024]{1,0:T(1,128)} %get-tuple-element.237.refs_4_.refs_3_), custom_call_target="tpu_custom_call" | custom-call | tf_op jit(solution)/shard_map/junction_backward/pallas_call | solution.py:1248
  426.2 3.8 convolution_convert_fusion.2.refs_3_
  430.0 52.8 %attend_back.2 = (bf16[1024,512]{1,0:T(8,128)(2,1)}, bf16[1024,512]{1,0:T(8,128)(2,1)}, bf16[1024,512]{1,0:T(8,128)(2,1)}, bf16[512,1024]{1,0:T(8,128)(2,1)}, bf...) custom-call(bf16[1024,512]{1,0:T(8,128)(2,1)} %fusion.8.refs_0_, ...), custom_call_target="tpu_custom_call" | custom-call | tf_op jit(solution)/shard_map/attend_back/pallas_call | solution.py:354
  482.9 6.8 junction_sum.1.enc_in
  489.7 10.2 %column_grads.1 = (bf16[4,1024,512]{2,1,0:T(8,128)(2,1)}, f32[8,512]{1,0:T(8,128)}) custom-call(bf16[1024,1024]{1,0:T(8,128)(2,1)} %get-tuple-element.145.refs_0_, bf16[1024,1024]{1,0:T(8,128)(2,1)} %get-tuple-element.147.refs_1_, bf16[1024,1024]{1,0:T(8,128)(2,1)} %get-tuple-element.178.refs_2_, bf16[1024,512]{1,0:T(8,128)(2,1)} %get-tuple-element.184.refs_3_.refs_0_, ...), custom_call_target="tpu_custom_call" | custom-call | tf_op jit(solution)/shard_map/column_grads/pallas_call | solution.py:1819
  499.9 11.2 %junction_backward.3 = (f32[512,1024]{1,0:T(8,128)}, bf16[1024,1024]{1,0:T(8,128)(2,1)}, f32[8,1024]{1,0:T(8,128)}) custom-call(bf16[1024,512]{1,0:T(8,128)(2,1)} %get-tuple-element.184.refs_3_.refs_0_, bf16[1024,512]{1,0:T(8,128)(2,1)} %get-tuple-element.146.refs_1_, f32[512,1024]{1,0:T(8,128)} %get-tuple-element.188.refs_2_, ...), custom_call_target="tpu_custom_call" | custom-call | tf_op jit(solution)/shard_map/junction_backward/pallas_call | solution.py:1248
  512.7 3.8 convolution_convert_fusion.1.refs_3_
  516.5 58.7 %attend_back.3 = (bf16[1024,512]{1,0:T(8,128)(2,1)}, bf16[2048,512]{1,0:T(8,128)(2,1)}, bf16[2048,512]{1,0:T(8,128)(2,1)}, bf16[512,1024]{1,0:T(8,128)(2,1)}, bf...) custom-call(bf16[1024,512]{1,0:T(8,128)(2,1)} %fusion.5.refs_0_, ...), custom_call_target="tpu_custom_call" | custom-call | tf_op jit(solution)/shard_map/attend_back/pallas_call | solution.py:354
  575.3 76.4 %fold.1 = (bf16[4,1024,512]{2,1,0:T(8,128)(2,1)}, f32[8,512]{1,0:T(8,128)}, bf16[512,1024]{1,0:T(8,128)(2,1)}, f32[8,1024]{1,0:T(8,128)}, bf16[1024,512]{1,0:T(8...) custom-call(bf16[1024,512]{1,0:T(8,128)(2,1)} %get-tuple-element.196.dq, ...), custom_call_target="tpu_custom_call" | custom-call | tf_op jit(solution)/shard_map/fold/pallas_call | solution.py:1560
  655.0 115.7 %finish.1 = (bf16[4,256,512]{2,1,0:T(8,128)(2,1)}, bf16[4,256,512]{2,1,0:T(8,128)(2,1)}, bf16[4,256,1024]{2,1,0:T(8,128)(2,1)}, f32[16,384]{1,0:T(8,128)}, f32[5...) custom-call(bf16[4,1024,512]{2,1,0:T(8,128)(2,1)} %get-tuple-element.207.gb, bf16[1024,512]{1,0:T(8,128)(2,1)} %get-tuple-element.208.a_sum, ...), custom_call_target="tpu_custom_call" | custom-call | tf_op jit(solution)/shard_map/finish/pallas_call | solution.py:1760
  770.7 1.6 fusion.12
  774.9 2.7 convert_element_type.67
  777.6 7.8 unpack.1
  (117 shorter events, 29.0 us)
Async XLA Ops:
  94.2 42.7 %collective-permute-start.3 = (bf16[256,1024]{1,0:T(8,128)(2,1)}, bf16[256,1024]{1,0:T(8,128)(2,1)}, u32[]{:S(2)}, u32[]{:S(2)}) collective-permute-start(bf16[256,1024]{1,0:T(8,128)(2,1)} %constant_dynamic-slice_fusion.4), channel_id=1, source_target_pairs={{0,3},{1,0},{2,1},{3,2},{4,7},{5,4},{6,5},{7,6},{8,11},{9,8},{10,9... | collective-permute-start | bytes 1572872 | tf_op jit(solution)/shard_map/ppermute | solution.py:1875
  96.5 73.2 %collective-permute-start.4 = (bf16[256,1024]{1,0:T(8,128)(2,1)}, bf16[256,1024]{1,0:T(8,128)(2,1)}, u32[]{:S(2)}, u32[]{:S(2)}) collective-permute-start(bf16[256,1024]{1,0:T(8,128)(2,1)} %constant_dynamic-slice_fusion.4), channel_id=1, source_target_pairs={{0,2},{1,3},{2,0},{3,1},{4,6},{5,7},{6,4},{7,5},{8,10},{9,11},{10,... | collective-permute-start | bytes 1572872 | tf_op jit(solution)/shard_map/ppermute | solution.py:1875
  105.9 68.8 %collective-permute-start.5 = (bf16[256,1024]{1,0:T(8,128)(2,1)}, bf16[256,1024]{1,0:T(8,128)(2,1)}, u32[]{:S(2)}, u32[]{:S(2)}) collective-permute-start(bf16[256,1024]{1,0:T(8,128)(2,1)} %constant_dynamic-slice_fusion.4), channel_id=1, source_target_pairs={{0,1},{1,2},{2,3},{3,0},{4,5},{5,6},{6,7},{7,4},{8,9},{9,10},{10,1... | collective-permute-start | bytes 1572872 | tf_op jit(solution)/shard_map/ppermute | solution.py:1875
  113.6 9.3 %copy-start = (bf16[4096,256]{0,1:T(8,128)(2,1)}, bf16[4096,256]{0,1:T(8,128)(2,1)S(1)}, u32[]{:S(2)}) copy-start(bf16[4096,256]{0,1:T(8,128)(2,1)S(1)} %copy.67) | copy-start | bytes 6291460
  113.6 11.6 %copy-start.21 = (f32[4,16,128]{2,1,0:T(8,128)S(1)}, f32[4,16,128]{2,1,0:T(8,128)}, u32[]{:S(2)}) copy-start(f32[4,16,128]{2,1,0:T(8,128)} %get-tuple-element.137) | copy-start | bytes 98308
  113.6 11.7 %copy-start.24 = (s32[1,4]{1,0:T(1,128)S(1)}, s32[1,4]{1,0:T(1,128)}, u32[]{:S(2)}) copy-start(s32[1,4]{1,0:T(1,128)} %param.32) | copy-start | bytes 52
  113.6 11.8 %copy-start.9 = (bf16[1024,512]{1,0:T(8,128)(2,1)S(1)}, bf16[1024,512]{1,0:T(8,128)(2,1)}, u32[]{:S(2)}) copy-start(bf16[1024,512]{1,0:T(8,128)(2,1)} %get-tuple-element.136.wq) | copy-start | bytes 3145732
  123.8 60.3 %collective-permute-start = (bf16[256,1024]{1,0:T(8,128)(2,1)}, bf16[256,1024]{1,0:T(8,128)(2,1)S(1)}, u32[]{:S(2)}, u32[]{:S(2)}) collective-permute-start(bf16[256,1024]{1,0:T(8,128)(2,1)} %constant_dynamic-slice_fusion.5), channel_id=1, source_target_pairs={{0,3},{1,0},{2,1},{3,2},{4,7},{5,4},{6,5},{7,6},{8,11},{9,8},{10,9... | collective-permute-start | bytes 1572872 | tf_op jit(solution)/shard_map/ppermute | solution.py:1875
  123.8 62.2 %collective-permute-start.1 = (bf16[256,1024]{1,0:T(8,128)(2,1)}, bf16[256,1024]{1,0:T(8,128)(2,1)S(1)}, u32[]{:S(2)}, u32[]{:S(2)}) collective-permute-start(bf16[256,1024]{1,0:T(8,128)(2,1)} %constant_dynamic-slice_fusion.5), channel_id=1, source_target_pairs={{0,2},{1,3},{2,0},{3,1},{4,6},{5,7},{6,4},{7,5},{8,10},{9,11},{10,... | collective-permute-start | bytes 1572872 | tf_op jit(solution)/shard_map/ppermute | solution.py:1875
  125.5 4.0 copy-start.1
  125.5 4.0 copy-start.11
  129.5 3.7 copy-start.10
  136.9 59.5 %collective-permute-start.2 = (bf16[256,1024]{1,0:T(8,128)(2,1)}, bf16[256,1024]{1,0:T(8,128)(2,1)S(1)}, u32[]{:S(2)}, u32[]{:S(2)}) collective-permute-start(bf16[256,1024]{1,0:T(8,128)(2,1)} %constant_dynamic-slice_fusion.5), channel_id=1, source_target_pairs={{0,1},{1,2},{2,3},{3,0},{4,5},{5,6},{6,7},{7,4},{8,9},{9,10},{10,1... | collective-permute-start | bytes 1572872 | tf_op jit(solution)/shard_map/ppermute | solution.py:1875
  139.4 29.2 %copy-start.19 = (s32[1024]{0:T(1024)}, s32[1024]{0:T(1024)S(1)}, u32[]{:S(2)}) copy-start(s32[1024]{0:T(1024)S(1)} %pad_dynamic-slice_fusion.2) | copy-start | bytes 12292
  141.0 27.6 %copy-start.6 = (bf16[2,512,1024]{2,1,0:T(8,128)(2,1)S(1)}, bf16[2,512,1024]{2,1,0:T(8,128)(2,1)}, u32[]{:S(2)}) copy-start(bf16[2,512,1024]{2,1,0:T(8,128)(2,1)} %get-tuple-element.132.x_ref) | copy-start | bytes 6291460
  196.5 7.5 copy-start.25
  196.5 12.6 %copy-start.2 = (bf16[768,1024]{1,0:T(8,128)(2,1)}, bf16[768,1024]{1,0:T(8,128)(2,1)S(1)}, u32[]{:S(2)}) copy-start(bf16[768,1024]{1,0:T(8,128)(2,1)S(1)} %constant_dynamic-update-slice_fusion.4.refs_5_.refs_4_) | copy-start | bytes 4718596
  196.5 48.8 %collective-permute-start.8 = (bf16[768,1024]{1,0:T(8,128)(2,1)S(1)}, bf16[768,1024]{1,0:T(8,128)(2,1)}, u32[]{:S(2)}, u32[]{:S(2)}) collective-permute-start(bf16[768,1024]{1,0:T(8,128)(2,1)S(1)} %constant_dynamic-update-slice_fusion.4.refs_5_.refs_4_), channel_id=1, source_target_pairs={{0,8},{8,0},{16,24},{24,16},{1,9},{9,1},{17,25},{25,17},{2,10},{10... | collective-permute-start | bytes 4718600 | tf_op jit(solution)/shard_map/ppermute | solution.py:1878
  198.1 47.2 %collective-permute-start.9 = (bf16[768,1024]{1,0:T(8,128)(2,1)S(1)}, bf16[768,1024]{1,0:T(8,128)(2,1)}, u32[]{:S(2)}, u32[]{:S(2)}) collective-permute-start(bf16[768,1024]{1,0:T(8,128)(2,1)S(1)} %constant_dynamic-update-slice_fusion.4.refs_5_.refs_4_), channel_id=1, source_target_pairs={{0,16},{8,24},{16,0},{24,8},{1,17},{9,25},{17,1},{25,9},{2,18},{10... | collective-permute-start | bytes 4718600 | tf_op jit(solution)/shard_map/ppermute | solution.py:1878
  202.9 6.2 copy-start.3
  202.9 63.2 %collective-permute-start.6 = (bf16[768,1024]{1,0:T(8,128)(2,1)S(1)}, bf16[768,1024]{1,0:T(8,128)(2,1)}, u32[]{:S(2)}, u32[]{:S(2)}) collective-permute-start(bf16[768,1024]{1,0:T(8,128)(2,1)S(1)} %constant_dynamic-update-slice_fusion.1.refs_4_.refs_0_), channel_id=1, source_target_pairs={{0,8},{8,0},{16,24},{24,16},{1,9},{9,1},{17,25},{25,17},{2,10},{10... | collective-permute-start | bytes 4718600 | tf_op jit(solution)/shard_map/ppermute | solution.py:1878
  203.5 63.8 %collective-permute-start.7 = (bf16[768,1024]{1,0:T(8,128)(2,1)S(1)}, bf16[768,1024]{1,0:T(8,128)(2,1)}, u32[]{:S(2)}, u32[]{:S(2)}) collective-permute-start(bf16[768,1024]{1,0:T(8,128)(2,1)S(1)} %constant_dynamic-update-slice_fusion.1.refs_4_.refs_0_), channel_id=1, source_target_pairs={{0,16},{8,24},{16,0},{24,8},{1,17},{9,25},{17,1},{25,9},{2,18},{10... | collective-permute-start | bytes 4718600 | tf_op jit(solution)/shard_map/ppermute | solution.py:1878
  204.8 4.3 copy-start.7
  204.8 4.3 copy-start.12
  209.1 2.3 copy-start.8
  209.1 2.2 copy-start.16
  213.6 55.7 %copy-start.20 = (s32[1024]{0:T(1024)S(1)}, s32[1024]{0:T(1024)}, u32[]{:S(2)}) copy-start(s32[1024]{0:T(1024)} %convert_reduce_fusion.1) | copy-start | bytes 12292
  213.6 56.7 %copy-start.18 = (s32[2048]{0:T(1024)S(1)}, s32[2048]{0:T(1024)}, u32[]{:S(2)}) copy-start(s32[2048]{0:T(1024)} %pad_dynamic-slice_fusion.3) | copy-start | bytes 24580
  267.2 62.6 %collective-permute-start.10 = (bf16[768,1024]{1,0:T(8,128)(2,1)}, bf16[768,1024]{1,0:T(8,128)(2,1)S(1)}, u32[]{:S(2)}, u32[]{:S(2)}) collective-permute-start(bf16[768,1024]{1,0:T(8,128)(2,1)} %collective-permute-done.6.refs_4_.refs_1_), channel_id=1, source_target_pairs={{0,16},{8,24},{16,0},{24,8},{1,17},{9,25},{17,1},{25,9},{2,18},{10... | collective-permute-start | bytes 4718600 | tf_op jit(solution)/shard_map/ppermute | solution.py:1878
  268.8 61.1 %collective-permute-start.11 = (bf16[768,1024]{1,0:T(8,128)(2,1)}, bf16[768,1024]{1,0:T(8,128)(2,1)S(1)}, u32[]{:S(2)}, u32[]{:S(2)}) collective-permute-start(bf16[768,1024]{1,0:T(8,128)(2,1)} %collective-permute-done.9.refs_7_.refs_6_), channel_id=1, source_target_pairs={{0,8},{8,0},{16,24},{24,16},{1,9},{9,1},{17,25},{25,17},{2,10},{10... | collective-permute-start | bytes 4718600 | tf_op jit(solution)/shard_map/ppermute | solution.py:1878
  329.8 1.1 copy-start.4
  329.8 1.7 copy-start.5
  415.5 10.7 %copy-start.13 = (bf16[512,1024]{1,0:T(8,128)(2,1)S(1)}, bf16[512,1024]{1,0:T(8,128)(2,1)}, u32[]{:S(2)}) copy-start(bf16[512,1024]{1,0:T(8,128)(2,1)} %get-tuple-element.159.refs_1_) | copy-start | bytes 3145732
  499.9 12.8 %copy-start.23 = (f32[8,1024]{1,0:T(8,128)S(1)}, f32[8,1024]{1,0:T(8,128)}, u32[]{:S(2)}) copy-start(f32[8,1024]{1,0:T(8,128)} %get-tuple-element.212) | copy-start | bytes 98308
  499.9 12.8 %copy-start.14 = (bf16[512,1024]{1,0:T(8,128)(2,1)S(1)}, bf16[512,1024]{1,0:T(8,128)(2,1)}, u32[]{:S(2)}) copy-start(bf16[512,1024]{1,0:T(8,128)(2,1)} %get-tuple-element.143.refs_1_) | copy-start | bytes 3145732
  575.2 77.3 %copy-start.22 = (f32[4,1,1024]{2,1,0:T(1,128)S(1)}, f32[4,1,1024]{2,1,0:T(1,128)}, u32[]{:S(2)}) copy-start(f32[4,1,1024]{2,1,0:T(1,128)} %get-tuple-element.215) | copy-start | bytes 49156
  777.6 7.8 copy-start.15
  785.4 1.3 copy-start.17

commit v6 on v5

--- a/solution.py
+++ b/solution.py
@@ -108,6 +108,75 @@
         pltpu.make_async_copy(src, home.at[pl.ds(k * count, count), :], recvs.at[k]).wait()
 
 
+class LineSum:
+    def __init__(self, buf, in_l, in_r, sends, recvs, cols):
+        self.buf, self.in_l, self.in_r, self.sends, self.recvs = buf, in_l, in_r, sends, recvs
+        self.cols, self.n, self.col = cols, len(cols), lax.axis_index("col")
+
+    def right(self, d):
+        return remote(
+            self.buf.at[d - 1], self.in_l.at[d - 1], self.sends.at[0, d - 1],
+            self.recvs.at[0, d - 1], self.cols[1],
+        )
+
+    def left(self, d):
+        return remote(
+            self.buf.at[self.n - d - 1], self.in_r.at[d - 1], self.sends.at[1, d - 1],
+            self.recvs.at[1, d - 1], self.cols[self.n - 1],
+        )
+
+    def add(self, k, got):
+        self.buf[k - 1] = (self.buf[k - 1].astype(f32) + got.astype(f32)).astype(low)
+
+    def begin(self):
+        @pl.when(self.col == 0)
+        def _():
+            self.in_l[0] = jnp.zeros(self.in_l.shape[1:], low)
+            for d in range(self.n - 1, 0, -1):
+                self.right(d).start()
+
+        @pl.when(self.col == self.n - 1)
+        def _():
+            self.in_r[0] = jnp.zeros(self.in_r.shape[1:], low)
+            for d in range(self.n - 1, 0, -1):
+                self.left(d).start()
+
+    def go(self, d):
+        @pl.when((self.col > 0) & (self.col <= self.n - 1 - d))
+        def _():
+            self.right(d + 1).wait_recv()
+            self.add(d, self.in_l[d])
+            self.right(d).start()
+
+        @pl.when((self.col < self.n - 1) & (self.col >= d))
+        def _():
+            self.left(d + 1).wait_recv()
+            self.add(self.n - d, self.in_r[d])
+            self.left(d).start()
+
+    def total(self, value):
+        @pl.when(self.col > 0)
+        def _():
+            self.right(1).wait_recv()
+
+        @pl.when(self.col < self.n - 1)
+        def _():
+            self.left(1).wait_recv()
+
+        return value + self.in_l[0].astype(f32) + self.in_r[0].astype(f32)
+
+    def end(self):
+        for d in range(1, self.n):
+
+            @pl.when(self.col <= self.n - 1 - d)
+            def _():
+                self.right(d).wait_send()
+
+            @pl.when(self.col >= d)
+            def _():
+                self.left(d).wait_send()
+
+
 def plane():
     dp, row, col = here()
     flips = [dp + b - 2 * b * lax.rem(dp // b, 2) for b in (1, 2)]
@@ -120,26 +189,10 @@
     return first.astype(low), (1.0 - first).astype(low), lane < HEAD_DIM
 
 
-def attend_kernel(*refs, span, windowed, rider, n_ins, n_outs):
-    refs = list(refs)
-    q_ref, k_ref, v_ref, qid_ref, kid_ref = refs[:5]
-    rider_refs = refs[5 : 5 + n_ins]
-    refs = refs[5 + n_ins :]
-    o_ref, lse_ref = refs[:2]
-    rider_refs += refs[2 : 2 + n_outs]
-    bias = refs[2 + n_outs]
-    rider_refs += refs[3 + n_outs :]
+def attend_kernel(q_ref, k_ref, v_ref, qid_ref, kid_ref, o_ref, lse_ref, bias, *, span, windowed):
     rows = q_ref.shape[0]
     pairs = q_ref.shape[1] // PAIR
     step = pl.program_id(0)
-    if rider is not None:
-        hooks = rider(*rider_refs)
-        for at, hook in hooks:
-
-            @pl.when(step == at)
-            def _():
-                hook()
-
     start = step * rows if windowed else 0
     if windowed:
         start = pl.multiple_of(start, rows)
@@ -173,31 +226,15 @@
 
     lax.fori_loop(0, pairs, one_pair, 0)
 
-    if rider is not None:
-
-        @pl.when(step == pl.num_programs(0) - 1)
-        def _():
-            hooks.end()
-
-
-class Hooks(list):
-    end = None
-
-
-def attend(q, k, v, qid, kid, windowed, rider=None, riding=(), shapes=(), scratch=(), number=0):
+
+def attend(q, k, v, qid, kid, windowed):
     tokens, width = q.shape
     keys = k.shape[0]
     pairs = width // PAIR
     rows = QUERY_ROWS
     span = WIN + rows if windowed else keys
-    params = dict(vmem_limit_bytes=VMEM)
-    if rider is not None:
-        params.update(collective_id=number, has_side_effects=True)
     return pl.pallas_call(
-        functools.partial(
-            attend_kernel, span=span, windowed=windowed, rider=rider, n_ins=len(riding),
-            n_outs=len(shapes),
-        ),
+        functools.partial(attend_kernel, span=span, windowed=windowed),
         grid=(tokens // rows,),
         in_specs=[
             pl.BlockSpec((rows, width), lambda i: (i, 0)),
@@ -205,76 +242,19 @@
             pl.BlockSpec((keys, width), lambda i: (0, 0)),
             pl.BlockSpec((rows, 1), lambda i: (i, 0)),
             pl.BlockSpec((1, keys), lambda i: (0, 0)),
-        ]
-        + [pl.BlockSpec(x.shape, lambda i: (0, 0)) for x in riding],
+        ],
         out_specs=[
             pl.BlockSpec((rows, width), lambda i: (i, 0)),
             pl.BlockSpec((pairs, 8, rows), lambda i: (0, 0, i)),
-        ]
-        + [ANYWHERE] * len(shapes),
+        ],
         out_shape=[
             jax.ShapeDtypeStruct((tokens, width), low),
             jax.ShapeDtypeStruct((pairs, 8, tokens), f32),
-        ]
-        + [jax.ShapeDtypeStruct(*x) for x in shapes],
-        scratch_shapes=[pltpu.VMEM((rows, span), f32)] + list(scratch),
-        compiler_params=pltpu.CompilerParams(**params),
+        ],
+        scratch_shapes=[pltpu.VMEM((rows, span), f32)],
+        compiler_params=pltpu.CompilerParams(vmem_limit_bytes=VMEM),
         name="attend",
-    )(q, k, v, qid[:, None], kid[None, :], *riding)
-
-
-def cotangent_rider(cot, dz, c_s, c_r, d_s, d_r, *, n_col):
-    dp, row, col = here()
-    wide = cot.shape[1]
-    rows_here = cot.shape[0] // n_col
-
-    def piece(j):
-        to_col = 2 * row + j // 2
-        k = lax.rem(col + n_col - to_col, n_col)
-        src = cot.at[pl.ds(j * rows_here, rows_here), :]
-        dst = dz.at[j % 2, :, pl.ds(pl.multiple_of(k * wide, wide), wide)]
-        local = (row == j % 2) & (col == to_col)
-        return src, dst, k, local, (dp, j % 2, to_col)
-
-    def to_twin(k):
-        ref = dz.at[row, :, pl.ds(k * wide, wide)]
-        return remote(ref, ref, d_s.at[k], d_r.at[k], (dp, 1 - row, col))
-
-    def begin():
-        group = [
-            (dp, r, lax.rem(col + k, n_col)) for r in (row, 1 - row) for k in range(n_col)
-        ]
-        meet(group[1:])
-        for j in range(n_col):
-            src, dst, k, local, to = piece(j)
-
-            @pl.when(local)
-            def _():
-                pltpu.make_async_copy(src, dst, c_r.at[k]).start()
-
-            @pl.when(jnp.logical_not(local))
-            def _():
-                remote(src, dst, c_s.at[j], c_r.at[k], to).start()
-
-    def end():
-        for k in range(n_col):
-            pltpu.make_async_copy(
-                cot.at[pl.ds(0, rows_here), :], dz.at[row, :, pl.ds(k * wide, wide)], c_r.at[k]
-            ).wait()
-            to_twin(k).start()
-        for j in range(n_col):
-            src, dst, k, local, to = piece(j)
-
-            @pl.when(jnp.logical_not(local))
-            def _():
-                remote(src, dst, c_s.at[j], c_r.at[k], to).wait_send()
-
-        for k in range(n_col):
-            to_twin(k).wait()
-
-    hooks = Hooks([(0, begin)])
-    hooks.end = end
-    return hooks
+    )(q, k, v, qid[:, None], kid[None, :])
 
 
 def attend_back_kernel(*refs, span, windowed, rider, n_ins, n_outs):
@@ -291,13 +271,19 @@
     step = pl.program_id(0)
     start = pl.multiple_of(step * rows, rows) if windowed else 0
     keys = pl.ds(start, span)
-    begin, middle, end = rider(*rider_refs)
+    begin, middle, end, later = rider(*rider_refs)
 
     @pl.when(step == 0)
     def _():
         begin()
         dk_sum[...] = jnp.zeros_like(dk_sum)
         dv_sum[...] = jnp.zeros_like(dv_sum)
+
+    for at, hook in later.items():
+
+        @pl.when(step == at)
+        def _():
+            hook()
 
     allowed = kid_ref[keys, :] == qid_ref[...]
     if windowed:
@@ -388,10 +374,7 @@
     )(q, k, v, do, o, lse, qid[None, :], kid[:, None], *riding)
 
 
-def first_rider(
-    g1, g2, got_a, got_b, back_a, back_b, far_a, far_b,
-    load, mid, l_s, s_s, r_s,
-):
+def first_rider(g1, g2, got_a, got_b, back_a, back_b, far_a, far_b, load, mid, l_s, s_s, r_s):
     by_x, by_y = plane()
     half = back_a.shape[0]
     up, down = pl.ds(0, half), pl.ds(half, half)
@@ -400,15 +383,19 @@
         for i, src in enumerate((g1.at[2, up, :], got_a.at[0], g1.at[1, down, :], got_b.at[0]))
     ]
     hops = [
-        remote(g2.at[3, up, :], far_a, s_s.at[0], r_s.at[0], by_x),
-        remote(g2.at[3, down, :], far_b, s_s.at[1], r_s.at[1], by_y),
-        remote(mid.at[0], back_a, s_s.at[2], r_s.at[2], by_y),
-        remote(mid.at[1], back_b, s_s.at[3], r_s.at[3], by_x),
+        remote(mid.at[0], back_a, s_s.at[0], r_s.at[0], by_y),
+        remote(mid.at[1], back_b, s_s.at[1], r_s.at[1], by_x),
+    ]
+    count = far_a.shape[1]
+    lanes = pl.ds(g2.shape[2] - count, count)
+    far = [
+        remote(g2.at[3, up, lanes], far_a, s_s.at[2], r_s.at[2], by_x),
+        remote(g2.at[3, down, lanes], far_b, s_s.at[3], r_s.at[3], by_y),
     ]
 
     def begin():
         meet([by_x, by_y])
-        for copy in loads + hops[:2]:
+        for copy in loads + far:
             copy.start()
 
     def middle():
@@ -416,19 +403,19 @@
             loads[2 * i].wait()
             loads[2 * i + 1].wait()
             mid[i] = (load[2 * i].astype(f32) + load[2 * i + 1].astype(f32)).astype(low)
-            hops[2 + i].start()
+            hops[i].start()
 
     def end():
-        for copy in hops:
+        for copy in hops + far:
             copy.wait()
 
-    return begin, middle, end
+    return begin, middle, end, {}
 
 
 def second_rider(
-    g1, g2, got_a, got_b, back_a, back_b, far_a, far_b,
-    near_a, near_b, far_back_a, far_back_b, z_got, own,
-    load, mid, load_z, out_z, l_s, lz_s, s_s, r_s, z_s, z_r, o_s,
+    g1, g2, got_a, got_b, back_a, back_b, far_a, far_b, far_c, far_d,
+    near_a, near_b, far_back_a, far_back_b, own,
+    load, mid, load_z, out_z, out_own, z_l, z_r, l_s, lz_s, s_s, r_s, zs_s, zr_s, o_s,
     *, n_col,
 ):
     dp, row, col = here()
@@ -438,8 +425,16 @@
     up, down = pl.ds(0, half), pl.ds(half, half)
     loads = [
         pltpu.make_async_copy(src, load.at[i], l_s.at[i])
-        for i, src in enumerate((g2.at[2, up, :], far_a, g2.at[1, down, :], far_b))
+        for i, src in ((0, g2.at[2, up, :]), (2, g2.at[1, down, :]))
     ]
+    cut = far_a.shape[1]
+    for i, (one, two) in ((1, (far_a, far_c)), (3, (far_b, far_d))):
+        loads += [
+            pltpu.make_async_copy(one, load.at[i, :, pl.ds(0, cut)], l_s.at[i]),
+            pltpu.make_async_copy(
+                two, load.at[i, :, pl.ds(cut, two.shape[1])], l_s.at[4 + i // 2]
+            ),
+        ]
     loads_z = []
     for i, (source, got, back) in enumerate(((up, got_a, back_a), (down, got_b, back_b))):
         for n, src in enumerate((g1.at[0, source, :], got.at[1], back)):
@@ -453,11 +448,8 @@
         remote(mid.at[1], far_back_b, s_s.at[3], r_s.at[3], by_x),
     ]
     cols = [(dp, row, lax.rem(col + k, n_col)) for k in range(n_col)]
-    over = [
-        remote(out_z.at[k], z_got.at[k - 1], z_s.at[k - 1], z_r.at[k - 1], cols[k])
-        for k in range(1, n_col)
-    ]
-    keep = pltpu.make_async_copy(out_z.at[0], own, o_s)
+    line = LineSum(out_z, z_l, z_r, zs_s, zr_s, cols)
+    keep = pltpu.make_async_copy(out_own, own, o_s)
 
     def begin():
         meet([by_x, by_y] + cols[1:])
@@ -466,29 +458,88 @@
 
     def middle():
         for i in range(2):
-            loads[2 * i].wait()
-            loads[2 * i + 1].wait()
+            for n in ((0, 2, 3), (1, 4, 5))[i]:
+                loads[n].wait()
             mid[i] = (load[2 * i].astype(f32) + load[2 * i + 1].astype(f32)).astype(low)
             hops[2 + i].start()
         for copy in loads_z:
             copy.wait()
-        for k in list(range(1, n_col)) + [0]:
+        for k in range(n_col):
             at = pl.ds(k * wide, wide)
             value = load_z[0, at, :].astype(f32) + load_z[1, at, :].astype(f32)
-            out_z[k] = (value + load_z[2, at, :].astype(f32)).astype(low)
+            value = (value + load_z[2, at, :].astype(f32)).astype(low)
             if k:
-                over[k - 1].start()
+                out_z[k - 1] = value
+            else:
+                out_own[...] = value
+        line.begin()
+
+    def end():
+        out_own[...] = line.total(out_own[...].astype(f32)).astype(low)
         keep.start()
-
-    def end():
-        for copy in hops + over + [keep]:
+        for copy in hops + [keep]:
             copy.wait()
-
-    return begin, middle, end
+        line.end()
+
+    return begin, middle, end, {2: lambda: line.go(2), 3: lambda: line.go(1)}
 
 
 ROOT = 0.7978845608028654
 CUBE = 0.044715
+
+
+def cotangent_rider(cot, dz, c_s, c_r, d_s, d_r, *, n_col):
+    dp, row, col = here()
+    wide = cot.shape[1]
+    rows_here = cot.shape[0] // n_col
+
+    def piece(j):
+        to_col = 2 * row + j // 2
+        k = lax.rem(col + n_col - to_col, n_col)
+        src = cot.at[pl.ds(j * rows_here, rows_here), :]
+        dst = dz.at[j % 2, :, pl.ds(pl.multiple_of(k * wide, wide), wide)]
+        local = (row == j % 2) & (col == to_col)
+        return src, dst, k, local, (dp, j % 2, to_col)
+
+    def to_twin(k):
+        ref = dz.at[row, :, pl.ds(k * wide, wide)]
+        return remote(ref, ref, d_s.at[k], d_r.at[k], (dp, 1 - row, col))
+
+    def begin():
+        group = [
+            (dp, r, lax.rem(col + k, n_col)) for r in (row, 1 - row) for k in range(n_col)
+        ]
+        meet(group[1:])
+        for j in range(n_col):
+            src, dst, k, local, to = piece(j)
+
+            @pl.when(local)
+            def _():
+                pltpu.make_async_copy(src, dst, c_r.at[k]).start()
+
+            @pl.when(jnp.logical_not(local))
+            def _():
+                remote(src, dst, c_s.at[j], c_r.at[k], to).start()
+
+    def turn():
+        for k in range(n_col):
+            pltpu.make_async_copy(
+                cot.at[pl.ds(0, rows_here), :], dz.at[row, :, pl.ds(k * wide, wide)], c_r.at[k]
+            ).wait()
+            to_twin(k).start()
+
+    def end():
+        for j in range(n_col):
+            src, dst, k, local, to = piece(j)
+
+            @pl.when(jnp.logical_not(local))
+            def _():
+                remote(src, dst, c_s.at[j], c_r.at[k], to).wait_send()
+
+        for k in range(n_col):
+            to_twin(k).wait()
+
+    return begin, turn, end
 
 
 ORDER = (3, 1, 2, 0)
@@ -513,7 +564,7 @@
     ]
 
 
-def hidden_kernel(*refs, numbers, opening, closing):
+def hidden_kernel(*refs, numbers, opening, closing, riding, n_col):
     count = len(numbers)
     refs = list(refs)
 
@@ -527,7 +578,11 @@
         (sum_in,) = take(1)
     if closing:
         x_ref, bias = take(2)
+    if riding:
+        (cot,) = take(1)
     act_ref, slope_ref = take(2)
+    if riding:
+        (dz,) = take(1)
     (out_ref,) = take(1)
     total, w1, w2, w_sem = take(4)
     step, steps = pl.program_id(0), pl.num_programs(0)
@@ -551,6 +606,8 @@
 
     if closing:
         away, came, s_s, s_r = take(4)
+    if riding:
+        begin, turn, end = cotangent_rider(cot, dz, *take(4), n_col=n_col)
 
     @pl.when(step == 0)
     def _():
@@ -559,8 +616,10 @@
             total[...] = jnp.zeros_like(total)
         else:
             total[...] = sum_in[...]
-            if closing:
-                meet([twin])
+        if closing:
+            meet([twin])
+        if riding:
+            begin()
 
     @pl.when(step + 1 < steps)
     def _():
@@ -568,6 +627,12 @@
 
     for i, w in enumerate((w1, w2)):
         pltpu.make_async_copy(w.at[slot], w.at[slot], w_sem.at[i, slot]).wait()
+
+    if riding:
+
+        @pl.when(step == steps - 1)
+        def _():
+            turn()
 
     def one_part(t, carry):
         rows = pl.ds(pl.multiple_of(t * 256, 256), 256)
@@ -586,6 +651,8 @@
 
     @pl.when(step == steps - 1)
     def _():
+        if riding:
+            end()
         if not closing:
             out_ref[...] = total[...]
         else:
@@ -605,7 +672,8 @@
                 branch = total[pl.ds(begin, CUT), :] + came[at, :].astype(f32)
                 out_ref[at, :] = (x_ref[at, :] + (branch + bias[...])).astype(low)
 
-def hidden_forward(f, b1, own1, own2, rest1, rest2, numbers, number, sum_in=None, x=None, bias=None):
+def hidden_forward(f, b1, own1, own2, rest1, rest2, numbers, number, sum_in=None, x=None, bias=None,
+                   cotangent=None, n_col=0):
     tokens, width = f.shape
     inner = rest1[0].shape[1]
     count = len(numbers)
@@ -644,12 +712,19 @@
     else:
         out_shape.append(jax.ShapeDtypeStruct((tokens, width), f32))
     out_specs.append(still(out_shape[-1].shape))
+    if cotangent is not None:
+        args.append(cotangent)
+        in_specs.append(still(cotangent.shape))
+        out_shape.insert(2, jax.ShapeDtypeStruct((2, rows, width), low))
+        out_specs.insert(2, ANYWHERE)
+        scratch += [dma((n_col,))] * 4
     params = dict(vmem_limit_bytes=VMEM)
-    if closing:
+    if closing or cotangent is not None:
         params.update(collective_id=number, has_side_effects=True)
     return pl.pallas_call(
         functools.partial(
-            hidden_kernel, numbers=numbers, opening=opening, closing=closing
+            hidden_kernel, numbers=numbers, opening=opening, closing=closing,
+            riding=cotangent is not None, n_col=n_col,
         ),
         grid=(count * blocks,),
         in_specs=in_specs,
@@ -668,8 +743,8 @@
     calls = 1 + max(p[0] for p in places)
     acts, slopes = refs[2 * PARTS : 2 * PARTS + calls], refs[2 * PARTS + calls : 2 * (PARTS + calls)]
     (
-        g1_ref, g2_ref, gb_ref, df_ref, got_a, got_b, home, dh_low, total, away_a, away_b, s_s,
-        r_s, h_s, h_r, w1, w2, act_ref, slope_ref, w_sem,
+        g1_ref, g2_ref, gb_ref, df_ref, got_a, got_b, home, far_a, far_b, dh_low, total, away_a, away_b,
+        s_s, r_s, h_s, h_r, away_f, f_s, f_r, w1, w2, act_ref, slope_ref, w_sem,
     ) = refs[2 * (PARTS + calls) :]
     block = g1_ref.shape[2]
     inners = rest1[0].shape[1] // block
@@ -747,6 +822,10 @@
             r_s.at[which, slot, n], to,
         )
 
+    def far_hop(which):
+        got, to = [(far_a, by_x), (far_b, by_y)][which]
+        return remote(away_f.at[which], got, f_s.at[which], f_r.at[which], to)
+
     for at, which, slot in ((0, 0, 0), (0, 1, 0), (1, 0, 1), (2, 1, 1)):
 
         @pl.when(order == at)
@@ -760,8 +839,16 @@
             def _():
                 hop(which, slot, n).start()
 
+    @pl.when((order == 0) & (inner == 0))
+    def _():
+        for which in range(2):
+            away_f[which] = g2_ref[0, which * half : (which + 1) * half, :]
+            far_hop(which).start()
+
     @pl.when(step == last)
     def _():
+        for which in range(2):
+            far_hop(which).wait()
         df_ref[...] = total[...].astype(low)
         for which in range(2):
             for slot in range(2):
@@ -798,7 +885,7 @@
             weight,
             pl.BlockSpec((1, 1, block), lambda s: (number_of(s), 0, lax.rem(s, blocks))),
             still((tokens, width)),
-            ANYWHERE, ANYWHERE, ANYWHERE,
+            ANYWHERE, ANYWHERE, ANYWHERE, ANYWHERE, ANYWHERE,
         ],
         out_shape=[
             grad,
@@ -808,6 +895,8 @@
             landing,
             landing,
             jax.ShapeDtypeStruct((n_col * rows_out.shape[0], width // n_col), low),
+            jax.ShapeDtypeStruct((width // 2, block), low),
+            jax.ShapeDtypeStruct((width // 2, block), low),
         ],
         scratch_shapes=[
             vm((tokens, block), low),
@@ -818,6 +907,9 @@
             dma((2, 2, blocks)),
             dma((n_col,)),
             dma((n_col,)),
+            vm((2, width // 2, block), low),
+            dma((2,)),
+            dma((2,)),
             vm((2, width, block), low),
             vm((2, width, block), low),
             vm((2, tokens, block), low),
@@ -1274,75 +1366,6 @@
     return copy
 
 
-class LineSum:
-    def __init__(self, buf, in_l, in_r, sends, recvs, cols):
-        self.buf, self.in_l, self.in_r, self.sends, self.recvs = buf, in_l, in_r, sends, recvs
-        self.cols, self.n, self.col = cols, len(cols), lax.axis_index("col")
-
-    def right(self, d):
-        return remote(
-            self.buf.at[d - 1], self.in_l.at[d - 1], self.sends.at[0, d - 1],
-            self.recvs.at[0, d - 1], self.cols[1],
-        )
-
-    def left(self, d):
-        return remote(
-            self.buf.at[self.n - d - 1], self.in_r.at[d - 1], self.sends.at[1, d - 1],
-            self.recvs.at[1, d - 1], self.cols[self.n - 1],
-        )
-
-    def add(self, k, got):
-        self.buf[k - 1] = (self.buf[k - 1].astype(f32) + got.astype(f32)).astype(low)
-
-    def begin(self):
-        @pl.when(self.col == 0)
-        def _():
-            self.in_l[0] = jnp.zeros(self.in_l.shape[1:], low)
-            for d in range(self.n - 1, 0, -1):
-                self.right(d).start()
-
-        @pl.when(self.col == self.n - 1)
-        def _():
-            self.in_r[0] = jnp.zeros(self.in_r.shape[1:], low)
-            for d in range(self.n - 1, 0, -1):
-                self.left(d).start()
-
-    def go(self, d):
-        @pl.when((self.col > 0) & (self.col <= self.n - 1 - d))
-        def _():
-            self.right(d + 1).wait_recv()
-            self.add(d, self.in_l[d])
-            self.right(d).start()
-
-        @pl.when((self.col < self.n - 1) & (self.col >= d))
-        def _():
-            self.left(d + 1).wait_recv()
-            self.add(self.n - d, self.in_r[d])
-            self.left(d).start()
-
-    def total(self, value):
-        @pl.when(self.col > 0)
-        def _():
-            self.right(1).wait_recv()
-
-        @pl.when(self.col < self.n - 1)
-        def _():
-            self.left(1).wait_recv()
-
-        return value + self.in_l[0].astype(f32) + self.in_r[0].astype(f32)
-
-    def end(self):
-        for d in range(1, self.n):
-
-            @pl.when(self.col <= self.n - 1 - d)
-            def _():
-                self.right(d).wait_send()
-
-            @pl.when(self.col >= d)
-            def _():
-                self.left(d).wait_send()
-
-
 def with_other_bits(value, store, which, sends, recvs, partners):
     for i, partner in enumerate(partners):
         store[i, 0] = value.astype(low)
@@ -1361,13 +1384,68 @@
     return [(dp + b - 2 * b * lax.rem(dp // b, 2), row, col) for b in bits]
 
 
+class PlaneSum:
+    def __init__(self, src, first, mid, second, sems, n_col):
+        self.src, self.first, self.mid, self.second = src, first, mid, second
+        self.f_s, self.f_r, self.m_s, self.m_r = sems
+        self.n_col, self.size = n_col, mid.shape[0] // n_col
+        self.parts, self.ways = part_numbers(), plane()
+        self.turns = [q for pair in zip(range(n_col // 2), range(n_col // 2, n_col)) for q in pair]
+
+    def rows(self, q):
+        return pl.ds(q * self.size, self.size)
+
+    def upper(self, q):
+        return 2 * q < self.n_col
+
+    def hop(self, which, q):
+        to, side = (self.ways[1], 2) if self.upper(q) else (self.ways[0], 1)
+        src = self.src.at[self.parts[3] if which else self.parts[side], self.rows(q), :]
+        dst = self.first.at[which, self.rows(q), :]
+        return remote(src, dst, self.f_s.at[which, q], self.f_r.at[which, q], to)
+
+    def hop2(self, q):
+        to = self.ways[0] if self.upper(q) else self.ways[1]
+        at = self.rows(q)
+        return remote(self.mid.at[at, :], self.second.at[at, :], self.m_s.at[q], self.m_r.at[q], to)
+
+    def start(self):
+        for q in self.turns:
+            self.hop(1, q).start()
+
+    def turn(self):
+        for q in self.turns:
+            at = self.rows(q)
+            self.hop(1, q).wait_recv()
+            keep = self.parts[1] if self.upper(q) else self.parts[2]
+            value = self.src[keep, at, :].astype(f32) + self.first[1, at, :].astype(f32)
+            self.mid[at, :] = value.astype(low)
+            self.hop2(q).start()
+            self.hop(0, q).start()
+
+    def finish(self, out):
+        for q in self.turns:
+            at = self.rows(q)
+            self.hop(0, q).wait_recv()
+            self.hop2(q).wait_recv()
+            value = self.src[self.parts[0], at, :].astype(f32) + self.first[0, at, :].astype(f32)
+            out[at, :] = (value + self.second[at, :].astype(f32)).astype(low)
+
+    def end(self):
+        for q in self.turns:
+            self.hop(0, q).wait_send()
+            self.hop(1, q).wait_send()
+            self.hop2(q).wait_send()
+
+
 def fold_kernel(
-    dq, dk, dv, a_ext, dy, o, wq, wk, wv, res, x0, gain, ga,
-    g2, near_a, near_b, far_back_a, far_back_b, z_got, own1,
-    gb, sums, tg, stats, a_sum, hidden0, q_own,
-    load, load_own, load_got, h_out, h_l, h_r, first, second, mid, away_b, came_b, away_l, came_l,
-    da_got, extra,
-    l_s, lo_s, hz_s, hz_r, f_s, f_r, m_s, m_r, b_s, b_r, c_s, c_r, d_s, d_r, g_s, g_r, x_s, x_r,
+    dq, dk, dv, a_ext, wk, wv, res, gain, ga, enc_in,
+    dy_in, o_in, wq_in, x0_in, g2, near_a, near_b, far_back_a, far_back_b, own1,
+    sums, tg, stats, a_sum, b_sum, hidden0, q_own, enc_out,
+    load, load_own, own_q, h_out, h_l, h_r, gb, fa, ma, sa, fb, mb, sb, away_b, came_b, away_l,
+    came_l, da_got, enc_got, extra,
+    l_s, lo_s, r_s, hz_s, hz_r, fa_s, fa_r, ma_s, ma_r, fb_s, fb_r, mb_s, mb_r, b_s, b_r, c_s, c_r,
+    d_s, d_r, e_s, e_r, g_s, g_r, x_s, x_r,
     *, n_col, n_dp,
 ):
     dp, row, col = here()
@@ -1386,44 +1464,44 @@
     rows = tg.shape[0]
     cuts = rows // CUT
     window = dk.shape[0] - dq.shape[0]
-
-    def at(q):
-        return pl.ds(q * wide, wide)
+    sum_a = PlaneSum(ga, fa, ma, sa, (fa_s, fa_r, ma_s, ma_r), n_col)
+    sum_b = PlaneSum(gb, fb, mb, sb, (fb_s, fb_r, mb_s, mb_r), n_col)
+    line = LineSum(h_out, h_l, h_r, hz_s, hz_r, cols)
 
     loads = []
     for i, sources in enumerate(((near_a, far_back_a), (near_b, far_back_b))):
         spot = pl.ds(i * half, half)
         for n, src in enumerate((g2.at[0, spot, :],) + sources):
             loads.append(pltpu.make_async_copy(src, load.at[n, spot, :], l_s.at[i, n]))
-    loads_own = [
-        pltpu.make_async_copy(own1, load_own, lo_s.at[0]),
-        pltpu.make_async_copy(z_got, load_got, lo_s.at[1]),
+    load_p = pltpu.make_async_copy(own1, load_own, lo_s)
+    count = dq.shape[1]
+    dy, x0 = load.at[0], load.at[1, pl.ds(0, rows), :]
+    o, wq = load.at[2, :, pl.ds(0, count)], load.at[2, :, pl.ds(count, count)]
+    reloads = [
+        pltpu.make_async_copy(src, dst, r_s.at[n])
+        for n, (src, dst) in enumerate(((dy_in, dy), (x0_in, x0), (o_in, o), (wq_in, wq)))
     ]
 
-    def hop(which, q):
-        source = ga.at[parts[3] if which else parts[1], at(q), :]
-        return remote(source, first.at[which, at(q), :], f_s.at[which, q], f_r.at[which, q], by_x)
-
-    def hop2(q):
-        return remote(mid.at[at(q), :], second.at[at(q), :], m_s.at[q], m_r.at[q], by_y)
-
-    line = LineSum(h_out, h_l, h_r, hz_s, hz_r, cols)
-
-    def hidden_total(k):
-        value = load[0, at(k), :].astype(f32) + load[1, at(k), :].astype(f32)
-        return value + load[2, at(k), :].astype(f32)
-
-    for copy in loads + loads_own:
+    def enc_hop(k):
+        src = enc_in.at[:, pl.ds(k * wide, wide)]
+        return remote(src, enc_got.at[k - 1], e_s.at[k - 1], e_r.at[k - 1], cols[k])
+
+    for copy in loads + [load_p]:
         copy.start()
-    for which in (1, 0):
-        for q in range(n_col):
-            hop(which, q).start()
-
+    sum_a.start()
     for copy in loads:
         copy.wait()
-    for k in ks:
-        h_out[k - 1] = hidden_total(k).astype(low)
+    for k in range(n_col):
+        at = pl.ds(k * wide, wide)
+        value = load[0, at, :].astype(f32) + load[1, at, :].astype(f32)
+        value = (value + load[2, at, :].astype(f32)).astype(low)
+        if k:
+            h_out[k - 1] = value
+        else:
+            own_q[...] = value
     line.begin()
+    for copy in reloads:
+        copy.start()
 
     def before(begin):
         spot = pl.ds(begin, CUT)
@@ -1452,23 +1530,16 @@
     def _():
         da_got[...] = jnp.zeros_like(da_got)
 
-    for q in range(n_col):
-        hop(1, q).wait_recv()
-        value = ga[parts[2], at(q), :].astype(f32) + first[1, at(q), :].astype(f32)
-        mid[at(q), :] = value.astype(low)
-        hop2(q).start()
-    for copy in loads_own:
-        copy.wait()
-    value = load_own[...].astype(f32)
-    for k in ks:
-        value = value + load_got[k - 1].astype(f32)
-    value = with_other_bits(value, extra, 0, x_s, x_r, by_bit[2:])
+    sum_a.turn()
+    load_p.wait()
+    value = with_other_bits(load_own[...].astype(f32), extra, 0, x_s, x_r, by_bit[2:])
     hidden0[part] = value.astype(low)
     spread = plane_copies(hidden0, part, parts, by_x, by_y, g_s, g_r)
     spread(0).start()
     spread(1).start()
-
     line.go(2)
+    for copy in reloads:
+        copy.wait()
 
     def last(begin):
         spot = pl.ds(begin, CUT)
@@ -1494,9 +1565,14 @@
         return carry
 
     lax.fori_loop(0, n_col, one_block, 0)
+    sum_b.start()
     line.go(1)
+    for k in ks:
+        enc_hop(k).start()
     for n, (_, other) in enumerate(pairs):
         sums[n : n + 1, :] = jnp.sum(other[...].astype(f32), axis=0, keepdims=True)
+    sum_a.finish(a_sum)
+    sum_b.turn()
 
     @pl.when(col < n_col - 1)
     def _():
@@ -1523,23 +1599,22 @@
     for stage in range(2):
         spread(stage).wait_recv()
         spread(2 + stage).start()
-    for q in range(n_col):
-        hop(0, q).wait_recv()
-        hop2(q).wait_recv()
-        value = ga[part, at(q), :].astype(f32) + first[0, at(q), :].astype(f32)
-        a_sum[at(q), :] = (value + second[at(q), :].astype(f32)).astype(low)
-    value = line.total(hidden_total(0))
+    value = line.total(own_q[...].astype(f32))
     value = with_other_bits(value, extra, 1, x_s, x_r, by_bit[2:])
     q_own[...] = value.astype(low)
+    sum_b.finish(b_sum)
     spread(2).wait_recv()
     spread(3).wait_recv()
+    value = enc_in[:, pl.ds(0, wide)].astype(f32)
+    for k in ks:
+        enc_hop(k).wait()
+        value = value + enc_got[k - 1].astype(f32)
+    enc_out[...] = value
     for stage in range(4):
         spread(stage).wait_send()
     line.end()
-    for q in range(n_col):
-        hop(0, q).wait_send()
-        hop(1, q).wait_send()
-        hop2(q).wait_send()
+    sum_a.end()
+    sum_b.end()
     for t in range(cuts):
         exchange(away_b, came_b, b_s, b_r, t).wait_send()
         exchange(away_l, came_l, c_s, c_r, t).wait_send()
@@ -1549,7 +1624,7 @@
         da_hop.wait_send()
 
 
-def fold(dq, dk, dv, a_ext, dy, o, weights, res, x0, gain, ga, riding, n_col, n_dp):
+def fold(dq, dk, dv, a_ext, dy, o, weights, res, x0, gain, ga, enc_in, riding, n_col, n_dp):
     sd, vm, dma = jax.ShapeDtypeStruct, pltpu.VMEM, pltpu.SemaphoreType.DMA
     rows, deep = x0.shape
     wide = deep // n_col
@@ -1557,52 +1632,56 @@
     others, cuts = n_col - 1, rows // CUT
     more = max(n_dp.bit_length() - 3, 1)
     by_rows = vm((rows, deep), low)
+    plane_memory = [vm((2, deep, columns), low), vm((deep, columns), low), vm((deep, columns), low)]
+    plane_sems = [dma((2, n_col)), dma((2, n_col)), dma((n_col,)), dma((n_col,))]
+    wq, wk, wv = weights
     return pl.pallas_call(
         functools.partial(fold_kernel, n_col=n_col, n_dp=n_dp),
-        in_specs=[IN_VMEM] * 13 + [ANYWHERE] * 7,
-        out_specs=[IN_VMEM] * 7,
+        in_specs=[IN_VMEM] * 10 + [ANYWHERE] * 10,
+        out_specs=[IN_VMEM] * 8,
         out_shape=[
-            sd(ga.shape, low),
             sd((8, dq.shape[1]), f32),
             sd((rows, deep), low),
             sd((8, deep), f32),
             sd((deep, columns), low),
+            sd((deep, columns), low),
             sd((PARTS, wide, hidden), low),
             sd((wide, hidden), low),
+            sd((enc_in.shape[0], wide), f32),
         ],
         scratch_shapes=[
             vm((3, deep, hidden), low),
             vm((wide, hidden), low),
+            vm((wide, hidden), low),
             vm((others, wide, hidden), low),
             vm((others, wide, hidden), low),
             vm((others, wide, hidden), low),
-            vm((others, wide, hidden), low),
-            vm((2, deep, columns), low),
-            vm((deep, columns), low),
-            vm((deep, columns), low),
+            vm(ga.shape, low),
+            *plane_memory, *plane_memory,
             by_rows, by_rows, by_rows, by_rows, by_rows,
-            vm((more, 3, wide, hidden), low),
-            dma((2, 3)), dma((2,)),
+            vm((others, enc_in.shape[0], wide), low),
+            vm((more, 3, wide, hidden) if n_dp > PARTS else (1, 3, 16, 128), low),
+            dma((2, 3)), dma, dma((4,)),
             dma((2, others)), dma((2, others)),
-            dma((2, n_col)), dma((2, n_col)),
-            dma((n_col,)), dma((n_col,)),
+            *plane_sems, *plane_sems,
             dma((cuts,)), dma((cuts,)), dma((cuts,)), dma((cuts,)),
             dma, dma,
+            dma((others,)), dma((others,)),
             dma((4,)), dma((4,)),
             dma((2, more)), dma((2, more)),
         ],
         compiler_params=pltpu.CompilerParams(
-            collective_id=21, has_side_effects=True, vmem_limit_bytes=60 * 1024 * 1024
+            collective_id=21, has_side_effects=True, vmem_limit_bytes=62 * 1024 * 1024
         ),
         name="fold",
-    )(dq, dk, dv, a_ext, dy, o, *weights, res, x0, gain[None], ga, *riding)
+    )(dq, dk, dv, a_ext, wk, wv, res, gain[None], ga, enc_in, dy, o, wq, x0, *riding)
 
 
 def finish_kernel(
-    gb, a_sum, q_own, small, enc_in, tg,
-    full_a, full_b, hidden1, small_out, enc_out, tg_out,
-    first, second, mid, za, za_l, za_r, zb, zb_l, zb_r, enc_got, s_cur, s_got, s_z, extra,
-    f_s, f_r, m_s, m_r, za_s, za_t, zb_s, zb_t, g_s, g_r, e_s, e_r, s_s, s_r, sz_s, sz_r, t_s, t_r, x_s, x_r,
+    a_sum, b_sum, q_own, small, tg,
+    full_a, full_b, hidden1, small_out, tg_out,
+    za, za_l, za_r, zb, zb_l, zb_r, s_cur, s_got, s_z, extra,
+    za_s, za_t, zb_s, zb_t, g_s, g_r, s_s, s_r, sz_s, sz_r, t_s, t_r, x_s, x_r,
     *, n_col, n_dp,
 ):
     dp, row, col = here()
@@ -1613,29 +1692,10 @@
     twin = (dp, 1 - row, col)
     cols = [(dp, row, lax.rem(col + k, n_col)) for k in range(n_col)]
     meet([twin] + [(dp, 1 - row, c[2]) for c in cols[1:]] + cols[1:] + by_bit)
-    wide = gb.shape[1] // n_col
+    wide = a_sum.shape[0] // n_col
     ks = range(1, n_col)
-
-    def rows(q):
-        return pl.ds(q * wide, wide)
-
-    def hop(which, q):
-        to, side = (by_y, 2) if 2 * q < n_col else (by_x, 1)
-        source = gb.at[parts[3] if which else parts[side], rows(q), :]
-        return remote(source, first.at[which, rows(q), :], f_s.at[which, q], f_r.at[which, q], to)
-
-    def hop2(q):
-        to = by_x if 2 * q < n_col else by_y
-        return remote(mid.at[rows(q), :], second.at[rows(q), :], m_s.at[q], m_r.at[q], to)
-
-    turns = [q for pair in zip(range(n_col // 2), range(n_col // 2, n_col)) for q in pair]
-
     line_a = LineSum(za, za_l, za_r, za_s, za_t, cols)
     line_b = LineSum(zb, zb_l, zb_r, zb_s, zb_t, cols)
-
-    def enc_hop(k):
-        src = enc_in.at[:, pl.ds(k * wide, wide)]
-        return remote(src, enc_got.at[k - 1], e_s.at[k - 1], e_r.at[k - 1], cols[k])
 
     partners = [twin] + by_bit
 
@@ -1672,86 +1732,52 @@
     spread_q = plane_copies(hidden1, part, parts, by_x, by_y, g_s.at[0], g_r.at[0])
     spread_a = plane_copies(full_a, part, parts, by_x, by_y, g_s.at[1], g_r.at[1])
     spread_b = plane_copies(full_b, part, parts, by_x, by_y, g_s.at[2], g_r.at[2])
+    spreads = (spread_q, spread_a, spread_b)
 
     small_step(0)
-    for q in ks:
-        za[q - 1] = a_sum[rows(q), :]
-    hidden1[part] = q_own[...]
+    for line, buf, whole in ((line_a, za, a_sum), (line_b, zb, b_sum)):
+        for k in ks:
+            buf[k - 1] = whole[pl.ds(k * wide, wide), :]
+        line.begin()
     for i in range(1, len(partners)):
         small_step(i)
-    for q in turns:
-        hop(1, q).start()
+    hidden1[part] = q_own[...]
+    spread_q(0).start()
+    spread_q(1).start()
+    for d in range(n_col - 2, 0, -1):
+        line_a.go(d)
+        line_b.go(d)
     small_step(len(partners))
-    line_a.begin()
     send_home(tg, tg_out, t_s, t_r, n_col)
-    spread_q(0).start()
-    for q in turns:
-        hop(1, q).wait_recv()
-        keep = parts[1] if 2 * q < n_col else parts[2]
-        value = gb[keep, rows(q), :].astype(f32) + first[1, rows(q), :].astype(f32)
-        mid[rows(q), :] = value.astype(low)
-        hop2(q).start()
-        hop(0, q).start()
-    spread_q(1).start()
-    for q in list(ks) + [0]:
-        hop(0, q).wait_recv()
-        hop2(q).wait_recv()
-        value = gb[part, rows(q), :].astype(f32) + first[0, rows(q), :].astype(f32)
-        value = value + second[rows(q), :].astype(f32)
-        if q:
-            zb[q - 1] = value.astype(low)
-    line_b.begin()
-    line_a.go(2)
-    line_b.go(2)
-    line_a.go(1)
-    line_b.go(1)
-    for k in ks:
-        enc_hop(k).start()
-    for stage in range(2):
-        spread_q(stage).wait_recv()
-        spread_q(2 + stage).start()
-    value_a = line_a.total(a_sum[rows(0), :].astype(f32))
-    value_a = with_other_bits(value_a, extra, 0, x_s, x_r, by_bit[2:])
-    full_a[part] = value_a.astype(low)
-    spread_a(0).start()
-    spread_a(1).start()
-    value = line_b.total(value)
-    value = with_other_bits(value, extra, 1, x_s, x_r, by_bit[2:])
-    full_b[part] = value.astype(low)
-    spread_b(0).start()
-    spread_b(1).start()
-    for stage in range(2):
-        spread_a(stage).wait_recv()
-        spread_a(2 + stage).start()
+    for i, (line, whole, full, spread) in enumerate((
+        (line_a, a_sum, full_a, spread_a), (line_b, b_sum, full_b, spread_b),
+    )):
+        value = line.total(whole[pl.ds(0, wide), :].astype(f32))
+        value = with_other_bits(value, extra, i, x_s, x_r, by_bit[2:])
+        full[part] = value.astype(low)
+        spread(0).start()
+        spread(1).start()
+    for spread in spreads:
+        for stage in range(2):
+            spread(stage).wait_recv()
+            spread(2 + stage).start()
     small_step(len(partners) + 1)
-    for stage in range(2):
-        spread_b(stage).wait_recv()
-        spread_b(2 + stage).start()
-    value = enc_in[:, pl.ds(0, wide)].astype(f32)
-    for k in ks:
-        enc_hop(k).wait()
-        value = value + enc_got[k - 1].astype(f32)
-    enc_out[...] = value
-    for spread in (spread_q, spread_a, spread_b):
+    for spread in spreads:
         spread(2).wait_recv()
         spread(3).wait_recv()
         for stage in range(4):
             spread(stage).wait_send()
-    for q in range(n_col):
-        hop(0, q).wait_send()
-        hop(1, q).wait_send()
-        hop2(q).wait_send()
-        if q:
-            small_z(q).wait_send()
     line_a.end()
     line_b.end()
+    for k in ks:
+        small_z(k).wait_send()
     for i in range(len(partners)):
         small_hop(i).wait_send()
     wait_home(tg, tg_out, t_s, t_r, n_col)
 
 
-def finish(gb, a_sum, q_own, small, enc_in, tg, n_col, n_dp):
-    parts, deep, columns = gb.shape
+def finish(a_sum, b_sum, q_own, small, tg, n_col, n_dp):
+    columns = a_sum.shape[1]
     wide, hidden = q_own.shape
     steps = n_dp.bit_length()
     sd, vm, dma = jax.ShapeDtypeStruct, pltpu.VMEM, pltpu.SemaphoreType.DMA
@@ -1759,31 +1785,23 @@
     others = n_col - 1
     return pl.pallas_call(
         functools.partial(finish_kernel, n_col=n_col, n_dp=n_dp),
-        in_specs=[IN_VMEM] * 6,
-        out_specs=[IN_VMEM] * 5 + [ANYWHERE],
+        in_specs=[IN_VMEM] * 5,
+        out_specs=[IN_VMEM] * 4 + [ANYWHERE],
         out_shape=[
-            sd((parts, wide, columns), low),
-            sd((parts, wide, columns), low),
-            sd((parts, wide, hidden), low),
+            sd((PARTS, wide, columns), low),
+            sd((PARTS, wide, columns), low),
+            sd((PARTS, wide, hidden), low),
             sd(small.shape[1:], f32),
-            sd((enc_in.shape[0], wide), f32),
             sd((n_col * tg.shape[0], wide), low),
         ],
         scratch_shapes=[
-            vm((2, deep, columns), low),
-            vm((deep, columns), low),
-            vm((deep, columns), low),
             *[vm((others, wide, columns), low)] * 6,
-            vm((others, enc_in.shape[0], wide), low),
             vm((steps + 1,) + small.shape, f32),
             vm((steps,) + small.shape, f32),
             vm((others,) + small.shape[1:], f32),
             vm((more, 3, wide, columns), low),
-            dma((2, n_col)), dma((2, n_col)),
-            dma((n_col,)), dma((n_col,)),
             *[dma((2, others))] * 4,
             dma((3, 4)), dma((3, 4)),
-            dma((others,)), dma((others,)),
             dma((steps,)), dma((steps,)),
             dma((others,)), dma((others,)),
             dma((n_col,)), dma((n_col,)),
@@ -1793,7 +1811,7 @@
             collective_id=20, has_side_effects=True, vmem_limit_bytes=VMEM
         ),
         name="finish",
-    )(gb, a_sum, q_own, small, enc_in, tg)
+    )(a_sum, b_sum, q_own, small, tg)
 
 
 def column_grads_kernel(*refs, pairs, firsts):
@@ -1969,23 +1987,20 @@
         q2 = (mm(c, wq2) + q_bias2).astype(low) * scale
         k2 = mm(enc, wk2).astype(low)
         v2 = (mm(enc, wv2) + v_bias2).astype(low)
-        o2, lse2, dz = attend(
-            q2, k2, v2, query_ids, src_ids, False,
-            functools.partial(cotangent_rider, n_col=n_col), [cotangent],
-            [((2, chunk, n_col * wide), low)], [dma((n_col,))] * 4, 14,
-        )
-        near1, near2, o2 = lax.optimization_barrier((near1, near2, o2))
+        o2, lse2 = attend(q2, k2, v2, query_ids, src_ids, False)
+        near1, o2 = lax.optimization_barrier((near1, o2))
         far1 = across(near1[0], 2)
-        far2 = across(near2[1], 1)
         x2, f = junction("forward", [("nn", o2, wo2)], [x1, out_bias2, gain3, shift3], 4)
         rests1, rests2 = [rest1, *near1], [rest2, *near2]
         act0, slope0, part_sum = hidden_forward(
             f, hidden_bias[:1], hidden_in, hidden_out_t, rests1[:1], rests2[:1], (0,), 0
         )
+        near2, part_sum = lax.optimization_barrier((near2, part_sum))
+        far2 = across(near2[1], 1)
         rests1, rests2 = [rest1, *near1, far1], [rest2, *near2, far2]
-        act1, slope1, part_sum = hidden_forward(
-            f, hidden_bias[1:3], hidden_in, hidden_out_t, rests1[1:3], rests2[1:3], (1, 2), 0,
-            sum_in=part_sum,
+        act1, slope1, dz, part_sum = hidden_forward(
+            f, hidden_bias[1:3], hidden_in, hidden_out_t, rests1[1:3], rests2[1:3], (1, 2), 14,
+            sum_in=part_sum, cotangent=cotangent, n_col=n_col,
         )
         act2, slope2, rows_out = hidden_forward(
             f, hidden_bias[3:], hidden_in, hidden_out_t, rests1[3:], rests2[3:], (3,), 5,
@@ -1993,7 +2008,7 @@
         )
         dz = dz.reshape(span, -1)
 
-        g1, g2, hidden_bias_grad, df, got_a, got_b, layer_out = hidden_backward(
+        g1, g2, hidden_bias_grad, df, got_a, got_b, layer_out, far_a, far_b = hidden_backward(
             dz, f, hidden_in, hidden_out_t, rests1, rests2, [act0, act1, act2],
             [slope0, slope1, slope2], ((0, 0), (1, 0), (1, 1), (2, 0)), rows_out, n_col, 11,
         )
@@ -2003,9 +2018,10 @@
         dx2, dyc, stats3 = junction("backward", [("sum", df)], [dz, x2, gain3], 6)
 
         doc = mm_nt(dyc, wo2).astype(low)
-        dq2, dk2, dv2, back_a, back_b, far_a, far_b = attend_back(
+        later = ((half, inner - far_a.shape[1]), low)
+        dq2, dk2, dv2, back_a, back_b, far_c, far_d = attend_back(
             q2, k2, v2, doc, o2, lse2, query_ids, src_ids, False,
-            first_rider, [g1, g2, got_a, got_b], [one] * 4,
+            first_rider, [g1, g2, got_a, got_b], [one] * 2 + [later] * 2,
             [
                 pltpu.VMEM((4, half, inner), low), pltpu.VMEM((2, half, inner), low),
                 dma((4,)), dma((4,)), dma((4,)),
@@ -2021,23 +2037,25 @@
         cross_grads, enc_back, dy = lax.optimization_barrier((cross_grads, enc_back, dy))
         do = mm_nt(dy, wo1).astype(low)
         (
-            dq1, dk1, dv1, near_a, near_b, far_back_a, far_back_b, z_got, own1
+            dq1, dk1, dv1, near_a, near_b, far_back_a, far_back_b, own1
         ) = attend_back(
             q1, k1, v1, do, o1, lse1, query_ids, key_ids, True,
             functools.partial(second_rider, n_col=n_col),
-            [g1, g2, got_a, got_b, back_a, back_b, far_a, far_b],
-            [one] * 4 + [((n_col - 1, wide, inner), low), ((wide, inner), low)],
+            [g1, g2, got_a, got_b, back_a, back_b, far_a, far_b, far_c, far_d],
+            [one] * 4 + [((wide, inner), low)],
             [
                 pltpu.VMEM((4, half, inner), low), pltpu.VMEM((2, half, inner), low),
-                pltpu.VMEM((3, 2 * half, inner), low), pltpu.VMEM((n_col, wide, inner), low),
-                dma((4,)), dma((2, 3)), dma((4,)), dma((4,)),
-                dma((n_col - 1,)), dma((n_col - 1,)), dma,
+                pltpu.VMEM((3, 2 * half, inner), low), pltpu.VMEM((n_col - 1, wide, inner), low),
+                pltpu.VMEM((wide, inner), low), pltpu.VMEM((n_col - 1, wide, inner), low),
+                pltpu.VMEM((n_col - 1, wide, inner), low),
+                dma((6,)), dma((2, 3)), dma((4,)), dma((4,)),
+                dma((2, n_col - 1)), dma((2, n_col - 1)), dma,
             ],
             13,
         )
-        gb, self_columns, x0_grad, stats1, a_sum, hidden0, q_own = fold(
-            dq1, dk1, dv1, a_ext, dy, o1, [wq1, wk1, wv1], dx1, x0, gain1, cross_grads,
-            [g2, near_a, near_b, far_back_a, far_back_b, z_got, own1], n_col, n_dp,
+        self_columns, x0_grad, stats1, a_sum, b_sum, hidden0, q_own, encoder_grad = fold(
+            dq1, dk1, dv1, a_ext, dy, o1, [wq1, wk1, wv1], dx1, x0, gain1, cross_grads, enc_back,
+            [g2, near_a, near_b, far_back_a, far_back_b, own1], n_col, n_dp,
         )
 
         feature_grads = jnp.concatenate([
@@ -2062,8 +2080,8 @@
             ],
             axis=2,
         )
-        full_a, full_b, hidden1, small, encoder_grad, tokens_grad = finish(
-            gb, a_sum, q_own, small, enc_back, x0_grad, n_col, n_dp
+        full_a, full_b, hidden1, small, tokens_grad = finish(
+            a_sum, b_sum, q_own, small, x0_grad, n_col, n_dp
         )
         grads = unpack(full_a, full_b, hidden0, hidden1)
         tokens_grad = tokens_grad.astype(f32)

time: 797 us -> 754 us (0.946)
  waiting for transfers between devices: 39.2 us -> 10.4 us
  Pallas kernels: 647 us -> 628 us
    pallas_call x1, Pallas kernels: 116 us -> 81 us  [finish(): pl.pallas_call(functools.partial(finish_kernel, n_col=n_col, n_dp=n_dp),...]
    ppermute x6, waiting for transfers between devices: 21.9 us -> 0.02 us  [across(): return lax.ppermute(x, 'dp', [(i, i ^ bit) for i in range(n_dp)])]
    pallas_call x1, Pallas kernels: 76.4 us -> 97.6 us  [fold(): pl.pallas_call(functools.partial(fold_kernel, n_col=n_col, n_dp=n_dp), in...]
    pallas_call x2, Pallas kernels: 112 us -> 94.9 us  [attend_back(): pl.pallas_call(functools.partial(attend_back_kernel, span=span, windowed=...]
    pallas_call x3, Pallas kernels: 57.1 us -> 69.7 us  [hidden_forward(): pl.pallas_call(functools.partial(hidden_kernel, numbers=numbers, opening=...]
    pallas_call x2, Pallas kernels: 59.3 us -> 48.9 us  [attend(): pl.pallas_call(functools.partial(attend_kernel, span=span, windowed=windo...]
    pallas_call x1, Pallas kernels: 66.1 us -> 75.2 us  [hidden_backward(): pl.pallas_call(functools.partial(hidden_back_kernel, n_col=n_col, places=...]
  transfers between devices with their start and end apart: 12 -> 12, of which waited for: 5 -> 2; matrix products, arithmetic and copies ran while one was open for 6% -> 6% of each run, Pallas kernels for 16% -> 17%
where the time goes in v6:
time: 754 us; the launch traced here: 744 us
  Pallas kernels  628 us (83%)
  local copies, waits for them, and re-layouts  43.8 us (6%)
  matrix products  28.4 us (4%)
  starting transfers between devices  26 us (3%)
  waiting for transfers between devices  10.4 us (1%)
    pallas_call x1, Pallas kernels, fold(): pl.pallas_call(functools.partial(fold_kernel, n_col=n_col, n_dp=n_dp), in...  97.6 us
    pallas_call x2, Pallas kernels, attend_back(): pl.pallas_call(functools.partial(attend_back_kernel, span=span, windowed=...  94.9 us
    pallas_call x1, Pallas kernels, start(): pl.pallas_call(functools.partial(start_kernel, n_col=n_col), in_specs=[IN...  85.6 us
    pallas_call x1, Pallas kernels, finish(): pl.pallas_call(functools.partial(finish_kernel, n_col=n_col, n_dp=n_dp),...  81 us
    pallas_call x1, Pallas kernels, hidden_backward(): pl.pallas_call(functools.partial(hidden_back_kernel, n_col=n_col, places=...  75.2 us
    pallas_call x3, Pallas kernels, hidden_forward(): pl.pallas_call(functools.partial(hidden_kernel, numbers=numbers, opening=...  69.7 us
    pallas_call x2, Pallas kernels, attend(): pl.pallas_call(functools.partial(attend_kernel, span=span, windowed=windo...  48.9 us
    pallas_call x5, Pallas kernels, junction(): pl.pallas_call(functools.partial(junction_kernel, kinds=kinds, mode=mode)...  48.2 us
  transfers between devices with their start and end apart: 12, of which 2 were waited for; matrix products, arithmetic and copies ran while one was open for 6% of the time, Pallas kernels for 17%

profile of v6, /device:TPU:8, one launch (start us, length us, event | category | flops | bytes accessed | tf_op | source)
XLA Modules:
  0.0 744.0 jit_solution(181574896593395218)
XLA Ops:
  4.6 1.5 stack.63
  6.8 85.6 %start.1 = (bf16[2,512,1024]{2,1,0:T(8,128)(2,1)}, bf16[1024,1024]{1,0:T(8,128)(2,1)}, f32[16,1024]{1,0:T(8,128)}, f32[4,16,128]{2,1,0:T(8,128)}, bf16[1024,512]...) custom-call(bf16[2048,256]{1,0:T(8,128)(2,1)} %tokens.1, ...), custom_call_target="tpu_custom_call" | custom-call | tf_op jit(solution)/shard_map/start/pallas_call | solution.py:1175
  92.3 1.9 constant_dynamic-slice_fusion.5
  94.2 2.3 collective-permute-start
  96.5 9.4 %collective-permute-start.1 = (bf16[256,1024]{1,0:T(8,128)(2,1)}, bf16[256,1024]{1,0:T(8,128)(2,1)S(1)}, u32[]{:S(2)}, u32[]{:S(2)}) collective-permute-start(bf16[256,1024]{1,0:T(8,128)(2,1)} %constant_dynamic-slice_fusion.5), channel_id=1, source_target_pairs={{0,2},{1,3},{2,0},{3,1},{4,6},{5,7},{6,4},{7,5},{8,10},{9,11},{10,... | collective-permute-start | bytes 1572872 | tf_op jit(solution)/shard_map/ppermute | solution.py:1893
  105.9 2.9 collective-permute-start.2
  108.8 1.7 fusion.10
  110.5 2.9 copy.67
  113.5 9.3 %enter.1 = bf16[2,1024,1024]{2,1,0:T(8,128)(2,1)} custom-call(bf16[2,512,1024]{2,1,0:T(8,128)(2,1)} %get-tuple-element.135.x_ref, f32[1,1024]{1,0:T(1,128)} %get-tuple-element.247.gain, f32[1,1024]{1,0:T(1,128)} %get-tuple-element.246.shift), custom_call_target="tpu_custom_call" | custom-call | tf_op jit(solution)/shard_map/enter/pallas_call | solution.py:1228
  123.6 1.5 collective-permute-start.6
  125.1 6.0 convolution_convert_fusion.k_ref.refs_1_
  131.1 3.7 add_convert_fusion.v_ref.refs_2_
  134.9 2.2 fusion.5.q_ref.refs_0_
  139.1 27.4 %attend.2 = (bf16[1024,512]{1,0:T(8,128)(2,1)}, f32[4,8,1024]{2,1,0:T(8,128)}) custom-call(bf16[1024,512]{1,0:T(8,128)(2,1)} %fusion.5.q_ref.refs_0_, bf16[2048,512]{1,0:T(8,128)(2,1)} %convolution_convert_fusion.k_ref.refs_1_, bf16[2048,512]{1,0:T(8,128)(2,1)} %add_convert_fusion.v_ref.refs_2_, s32[1024,1]{1,0:T(8,128)} %copy.68.qid_ref, s32[1,2048]{1,0:T(1,128)} %bitcast.111), custom_call_target="tpu_custom_call" | custom-call | tf_op jit(solution)/shard_map/attend/pallas_call | solution.py:236
  166.5 2.8 collective-permute-start.7
  170.3 4.4 collective-permute-done.2
  178.0 1.6 collective-permute-start.3
  179.5 1.5 collective-permute-start.4
  181.1 9.4 %junction_forward.2 = (f32[512,1024]{1,0:T(8,128)}, bf16[1024,1024]{1,0:T(8,128)(2,1)}) custom-call(bf16[1024,512]{1,0:T(8,128)(2,1)} %get-tuple-element.147.refs_0_.refs_4_.o_in, bf16[512,1024]{1,0:T(8,128)(2,1)} %get-tuple-element.148.refs_1_, bf16[512,1024]{1,0:T(8,128)(2,1)} %slice_bitcast_fusion.refs_2_.x0_in, f32[1,1024]{1,0:T(1,128)} %get-tuple-element.245.refs_3_, ...), custom_call_target="tpu_custom_call" | custom-call | tf_op jit(solution)/shard_map/junction_forward/pallas_call | solution.py:1340
  190.5 6.0 collective-permute-done.7
  196.4 1.9 constant_dynamic-update-slice_fusion.6
  198.3 1.9 constant_dynamic-update-slice_fusion.5
  201.0 1.5 collective-permute-start.8
  202.5 1.5 collective-permute-start.9
  205.5 4.2 convolution_convert_fusion.3.k_ref.refs_1_
  209.7 2.2 add_convert_fusion.1.v_ref.refs_2_
  212.0 2.2 fusion.8.q_ref.refs_0_
  214.2 21.5 %attend.3 = (bf16[1024,512]{1,0:T(8,128)(2,1)}, f32[4,8,1024]{2,1,0:T(8,128)}) custom-call(bf16[1024,512]{1,0:T(8,128)(2,1)} %fusion.8.q_ref.refs_0_, bf16[1024,512]{1,0:T(8,128)(2,1)} %convolution_convert_fusion.3.k_ref.refs_1_, bf16[1024,512]{1,0:T(8,128)(2,1)} %add_convert_fusion.1.v_ref.refs_2_, s32[1024,1]{1,0:T(8,128)} %copy.68.qid_ref, ...), custom_call_target="tpu_custom_call" | custom-call | tf_op jit(solution)/shard_map/attend/pallas_call | solution.py:236
  235.7 10.2 %junction_forward.3 = (f32[512,1024]{1,0:T(8,128)}, bf16[1024,1024]{1,0:T(8,128)(2,1)}) custom-call(bf16[1024,512]{1,0:T(8,128)(2,1)} %get-tuple-element.156.refs_0_.refs_4_.refs_6_, bf16[512,1024]{1,0:T(8,128)(2,1)} %get-tuple-element.157.refs_1_, f32[512,1024]{1,0:T(8,128)} %get-tuple-element.158.refs_2_.refs_3_, f32[1,1024]{1,0:T(1,128)} %get-tuple-element.242.refs_3_, ...), custom_call_target="tpu_custom_call" | custom-call | tf_op jit(solution)/shard_map/junction_forward/pallas_call | solution.py:1340
  246.0 14.7 %hidden_forward.3 = (bf16[1,1024,1024]{2,1,0:T(8,128)(2,1)}, bf16[1,1024,1024]{2,1,0:T(8,128)(2,1)}, f32[1024,1024]{1,0:T(8,128)}) custom-call(bf16[1024,1024]{1,0:T(8,128)(2,1)} %get-tuple-element.159.refs_0_, f32[1,1,1024]{2,1,0:T(1,128)} %get-tuple-element.276.refs_1_, bf16[256,4096]{1,0:T(8,128)(2,1)} %own1, bf16[256,4096]{1,0:T(8,128)(2,1)} %bitcast.97, ...), custom_call_target="tpu_custom_call" | custom-call | tf_op jit(solution)/shard_map/hidden_forward/pallas_call | solution.py:724
  264.8 2.5 copy.70
  267.4 35.3 %hidden_forward.4 = (bf16[2,1024,1024]{2,1,0:T(8,128)(2,1)}, bf16[2,1024,1024]{2,1,0:T(8,128)(2,1)}, bf16[2,512,1024]{2,1,0:T(8,128)(2,1)}, f32[1024,1024]{1,0:T(8,128)}) custom-call(bf16[1024,1024]{1,0:T(8,128)(2,1)} %get-tuple-element.159.refs_0_, f32[2,1,1024]{2,1,0:T(1,128)} %pad_maximum_fusion.1.refs_1_, bf16[256,4096]{1,0:T(8,128)(2,1)} %own1, ...), custom_call_target="tpu_custom_call" | custom-call | tf_op jit(solution)/shard_map/hidden_forward/pallas_call | solution.py:724
  302.7 3.9 copy.71.dzt_ref
  306.7 19.7 %hidden_forward.5 = (bf16[1,1024,1024]{2,1,0:T(8,128)(2,1)}, bf16[1,1024,1024]{2,1,0:T(8,128)(2,1)}, bf16[512,1024]{1,0:T(8,128)(2,1)}) custom-call(bf16[1024,1024]{1,0:T(8,128)(2,1)} %get-tuple-element.159.refs_0_, f32[1,1,1024]{2,1,0:T(1,128)} %get-tuple-element.275.refs_1_, bf16[256,4096]{1,0:T(8,128)(2,1)} %own1, bf16[256,4096]{1,0:T(8,128)(2,1)} %bitcast.99, ...), custom_call_target="tpu_custom_call" | custom-call | tf_op jit(solution)/shard_map/hidden_forward/pallas_call | solution.py:724
  326.3 75.2 %hidden_backward.1 = (bf16[4,1024,1024]{2,1,0:T(8,128)(2,1)}, bf16[4,1024,1024]{2,1,0:T(8,128)(2,1)}, f32[4,1,1024]{2,1,0:T(1,128)}, bf16[1024,1024]{1,0:T(8,128...) custom-call(bf16[1024,1024]{1,0:T(8,128)(2,1)} %bitcast.102, ...), custom_call_target="tpu_custom_call" | custom-call | tf_op jit(solution)/shard_map/hidden_backward/pallas_call | solution.py:877
  401.6 10.6 %junction_backward.2 = (f32[512,1024]{1,0:T(8,128)}, bf16[1024,1024]{1,0:T(8,128)(2,1)}, f32[8,1024]{1,0:T(8,128)}) custom-call(bf16[1024,1024]{1,0:T(8,128)(2,1)} %get-tuple-element.180.refs_0_, bf16[1024,1024]{1,0:T(8,128)(2,1)} %bitcast.103, f32[512,1024]{1,0:T(8,128)} %get-tuple-element.171.refs_7_.refs_2_, f32[1,1024]{1,0:T(1,128)} %get-tuple-element.241.refs_4_.refs_3_), custom_call_target="tpu_custom_call" | custom-call | tf_op jit(solution)/shard_map/junction_backward/pallas_call | solution.py:1340
  412.2 3.8 convolution_convert_fusion.2.refs_3_
  416.1 40.6 %attend_back.2 = (bf16[1024,512]{1,0:T(8,128)(2,1)}, bf16[1024,512]{1,0:T(8,128)(2,1)}, bf16[1024,512]{1,0:T(8,128)(2,1)}, bf16[512,1024]{1,0:T(8,128)(2,1)}, bf...) custom-call(bf16[1024,512]{1,0:T(8,128)(2,1)} %fusion.8.q_ref.refs_0_, ...), custom_call_target="tpu_custom_call" | custom-call | tf_op jit(solution)/shard_map/attend_back/pallas_call | solution.py:340
  456.7 6.8 junction_sum.1.enc_in
  463.5 10.4 %column_grads.1 = (bf16[4,1024,512]{2,1,0:T(8,128)(2,1)}, f32[8,512]{1,0:T(8,128)}) custom-call(bf16[1024,1024]{1,0:T(8,128)(2,1)} %get-tuple-element.150.refs_0_, bf16[1024,1024]{1,0:T(8,128)(2,1)} %get-tuple-element.152.refs_1_, bf16[1024,1024]{1,0:T(8,128)(2,1)} %get-tuple-element.181.refs_2_, bf16[1024,512]{1,0:T(8,128)(2,1)} %get-tuple-element.187.refs_3_.refs_0_, ...), custom_call_target="tpu_custom_call" | custom-call | tf_op jit(solution)/shard_map/column_grads/pallas_call | solution.py:1837
  473.8 11.1 %junction_backward.3 = (f32[512,1024]{1,0:T(8,128)}, bf16[1024,1024]{1,0:T(8,128)(2,1)}, f32[8,1024]{1,0:T(8,128)}) custom-call(bf16[1024,512]{1,0:T(8,128)(2,1)} %get-tuple-element.187.refs_3_.refs_0_, bf16[1024,512]{1,0:T(8,128)(2,1)} %get-tuple-element.151.refs_1_, f32[512,1024]{1,0:T(8,128)} %get-tuple-element.191.refs_2_, ...), custom_call_target="tpu_custom_call" | custom-call | tf_op jit(solution)/shard_map/junction_backward/pallas_call | solution.py:1340
  486.6 3.9 convolution_convert_fusion.1.refs_3_
  490.5 54.4 %attend_back.3 = (bf16[1024,512]{1,0:T(8,128)(2,1)}, bf16[2048,512]{1,0:T(8,128)(2,1)}, bf16[2048,512]{1,0:T(8,128)(2,1)}, bf16[512,1024]{1,0:T(8,128)(2,1)}, bf...) custom-call(bf16[1024,512]{1,0:T(8,128)(2,1)} %fusion.5.q_ref.refs_0, ...), custom_call_target="tpu_custom_call" | custom-call | tf_op jit(solution)/shard_map/attend_back/pallas_call | solution.py:340
  544.9 97.6 %fold.1 = (f32[8,512]{1,0:T(8,128)}, bf16[512,1024]{1,0:T(8,128)(2,1)}, f32[8,1024]{1,0:T(8,128)}, bf16[1024,512]{1,0:T(8,128)(2,1)}, bf16[1024,512]{1,0:T(8,128...) custom-call(bf16[1024,512]{1,0:T(8,128)(2,1)} %get-tuple-element.201.dq, ...), custom_call_target="tpu_custom_call" | custom-call | tf_op jit(solution)/shard_map/fold/pallas_call | solution.py:1638
  645.7 81.0 %finish.1 = (bf16[4,256,512]{2,1,0:T(8,128)(2,1)}, bf16[4,256,512]{2,1,0:T(8,128)(2,1)}, bf16[4,256,1024]{2,1,0:T(8,128)(2,1)}, f32[16,384]{1,0:T(8,128)}, bf16[2048,256]{1,0:T(8,128)(2,1)}) custom-call(bf16[1024,512]{1,0:T(8,128)(2,1)} %get-tuple-element.212.a_sum, bf16[1024,512]{1,0:T(8,128)(2,1)} %get-tuple-element.213.b_sum, ...), custom_call_target="tpu_custom_call" | custom-call | tf_op jit(solution)/shard_map/finish/pallas_call | solution.py:1786
  726.7 1.6 fusion.12
  730.9 2.7 convert_element_type.67
  733.6 7.8 %unpack.1 = (f32[256,512]{1,0:T(8,128)}, f32[256,512]{1,0:T(8,128)}, f32[256,512]{1,0:T(8,128)}, f32[512,256]{1,0:T(8,128)}, f32[256,512]{1,0:T(8,128)}, /*index...) custom-call(bf16[4,256,512]{2,1,0:T(8,128)(2,1)} %get-tuple-element.225, ...), custom_call_target="tpu_custom_call" | custom-call | tf_op jit(solution)/shard_map/unpack/pallas_call | solution.py:1875
  (119 shorter events, 27.7 us)
Async XLA Ops:
  94.2 72.3 %collective-permute-start = (bf16[256,1024]{1,0:T(8,128)(2,1)}, bf16[256,1024]{1,0:T(8,128)(2,1)S(1)}, u32[]{:S(2)}, u32[]{:S(2)}) collective-permute-start(bf16[256,1024]{1,0:T(8,128)(2,1)} %constant_dynamic-slice_fusion.5), channel_id=1, source_target_pairs={{0,3},{1,0},{2,1},{3,2},{4,7},{5,4},{6,5},{7,6},{8,11},{9,8},{10,9... | collective-permute-start | bytes 1572872 | tf_op jit(solution)/shard_map/ppermute | solution.py:1893
  96.5 73.8 %collective-permute-start.1 = (bf16[256,1024]{1,0:T(8,128)(2,1)}, bf16[256,1024]{1,0:T(8,128)(2,1)S(1)}, u32[]{:S(2)}, u32[]{:S(2)}) collective-permute-start(bf16[256,1024]{1,0:T(8,128)(2,1)} %constant_dynamic-slice_fusion.5), channel_id=1, source_target_pairs={{0,2},{1,3},{2,0},{3,1},{4,6},{5,7},{6,4},{7,5},{8,10},{9,11},{10,... | collective-permute-start | bytes 1572872 | tf_op jit(solution)/shard_map/ppermute | solution.py:1893
  105.9 68.8 %collective-permute-start.2 = (bf16[256,1024]{1,0:T(8,128)(2,1)}, bf16[256,1024]{1,0:T(8,128)(2,1)}, u32[]{:S(2)}, u32[]{:S(2)}) collective-permute-start(bf16[256,1024]{1,0:T(8,128)(2,1)} %constant_dynamic-slice_fusion.5), channel_id=1, source_target_pairs={{0,1},{1,2},{2,3},{3,0},{4,5},{5,6},{6,7},{7,4},{8,9},{9,10},{10,1... | collective-permute-start | bytes 1572872 | tf_op jit(solution)/shard_map/ppermute | solution.py:1893
  113.4 9.3 %copy-start = (bf16[4096,256]{0,1:T(8,128)(2,1)}, bf16[4096,256]{0,1:T(8,128)(2,1)S(1)}, u32[]{:S(2)}) copy-start(bf16[4096,256]{0,1:T(8,128)(2,1)S(1)} %copy.67) | copy-start | bytes 6291460
  113.4 11.6 %copy-start.22 = (f32[4,16,128]{2,1,0:T(8,128)S(1)}, f32[4,16,128]{2,1,0:T(8,128)}, u32[]{:S(2)}) copy-start(f32[4,16,128]{2,1,0:T(8,128)} %get-tuple-element.138) | copy-start | bytes 98308
  113.4 11.7 %copy-start.9 = (bf16[1024,512]{1,0:T(8,128)(2,1)S(1)}, bf16[1024,512]{1,0:T(8,128)(2,1)}, u32[]{:S(2)}) copy-start(bf16[1024,512]{1,0:T(8,128)(2,1)} %get-tuple-element.140.wk) | copy-start | bytes 3145732
  123.6 66.8 %collective-permute-start.5 = (bf16[256,1024]{1,0:T(8,128)(2,1)}, bf16[256,1024]{1,0:T(8,128)(2,1)}, u32[]{:S(2)}, u32[]{:S(2)}) collective-permute-start(bf16[256,1024]{1,0:T(8,128)(2,1)} %constant_dynamic-slice_fusion.4), channel_id=1, source_target_pairs={{0,3},{1,0},{2,1},{3,2},{4,7},{5,4},{6,5},{7,6},{8,11},{9,8},{10,9... | collective-permute-start | bytes 1572872 | tf_op jit(solution)/shard_map/ppermute | solution.py:1893
  123.6 66.8 %collective-permute-start.6 = (bf16[256,1024]{1,0:T(8,128)(2,1)}, bf16[256,1024]{1,0:T(8,128)(2,1)}, u32[]{:S(2)}, u32[]{:S(2)}) collective-permute-start(bf16[256,1024]{1,0:T(8,128)(2,1)} %constant_dynamic-slice_fusion.4), channel_id=1, source_target_pairs={{0,2},{1,3},{2,0},{3,1},{4,6},{5,7},{6,4},{7,5},{8,10},{9,11},{10,... | collective-permute-start | bytes 1572872 | tf_op jit(solution)/shard_map/ppermute | solution.py:1893
  125.1 6.0 copy-start.2
  125.1 6.0 copy-start.10
  131.1 3.7 copy-start.8
  134.9 2.2 copy-start.25
  137.4 29.1 %copy-start.20 = (s32[1024]{0:T(1024)}, s32[1024]{0:T(1024)S(1)}, u32[]{:S(2)}) copy-start(s32[1024]{0:T(1024)S(1)} %pad_dynamic-slice_fusion.2) | copy-start | bytes 12292
  139.1 30.2 %copy-start.5 = (bf16[2,512,1024]{2,1,0:T(8,128)(2,1)S(1)}, bf16[2,512,1024]{2,1,0:T(8,128)(2,1)}, u32[]{:S(2)}) copy-start(bf16[2,512,1024]{2,1,0:T(8,128)(2,1)} %get-tuple-element.135.x_ref) | copy-start | bytes 6291460
  166.5 8.2 %copy-start.17 = (bf16[256,1024]{1,0:T(8,128)(2,1)}, bf16[256,1024]{1,0:T(8,128)(2,1)S(1)}, u32[]{:S(2)}) copy-start(bf16[256,1024]{1,0:T(8,128)(2,1)S(1)} %collective-permute-done) | copy-start | bytes 1572868
  166.5 29.9 %collective-permute-start.7 = (bf16[256,1024]{1,0:T(8,128)(2,1)}, bf16[256,1024]{1,0:T(8,128)(2,1)S(1)}, u32[]{:S(2)}, u32[]{:S(2)}) collective-permute-start(bf16[256,1024]{1,0:T(8,128)(2,1)} %constant_dynamic-slice_fusion.4), channel_id=1, source_target_pairs={{0,1},{1,2},{2,3},{3,0},{4,5},{5,6},{6,7},{7,4},{8,9},{9,10},{10,1... | collective-permute-start | bytes 1572872 | tf_op jit(solution)/shard_map/ppermute | solution.py:1893
  170.3 4.4 copy-start.18
  178.0 20.3 %copy-start.3 = (bf16[768,1024]{1,0:T(8,128)(2,1)}, bf16[768,1024]{1,0:T(8,128)(2,1)S(1)}, u32[]{:S(2)}) copy-start(bf16[768,1024]{1,0:T(8,128)(2,1)S(1)} %constant_dynamic-update-slice_fusion.1.refs_4_.refs_0_) | copy-start | bytes 4718596
  178.0 57.7 %collective-permute-start.3 = (bf16[768,1024]{1,0:T(8,128)(2,1)S(1)}, bf16[768,1024]{1,0:T(8,128)(2,1)}, u32[]{:S(2)}, u32[]{:S(2)}) collective-permute-start(bf16[768,1024]{1,0:T(8,128)(2,1)S(1)} %constant_dynamic-update-slice_fusion.1.refs_4_.refs_0_), channel_id=1, source_target_pairs={{0,8},{8,0},{16,24},{24,16},{1,9},{9,1},{17,25},{25,17},{2,10},{10... | collective-permute-start | bytes 4718600 | tf_op jit(solution)/shard_map/ppermute | solution.py:1896
  179.5 56.2 %collective-permute-start.4 = (bf16[768,1024]{1,0:T(8,128)(2,1)S(1)}, bf16[768,1024]{1,0:T(8,128)(2,1)S(1)}, u32[]{:S(2)}, u32[]{:S(2)}) collective-permute-start(bf16[768,1024]{1,0:T(8,128)(2,1)S(1)} %constant_dynamic-update-slice_fusion.1.refs_4_.refs_0_), channel_id=1, source_target_pairs={{0,16},{8,24},{16,0},{24,8},{1,17},{9,25},{17,1},{25,9},{2,18},{10... | collective-permute-start | bytes 4718600 | tf_op jit(solution)/shard_map/ppermute | solution.py:1896
  190.4 13.6 %copy-start.26 = (s32[1,4]{1,0:T(1,128)S(1)}, s32[1,4]{1,0:T(1,128)}, u32[]{:S(2)}) copy-start(s32[1,4]{1,0:T(1,128)} %param.33) | copy-start | bytes 52
  201.0 59.7 %collective-permute-start.8 = (bf16[768,1024]{1,0:T(8,128)(2,1)}, bf16[768,1024]{1,0:T(8,128)(2,1)}, u32[]{:S(2)}, u32[]{:S(2)}) collective-permute-start(bf16[768,1024]{1,0:T(8,128)(2,1)} %constant_dynamic-update-slice_fusion.4.refs_5_.refs_4_), channel_id=1, source_target_pairs={{0,8},{8,0},{16,24},{24,16},{1,9},{9,1},{17,25},{25,17},{2,10},{10... | collective-permute-start | bytes 4718600 | tf_op jit(solution)/shard_map/ppermute | solution.py:1896
  202.5 58.2 %collective-permute-start.9 = (bf16[768,1024]{1,0:T(8,128)(2,1)}, bf16[768,1024]{1,0:T(8,128)(2,1)}, u32[]{:S(2)}, u32[]{:S(2)}) collective-permute-start(bf16[768,1024]{1,0:T(8,128)(2,1)} %constant_dynamic-update-slice_fusion.4.refs_5_.refs_4_), channel_id=1, source_target_pairs={{0,16},{8,24},{16,0},{24,8},{1,17},{9,25},{17,1},{25,9},{2,18},{10... | collective-permute-start | bytes 4718600 | tf_op jit(solution)/shard_map/ppermute | solution.py:1896
  205.5 4.2 copy-start.6
  205.5 4.2 copy-start.11
  209.7 2.3 copy-start.7
  209.7 2.3 copy-start.15
  235.7 10.3 %copy-start.4 = (bf16[768,1024]{1,0:T(8,128)(2,1)}, bf16[768,1024]{1,0:T(8,128)(2,1)S(1)}, u32[]{:S(2)}) copy-start(bf16[768,1024]{1,0:T(8,128)(2,1)S(1)} %collective-permute-done.4.refs_5_.refs_2_) | copy-start | bytes 4718596
  246.0 15.9 %copy-start.21 = (s32[1024]{0:T(1024)S(1)}, s32[1024]{0:T(1024)}, u32[]{:S(2)}) copy-start(s32[1024]{0:T(1024)} %convert_reduce_fusion.1) | copy-start | bytes 12292
  246.0 16.9 %copy-start.19 = (s32[2048]{0:T(1024)S(1)}, s32[2048]{0:T(1024)}, u32[]{:S(2)}) copy-start(s32[2048]{0:T(1024)} %pad_dynamic-slice_fusion.3) | copy-start | bytes 24580
  246.0 18.9 %copy-start.1 = (bf16[1024,1024]{1,0:T(8,128)(2,1)S(1)}, bf16[1024,1024]{1,0:T(8,128)(2,1)}, u32[]{:S(2)}) copy-start(bf16[1024,1024]{1,0:T(8,128)(2,1)} %get-tuple-element.159.refs_0_) | copy-start | bytes 6291460
  260.7 45.9 %collective-permute-start.11 = (bf16[768,1024]{1,0:T(8,128)(2,1)}, bf16[768,1024]{1,0:T(8,128)(2,1)}, u32[]{:S(2)}, u32[]{:S(2)}) collective-permute-start(bf16[768,1024]{1,0:T(8,128)(2,1)} %collective-permute-done.9.refs_7_.refs_6_), channel_id=1, source_target_pairs={{0,8},{8,0},{16,24},{24,16},{1,9},{9,1},{17,25},{25,17},{2,10},{10... | collective-permute-start | bytes 4718600 | tf_op jit(solution)/shard_map/ppermute | solution.py:1896
  261.3 45.3 %collective-permute-start.10 = (bf16[768,1024]{1,0:T(8,128)(2,1)}, bf16[768,1024]{1,0:T(8,128)(2,1)}, u32[]{:S(2)}, u32[]{:S(2)}) collective-permute-start(bf16[768,1024]{1,0:T(8,128)(2,1)} %collective-permute-done.3.refs_4_.refs_1_), channel_id=1, source_target_pairs={{0,16},{8,24},{16,0},{24,8},{1,17},{9,25},{17,1},{25,9},{2,18},{10... | collective-permute-start | bytes 4718600 | tf_op jit(solution)/shard_map/ppermute | solution.py:1896
  401.5 10.7 %copy-start.12 = (bf16[512,1024]{1,0:T(8,128)(2,1)S(1)}, bf16[512,1024]{1,0:T(8,128)(2,1)}, u32[]{:S(2)}) copy-start(bf16[512,1024]{1,0:T(8,128)(2,1)} %get-tuple-element.157.refs_1_) | copy-start | bytes 3145732
  473.8 12.7 %copy-start.24 = (f32[8,1024]{1,0:T(8,128)S(1)}, f32[8,1024]{1,0:T(8,128)}, u32[]{:S(2)}) copy-start(f32[8,1024]{1,0:T(8,128)} %get-tuple-element.217) | copy-start | bytes 98308
  473.8 12.7 %copy-start.13 = (bf16[512,1024]{1,0:T(8,128)(2,1)S(1)}, bf16[512,1024]{1,0:T(8,128)(2,1)}, u32[]{:S(2)}) copy-start(bf16[512,1024]{1,0:T(8,128)(2,1)} %get-tuple-element.148.refs_1_) | copy-start | bytes 3145732
  544.8 98.4 %copy-start.23 = (f32[4,1,1024]{2,1,0:T(1,128)S(1)}, f32[4,1,1024]{2,1,0:T(1,128)}, u32[]{:S(2)}) copy-start(f32[4,1,1024]{2,1,0:T(1,128)} %get-tuple-element.220) | copy-start | bytes 49156
  733.6 7.8 %copy-start.14 = (bf16[2048,256]{1,0:T(8,128)(2,1)S(1)}, bf16[2048,256]{1,0:T(8,128)(2,1)}, u32[]{:S(2)}) copy-start(bf16[2048,256]{1,0:T(8,128)(2,1)} %get-tuple-element.306) | copy-start | bytes 3145732
  741.4 1.3 copy-start.16

commit v7 on v6

--- a/solution.py
+++ b/solution.py
@@ -1238,7 +1238,7 @@
     )(x_ext, gain[None], shift[None])
 
 
-def junction_kernel(*refs, kinds, mode):
+def junction_kernel(*refs, kinds, mode, then):
     dp, row, col = here()
     twin = (dp, 1 - row, col)
     meet([twin])
@@ -1246,14 +1246,28 @@
     sources = []
     for kind in kinds:
         sources.append((kind, refs.pop(0), refs.pop(0) if kind != "sum" else None))
+    if then:
+        then_w, then_b = refs.pop(0), refs.pop(0)
     if mode == "forward":
-        x_ref, bias, gain, shift, x_out, full, away, came, s1, r1, s2, r2 = refs
+        x_ref, bias, gain, shift, x_out, full, *refs = refs
     elif mode == "backward":
-        res_ref, x_ref, gain, dx_out, full, stats, away, came, s1, r1, s2, r2 = refs
+        res_ref, x_ref, gain, dx_out, full, stats, *refs = refs
+    if mode != "sum":
+        if then:
+            then_out = refs.pop(0)
+        away, came, s1, r1, s2, r2 = refs
     else:
         out, away, came, s1, r1 = refs
     rows = came.shape[0]
     cuts = rows // CUT
+
+    def follow(begin):
+        at = pl.ds(begin, CUT)
+        if then == "queries":
+            value = (mm(full[at, :], then_w[...]) + then_b[...]).astype(low)
+            then_out[at, :] = value * low(HEAD_DIM**-0.5)
+        elif then:
+            then_out[at, :] = mm_nt(full[at, :], then_w[...]).astype(low)
 
     def partial(begin):
         total = None
@@ -1307,16 +1321,18 @@
         copy = remote(place, place, s2.at[t], r2.at[t], twin)
         copy.start()
         gathered.append(copy)
+        follow(begin)
     if mode == "backward":
         for i in range(4):
             stats[i : i + 1, :] = sums[i]
     for copy in sent:
         copy.wait_send()
-    for copy in gathered:
+    for t, copy in enumerate(gathered):
         copy.wait()
-
-
-def junction(mode, sources, others, number):
+        follow(pl.multiple_of((1 - row) * rows + t * CUT, CUT))
+
+
+def junction(mode, sources, others, number, then=None):
     kinds = [x[0] for x in sources]
     first = sources[0]
     tokens = first[1].shape[0]
@@ -1336,9 +1352,15 @@
     scratch = [pltpu.VMEM((rows, deep), low), pltpu.VMEM((rows, deep), low), dma, dma]
     if mode in ("forward", "backward"):
         scratch += [dma, dma]
+    if then:
+        columns = then[1].shape[1 if then[0] == "queries" else 0]
+        shapes.append(jax.ShapeDtypeStruct((tokens, columns), low))
+        others = [*then[1:], *others]
     args = flat + [x[None] if x.ndim == 1 else x for x in others]
     out = pl.pallas_call(
-        functools.partial(junction_kernel, kinds=kinds, mode=mode),
+        functools.partial(
+            junction_kernel, kinds=kinds, mode=mode, then=then[0] if then else None
+        ),
         in_specs=[IN_VMEM] * len(args),
         out_specs=[IN_VMEM] * len(shapes),
         out_shape=shapes,
@@ -1852,7 +1874,7 @@
     )(*firsts, *others)
 
 
-def unpack_kernel(full_a, full_b, hidden0, hidden1, *outs):
+def unpack_kernel(full_a, full_b, hidden0, hidden1, rows, *outs):
     size = full_a.shape[2] // 4
     for g, full in enumerate((full_a, full_b)):
         for i in range(4):
@@ -1860,9 +1882,10 @@
             outs[4 * g + i][...] = value if i < 3 else jnp.transpose(value)
     outs[8][...] = hidden0[0].astype(f32)
     outs[9][...] = jnp.transpose(hidden1[0].astype(f32))
-
-
-def unpack(full_a, full_b, hidden0, hidden1):
+    outs[10][...] = rows[...].astype(f32)
+
+
+def unpack(full_a, full_b, hidden0, hidden1, rows):
     parts, wide, columns = full_a.shape
     inner = hidden0.shape[2]
     size = columns // 4
@@ -1872,18 +1895,21 @@
         (pl.BlockSpec((wide, inner), lambda p: (0, p)), (wide, parts * inner)),
         (pl.BlockSpec((inner, wide), lambda p: (p, 0)), (parts * inner, wide)),
     ]
+    by_rows = pl.BlockSpec((rows.shape[0] // parts, wide), lambda p: (p, 0))
+    layouts.append((by_rows, rows.shape))
     return pl.pallas_call(
         unpack_kernel,
         grid=(parts,),
         in_specs=[
             pl.BlockSpec((1, wide, x.shape[2]), lambda p: (p, 0, 0))
             for x in (full_a, full_b, hidden0, hidden1)
-        ],
+        ]
+        + [by_rows],
         out_specs=[x[0] for x in layouts],
         out_shape=[jax.ShapeDtypeStruct(x[1], f32) for x in layouts],
         compiler_params=pltpu.CompilerParams(vmem_limit_bytes=VMEM),
         name="unpack",
-    )(full_a, full_b, hidden0, hidden1)
+    )(full_a, full_b, hidden0, hidden1, rows)
 
 
 def build_local(mesh):
@@ -1979,12 +2005,14 @@
         pieces1, o1 = lax.optimization_barrier((pieces1, o1))
         rest1 = jnp.concatenate(pieces1, axis=0)
         near1 = [across(rest1, 1), across(rest1, 2)]
-        x1, c = junction("forward", [("nn", o1, wo1)], [x0, out_bias1, gain2, shift2], 3)
-
-        pieces2, c = lax.optimization_barrier((pieces2, c))
+        x1, c, q2 = junction(
+            "forward", [("nn", o1, wo1)], [x0, out_bias1, gain2, shift2], 3,
+            ("queries", wq2, q_bias2),
+        )
+
+        pieces2, q2 = lax.optimization_barrier((pieces2, q2))
         rest2 = jnp.concatenate(pieces2, axis=0)
         near2 = [across(rest2, 1), across(rest2, 2)]
-        q2 = (mm(c, wq2) + q_bias2).astype(low) * scale
         k2 = mm(enc, wk2).astype(low)
         v2 = (mm(enc, wv2) + v_bias2).astype(low)
         o2, lse2 = attend(q2, k2, v2, query_ids, src_ids, False)
@@ -2015,9 +2043,10 @@
         inner = g1.shape[2]
         half = g1.shape[1] // 2
         one = ((half, inner), low)
-        dx2, dyc, stats3 = junction("backward", [("sum", df)], [dz, x2, gain3], 6)
-
-        doc = mm_nt(dyc, wo2).astype(low)
+        dx2, dyc, stats3, doc = junction(
+            "backward", [("sum", df)], [dz, x2, gain3], 6, ("turned", wo2, gain3)
+        )
+
         later = ((half, inner - far_a.shape[1]), low)
         dq2, dk2, dv2, back_a, back_b, far_c, far_d = attend_back(
             q2, k2, v2, doc, o2, lse2, query_ids, src_ids, False,
@@ -2032,10 +2061,11 @@
             [c, enc, dyc], [(0, 0), (1, 0), (1, 0), (2, 0)], [dq2, dk2, dv2, o2]
         )
         enc_back = junction("sum", [("nt", dk2, wk2), ("nt", dv2, wv2)], [], 7)
-        dx1, dy, stats2 = junction("backward", [("nt", dq2, wq2)], [dx2, x1, gain2], 8)
-
-        cross_grads, enc_back, dy = lax.optimization_barrier((cross_grads, enc_back, dy))
-        do = mm_nt(dy, wo1).astype(low)
+        dx1, dy, stats2, do = junction(
+            "backward", [("nt", dq2, wq2)], [dx2, x1, gain2], 8, ("turned", wo1, gain2)
+        )
+
+        cross_grads, enc_back, do = lax.optimization_barrier((cross_grads, enc_back, do))
         (
             dq1, dk1, dv1, near_a, near_b, far_back_a, far_back_b, own1
         ) = attend_back(
@@ -2083,8 +2113,8 @@
         full_a, full_b, hidden1, small, tokens_grad = finish(
             a_sum, b_sum, q_own, small, x0_grad, n_col, n_dp
         )
-        grads = unpack(full_a, full_b, hidden0, hidden1)
-        tokens_grad = tokens_grad.astype(f32)
+        grads = unpack(full_a, full_b, hidden0, hidden1, tokens_grad)
+        tokens_grad = grads[10]
         feature_grads = small[:, :wide]
         column_grads = small[:, wide:].reshape(-1)
 

time: 754 us -> 745 us (0.988)
  matrix products: 28.4 us -> 18.4 us
    dot_general x2 -> x0, matrix products: 7.78 us -> none  [mm_nt(): lax.dot_general(a, b, (((1,), (1,)), ((), ())), preferred_element_type=f32)]
    dot_general x6 -> x5, matrix products: 20.6 us -> 18.4 us  [mm(): lax.dot_general(a, b, (((1,), (0,)), ((), ())), preferred_element_type=f32)]
  transfers between devices with their start and end apart: 12 -> 12, of which waited for: 2 -> 2; matrix products, arithmetic and copies ran while one was open for 6% -> 6% of each run, Pallas kernels for 17% -> 18%
where the time goes in v7:
time: 745 us; the launch traced here: 735 us
  Pallas kernels  633 us (85%)
  local copies, waits for them, and re-layouts  44.5 us (6%)
  starting transfers between devices  25.9 us (3%)
  matrix products  18.4 us (2%)
  waiting for transfers between devices  8.78 us (1%)
    pallas_call x1, Pallas kernels, fold(): pl.pallas_call(functools.partial(fold_kernel, n_col=n_col, n_dp=n_dp), in...  97.7 us
    pallas_call x2, Pallas kernels, attend_back(): pl.pallas_call(functools.partial(attend_back_kernel, span=span, windowed=...  95.4 us
    pallas_call x1, Pallas kernels, start(): pl.pallas_call(functools.partial(start_kernel, n_col=n_col), in_specs=[IN...  85.6 us
    pallas_call x1, Pallas kernels, finish(): pl.pallas_call(functools.partial(finish_kernel, n_col=n_col, n_dp=n_dp),...  81 us
    pallas_call x1, Pallas kernels, hidden_backward(): pl.pallas_call(functools.partial(hidden_back_kernel, n_col=n_col, places=...  75.5 us
    pallas_call x3, Pallas kernels, hidden_forward(): pl.pallas_call(functools.partial(hidden_kernel, numbers=numbers, opening=...  69.7 us
    pallas_call x5, Pallas kernels, junction(): pl.pallas_call(functools.partial(junction_kernel, kinds=kinds, mode=mode,...  51.6 us
    pallas_call x2, Pallas kernels, attend(): pl.pallas_call(functools.partial(attend_kernel, span=span, windowed=windo...  48.9 us
  transfers between devices with their start and end apart: 12, of which 2 were waited for; matrix products, arithmetic and copies ran while one was open for 6% of the time, Pallas kernels for 18%

profile of v7, /device:TPU:8, one launch (start us, length us, event | category | flops | bytes accessed | tf_op | source)
XLA Modules:
  0.0 735.1 jit_solution(9092101100617030084)
XLA Ops:
  4.6 1.5 stack.63
  6.8 85.6 %start.1 = (bf16[2,512,1024]{2,1,0:T(8,128)(2,1)}, bf16[1024,1024]{1,0:T(8,128)(2,1)}, f32[16,1024]{1,0:T(8,128)}, f32[4,16,128]{2,1,0:T(8,128)}, bf16[1024,512]...) custom-call(bf16[2048,256]{1,0:T(8,128)(2,1)} %tokens.1, ...), custom_call_target="tpu_custom_call" | custom-call | tf_op jit(solution)/shard_map/start/pallas_call | solution.py:1175
  92.3 1.9 constant_dynamic-slice_fusion.5
  94.2 2.3 collective-permute-start
  96.5 9.4 %collective-permute-start.1 = (bf16[256,1024]{1,0:T(8,128)(2,1)}, bf16[256,1024]{1,0:T(8,128)(2,1)S(1)}, u32[]{:S(2)}, u32[]{:S(2)}) collective-permute-start(bf16[256,1024]{1,0:T(8,128)(2,1)} %constant_dynamic-slice_fusion.5), channel_id=1, source_target_pairs={{0,2},{1,3},{2,0},{3,1},{4,6},{5,7},{6,4},{7,5},{8,10},{9,11},{10,... | collective-permute-start | bytes 1572872 | tf_op jit(solution)/shard_map/ppermute | solution.py:1919
  105.9 2.9 collective-permute-start.2
  108.8 1.8 fusion.9
  110.6 2.9 copy.67
  113.5 9.3 %enter.1 = bf16[2,1024,1024]{2,1,0:T(8,128)(2,1)} custom-call(bf16[2,512,1024]{2,1,0:T(8,128)(2,1)} %get-tuple-element.139.x_ref, f32[1,1024]{1,0:T(1,128)} %get-tuple-element.255.gain, f32[1,1024]{1,0:T(1,128)} %get-tuple-element.254.shift), custom_call_target="tpu_custom_call" | custom-call | tf_op jit(solution)/shard_map/enter/pallas_call | solution.py:1228
  123.7 1.5 collective-permute-start.6
  125.8 6.0 convolution_convert_fusion.k_ref.refs_1_
  131.8 3.7 add_convert_fusion.v_ref.refs_2_
  135.5 2.2 fusion.5.q_ref.refs_0_
  139.7 27.4 %attend.2 = (bf16[1024,512]{1,0:T(8,128)(2,1)}, f32[4,8,1024]{2,1,0:T(8,128)}) custom-call(bf16[1024,512]{1,0:T(8,128)(2,1)} %fusion.5.q_ref.refs_0_, bf16[2048,512]{1,0:T(8,128)(2,1)} %convolution_convert_fusion.k_ref.refs_1_, bf16[2048,512]{1,0:T(8,128)(2,1)} %add_convert_fusion.v_ref.refs_2_, s32[1024,1]{1,0:T(8,128)} %copy.68.qid_ref, s32[1,2048]{1,0:T(1,128)} %bitcast.104), custom_call_target="tpu_custom_call" | custom-call | tf_op jit(solution)/shard_map/attend/pallas_call | solution.py:236
  167.1 2.6 collective-permute-start.7
  170.8 3.9 collective-permute-done.2
  175.8 1.1 constant_dynamic-update-slice_fusion.2
  178.0 1.6 collective-permute-start.3
  179.5 1.5 collective-permute-start.4
  181.1 10.5 %junction_forward.2 = (f32[512,1024]{1,0:T(8,128)}, bf16[1024,1024]{1,0:T(8,128)(2,1)}, bf16[1024,512]{1,0:T(8,128)(2,1)}) custom-call(bf16[1024,512]{1,0:T(8,128)(2,1)} %get-tuple-element.151.refs_0_.refs_4_.o_in, bf16[512,1024]{1,0:T(8,128)(2,1)} %get-tuple-element.152.refs_1_.refs_2_, bf16[1024,512]{1,0:T(8,128)(2,1)} %get-tuple-element.153.refs_2_.refs_1_, ...), custom_call_target="tpu_custom_call" | custom-call | tf_op jit(solution)/shard_map/junction_forward/pallas_call | solution.py:1360
  191.6 4.9 collective-permute-done.7
  196.4 1.9 constant_dynamic-update-slice_fusion.6
  198.3 1.9 constant_dynamic-update-slice_fusion.5
  201.0 1.5 collective-permute-start.8
  202.5 1.5 collective-permute-start.9
  205.5 4.2 convolution_convert_fusion.1.k_ref.refs_1_
  209.7 2.2 add_convert_fusion.1.v_ref.refs_2_
  211.9 21.5 %attend.3 = (bf16[1024,512]{1,0:T(8,128)(2,1)}, f32[4,8,1024]{2,1,0:T(8,128)}) custom-call(bf16[1024,512]{1,0:T(8,128)(2,1)} %get-tuple-element.155.q_ref.refs_0_, bf16[1024,512]{1,0:T(8,128)(2,1)} %convolution_convert_fusion.1.k_ref.refs_1_, bf16[1024,512]{1,0:T(8,128)(2,1)} %add_convert_fusion.1.v_ref.refs_2_, s32[1024,1]{1,0:T(8,128)} %copy.68.qid_ref, ...), custom_call_target="tpu_custom_call" | custom-call | tf_op jit(solution)/shard_map/attend/pallas_call | solution.py:236
  233.4 10.3 %junction_forward.3 = (f32[512,1024]{1,0:T(8,128)}, bf16[1024,1024]{1,0:T(8,128)(2,1)}) custom-call(bf16[1024,512]{1,0:T(8,128)(2,1)} %get-tuple-element.160.refs_0_.refs_4_.refs_6_, bf16[512,1024]{1,0:T(8,128)(2,1)} %get-tuple-element.161.refs_1_, f32[512,1024]{1,0:T(8,128)} %get-tuple-element.162.refs_2_.refs_5_, f32[1,1024]{1,0:T(1,128)} %get-tuple-element.250.refs_3_, ...), custom_call_target="tpu_custom_call" | custom-call | tf_op jit(solution)/shard_map/junction_forward/pallas_call | solution.py:1360
  243.8 14.8 %hidden_forward.3 = (bf16[1,1024,1024]{2,1,0:T(8,128)(2,1)}, bf16[1,1024,1024]{2,1,0:T(8,128)(2,1)}, f32[1024,1024]{1,0:T(8,128)}) custom-call(bf16[1024,1024]{1,0:T(8,128)(2,1)} %get-tuple-element.163.refs_0_, f32[1,1,1024]{2,1,0:T(1,128)} %get-tuple-element.284.refs_1_, bf16[256,4096]{1,0:T(8,128)(2,1)} %own1, bf16[256,4096]{1,0:T(8,128)(2,1)} %bitcast.90, ...), custom_call_target="tpu_custom_call" | custom-call | tf_op jit(solution)/shard_map/hidden_forward/pallas_call | solution.py:724
  260.7 1.4 copy.73.refs_7_
  262.7 2.5 copy.70
  265.2 35.3 %hidden_forward.4 = (bf16[2,1024,1024]{2,1,0:T(8,128)(2,1)}, bf16[2,1024,1024]{2,1,0:T(8,128)(2,1)}, bf16[2,512,1024]{2,1,0:T(8,128)(2,1)}, f32[1024,1024]{1,0:T(8,128)}) custom-call(bf16[1024,1024]{1,0:T(8,128)(2,1)} %get-tuple-element.163.refs_0_, f32[2,1,1024]{2,1,0:T(1,128)} %pad_maximum_fusion.1.refs_1_, bf16[256,4096]{1,0:T(8,128)(2,1)} %own1, ...), custom_call_target="tpu_custom_call" | custom-call | tf_op jit(solution)/shard_map/hidden_forward/pallas_call | solution.py:724
  300.5 3.9 copy.71.dzt_ref
  304.4 19.7 %hidden_forward.5 = (bf16[1,1024,1024]{2,1,0:T(8,128)(2,1)}, bf16[1,1024,1024]{2,1,0:T(8,128)(2,1)}, bf16[512,1024]{1,0:T(8,128)(2,1)}) custom-call(bf16[1024,1024]{1,0:T(8,128)(2,1)} %get-tuple-element.163.refs_0_, f32[1,1,1024]{2,1,0:T(1,128)} %get-tuple-element.283.refs_1_, bf16[256,4096]{1,0:T(8,128)(2,1)} %own1, bf16[256,4096]{1,0:T(8,128)(2,1)} %bitcast.92, ...), custom_call_target="tpu_custom_call" | custom-call | tf_op jit(solution)/shard_map/hidden_forward/pallas_call | solution.py:724
  324.1 75.5 %hidden_backward.1 = (bf16[4,1024,1024]{2,1,0:T(8,128)(2,1)}, bf16[4,1024,1024]{2,1,0:T(8,128)(2,1)}, f32[4,1,1024]{2,1,0:T(1,128)}, bf16[1024,1024]{1,0:T(8,128...) custom-call(bf16[1024,1024]{1,0:T(8,128)(2,1)} %bitcast.95, ...), custom_call_target="tpu_custom_call" | custom-call | tf_op jit(solution)/shard_map/hidden_backward/pallas_call | solution.py:877
  399.6 11.8 %junction_backward.2 = (f32[512,1024]{1,0:T(8,128)}, bf16[1024,1024]{1,0:T(8,128)(2,1)}, f32[8,1024]{1,0:T(8,128)}, bf16[1024,512]{1,0:T(8,128)(2,1)}) custom-call(bf16[1024,1024]{1,0:T(8,128)(2,1)} %get-tuple-element.185.refs_0_, bf16[512,1024]{1,0:T(8,128)(2,1)} %get-tuple-element.161.refs_1_, f32[1,1024]{1,0:T(1,128)} %get-tuple-element.249.refs_4_.refs_2_.refs_5_, ...), custom_call_target="tpu_custom_call" | custom-call | tf_op jit(solution)/shard_map/junction_backward/pallas_call | solution.py:1360
  411.4 40.8 %attend_back.2 = (bf16[1024,512]{1,0:T(8,128)(2,1)}, bf16[1024,512]{1,0:T(8,128)(2,1)}, bf16[1024,512]{1,0:T(8,128)(2,1)}, bf16[512,1024]{1,0:T(8,128)(2,1)}, bf...) custom-call(bf16[1024,512]{1,0:T(8,128)(2,1)} %get-tuple-element.155.q_ref.refs_0_, ...), custom_call_target="tpu_custom_call" | custom-call | tf_op jit(solution)/shard_map/attend_back/pallas_call | solution.py:340
  452.2 12.2 %junction_backward.3 = (f32[512,1024]{1,0:T(8,128)}, bf16[1024,1024]{1,0:T(8,128)(2,1)}, f32[8,1024]{1,0:T(8,128)}, bf16[1024,512]{1,0:T(8,128)(2,1)}) custom-call(bf16[1024,512]{1,0:T(8,128)(2,1)} %get-tuple-element.193.refs_3_.refs_0_, bf16[1024,512]{1,0:T(8,128)(2,1)} %get-tuple-element.153.refs_2_.refs_1_, ...), custom_call_target="tpu_custom_call" | custom-call | tf_op jit(solution)/shard_map/junction_backward/pallas_call | solution.py:1360
  466.0 6.8 junction_sum.1.enc_in
  472.9 10.2 %column_grads.1 = (bf16[4,1024,512]{2,1,0:T(8,128)(2,1)}, f32[8,512]{1,0:T(8,128)}) custom-call(bf16[1024,1024]{1,0:T(8,128)(2,1)} %get-tuple-element.184.refs_0_, bf16[1024,1024]{1,0:T(8,128)(2,1)} %get-tuple-element.156.refs_1_, bf16[1024,1024]{1,0:T(8,128)(2,1)} %get-tuple-element.186.refs_2_, bf16[1024,512]{1,0:T(8,128)(2,1)} %get-tuple-element.193.refs_3_.refs_0_, ...), custom_call_target="tpu_custom_call" | custom-call | tf_op jit(solution)/shard_map/column_grads/pallas_call | solution.py:1859
  483.0 54.6 %attend_back.3 = (bf16[1024,512]{1,0:T(8,128)(2,1)}, bf16[2048,512]{1,0:T(8,128)(2,1)}, bf16[2048,512]{1,0:T(8,128)(2,1)}, bf16[512,1024]{1,0:T(8,128)(2,1)}, bf...) custom-call(bf16[1024,512]{1,0:T(8,128)(2,1)} %fusion.5.q_ref.refs_0, ...), custom_call_target="tpu_custom_call" | custom-call | tf_op jit(solution)/shard_map/attend_back/pallas_call | solution.py:340
  537.6 97.7 %fold.1 = (f32[8,512]{1,0:T(8,128)}, bf16[512,1024]{1,0:T(8,128)(2,1)}, f32[8,1024]{1,0:T(8,128)}, bf16[1024,512]{1,0:T(8,128)(2,1)}, bf16[1024,512]{1,0:T(8,128...) custom-call(bf16[1024,512]{1,0:T(8,128)(2,1)} %get-tuple-element.207.dq, ...), custom_call_target="tpu_custom_call" | custom-call | tf_op jit(solution)/shard_map/fold/pallas_call | solution.py:1660
  638.6 81.0 %finish.1 = (bf16[4,256,512]{2,1,0:T(8,128)(2,1)}, bf16[4,256,512]{2,1,0:T(8,128)(2,1)}, bf16[4,256,1024]{2,1,0:T(8,128)(2,1)}, f32[16,384]{1,0:T(8,128)}, bf16[2048,256]{1,0:T(8,128)(2,1)}) custom-call(bf16[1024,512]{1,0:T(8,128)(2,1)} %get-tuple-element.219.a_sum, bf16[1024,512]{1,0:T(8,128)(2,1)} %get-tuple-element.220.b_sum, ...), custom_call_target="tpu_custom_call" | custom-call | tf_op jit(solution)/shard_map/finish/pallas_call | solution.py:1808
  719.6 1.6 fusion.11
  721.2 1.3 slice_bitcast_fusion.1
  722.5 1.4 slice_bitcast_fusion.5
  723.9 8.6 %unpack.1 = (f32[256,512]{1,0:T(8,128)}, f32[256,512]{1,0:T(8,128)}, f32[256,512]{1,0:T(8,128)}, f32[512,256]{1,0:T(8,128)}, f32[256,512]{1,0:T(8,128)}, /*index...) custom-call(bf16[4,256,512]{2,1,0:T(8,128)(2,1)} %get-tuple-element., ...), custom_call_target="tpu_custom_call" | custom-call | tf_op jit(solution)/shard_map/unpack/pallas_call | solution.py:1900
  (107 shorter events, 23.1 us)
Async XLA Ops:
  94.2 72.9 %collective-permute-start = (bf16[256,1024]{1,0:T(8,128)(2,1)}, bf16[256,1024]{1,0:T(8,128)(2,1)S(1)}, u32[]{:S(2)}, u32[]{:S(2)}) collective-permute-start(bf16[256,1024]{1,0:T(8,128)(2,1)} %constant_dynamic-slice_fusion.5), channel_id=1, source_target_pairs={{0,3},{1,0},{2,1},{3,2},{4,7},{5,4},{6,5},{7,6},{8,11},{9,8},{10,9... | collective-permute-start | bytes 1572872 | tf_op jit(solution)/shard_map/ppermute | solution.py:1919
  96.5 74.3 %collective-permute-start.1 = (bf16[256,1024]{1,0:T(8,128)(2,1)}, bf16[256,1024]{1,0:T(8,128)(2,1)S(1)}, u32[]{:S(2)}, u32[]{:S(2)}) collective-permute-start(bf16[256,1024]{1,0:T(8,128)(2,1)} %constant_dynamic-slice_fusion.5), channel_id=1, source_target_pairs={{0,2},{1,3},{2,0},{3,1},{4,6},{5,7},{6,4},{7,5},{8,10},{9,11},{10,... | collective-permute-start | bytes 1572872 | tf_op jit(solution)/shard_map/ppermute | solution.py:1919
  105.9 68.8 %collective-permute-start.2 = (bf16[256,1024]{1,0:T(8,128)(2,1)}, bf16[256,1024]{1,0:T(8,128)(2,1)}, u32[]{:S(2)}, u32[]{:S(2)}) collective-permute-start(bf16[256,1024]{1,0:T(8,128)(2,1)} %constant_dynamic-slice_fusion.5), channel_id=1, source_target_pairs={{0,1},{1,2},{2,3},{3,0},{4,5},{5,6},{6,7},{7,4},{8,9},{9,10},{10,1... | collective-permute-start | bytes 1572872 | tf_op jit(solution)/shard_map/ppermute | solution.py:1919
  113.5 9.3 %copy-start = (bf16[4096,256]{0,1:T(8,128)(2,1)}, bf16[4096,256]{0,1:T(8,128)(2,1)S(1)}, u32[]{:S(2)}) copy-start(bf16[4096,256]{0,1:T(8,128)(2,1)S(1)} %copy.67) | copy-start | bytes 6291460
  113.5 11.6 %copy-start.18 = (f32[4,16,128]{2,1,0:T(8,128)S(1)}, f32[4,16,128]{2,1,0:T(8,128)}, u32[]{:S(2)}) copy-start(f32[4,16,128]{2,1,0:T(8,128)} %get-tuple-element.142) | copy-start | bytes 98308
  113.5 12.2 %copy-start.8 = (bf16[1024,512]{1,0:T(8,128)(2,1)S(1)}, bf16[1024,512]{1,0:T(8,128)(2,1)}, u32[]{:S(2)}) copy-start(bf16[1024,512]{1,0:T(8,128)(2,1)} %get-tuple-element.144.wk) | copy-start | bytes 3145732
  123.7 67.9 %collective-permute-start.5 = (bf16[256,1024]{1,0:T(8,128)(2,1)}, bf16[256,1024]{1,0:T(8,128)(2,1)}, u32[]{:S(2)}, u32[]{:S(2)}) collective-permute-start(bf16[256,1024]{1,0:T(8,128)(2,1)} %constant_dynamic-slice_fusion.4), channel_id=1, source_target_pairs={{0,3},{1,0},{2,1},{3,2},{4,7},{5,4},{6,5},{7,6},{8,11},{9,8},{10,9... | collective-permute-start | bytes 1572872 | tf_op jit(solution)/shard_map/ppermute | solution.py:1919
  123.7 67.9 %collective-permute-start.6 = (bf16[256,1024]{1,0:T(8,128)(2,1)}, bf16[256,1024]{1,0:T(8,128)(2,1)}, u32[]{:S(2)}, u32[]{:S(2)}) collective-permute-start(bf16[256,1024]{1,0:T(8,128)(2,1)} %constant_dynamic-slice_fusion.4), channel_id=1, source_target_pairs={{0,2},{1,3},{2,0},{3,1},{4,6},{5,7},{6,4},{7,5},{8,10},{9,11},{10,... | collective-permute-start | bytes 1572872 | tf_op jit(solution)/shard_map/ppermute | solution.py:1919
  125.8 6.0 copy-start.2
  125.8 6.0 copy-start.9
  131.8 3.7 copy-start.7
  135.5 2.2 copy-start.21
  138.0 29.1 %copy-start.16 = (s32[1024]{0:T(1024)}, s32[1024]{0:T(1024)S(1)}, u32[]{:S(2)}) copy-start(s32[1024]{0:T(1024)S(1)} %pad_dynamic-slice_fusion.2) | copy-start | bytes 12292
  139.7 30.1 %copy-start.5 = (bf16[2,512,1024]{2,1,0:T(8,128)(2,1)S(1)}, bf16[2,512,1024]{2,1,0:T(8,128)(2,1)}, u32[]{:S(2)}) copy-start(bf16[2,512,1024]{2,1,0:T(8,128)(2,1)} %get-tuple-element.139.x_ref) | copy-start | bytes 6291460
  167.1 7.6 %copy-start.13 = (bf16[256,1024]{1,0:T(8,128)(2,1)}, bf16[256,1024]{1,0:T(8,128)(2,1)S(1)}, u32[]{:S(2)}) copy-start(bf16[256,1024]{1,0:T(8,128)(2,1)S(1)} %collective-permute-done) | copy-start | bytes 1572868
  167.1 29.3 %collective-permute-start.7 = (bf16[256,1024]{1,0:T(8,128)(2,1)}, bf16[256,1024]{1,0:T(8,128)(2,1)S(1)}, u32[]{:S(2)}, u32[]{:S(2)}) collective-permute-start(bf16[256,1024]{1,0:T(8,128)(2,1)} %constant_dynamic-slice_fusion.4), channel_id=1, source_target_pairs={{0,1},{1,2},{2,3},{3,0},{4,5},{5,6},{6,7},{7,4},{8,9},{9,10},{10,1... | collective-permute-start | bytes 1572872 | tf_op jit(solution)/shard_map/ppermute | solution.py:1919
  170.8 3.9 copy-start.14
  178.0 13.6 %copy-start.3 = (bf16[768,1024]{1,0:T(8,128)(2,1)}, bf16[768,1024]{1,0:T(8,128)(2,1)S(1)}, u32[]{:S(2)}) copy-start(bf16[768,1024]{1,0:T(8,128)(2,1)S(1)} %constant_dynamic-update-slice_fusion.1.refs_4_.refs_0_) | copy-start | bytes 4718596
  178.0 55.4 %collective-permute-start.3 = (bf16[768,1024]{1,0:T(8,128)(2,1)S(1)}, bf16[768,1024]{1,0:T(8,128)(2,1)}, u32[]{:S(2)}, u32[]{:S(2)}) collective-permute-start(bf16[768,1024]{1,0:T(8,128)(2,1)S(1)} %constant_dynamic-update-slice_fusion.1.refs_4_.refs_0_), channel_id=1, source_target_pairs={{0,8},{8,0},{16,24},{24,16},{1,9},{9,1},{17,25},{25,17},{2,10},{10... | collective-permute-start | bytes 4718600 | tf_op jit(solution)/shard_map/ppermute | solution.py:1922
  179.5 53.9 %collective-permute-start.4 = (bf16[768,1024]{1,0:T(8,128)(2,1)S(1)}, bf16[768,1024]{1,0:T(8,128)(2,1)S(1)}, u32[]{:S(2)}, u32[]{:S(2)}) collective-permute-start(bf16[768,1024]{1,0:T(8,128)(2,1)S(1)} %constant_dynamic-update-slice_fusion.1.refs_4_.refs_0_), channel_id=1, source_target_pairs={{0,16},{8,24},{16,0},{24,8},{1,17},{9,25},{17,1},{25,9},{2,18},{10... | collective-permute-start | bytes 4718600 | tf_op jit(solution)/shard_map/ppermute | solution.py:1922
  191.5 12.5 %copy-start.22 = (s32[1,4]{1,0:T(1,128)S(1)}, s32[1,4]{1,0:T(1,128)}, u32[]{:S(2)}) copy-start(s32[1,4]{1,0:T(1,128)} %param.33) | copy-start | bytes 52
  201.0 57.6 %collective-permute-start.8 = (bf16[768,1024]{1,0:T(8,128)(2,1)}, bf16[768,1024]{1,0:T(8,128)(2,1)}, u32[]{:S(2)}, u32[]{:S(2)}) collective-permute-start(bf16[768,1024]{1,0:T(8,128)(2,1)} %constant_dynamic-update-slice_fusion.4.refs_5_.refs_4_), channel_id=1, source_target_pairs={{0,8},{8,0},{16,24},{24,16},{1,9},{9,1},{17,25},{25,17},{2,10},{10... | collective-permute-start | bytes 4718600 | tf_op jit(solution)/shard_map/ppermute | solution.py:1922
  202.5 56.1 %collective-permute-start.9 = (bf16[768,1024]{1,0:T(8,128)(2,1)}, bf16[768,1024]{1,0:T(8,128)(2,1)}, u32[]{:S(2)}, u32[]{:S(2)}) collective-permute-start(bf16[768,1024]{1,0:T(8,128)(2,1)} %constant_dynamic-update-slice_fusion.4.refs_5_.refs_4_), channel_id=1, source_target_pairs={{0,16},{8,24},{16,0},{24,8},{1,17},{9,25},{17,1},{25,9},{2,18},{10... | collective-permute-start | bytes 4718600 | tf_op jit(solution)/shard_map/ppermute | solution.py:1922
  205.5 4.2 copy-start.6
  205.5 4.2 copy-start.10
  233.4 10.3 %copy-start.4 = (bf16[768,1024]{1,0:T(8,128)(2,1)}, bf16[768,1024]{1,0:T(8,128)(2,1)S(1)}, u32[]{:S(2)}) copy-start(bf16[768,1024]{1,0:T(8,128)(2,1)S(1)} %collective-permute-done.4.refs_5_.refs_2_) | copy-start | bytes 4718596
  243.7 15.9 %copy-start.17 = (s32[1024]{0:T(1024)S(1)}, s32[1024]{0:T(1024)}, u32[]{:S(2)}) copy-start(s32[1024]{0:T(1024)} %convert_reduce_fusion.1) | copy-start | bytes 12292
  243.8 16.9 %copy-start.15 = (s32[2048]{0:T(1024)S(1)}, s32[2048]{0:T(1024)}, u32[]{:S(2)}) copy-start(s32[2048]{0:T(1024)} %pad_dynamic-slice_fusion.3) | copy-start | bytes 24580
  243.8 18.9 %copy-start.1 = (bf16[1024,1024]{1,0:T(8,128)(2,1)S(1)}, bf16[1024,1024]{1,0:T(8,128)(2,1)}, u32[]{:S(2)}) copy-start(bf16[1024,1024]{1,0:T(8,128)(2,1)} %get-tuple-element.163.refs_0_) | copy-start | bytes 6291460
  258.6 45.9 %collective-permute-start.11 = (bf16[768,1024]{1,0:T(8,128)(2,1)}, bf16[768,1024]{1,0:T(8,128)(2,1)}, u32[]{:S(2)}, u32[]{:S(2)}) collective-permute-start(bf16[768,1024]{1,0:T(8,128)(2,1)} %collective-permute-done.9.refs_7_.refs_6_), channel_id=1, source_target_pairs={{0,8},{8,0},{16,24},{24,16},{1,9},{9,1},{17,25},{25,17},{2,10},{10... | collective-permute-start | bytes 4718600 | tf_op jit(solution)/shard_map/ppermute | solution.py:1922
  259.1 45.3 %collective-permute-start.10 = (bf16[768,1024]{1,0:T(8,128)(2,1)}, bf16[768,1024]{1,0:T(8,128)(2,1)}, u32[]{:S(2)}, u32[]{:S(2)}) collective-permute-start(bf16[768,1024]{1,0:T(8,128)(2,1)} %collective-permute-done.3.refs_4_.refs_1_), channel_id=1, source_target_pairs={{0,16},{8,24},{16,0},{24,8},{1,17},{9,25},{17,1},{25,9},{2,18},{10... | collective-permute-start | bytes 4718600 | tf_op jit(solution)/shard_map/ppermute | solution.py:1922
  452.2 13.8 %copy-start.20 = (f32[8,1024]{1,0:T(8,128)S(1)}, f32[8,1024]{1,0:T(8,128)}, u32[]{:S(2)}) copy-start(f32[8,1024]{1,0:T(8,128)} %get-tuple-element.224) | copy-start | bytes 98308
  537.6 98.6 %copy-start.19 = (f32[4,1,1024]{2,1,0:T(1,128)S(1)}, f32[4,1,1024]{2,1,0:T(1,128)}, u32[]{:S(2)}) copy-start(f32[4,1,1024]{2,1,0:T(1,128)} %get-tuple-element.227) | copy-start | bytes 49156
  723.9 8.6 %copy-start.11 = (bf16[2048,256]{1,0:T(8,128)(2,1)S(1)}, bf16[2048,256]{1,0:T(8,128)(2,1)}, u32[]{:S(2)}) copy-start(bf16[2048,256]{1,0:T(8,128)(2,1)} %get-tuple-element.314) | copy-start | bytes 3145732
  732.5 1.3 copy-start.12

commit v8 on v7

--- a/solution.py
+++ b/solution.py
@@ -628,12 +628,6 @@
     for i, w in enumerate((w1, w2)):
         pltpu.make_async_copy(w.at[slot], w.at[slot], w_sem.at[i, slot]).wait()
 
-    if riding:
-
-        @pl.when(step == steps - 1)
-        def _():
-            turn()
-
     def one_part(t, carry):
         rows = pl.ds(pl.multiple_of(t * 256, 256), 256)
         h = mm(f_ref[rows, :], w1[slot]) + b1_ref[0]
@@ -652,7 +646,7 @@
     @pl.when(step == steps - 1)
     def _():
         if riding:
-            end()
+            turn()
         if not closing:
             out_ref[...] = total[...]
         else:
@@ -671,6 +665,9 @@
                 sent[t].wait()
                 branch = total[pl.ds(begin, CUT), :] + came[at, :].astype(f32)
                 out_ref[at, :] = (x_ref[at, :] + (branch + bias[...])).astype(low)
+        if riding:
+            end()
+
 
 def hidden_forward(f, b1, own1, own2, rest1, rest2, numbers, number, sum_in=None, x=None, bias=None,
                    cotangent=None, n_col=0):
@@ -1761,6 +1758,7 @@
         for k in ks:
             buf[k - 1] = whole[pl.ds(k * wide, wide), :]
         line.begin()
+    send_home(tg, tg_out, t_s, t_r, n_col)
     for i in range(1, len(partners)):
         small_step(i)
     hidden1[part] = q_own[...]
@@ -1770,7 +1768,6 @@
         line_a.go(d)
         line_b.go(d)
     small_step(len(partners))
-    send_home(tg, tg_out, t_s, t_r, n_col)
     for i, (line, whole, full, spread) in enumerate((
         (line_a, a_sum, full_a, spread_a), (line_b, b_sum, full_b, spread_b),
     )):

time: 745 us -> 741 us (level)
  no operation moved by 1% of the time
where the time goes in v8:
time: 741 us; the launch traced here: 731 us
  Pallas kernels  630 us (85%)
  local copies, waits for them, and re-layouts  44.5 us (6%)
  starting transfers between devices  25.9 us (3%)
  matrix products  18.4 us (2%)
  waiting for transfers between devices  8.78 us (1%)
    pallas_call x1, Pallas kernels, fold(): pl.pallas_call(functools.partial(fold_kernel, n_col=n_col, n_dp=n_dp), in...  97.7 us
    pallas_call x2, Pallas kernels, attend_back(): pl.pallas_call(functools.partial(attend_back_kernel, span=span, windowed=...  95.4 us
    pallas_call x1, Pallas kernels, start(): pl.pallas_call(functools.partial(start_kernel, n_col=n_col), in_specs=[IN...  85.6 us
    pallas_call x1, Pallas kernels, finish(): pl.pallas_call(functools.partial(finish_kernel, n_col=n_col, n_dp=n_dp),...  80 us
    pallas_call x1, Pallas kernels, hidden_backward(): pl.pallas_call(functools.partial(hidden_back_kernel, n_col=n_col, places=...  75.2 us
    pallas_call x3, Pallas kernels, hidden_forward(): pl.pallas_call(functools.partial(hidden_kernel, numbers=numbers, opening=...  67.6 us
    pallas_call x5, Pallas kernels, junction(): pl.pallas_call(functools.partial(junction_kernel, kinds=kinds, mode=mode,...  51.6 us
    pallas_call x2, Pallas kernels, attend(): pl.pallas_call(functools.partial(attend_kernel, span=span, windowed=windo...  48.9 us
  transfers between devices with their start and end apart: 12, of which 2 were waited for; matrix products, arithmetic and copies ran while one was open for 6% of the time, Pallas kernels for 18%

profile of v8, /device:TPU:8, one launch (start us, length us, event | category | flops | bytes accessed | tf_op | source)
XLA Modules:
  0.0 731.5 jit_solution(17032818145279824768)
XLA Ops:
  4.6 1.5 stack.63
  6.8 85.6 %start.1 = (bf16[2,512,1024]{2,1,0:T(8,128)(2,1)}, bf16[1024,1024]{1,0:T(8,128)(2,1)}, f32[16,1024]{1,0:T(8,128)}, f32[4,16,128]{2,1,0:T(8,128)}, bf16[1024,512]...) custom-call(bf16[2048,256]{1,0:T(8,128)(2,1)} %tokens.1, ...), custom_call_target="tpu_custom_call" | custom-call | tf_op jit(solution)/shard_map/start/pallas_call | solution.py:1172
  92.3 1.9 constant_dynamic-slice_fusion.5
  94.2 2.3 collective-permute-start
  96.5 9.4 %collective-permute-start.1 = (bf16[256,1024]{1,0:T(8,128)(2,1)}, bf16[256,1024]{1,0:T(8,128)(2,1)S(1)}, u32[]{:S(2)}, u32[]{:S(2)}) collective-permute-start(bf16[256,1024]{1,0:T(8,128)(2,1)} %constant_dynamic-slice_fusion.5), channel_id=1, source_target_pairs={{0,2},{1,3},{2,0},{3,1},{4,6},{5,7},{6,4},{7,5},{8,10},{9,11},{10,... | collective-permute-start | bytes 1572872 | tf_op jit(solution)/shard_map/ppermute | solution.py:1916
  105.9 2.9 collective-permute-start.2
  108.8 1.8 fusion.9
  110.6 2.9 copy.67
  113.5 9.3 %enter.1 = bf16[2,1024,1024]{2,1,0:T(8,128)(2,1)} custom-call(bf16[2,512,1024]{2,1,0:T(8,128)(2,1)} %get-tuple-element.139.x_ref, f32[1,1024]{1,0:T(1,128)} %get-tuple-element.255.gain, f32[1,1024]{1,0:T(1,128)} %get-tuple-element.254.shift), custom_call_target="tpu_custom_call" | custom-call | tf_op jit(solution)/shard_map/enter/pallas_call | solution.py:1225
  123.7 1.5 collective-permute-start.6
  125.8 6.0 convolution_convert_fusion.k_ref.refs_1_
  131.8 3.7 add_convert_fusion.v_ref.refs_2_
  135.5 2.2 fusion.5.q_ref.refs_0_
  139.7 27.4 %attend.2 = (bf16[1024,512]{1,0:T(8,128)(2,1)}, f32[4,8,1024]{2,1,0:T(8,128)}) custom-call(bf16[1024,512]{1,0:T(8,128)(2,1)} %fusion.5.q_ref.refs_0_, bf16[2048,512]{1,0:T(8,128)(2,1)} %convolution_convert_fusion.k_ref.refs_1_, bf16[2048,512]{1,0:T(8,128)(2,1)} %add_convert_fusion.v_ref.refs_2_, s32[1024,1]{1,0:T(8,128)} %copy.68.qid_ref, s32[1,2048]{1,0:T(1,128)} %bitcast.104), custom_call_target="tpu_custom_call" | custom-call | tf_op jit(solution)/shard_map/attend/pallas_call | solution.py:236
  167.1 2.6 collective-permute-start.7
  170.8 3.9 collective-permute-done.2
  175.8 1.1 constant_dynamic-update-slice_fusion.2
  178.0 1.6 collective-permute-start.3
  179.5 1.5 collective-permute-start.4
  181.1 10.5 %junction_forward.2 = (f32[512,1024]{1,0:T(8,128)}, bf16[1024,1024]{1,0:T(8,128)(2,1)}, bf16[1024,512]{1,0:T(8,128)(2,1)}) custom-call(bf16[1024,512]{1,0:T(8,128)(2,1)} %get-tuple-element.151.refs_0_.refs_4_.o_in, bf16[512,1024]{1,0:T(8,128)(2,1)} %get-tuple-element.152.refs_1_.refs_2_, bf16[1024,512]{1,0:T(8,128)(2,1)} %get-tuple-element.153.refs_2_.refs_1_, ...), custom_call_target="tpu_custom_call" | custom-call | tf_op jit(solution)/shard_map/junction_forward/pallas_call | solution.py:1357
  191.6 4.9 collective-permute-done.7
  196.4 1.9 constant_dynamic-update-slice_fusion.6
  198.3 1.9 constant_dynamic-update-slice_fusion.5
  201.0 1.5 collective-permute-start.8
  202.5 1.5 collective-permute-start.9
  205.5 4.2 convolution_convert_fusion.1.k_ref.refs_1_
  209.7 2.2 add_convert_fusion.1.v_ref.refs_2_
  211.9 21.5 %attend.3 = (bf16[1024,512]{1,0:T(8,128)(2,1)}, f32[4,8,1024]{2,1,0:T(8,128)}) custom-call(bf16[1024,512]{1,0:T(8,128)(2,1)} %get-tuple-element.155.q_ref.refs_0_, bf16[1024,512]{1,0:T(8,128)(2,1)} %convolution_convert_fusion.1.k_ref.refs_1_, bf16[1024,512]{1,0:T(8,128)(2,1)} %add_convert_fusion.1.v_ref.refs_2_, s32[1024,1]{1,0:T(8,128)} %copy.68.qid_ref, ...), custom_call_target="tpu_custom_call" | custom-call | tf_op jit(solution)/shard_map/attend/pallas_call | solution.py:236
  233.4 10.3 %junction_forward.3 = (f32[512,1024]{1,0:T(8,128)}, bf16[1024,1024]{1,0:T(8,128)(2,1)}) custom-call(bf16[1024,512]{1,0:T(8,128)(2,1)} %get-tuple-element.160.refs_0_.refs_4_.refs_6_, bf16[512,1024]{1,0:T(8,128)(2,1)} %get-tuple-element.161.refs_1_, f32[512,1024]{1,0:T(8,128)} %get-tuple-element.162.refs_2_.refs_5_, f32[1,1024]{1,0:T(1,128)} %get-tuple-element.250.refs_3_, ...), custom_call_target="tpu_custom_call" | custom-call | tf_op jit(solution)/shard_map/junction_forward/pallas_call | solution.py:1357
  243.8 14.8 %hidden_forward.3 = (bf16[1,1024,1024]{2,1,0:T(8,128)(2,1)}, bf16[1,1024,1024]{2,1,0:T(8,128)(2,1)}, f32[1024,1024]{1,0:T(8,128)}) custom-call(bf16[1024,1024]{1,0:T(8,128)(2,1)} %get-tuple-element.163.refs_0_, f32[1,1,1024]{2,1,0:T(1,128)} %get-tuple-element.284.refs_1_, bf16[256,4096]{1,0:T(8,128)(2,1)} %own1, bf16[256,4096]{1,0:T(8,128)(2,1)} %bitcast.90, ...), custom_call_target="tpu_custom_call" | custom-call | tf_op jit(solution)/shard_map/hidden_forward/pallas_call | solution.py:721
  260.7 1.4 copy.73.refs_7_
  262.7 2.5 copy.70
  265.2 35.0 %hidden_forward.4 = (bf16[2,1024,1024]{2,1,0:T(8,128)(2,1)}, bf16[2,1024,1024]{2,1,0:T(8,128)(2,1)}, bf16[2,512,1024]{2,1,0:T(8,128)(2,1)}, f32[1024,1024]{1,0:T(8,128)}) custom-call(bf16[1024,1024]{1,0:T(8,128)(2,1)} %get-tuple-element.163.refs_0_, f32[2,1,1024]{2,1,0:T(1,128)} %pad_maximum_fusion.1.refs_1_, bf16[256,4096]{1,0:T(8,128)(2,1)} %own1, ...), custom_call_target="tpu_custom_call" | custom-call | tf_op jit(solution)/shard_map/hidden_forward/pallas_call | solution.py:721
  300.2 3.9 copy.71.dzt_ref
  304.2 17.8 %hidden_forward.5 = (bf16[1,1024,1024]{2,1,0:T(8,128)(2,1)}, bf16[1,1024,1024]{2,1,0:T(8,128)(2,1)}, bf16[512,1024]{1,0:T(8,128)(2,1)}) custom-call(bf16[1024,1024]{1,0:T(8,128)(2,1)} %get-tuple-element.163.refs_0_, f32[1,1,1024]{2,1,0:T(1,128)} %get-tuple-element.283.refs_1_, bf16[256,4096]{1,0:T(8,128)(2,1)} %own1, bf16[256,4096]{1,0:T(8,128)(2,1)} %bitcast.92, ...), custom_call_target="tpu_custom_call" | custom-call | tf_op jit(solution)/shard_map/hidden_forward/pallas_call | solution.py:721
  321.9 75.2 %hidden_backward.1 = (bf16[4,1024,1024]{2,1,0:T(8,128)(2,1)}, bf16[4,1024,1024]{2,1,0:T(8,128)(2,1)}, f32[4,1,1024]{2,1,0:T(1,128)}, bf16[1024,1024]{1,0:T(8,128...) custom-call(bf16[1024,1024]{1,0:T(8,128)(2,1)} %bitcast.95, ...), custom_call_target="tpu_custom_call" | custom-call | tf_op jit(solution)/shard_map/hidden_backward/pallas_call | solution.py:874
  397.1 11.8 %junction_backward.2 = (f32[512,1024]{1,0:T(8,128)}, bf16[1024,1024]{1,0:T(8,128)(2,1)}, f32[8,1024]{1,0:T(8,128)}, bf16[1024,512]{1,0:T(8,128)(2,1)}) custom-call(bf16[1024,1024]{1,0:T(8,128)(2,1)} %get-tuple-element.185.refs_0_, bf16[512,1024]{1,0:T(8,128)(2,1)} %get-tuple-element.161.refs_1_, f32[1,1024]{1,0:T(1,128)} %get-tuple-element.249.refs_4_.refs_2_.refs_5_, ...), custom_call_target="tpu_custom_call" | custom-call | tf_op jit(solution)/shard_map/junction_backward/pallas_call | solution.py:1357
  408.9 40.8 %attend_back.2 = (bf16[1024,512]{1,0:T(8,128)(2,1)}, bf16[1024,512]{1,0:T(8,128)(2,1)}, bf16[1024,512]{1,0:T(8,128)(2,1)}, bf16[512,1024]{1,0:T(8,128)(2,1)}, bf...) custom-call(bf16[1024,512]{1,0:T(8,128)(2,1)} %get-tuple-element.155.q_ref.refs_0_, ...), custom_call_target="tpu_custom_call" | custom-call | tf_op jit(solution)/shard_map/attend_back/pallas_call | solution.py:340
  449.7 12.2 %junction_backward.3 = (f32[512,1024]{1,0:T(8,128)}, bf16[1024,1024]{1,0:T(8,128)(2,1)}, f32[8,1024]{1,0:T(8,128)}, bf16[1024,512]{1,0:T(8,128)(2,1)}) custom-call(bf16[1024,512]{1,0:T(8,128)(2,1)} %get-tuple-element.193.refs_3_.refs_0_, bf16[1024,512]{1,0:T(8,128)(2,1)} %get-tuple-element.153.refs_2_.refs_1_, ...), custom_call_target="tpu_custom_call" | custom-call | tf_op jit(solution)/shard_map/junction_backward/pallas_call | solution.py:1357
  463.5 6.8 junction_sum.1.enc_in
  470.3 10.2 %column_grads.1 = (bf16[4,1024,512]{2,1,0:T(8,128)(2,1)}, f32[8,512]{1,0:T(8,128)}) custom-call(bf16[1024,1024]{1,0:T(8,128)(2,1)} %get-tuple-element.184.refs_0_, bf16[1024,1024]{1,0:T(8,128)(2,1)} %get-tuple-element.156.refs_1_, bf16[1024,1024]{1,0:T(8,128)(2,1)} %get-tuple-element.186.refs_2_, bf16[1024,512]{1,0:T(8,128)(2,1)} %get-tuple-element.193.refs_3_.refs_0_, ...), custom_call_target="tpu_custom_call" | custom-call | tf_op jit(solution)/shard_map/column_grads/pallas_call | solution.py:1856
  480.5 54.6 %attend_back.3 = (bf16[1024,512]{1,0:T(8,128)(2,1)}, bf16[2048,512]{1,0:T(8,128)(2,1)}, bf16[2048,512]{1,0:T(8,128)(2,1)}, bf16[512,1024]{1,0:T(8,128)(2,1)}, bf...) custom-call(bf16[1024,512]{1,0:T(8,128)(2,1)} %fusion.5.q_ref.refs_0, ...), custom_call_target="tpu_custom_call" | custom-call | tf_op jit(solution)/shard_map/attend_back/pallas_call | solution.py:340
  535.1 97.7 %fold.1 = (f32[8,512]{1,0:T(8,128)}, bf16[512,1024]{1,0:T(8,128)(2,1)}, f32[8,1024]{1,0:T(8,128)}, bf16[1024,512]{1,0:T(8,128)(2,1)}, bf16[1024,512]{1,0:T(8,128...) custom-call(bf16[1024,512]{1,0:T(8,128)(2,1)} %get-tuple-element.207.dq, ...), custom_call_target="tpu_custom_call" | custom-call | tf_op jit(solution)/shard_map/fold/pallas_call | solution.py:1657
  636.1 80.0 %finish.1 = (bf16[4,256,512]{2,1,0:T(8,128)(2,1)}, bf16[4,256,512]{2,1,0:T(8,128)(2,1)}, bf16[4,256,1024]{2,1,0:T(8,128)(2,1)}, f32[16,384]{1,0:T(8,128)}, bf16[2048,256]{1,0:T(8,128)(2,1)}) custom-call(bf16[1024,512]{1,0:T(8,128)(2,1)} %get-tuple-element.219.a_sum, bf16[1024,512]{1,0:T(8,128)(2,1)} %get-tuple-element.220.b_sum, ...), custom_call_target="tpu_custom_call" | custom-call | tf_op jit(solution)/shard_map/finish/pallas_call | solution.py:1805
  716.1 1.6 fusion.11
  717.7 1.3 slice_bitcast_fusion.1
  719.0 1.4 slice_bitcast_fusion.5
  720.3 8.6 %unpack.1 = (f32[256,512]{1,0:T(8,128)}, f32[256,512]{1,0:T(8,128)}, f32[256,512]{1,0:T(8,128)}, f32[512,256]{1,0:T(8,128)}, f32[256,512]{1,0:T(8,128)}, /*index...) custom-call(bf16[4,256,512]{2,1,0:T(8,128)(2,1)} %get-tuple-element., ...), custom_call_target="tpu_custom_call" | custom-call | tf_op jit(solution)/shard_map/unpack/pallas_call | solution.py:1897
  (107 shorter events, 23.1 us)
Async XLA Ops:
  94.2 72.9 %collective-permute-start = (bf16[256,1024]{1,0:T(8,128)(2,1)}, bf16[256,1024]{1,0:T(8,128)(2,1)S(1)}, u32[]{:S(2)}, u32[]{:S(2)}) collective-permute-start(bf16[256,1024]{1,0:T(8,128)(2,1)} %constant_dynamic-slice_fusion.5), channel_id=1, source_target_pairs={{0,3},{1,0},{2,1},{3,2},{4,7},{5,4},{6,5},{7,6},{8,11},{9,8},{10,9... | collective-permute-start | bytes 1572872 | tf_op jit(solution)/shard_map/ppermute | solution.py:1916
  96.5 74.3 %collective-permute-start.1 = (bf16[256,1024]{1,0:T(8,128)(2,1)}, bf16[256,1024]{1,0:T(8,128)(2,1)S(1)}, u32[]{:S(2)}, u32[]{:S(2)}) collective-permute-start(bf16[256,1024]{1,0:T(8,128)(2,1)} %constant_dynamic-slice_fusion.5), channel_id=1, source_target_pairs={{0,2},{1,3},{2,0},{3,1},{4,6},{5,7},{6,4},{7,5},{8,10},{9,11},{10,... | collective-permute-start | bytes 1572872 | tf_op jit(solution)/shard_map/ppermute | solution.py:1916
  105.9 68.8 %collective-permute-start.2 = (bf16[256,1024]{1,0:T(8,128)(2,1)}, bf16[256,1024]{1,0:T(8,128)(2,1)}, u32[]{:S(2)}, u32[]{:S(2)}) collective-permute-start(bf16[256,1024]{1,0:T(8,128)(2,1)} %constant_dynamic-slice_fusion.5), channel_id=1, source_target_pairs={{0,1},{1,2},{2,3},{3,0},{4,5},{5,6},{6,7},{7,4},{8,9},{9,10},{10,1... | collective-permute-start | bytes 1572872 | tf_op jit(solution)/shard_map/ppermute | solution.py:1916
  113.5 9.3 %copy-start = (bf16[4096,256]{0,1:T(8,128)(2,1)}, bf16[4096,256]{0,1:T(8,128)(2,1)S(1)}, u32[]{:S(2)}) copy-start(bf16[4096,256]{0,1:T(8,128)(2,1)S(1)} %copy.67) | copy-start | bytes 6291460
  113.5 11.6 %copy-start.18 = (f32[4,16,128]{2,1,0:T(8,128)S(1)}, f32[4,16,128]{2,1,0:T(8,128)}, u32[]{:S(2)}) copy-start(f32[4,16,128]{2,1,0:T(8,128)} %get-tuple-element.142) | copy-start | bytes 98308
  113.5 12.2 %copy-start.8 = (bf16[1024,512]{1,0:T(8,128)(2,1)S(1)}, bf16[1024,512]{1,0:T(8,128)(2,1)}, u32[]{:S(2)}) copy-start(bf16[1024,512]{1,0:T(8,128)(2,1)} %get-tuple-element.144.wk) | copy-start | bytes 3145732
  123.7 67.9 %collective-permute-start.5 = (bf16[256,1024]{1,0:T(8,128)(2,1)}, bf16[256,1024]{1,0:T(8,128)(2,1)}, u32[]{:S(2)}, u32[]{:S(2)}) collective-permute-start(bf16[256,1024]{1,0:T(8,128)(2,1)} %constant_dynamic-slice_fusion.4), channel_id=1, source_target_pairs={{0,3},{1,0},{2,1},{3,2},{4,7},{5,4},{6,5},{7,6},{8,11},{9,8},{10,9... | collective-permute-start | bytes 1572872 | tf_op jit(solution)/shard_map/ppermute | solution.py:1916
  123.7 67.9 %collective-permute-start.6 = (bf16[256,1024]{1,0:T(8,128)(2,1)}, bf16[256,1024]{1,0:T(8,128)(2,1)}, u32[]{:S(2)}, u32[]{:S(2)}) collective-permute-start(bf16[256,1024]{1,0:T(8,128)(2,1)} %constant_dynamic-slice_fusion.4), channel_id=1, source_target_pairs={{0,2},{1,3},{2,0},{3,1},{4,6},{5,7},{6,4},{7,5},{8,10},{9,11},{10,... | collective-permute-start | bytes 1572872 | tf_op jit(solution)/shard_map/ppermute | solution.py:1916
  125.8 6.0 copy-start.2
  125.8 6.0 copy-start.9
  131.8 3.7 copy-start.7
  135.5 2.2 copy-start.21
  138.0 29.1 %copy-start.16 = (s32[1024]{0:T(1024)}, s32[1024]{0:T(1024)S(1)}, u32[]{:S(2)}) copy-start(s32[1024]{0:T(1024)S(1)} %pad_dynamic-slice_fusion.2) | copy-start | bytes 12292
  139.7 30.1 %copy-start.5 = (bf16[2,512,1024]{2,1,0:T(8,128)(2,1)S(1)}, bf16[2,512,1024]{2,1,0:T(8,128)(2,1)}, u32[]{:S(2)}) copy-start(bf16[2,512,1024]{2,1,0:T(8,128)(2,1)} %get-tuple-element.139.x_ref) | copy-start | bytes 6291460
  167.1 7.6 %copy-start.13 = (bf16[256,1024]{1,0:T(8,128)(2,1)}, bf16[256,1024]{1,0:T(8,128)(2,1)S(1)}, u32[]{:S(2)}) copy-start(bf16[256,1024]{1,0:T(8,128)(2,1)S(1)} %collective-permute-done) | copy-start | bytes 1572868
  167.1 29.3 %collective-permute-start.7 = (bf16[256,1024]{1,0:T(8,128)(2,1)}, bf16[256,1024]{1,0:T(8,128)(2,1)S(1)}, u32[]{:S(2)}, u32[]{:S(2)}) collective-permute-start(bf16[256,1024]{1,0:T(8,128)(2,1)} %constant_dynamic-slice_fusion.4), channel_id=1, source_target_pairs={{0,1},{1,2},{2,3},{3,0},{4,5},{5,6},{6,7},{7,4},{8,9},{9,10},{10,1... | collective-permute-start | bytes 1572872 | tf_op jit(solution)/shard_map/ppermute | solution.py:1916
  170.8 3.9 copy-start.14
  178.0 13.6 %copy-start.3 = (bf16[768,1024]{1,0:T(8,128)(2,1)}, bf16[768,1024]{1,0:T(8,128)(2,1)S(1)}, u32[]{:S(2)}) copy-start(bf16[768,1024]{1,0:T(8,128)(2,1)S(1)} %constant_dynamic-update-slice_fusion.1.refs_4_.refs_0_) | copy-start | bytes 4718596
  178.0 55.4 %collective-permute-start.3 = (bf16[768,1024]{1,0:T(8,128)(2,1)S(1)}, bf16[768,1024]{1,0:T(8,128)(2,1)}, u32[]{:S(2)}, u32[]{:S(2)}) collective-permute-start(bf16[768,1024]{1,0:T(8,128)(2,1)S(1)} %constant_dynamic-update-slice_fusion.1.refs_4_.refs_0_), channel_id=1, source_target_pairs={{0,8},{8,0},{16,24},{24,16},{1,9},{9,1},{17,25},{25,17},{2,10},{10... | collective-permute-start | bytes 4718600 | tf_op jit(solution)/shard_map/ppermute | solution.py:1919
  179.5 53.9 %collective-permute-start.4 = (bf16[768,1024]{1,0:T(8,128)(2,1)S(1)}, bf16[768,1024]{1,0:T(8,128)(2,1)S(1)}, u32[]{:S(2)}, u32[]{:S(2)}) collective-permute-start(bf16[768,1024]{1,0:T(8,128)(2,1)S(1)} %constant_dynamic-update-slice_fusion.1.refs_4_.refs_0_), channel_id=1, source_target_pairs={{0,16},{8,24},{16,0},{24,8},{1,17},{9,25},{17,1},{25,9},{2,18},{10... | collective-permute-start | bytes 4718600 | tf_op jit(solution)/shard_map/ppermute | solution.py:1919
  191.5 12.5 %copy-start.22 = (s32[1,4]{1,0:T(1,128)S(1)}, s32[1,4]{1,0:T(1,128)}, u32[]{:S(2)}) copy-start(s32[1,4]{1,0:T(1,128)} %param.33) | copy-start | bytes 52
  201.0 57.6 %collective-permute-start.8 = (bf16[768,1024]{1,0:T(8,128)(2,1)}, bf16[768,1024]{1,0:T(8,128)(2,1)}, u32[]{:S(2)}, u32[]{:S(2)}) collective-permute-start(bf16[768,1024]{1,0:T(8,128)(2,1)} %constant_dynamic-update-slice_fusion.4.refs_5_.refs_4_), channel_id=1, source_target_pairs={{0,8},{8,0},{16,24},{24,16},{1,9},{9,1},{17,25},{25,17},{2,10},{10... | collective-permute-start | bytes 4718600 | tf_op jit(solution)/shard_map/ppermute | solution.py:1919
  202.5 56.1 %collective-permute-start.9 = (bf16[768,1024]{1,0:T(8,128)(2,1)}, bf16[768,1024]{1,0:T(8,128)(2,1)}, u32[]{:S(2)}, u32[]{:S(2)}) collective-permute-start(bf16[768,1024]{1,0:T(8,128)(2,1)} %constant_dynamic-update-slice_fusion.4.refs_5_.refs_4_), channel_id=1, source_target_pairs={{0,16},{8,24},{16,0},{24,8},{1,17},{9,25},{17,1},{25,9},{2,18},{10... | collective-permute-start | bytes 4718600 | tf_op jit(solution)/shard_map/ppermute | solution.py:1919
  205.5 4.2 copy-start.6
  205.5 4.2 copy-start.10
  233.4 10.3 %copy-start.4 = (bf16[768,1024]{1,0:T(8,128)(2,1)}, bf16[768,1024]{1,0:T(8,128)(2,1)S(1)}, u32[]{:S(2)}) copy-start(bf16[768,1024]{1,0:T(8,128)(2,1)S(1)} %collective-permute-done.4.refs_5_.refs_2_) | copy-start | bytes 4718596
  243.7 15.9 %copy-start.17 = (s32[1024]{0:T(1024)S(1)}, s32[1024]{0:T(1024)}, u32[]{:S(2)}) copy-start(s32[1024]{0:T(1024)} %convert_reduce_fusion.1) | copy-start | bytes 12292
  243.8 16.9 %copy-start.15 = (s32[2048]{0:T(1024)S(1)}, s32[2048]{0:T(1024)}, u32[]{:S(2)}) copy-start(s32[2048]{0:T(1024)} %pad_dynamic-slice_fusion.3) | copy-start | bytes 24580
  243.8 18.9 %copy-start.1 = (bf16[1024,1024]{1,0:T(8,128)(2,1)S(1)}, bf16[1024,1024]{1,0:T(8,128)(2,1)}, u32[]{:S(2)}) copy-start(bf16[1024,1024]{1,0:T(8,128)(2,1)} %get-tuple-element.163.refs_0_) | copy-start | bytes 6291460
  258.6 45.6 %collective-permute-start.11 = (bf16[768,1024]{1,0:T(8,128)(2,1)}, bf16[768,1024]{1,0:T(8,128)(2,1)}, u32[]{:S(2)}, u32[]{:S(2)}) collective-permute-start(bf16[768,1024]{1,0:T(8,128)(2,1)} %collective-permute-done.9.refs_7_.refs_6_), channel_id=1, source_target_pairs={{0,8},{8,0},{16,24},{24,16},{1,9},{9,1},{17,25},{25,17},{2,10},{10... | collective-permute-start | bytes 4718600 | tf_op jit(solution)/shard_map/ppermute | solution.py:1919
  259.1 45.0 %collective-permute-start.10 = (bf16[768,1024]{1,0:T(8,128)(2,1)}, bf16[768,1024]{1,0:T(8,128)(2,1)}, u32[]{:S(2)}, u32[]{:S(2)}) collective-permute-start(bf16[768,1024]{1,0:T(8,128)(2,1)} %collective-permute-done.3.refs_4_.refs_1_), channel_id=1, source_target_pairs={{0,16},{8,24},{16,0},{24,8},{1,17},{9,25},{17,1},{25,9},{2,18},{10... | collective-permute-start | bytes 4718600 | tf_op jit(solution)/shard_map/ppermute | solution.py:1919
  449.7 13.8 %copy-start.20 = (f32[8,1024]{1,0:T(8,128)S(1)}, f32[8,1024]{1,0:T(8,128)}, u32[]{:S(2)}) copy-start(f32[8,1024]{1,0:T(8,128)} %get-tuple-element.224) | copy-start | bytes 98308
  535.1 98.6 %copy-start.19 = (f32[4,1,1024]{2,1,0:T(1,128)S(1)}, f32[4,1,1024]{2,1,0:T(1,128)}, u32[]{:S(2)}) copy-start(f32[4,1,1024]{2,1,0:T(1,128)} %get-tuple-element.227) | copy-start | bytes 49156
  720.3 8.6 %copy-start.11 = (bf16[2048,256]{1,0:T(8,128)(2,1)S(1)}, bf16[2048,256]{1,0:T(8,128)(2,1)}, u32[]{:S(2)}) copy-start(bf16[2048,256]{1,0:T(8,128)(2,1)} %get-tuple-element.314) | copy-start | bytes 3145732
  728.9 1.3 copy-start.12
